TPU v7x, 32 devices: a whole 2x2x4 slice. The times are simulated.
32 devices in a mesh: dp: 8 (over y, x, core), mp: 4 (over z).
Axes of the slice: x: 2, y: 2, z: 4, core: 2. Of those that a mesh axis runs over, the one named last changes fastest.
Arguments:
- frames: bfloat16 [8, 1024, 1024], P('dp', 'mp'), may hold values from -6 to 6
- cotangent: bfloat16 [8, 1024, 1024], P('dp', 'mp'), may hold values from -6 to 6
- segment_ids: int32 [8, 1024], P('dp'), may hold values from 0 to 5, as said below
- owners: int32 [8], replicated, may hold values from 0 to 7, each once
- rot_model: float32 [1024, 128], P('dp'), as said below
- rot_hidden: float32 [4096, 1024], P('mp'), as said below
- rot_inner: float32 [1024, 256], P('mp'), as said below
- inner_weight: float32 [5, 1024, 1024], P(None, 'dp', 'mp'), may hold values from -0.1875 to 0.1875
- inner_first: float32 [5, 1024, 1024], P(None, 'dp', 'mp')
- inner_second: float32 [5, 1024, 1024], P(None, 'dp', 'mp'), as said below
- inner_average: float32 [5, 1024, 1024], P(None, 'dp', 'mp'), may hold values from -0.1875 to 0.1875
- expand_weight: float32 [2, 1024, 4096], P(None, 'dp', 'mp'), may hold values from -0.1875 to 0.1875
- expand_first: float32 [2, 1024, 4096], P(None, 'dp', 'mp')
- expand_second: float32 [2, 1024, 4096], P(None, 'dp', 'mp'), as said below
- expand_average: float32 [2, 1024, 4096], P(None, 'dp', 'mp'), may hold values from -0.1875 to 0.1875
- output_weight: float32 [2, 1024, 1024], P(None, 'mp', 'dp')
- output_first: float32 [2, 1024, 1024], P(None, 'mp', 'dp')
- output_second: float32 [2, 1024, 1024], P(None, 'mp', 'dp'), as said below
- output_average: float32 [2, 1024, 1024], P(None, 'mp', 'dp')
- shrink_weight: float32 [2, 4096, 1024], P(None, 'mp', 'dp'), may hold values from -0.09375 to 0.09375
- shrink_first: float32 [2, 4096, 1024], P(None, 'mp', 'dp')
- shrink_second: float32 [2, 4096, 1024], P(None, 'mp', 'dp'), as said below
- shrink_average: float32 [2, 4096, 1024], P(None, 'mp', 'dp'), may hold values from -0.09375 to 0.09375
- small_weight: float32 [17, 1024], P(None, ('dp', 'mp'))
- small_first: float32 [17, 1024], P(None, ('dp', 'mp'))
- small_second: float32 [17, 1024], P(None, ('dp', 'mp')), as said below
- small_average: float32 [17, 1024], P(None, ('dp', 'mp'))
Outputs:
- block_output: bfloat16 [8, 1024, 1024], P('dp', 'mp')
- input_grad: bfloat16 [8, 1024, 1024], P('dp', 'mp')
- new_inner_first: float32 [5, 1024, 1024], P(None, 'dp', 'mp')
- new_inner_second: float32 [5, 1024, 1024], P(None, 'dp', 'mp')
- new_inner_weight: float32 [5, 1024, 1024], P(None, 'dp', 'mp')
- new_inner_average: float32 [5, 1024, 1024], P(None, 'dp', 'mp')
- new_expand_first: float32 [2, 1024, 4096], P(None, 'dp', 'mp')
- new_expand_second: float32 [2, 1024, 4096], P(None, 'dp', 'mp')
- new_expand_weight: float32 [2, 1024, 4096], P(None, 'dp', 'mp')
- new_expand_average: float32 [2, 1024, 4096], P(None, 'dp', 'mp')
- new_output_first: float32 [2, 1024, 1024], P(None, 'mp', 'dp')
- new_output_second: float32 [2, 1024, 1024], P(None, 'mp', 'dp')
- new_output_weight: float32 [2, 1024, 1024], P(None, 'mp', 'dp')
- new_output_average: float32 [2, 1024, 1024], P(None, 'mp', 'dp')
- new_shrink_first: float32 [2, 4096, 1024], P(None, 'mp', 'dp')
- new_shrink_second: float32 [2, 4096, 1024], P(None, 'mp', 'dp')
- new_shrink_weight: float32 [2, 4096, 1024], P(None, 'mp', 'dp')
- new_shrink_average: float32 [2, 4096, 1024], P(None, 'mp', 'dp')
- new_small_first: float32 [17, 1024], P(None, ('dp', 'mp'))
- new_small_second: float32 [17, 1024], P(None, ('dp', 'mp'))
- new_small_weight: float32 [17, 1024], P(None, ('dp', 'mp'))
- new_small_average: float32 [17, 1024], P(None, ('dp', 'mp'))
Inputs may be any that keep to these rules, and one draw needn't show every extreme that they name: `segment_ids`: every row has exactly 6 segments: its ids start at 0 and rise by one at each boundary. In each aligned block of 1 row one row, drawn from the seed, has each of its boundaries within its first 64 frames or within its last 64 frames, at least one in each, so that one of its segments covers the rest of the row; the other rows' boundaries lie anywhere. `owners`: A permutation. `rot_model`: each aligned block of 128 rows is an orthogonal matrix. `rot_hidden`: each aligned block of 1024 rows is an orthogonal matrix. `rot_inner`: each aligned block of 256 rows is an orthogonal matrix. `inner_second`: Positive. `expand_second`: Positive. `output_second`: Positive. `shrink_second`: Positive. `small_second`: Positive.
All inputs are finite; a program needn't handle non-finite values.
Results may differ from a plain program's by a relative error of at most 0.025.
Values may be sent and summed in bfloat16 or wider, within the bound.
No kernel may reach another device: no remote copies, remote signals or barrier semaphores. Data moves between devices by JAX's collectives and lax.ppermute only.
A program may use at most 192 MiB of HBM per device.

v0:
```python
from functools import partial

import jax
import jax.numpy as jnp
from jax import lax
from jax.sharding import PartitionSpec as P

HEAD_DIM = 128
KERNEL = 5
STEP = 10


NORM_EPS = 1e-05
MASKED = -1e30
BETA_ONE = 0.9
BETA_TWO = 0.95
ADAM_EPS = 1e-08
DECAY = 0.01
EMA_DECAY = 0.7
RATE_INNER = 0.03
RATE_EXPAND = 0.03
RATE_OUTPUT = 0.25
RATE_SHRINK = 0.015
RATE_SMALL = 0.5
HIGHEST = lax.Precision.HIGHEST


def arrange(stored, order, block_axis):
    layout = stored.shape
    blocks = order.shape[0]
    blocked = (
        layout[:block_axis] + (blocks, layout[block_axis] // blocks) + layout[block_axis + 1 :]
    )
    return jnp.take(stored.reshape(blocked), order, axis=block_axis).reshape(layout)


def norm_forward(stream, norm_gain, norm_bias):
    centre = jnp.mean(stream, axis=-1, keepdims=True)
    centred = stream - centre
    inverse = lax.rsqrt(jnp.mean(centred * centred, axis=-1, keepdims=True) + NORM_EPS)
    unit_rows = centred * inverse
    return (unit_rows * norm_gain + norm_bias, unit_rows, inverse)


def norm_backward(upstream, unit_rows, inverse, norm_gain):
    scaled = upstream * norm_gain
    through = inverse * (
        scaled
        - jnp.mean(scaled, axis=-1, keepdims=True)
        - unit_rows * jnp.mean(scaled * unit_rows, axis=-1, keepdims=True)
    )
    return (through, jnp.sum(upstream * unit_rows, axis=(0, 1)), jnp.sum(upstream, axis=(0, 1)))


def project(rows_in, matrix):
    return jnp.einsum("rld,dc->rlc", rows_in, matrix, preferred_element_type=jnp.float32)


def project_back(rows_in, matrix):
    return jnp.einsum("rlc,dc->rld", rows_in, matrix, preferred_element_type=jnp.float32)


def weight_grad(left_rows, right_rows):
    return jnp.einsum("rld,rlc->dc", left_rows, right_rows, preferred_element_type=jnp.float32)


def spread(local_rows):
    return lax.all_gather(local_rows, "mp", axis=1, tiled=True)


def collect(partial_sum):
    return lax.psum_scatter(
        partial_sum.astype(jnp.bfloat16), "mp", scatter_dimension=1, tiled=True
    ).astype(jnp.float32)


def spread_back(local_rows):
    return lax.all_gather(local_rows, "mp", axis=1, tiled=True)


def collect_back(partial_sum):
    return lax.psum_scatter(
        partial_sum.astype(jnp.bfloat16), "mp", scatter_dimension=1, tiled=True
    ).astype(jnp.float32)


def shift_rows(values, offset):
    radius = KERNEL // 2
    padded = jnp.pad(values, ((0, 0), (radius, radius), (0, 0)))
    return lax.slice_in_dim(padded, radius + offset, radius + offset + values.shape[1], axis=1)


def tap_windows(segments):
    radius = KERNEL // 2
    padded_ids = jnp.pad(segments, ((0, 0), (radius, radius)), constant_values=-1)
    length = segments.shape[1]
    return [
        (padded_ids[:, offset : offset + length] == segments).astype(jnp.float32)[:, :, None]
        for offset in range(KERNEL)
    ]


def feed_forward(stream, norm_gain, norm_bias, weight_in, weight_out):
    normed, unit_rows, inverse = norm_forward(stream, norm_gain, norm_bias)
    local_rows = normed.astype(jnp.bfloat16)
    full_rows = spread(local_rows)
    preact = project(full_rows, weight_in)
    hidden = jax.nn.silu(preact).astype(jnp.bfloat16)
    branch = collect(project(hidden, weight_out))
    return (stream + 0.5 * branch, (full_rows, unit_rows, inverse, preact))


def feed_back(gradient, kept_state, norm_gain, weight_in, weight_out):
    stored, unit_rows, inverse, preact = kept_state
    incoming = spread_back((0.5 * gradient).astype(jnp.bfloat16))
    hidden = jax.nn.silu(preact).astype(jnp.bfloat16)
    grad_out = weight_grad(hidden, incoming)
    sigmoid_pre = jax.nn.sigmoid(preact)
    grad_hidden = project_back(incoming, weight_out)
    grad_pre = (grad_hidden * sigmoid_pre * (1.0 + preact * (1.0 - sigmoid_pre))).astype(
        jnp.bfloat16
    )
    grad_in = weight_grad(stored, grad_pre)
    through, grad_gain, grad_bias = norm_backward(
        collect_back(project_back(grad_pre, weight_in)), unit_rows, inverse, norm_gain
    )
    return (gradient + through, grad_in, grad_out, grad_gain, grad_bias)


def split_heads(values):
    return values.astype(jnp.bfloat16).reshape(values.shape[0], values.shape[1], -1, HEAD_DIM)


def merge_heads(values):
    return values.reshape(values.shape[0], values.shape[1], -1)


def score_rows(queries, keyset, matching):
    scores = jnp.einsum(
        "rqhd,rkhd->rhqk", queries, keyset, preferred_element_type=jnp.float32
    ) * HEAD_DIM ** (-0.5)
    return jnp.where(matching[:, None], scores, MASKED)


def attention(stream, norm_gain, norm_bias, narrow, weight_out, matching):
    normed, unit_rows, inverse = norm_forward(stream, norm_gain, norm_bias)
    local_rows = normed.astype(jnp.bfloat16)
    full_rows = spread(local_rows)
    queries = split_heads(project(full_rows, narrow[0]))
    keyset = split_heads(project(full_rows, narrow[1]))
    values = split_heads(project(full_rows, narrow[2]))
    scores = score_rows(queries, keyset, matching)
    row_max = jnp.max(scores, axis=-1, keepdims=True)
    weights = jnp.exp(scores - row_max)
    totals = jnp.sum(weights, axis=-1, keepdims=True)
    log_total = row_max + jnp.log(totals)
    attended = (weights / totals).astype(jnp.bfloat16)
    mixture = jnp.einsum("rhqk,rkhd->rqhd", attended, values, preferred_element_type=jnp.float32)
    mixture = merge_heads(mixture.astype(jnp.bfloat16))
    branch = collect(project(mixture, weight_out))
    return (
        stream + branch,
        (full_rows, unit_rows, inverse, queries, keyset, values, mixture, log_total),
    )


def attention_back(gradient, kept_state, norm_gain, narrow, weight_out, matching):
    stored, unit_rows, inverse, queries, keyset, values, mixture, log_total = kept_state
    incoming = spread_back(gradient.astype(jnp.bfloat16))
    grad_out = weight_grad(mixture, incoming)
    grad_mix = project_back(incoming, weight_out).astype(jnp.bfloat16).reshape(queries.shape)
    attended = jnp.exp(score_rows(queries, keyset, matching) - log_total)
    grad_values = jnp.einsum(
        "rhqk,rqhd->rkhd",
        attended.astype(jnp.bfloat16),
        grad_mix,
        preferred_element_type=jnp.float32,
    ).astype(jnp.bfloat16)
    grad_attended = jnp.einsum(
        "rqhd,rkhd->rhqk", grad_mix, values, preferred_element_type=jnp.float32
    )
    grad_scores = (
        attended * (grad_attended - jnp.sum(grad_attended * attended, axis=-1, keepdims=True))
    ).astype(jnp.bfloat16)
    factor = HEAD_DIM ** (-0.5)
    grad_queries = (
        jnp.einsum("rhqk,rkhd->rqhd", grad_scores, keyset, preferred_element_type=jnp.float32)
        * factor
    ).astype(jnp.bfloat16)
    grad_keyset = (
        jnp.einsum("rhqk,rqhd->rkhd", grad_scores, queries, preferred_element_type=jnp.float32)
        * factor
    ).astype(jnp.bfloat16)
    pieces = [merge_heads(grad_queries), merge_heads(grad_keyset), merge_heads(grad_values)]
    grad_in = jnp.stack([weight_grad(stored, member) for member in pieces])
    partial_sum = (
        project_back(pieces[0], narrow[0])
        + project_back(pieces[1], narrow[1])
        + project_back(pieces[2], narrow[2])
    )
    through, grad_gain, grad_bias = norm_backward(
        collect_back(partial_sum), unit_rows, inverse, norm_gain
    )
    return (gradient + through, grad_in, grad_out, grad_gain, grad_bias)


def depth_conv(gated_rows, depthwise, windows):
    radius = KERNEL // 2
    summed = jnp.zeros_like(gated_rows)
    for offset in range(KERNEL):
        summed = (
            summed + shift_rows(gated_rows, offset - radius) * windows[offset] * depthwise[offset]
        )
    return summed


def convolve(stream, norm_gain, norm_bias, narrow, weight_out, depthwise, windows):
    normed, unit_rows, inverse = norm_forward(stream, norm_gain, norm_bias)
    local_rows = normed.astype(jnp.bfloat16)
    full_rows = spread(local_rows)
    content = project(full_rows, narrow[3])
    opening = project(full_rows, narrow[4])
    summed = depth_conv(content * jax.nn.sigmoid(opening), depthwise, windows)
    normal_conv = summed * depthwise[KERNEL] + depthwise[KERNEL + 1]
    activated = jax.nn.silu(normal_conv).astype(jnp.bfloat16)
    branch = collect(project(activated, weight_out))
    return (stream + branch, (full_rows, unit_rows, inverse, content, opening, summed))


def convolve_back(gradient, kept_state, norm_gain, narrow, weight_out, depthwise, windows):
    stored, unit_rows, inverse, content, opening, summed = kept_state
    incoming = spread_back(gradient.astype(jnp.bfloat16))
    normal_conv = summed * depthwise[KERNEL] + depthwise[KERNEL + 1]
    sigmoid_conv = jax.nn.sigmoid(normal_conv)
    activated = jax.nn.silu(normal_conv).astype(jnp.bfloat16)
    grad_out = weight_grad(activated, incoming)
    grad_normal = (
        project_back(incoming, weight_out)
        * sigmoid_conv
        * (1.0 + normal_conv * (1.0 - sigmoid_conv))
    )
    grad_summed = grad_normal * depthwise[KERNEL]
    radius = KERNEL // 2
    gate_open = jax.nn.sigmoid(opening)
    gated_rows = content * gate_open
    kernel_rows = []
    grad_gated = jnp.zeros_like(gated_rows)
    for offset in range(KERNEL):
        masked = grad_summed * windows[offset]
        kernel_rows.append(jnp.sum(masked * shift_rows(gated_rows, offset - radius), axis=(0, 1)))
        grad_gated = grad_gated + shift_rows(masked * depthwise[offset], radius - offset)
    kernel_rows.append(jnp.sum(grad_normal * summed, axis=(0, 1)))
    kernel_rows.append(jnp.sum(grad_normal, axis=(0, 1)))
    grad_content = (grad_gated * gate_open).astype(jnp.bfloat16)
    grad_opening = (grad_gated * content * gate_open * (1.0 - gate_open)).astype(jnp.bfloat16)
    grad_in = jnp.stack([weight_grad(stored, grad_content), weight_grad(stored, grad_opening)])
    partial_sum = project_back(grad_content, narrow[3]) + project_back(grad_opening, narrow[4])
    through, grad_gain, grad_bias = norm_backward(
        collect_back(partial_sum), unit_rows, inverse, norm_gain
    )
    return (gradient + through, grad_in, grad_out, grad_gain, grad_bias, jnp.stack(kernel_rows))


def rotate_entry(gradients, left, right):
    turned = jnp.einsum("src,rx->sxc", gradients, left, precision=HIGHEST)
    return jnp.einsum("sxc,cy->sxy", turned, right, precision=HIGHEST)


def restore_entry(steps, left, right):
    turned = jnp.einsum("sxy,rx->sry", steps, left, precision=HIGHEST)
    return jnp.einsum("sry,cy->src", turned, right, precision=HIGHEST)


def rotate_exit(gradients, left, right):
    turned = jnp.einsum("scr,cy->syr", gradients, right, precision=HIGHEST)
    return jnp.einsum("syr,rx->syx", turned, left, precision=HIGHEST)


def restore_exit(steps, left, right):
    turned = jnp.einsum("syx,cy->scx", steps, right, precision=HIGHEST)
    return jnp.einsum("scx,rx->scr", turned, left, precision=HIGHEST)


def keep_same(steps):
    return steps


def adam_update(turned, weight, first, second, average, rate, restore):
    first_new = BETA_ONE * first + (1.0 - BETA_ONE) * turned
    second_new = BETA_TWO * second + (1.0 - BETA_TWO) * turned * turned
    normal_step = (
        first_new
        / (1.0 - BETA_ONE**STEP)
        / (jnp.sqrt(second_new / (1.0 - BETA_TWO**STEP)) + ADAM_EPS)
    )
    weight_new = weight - rate * (restore(normal_step) + DECAY * weight)
    average_new = EMA_DECAY * average + (1.0 - EMA_DECAY) * weight_new
    return (first_new, second_new, weight_new, average_new)


def shards(
    frames,
    cotangent,
    segment_ids,
    owners,
    rot_model,
    rot_hidden,
    rot_inner,
    inner_weight,
    inner_first,
    inner_second,
    inner_average,
    expand_weight,
    expand_first,
    expand_second,
    expand_average,
    output_weight,
    output_first,
    output_second,
    output_average,
    shrink_weight,
    shrink_first,
    shrink_second,
    shrink_average,
    small_weight,
    small_first,
    small_second,
    small_average,
):
    gathered = (
        lax.all_gather(inner_weight.astype(jnp.bfloat16), "dp", axis=1, tiled=True),
        lax.all_gather(expand_weight.astype(jnp.bfloat16), "dp", axis=1, tiled=True),
        lax.all_gather(output_weight.astype(jnp.bfloat16), "dp", axis=2, tiled=True),
        lax.all_gather(shrink_weight.astype(jnp.bfloat16), "dp", axis=2, tiled=True),
    )
    narrow = arrange(gathered[0], owners, 1)
    expand = arrange(gathered[1], owners, 1)
    output = arrange(gathered[2], owners, 2)
    shrink = arrange(gathered[3], owners, 2)
    small = lax.all_gather(
        small_weight.astype(jnp.bfloat16), ("dp", "mp"), axis=1, tiled=True
    ).astype(jnp.float32)
    slots = jnp.arange(owners.shape[0], dtype=jnp.int32)
    inverse_order = jnp.sum(jnp.where(owners[None, :] == slots[:, None], slots[None, :], 0), axis=1)
    channels = narrow.shape[2]
    narrow_index = lax.axis_index("mp")
    depthwise = lax.dynamic_slice_in_dim(small[10:], narrow_index * channels, channels, axis=1)
    matching = segment_ids[:, :, None] == segment_ids[:, None, :]
    windows = tap_windows(segment_ids)
    stream = frames.astype(jnp.float32)
    stream, early_state = feed_forward(stream, small[0], small[1], expand[0], shrink[0])
    stream, attend_state = attention(stream, small[2], small[3], narrow, output[0], matching)
    stream, conv_state = convolve(stream, small[4], small[5], narrow, output[1], depthwise, windows)
    stream, late_state = feed_forward(stream, small[6], small[7], expand[1], shrink[1])
    result, unit_final, inverse_final = norm_forward(stream, small[8], small[9])
    gradient, final_gain, final_bias = norm_backward(
        cotangent.astype(jnp.float32), unit_final, inverse_final, small[8]
    )
    gradient, late_in, late_out, late_gain, late_bias = feed_back(
        gradient, late_state, small[6], expand[1], shrink[1]
    )
    gradient, conv_in, conv_out, conv_gain, conv_bias, depth_grad = convolve_back(
        gradient, conv_state, small[4], narrow, output[1], depthwise, windows
    )
    gradient, attend_in, attend_out, attend_gain, attend_bias = attention_back(
        gradient, attend_state, small[2], narrow, output[0], matching
    )
    gradient, early_in, early_out, early_gain, early_bias = feed_back(
        gradient, early_state, small[0], expand[0], shrink[0]
    )
    inner_grad, expand_grad, output_grad, shrink_grad = (
        lax.psum_scatter(
            arrange(jnp.concatenate([attend_in, conv_in], axis=0), inverse_order, 1).astype(
                jnp.bfloat16
            ),
            "dp",
            scatter_dimension=1,
            tiled=True,
        ).astype(jnp.float32),
        lax.psum_scatter(
            arrange(jnp.stack([early_in, late_in]), inverse_order, 1).astype(jnp.bfloat16),
            "dp",
            scatter_dimension=1,
            tiled=True,
        ).astype(jnp.float32),
        lax.psum_scatter(
            arrange(jnp.stack([attend_out, conv_out]), inverse_order, 2).astype(jnp.bfloat16),
            "dp",
            scatter_dimension=2,
            tiled=True,
        ).astype(jnp.float32),
        lax.psum_scatter(
            arrange(jnp.stack([early_out, late_out]), inverse_order, 2).astype(jnp.bfloat16),
            "dp",
            scatter_dimension=2,
            tiled=True,
        ).astype(jnp.float32),
    )
    norm_rows = jnp.stack(
        [
            early_gain,
            early_bias,
            attend_gain,
            attend_bias,
            conv_gain,
            conv_bias,
            late_gain,
            late_bias,
            final_gain,
            final_bias,
        ]
    )
    depth_rows = lax.dynamic_update_slice_in_dim(
        jnp.zeros((KERNEL + 2, norm_rows.shape[1]), jnp.float32),
        depth_grad,
        narrow_index * channels,
        axis=1,
    )
    small_grad = lax.psum_scatter(
        jnp.concatenate([norm_rows, depth_rows], axis=0),
        ("dp", "mp"),
        scatter_dimension=1,
        tiled=True,
    )
    new_inner = adam_update(
        rotate_entry(inner_grad, rot_model, rot_inner),
        inner_weight,
        inner_first,
        inner_second,
        inner_average,
        RATE_INNER,
        partial(restore_entry, left=rot_model, right=rot_inner),
    )
    new_expand = adam_update(
        rotate_entry(expand_grad, rot_model, rot_hidden),
        expand_weight,
        expand_first,
        expand_second,
        expand_average,
        RATE_EXPAND,
        partial(restore_entry, left=rot_model, right=rot_hidden),
    )
    new_output = adam_update(
        rotate_exit(output_grad, rot_model, rot_inner),
        output_weight,
        output_first,
        output_second,
        output_average,
        RATE_OUTPUT,
        partial(restore_exit, left=rot_model, right=rot_inner),
    )
    new_shrink = adam_update(
        rotate_exit(shrink_grad, rot_model, rot_hidden),
        shrink_weight,
        shrink_first,
        shrink_second,
        shrink_average,
        RATE_SHRINK,
        partial(restore_exit, left=rot_model, right=rot_hidden),
    )
    new_small = adam_update(
        small_grad, small_weight, small_first, small_second, small_average, RATE_SMALL, keep_same
    )
    return (
        (result.astype(jnp.bfloat16), gradient.astype(jnp.bfloat16))
        + new_inner
        + new_expand
        + new_output
        + new_shrink
        + new_small
    )


def solution(mesh):
    return jax.shard_map(
        shards,
        mesh=mesh,
        in_specs=(
            P("dp", "mp", None),
            P("dp", "mp", None),
            P("dp", None),
            P(),
            P("dp", None),
            P("mp", None),
            P("mp", None),
            P(None, "dp", "mp"),
            P(None, "dp", "mp"),
            P(None, "dp", "mp"),
            P(None, "dp", "mp"),
            P(None, "dp", "mp"),
            P(None, "dp", "mp"),
            P(None, "dp", "mp"),
            P(None, "dp", "mp"),
            P(None, "mp", "dp"),
            P(None, "mp", "dp"),
            P(None, "mp", "dp"),
            P(None, "mp", "dp"),
            P(None, "mp", "dp"),
            P(None, "mp", "dp"),
            P(None, "mp", "dp"),
            P(None, "mp", "dp"),
            P(None, ("dp", "mp")),
            P(None, ("dp", "mp")),
            P(None, ("dp", "mp")),
            P(None, ("dp", "mp")),
        ),
        out_specs=(
            P("dp", "mp", None),
            P("dp", "mp", None),
            P(None, "dp", "mp"),
            P(None, "dp", "mp"),
            P(None, "dp", "mp"),
            P(None, "dp", "mp"),
            P(None, "dp", "mp"),
            P(None, "dp", "mp"),
            P(None, "dp", "mp"),
            P(None, "dp", "mp"),
            P(None, "mp", "dp"),
            P(None, "mp", "dp"),
            P(None, "mp", "dp"),
            P(None, "mp", "dp"),
            P(None, "mp", "dp"),
            P(None, "mp", "dp"),
            P(None, "mp", "dp"),
            P(None, "mp", "dp"),
            P(None, ("dp", "mp")),
            P(None, ("dp", "mp")),
            P(None, ("dp", "mp")),
            P(None, ("dp", "mp")),
        ),
        check_vma=False,
    )
```

profile of v0, /device:TPU:0, one launch (start us, length us, event | category | flops | bytes accessed | tf_op | source)
XLA Modules:
  0.0 1337.6 jit_solution(6664641187684516522)
XLA Ops:
  10.7 72.0 %all-gather = bf16[32,32,17]{1,2,0:T(8,128)(2,1)S(1)} all-gather(bf16[1,32,17]{1,2,0:T(8,128)(2,1)S(1)} %convert_bitcast_fusion.6), channel_id=1, replica_groups=mesh['dp'=8,'mp'=4] {'dp','mp'}, dimensions={0}, use_global_device_ids=true | all-gather | bytes 35904 | tf_op jit(solution)/shard_map/all_gather | solution.py:340
  85.8 6.3 copy.269
  92.1 5.0 gather_fusion
  97.1 5.5 gather_fusion.1
  102.6 2.7 select_bitcast_fusion
  106.8 2.6 copy.270
  109.5 2.7 select_bitcast_fusion.1
  113.9 23.8 %all-gather.14.cloned.1.call-done = bf16[1,1024,1024]{2,1,0:T(8,128)(2,1)} async-done(((bf16[1,256,1024]{2,1,0:T(8,128)(2,1)}), bf16[1,1024,1024]{2,1,0:T(8,128)(2,1)}) %all-gather.14.cloned.1.call-update) | async-done | bytes 2097168 | tf_op jit(solution)/shard_map/all_gather | solution.py:68
  137.8 4.1 fusion.39
  143.9 3.7 convert_bitcast_fusion.5
  149.5 40.8 %reduce-scatter.18.cloned.1.call-done = bf16[1,256,1024]{2,1,0:T(8,128)(2,1)} async-done(((bf16[1,1024,1024]{2,1,0:T(8,128)(2,1)}), bf16[1,256,1024]{2,1,0:T(8,128)(2,1)}) %reduce-scatter.18.cloned.1.call-update) | async-done | bytes 524304 | tf_op jit(solution)/shard_map/reduce_scatter | solution.py:72
  197.4 18.3 %all-gather.24.cloned.1.call-done = bf16[2,256,1024]{1,2,0:T(8,128)(2,1)} async-done(((bf16[2,256,128]{1,2,0:T(8,128)(2,1)}), bf16[2,256,1024]{1,2,0:T(8,128)(2,1)}) %all-gather.24.cloned.1.call-update) | async-done | bytes 1048592 | tf_op jit(solution)/shard_map/all_gather | solution.py:333
  220.2 28.2 %all-gather.22.cloned.1.call-done = bf16[5,1024,256]{2,1,0:T(8,128)(2,1)} async-done(((bf16[5,128,256]{2,1,0:T(8,128)(2,1)}), bf16[5,1024,256]{2,1,0:T(8,128)(2,1)}) %all-gather.22.cloned.1.call-update) | async-done | bytes 2621456 | tf_op jit(solution)/shard_map/all_gather | solution.py:331
  251.4 45.2 %all-gather.20.cloned.1.call-done = bf16[1,1024,1024]{2,1,0:T(8,128)(2,1)} async-done(((bf16[1,256,1024]{2,1,0:T(8,128)(2,1)}), bf16[1,1024,1024]{2,1,0:T(8,128)(2,1)}) %all-gather.20.cloned.1.call-update) | async-done | bytes 2097168 | tf_op jit(solution)/shard_map/all_gather | solution.py:68
  309.9 42.7 %reduce-scatter.20.cloned.1.call-done = bf16[1,256,1024]{2,1,0:T(8,128)(2,1)} async-done(((bf16[1,1024,1024]{2,1,0:T(8,128)(2,1)}), bf16[1,256,1024]{2,1,0:T(8,128)(2,1)}) %reduce-scatter.20.cloned.1.call-update) | async-done | bytes 524304 | tf_op jit(solution)/shard_map/reduce_scatter | solution.py:72
  359.2 42.0 %all-gather.26.cloned.1.call-done = bf16[1,1024,1024]{2,1,0:T(8,128)(2,1)} async-done(((bf16[1,256,1024]{2,1,0:T(8,128)(2,1)}), bf16[1,1024,1024]{2,1,0:T(8,128)(2,1)}) %all-gather.26.cloned.1.call-update) | async-done | bytes 2097168 | tf_op jit(solution)/shard_map/all_gather | solution.py:68
  408.9 42.7 %reduce-scatter.22.cloned.1.call-done = bf16[1,256,1024]{2,1,0:T(8,128)(2,1)} async-done(((bf16[1,1024,1024]{2,1,0:T(8,128)(2,1)}), bf16[1,256,1024]{2,1,0:T(8,128)(2,1)}) %reduce-scatter.22.cloned.1.call-update) | async-done | bytes 524304 | tf_op jit(solution)/shard_map/reduce_scatter | solution.py:72
  454.2 3.9 copy.278
  458.1 41.4 %all-gather.28.cloned.1.call-done = bf16[1,1024,1024]{2,1,0:T(8,128)(2,1)} async-done(((bf16[1,256,1024]{2,1,0:T(8,128)(2,1)}), bf16[1,1024,1024]{2,1,0:T(8,128)(2,1)}) %all-gather.28.cloned.1.call-update) | async-done | bytes 2097168 | tf_op jit(solution)/shard_map/all_gather | solution.py:68
  499.5 4.7 fusion.27
  506.2 3.7 convert_bitcast_fusion.2
  510.0 42.7 %reduce-scatter.24.cloned.1.call-done = bf16[1,256,1024]{2,1,0:T(8,128)(2,1)} async-done(((bf16[1,1024,1024]{2,1,0:T(8,128)(2,1)}), bf16[1,256,1024]{2,1,0:T(8,128)(2,1)}) %reduce-scatter.24.cloned.1.call-update) | async-done | bytes 524304 | tf_op jit(solution)/shard_map/reduce_scatter | solution.py:72
  557.6 45.2 %all-gather.30.cloned.1.call-done = bf16[1,1024,1024]{2,1,0:T(8,128)(2,1)} async-done(((bf16[1,256,1024]{2,1,0:T(8,128)(2,1)}), bf16[1,1024,1024]{2,1,0:T(8,128)(2,1)}) %all-gather.30.cloned.1.call-update) | async-done | bytes 2097168 | tf_op jit(solution)/shard_map/all_gather | solution.py:78
  602.8 6.7 multiply_convert_fusion.2
  610.9 3.7 convert_bitcast_fusion.1
  614.6 42.7 %reduce-scatter.26.cloned.1.call-done = bf16[1,256,1024]{2,1,0:T(8,128)(2,1)} async-done(((bf16[1,1024,1024]{2,1,0:T(8,128)(2,1)}), bf16[1,256,1024]{2,1,0:T(8,128)(2,1)}) %reduce-scatter.26.cloned.1.call-update) | async-done | bytes 524304 | tf_op jit(solution)/shard_map/reduce_scatter | solution.py:82
  658.9 3.5 fusion.244
  662.6 45.3 %all-gather.32.cloned.1.call-done = bf16[1,1024,1024]{2,1,0:T(8,128)(2,1)} async-done(((bf16[1,256,1024]{2,1,0:T(8,128)(2,1)}), bf16[1,1024,1024]{2,1,0:T(8,128)(2,1)}) %all-gather.32.cloned.1.call-update) | async-done | bytes 2097168 | tf_op jit(solution)/shard_map/all_gather | solution.py:78
  707.9 6.1 multiply_reduce_fusion.2
  719.3 42.7 %reduce-scatter.28.cloned.1.call-done = bf16[1,256,1024]{2,1,0:T(8,128)(2,1)} async-done(((bf16[1,1024,1024]{2,1,0:T(8,128)(2,1)}), bf16[1,256,1024]{2,1,0:T(8,128)(2,1)}) %reduce-scatter.28.cloned.1.call-update) | async-done | bytes 524304 | tf_op jit(solution)/shard_map/reduce_scatter | solution.py:82
  763.6 2.6 fusion.241
  766.8 44.9 %all-gather.34.cloned.1.call-done = bf16[1,1024,1024]{2,1,0:T(8,128)(2,1)} async-done(((bf16[1,256,1024]{2,1,0:T(8,128)(2,1)}), bf16[1,1024,1024]{2,1,0:T(8,128)(2,1)}) %all-gather.34.cloned.1.call-update) | async-done | bytes 2097168 | tf_op jit(solution)/shard_map/all_gather | solution.py:78
  814.1 5.1 fusion.116
  819.3 5.5 multiply_reduce_fusion
  834.1 42.7 %reduce-scatter.30.cloned.1.call-done = bf16[1,256,1024]{2,1,0:T(8,128)(2,1)} async-done(((bf16[1,1024,1024]{2,1,0:T(8,128)(2,1)}), bf16[1,256,1024]{2,1,0:T(8,128)(2,1)}) %reduce-scatter.30.cloned.1.call-update) | async-done | bytes 524304 | tf_op jit(solution)/shard_map/reduce_scatter | solution.py:82
  878.5 2.7 multiply_convert_fusion.5
  881.5 45.2 %all-gather.36.cloned.1.call-done = bf16[1,1024,1024]{2,1,0:T(8,128)(2,1)} async-done(((bf16[1,256,1024]{2,1,0:T(8,128)(2,1)}), bf16[1,1024,1024]{2,1,0:T(8,128)(2,1)}) %all-gather.36.cloned.1.call-update) | async-done | bytes 2097168 | tf_op jit(solution)/shard_map/all_gather | solution.py:78
  926.7 6.6 multiply_convert_fusion.1
  934.6 3.8 convert_bitcast_fusion
  942.6 4.3 copy.367
  946.9 2.6 copy.357
  949.5 3.7 convolution_bitcast_fusion.4
  961.1 3.3 fusion.71
  979.9 4.1 copy.354
  986.6 6.0 convolution_bitcast_fusion.2
  992.6 3.7 convolution_bitcast_fusion
  996.4 4.1 convolution_bitcast_fusion.3
  1002.8 5.2 gather_fusion.5
  1008.0 5.0 copy.299
  1015.6 5.4 convolution_bitcast_fusion.1
  1023.5 5.3 gather_fusion.7
  1028.8 6.4 copy.315
  1035.2 6.4 copy.316
  1044.5 7.5 select_convert_fusion
  1052.0 11.4 copy.362
  1063.4 5.6 copy.368
  1082.5 121.7 %reduce-scatter.42.cloned.1.call-done = f32[32,17]{1,0:T(8,128)} async-done(((f32[1024,17]{1,0:T(8,128)}), f32[32,17]{1,0:T(8,128)}) %reduce-scatter.42.cloned.1.call-update) | async-done | bytes 2192
  1205.7 50.2 %reduce-scatter.40.cloned.1.call-done = bf16[128,2048]{1,0:T(8,128)(2,1)} async-done(((bf16[1024,2048]{1,0:T(8,128)(2,1)}), bf16[128,2048]{1,0:T(8,128)(2,1)}) %reduce-scatter.40.cloned.1.call-update) | async-done | bytes 524304
  1257.3 4.6 fusion.84
  1264.1 7.7 fusion.87
  1271.9 3.2 multiply_add_fusion
  1275.1 35.4 %reduce-scatter.36.cloned.1.call-done = bf16[2,128,1024]{2,1,0:T(8,128)(2,1)} async-done(((bf16[2,1024,1024]{2,1,0:T(8,128)(2,1)}), bf16[2,128,1024]{2,1,0:T(8,128)(2,1)}) %reduce-scatter.36.cloned.1.call-update) | async-done | bytes 524304 | tf_op jit(solution)/shard_map/reduce_scatter | solution.py:380
  1312.3 7.0 fusion.159
  1322.3 8.6 multiply_add_fusion.2
  (447 shorter events, 153.2 us)
Async XLA Ops:
  7.2 1062.7 %copy-start = (f32[256,256]{1,0:T(8,128)S(1)}, f32[256,256]{1,0:T(8,128)}, u32[]{:S(2)}) copy-start(f32[256,256]{1,0:T(8,128)} %param.33) | copy-start | bytes 786436
  7.2 75.6 %copy-start.4 = (bf16[1,256,1024]{2,1,0:T(8,128)(2,1)S(1)}, bf16[1,256,1024]{2,1,0:T(8,128)(2,1)}, u32[]{:S(2)}) copy-start(bf16[1,256,1024]{2,1,0:T(8,128)(2,1)} %param.27) | copy-start | bytes 1572868
  7.2 78.5 %all-gather.18.cloned.1.call-start = ((), (), s32[]{:S(2)}) async-start(), calls=%async_computation.15 | async-start | bytes 4718592 | tf_op jit(solution)/shard_map/all_gather | solution.py:334
  9.7 76.0 %copy-start.120 = (s32[8]{0:T(128)S(1)}, s32[8]{0:T(128)}, u32[]{:S(2)}) copy-start(s32[8]{0:T(128)} %param.30) | copy-start | bytes 100
  9.7 82.4 %all-gather.16.cloned.1.call-start = ((), (), s32[]{:S(2)}) async-start(), calls=%async_computation.14 | async-start | bytes 4718592 | tf_op jit(solution)/shard_map/all_gather | solution.py:332
  10.6 127.1 %all-gather.14.cloned.1.call-start = ((), (), s32[]{:S(2)}) async-start(), calls=%async_computation.13 | async-start | bytes 2621440 | tf_op jit(solution)/shard_map/all_gather | solution.py:68
  85.6 104.7 %reduce-scatter.18.cloned.1.call-start = ((), (), s32[]{:S(2)}) async-start(), calls=%async_computation.16 | async-start | bytes 2621440 | tf_op jit(solution)/shard_map/reduce_scatter | solution.py:72
  113.9 27.9 %copy-start.56 = (bf16[1,8,128,1024]{3,2,0,1:T(8,128)(2,1)}, bf16[1,8,128,1024]{3,2,0,1:T(8,128)(2,1)S(1)}, u32[]{:S(2)}) copy-start(bf16[1,8,128,1024]{3,2,0,1:T(8,128)(2,1)S(1)} %get-tuple-element.66) | copy-start | bytes 6291460
  147.6 68.1 %all-gather.24.cloned.1.call-start = ((), (), s32[]{:S(2)}) async-start(), calls=%async_computation.19 | async-start | bytes 1179648 | tf_op jit(solution)/shard_map/all_gather | solution.py:333
  148.5 47.3 %copy-start.96 = (s32[1,1024]{1,0:T(1,128)S(1)}, s32[1,1024]{1,0:T(1,128)}, u32[]{:S(2)}) copy-start(s32[1,1024]{1,0:T(1,128)} %param.29) | copy-start | bytes 12292
  148.5 99.9 %all-gather.22.cloned.1.call-start = ((), (), s32[]{:S(2)}) async-start(), calls=%async_computation.18 | async-start | bytes 2949120 | tf_op jit(solution)/shard_map/all_gather | solution.py:331
  149.5 147.1 %all-gather.20.cloned.1.call-start = ((), (), s32[]{:S(2)}) async-start(), calls=%async_computation.17 | async-start | bytes 2621440 | tf_op jit(solution)/shard_map/all_gather | solution.py:68
  191.7 24.1 %copy-start.103 = (f32[256]{0:T(256)}, f32[256]{0:T(256)S(1)}, u32[]{:S(2)}) copy-start(f32[256]{0:T(256)S(1)} %broadcast_multiply_fusion.14) | copy-start | bytes 3076
  193.1 24.3 %copy-start.111 = (f32[256]{0:T(256)}, f32[256]{0:T(256)S(1)}, u32[]{:S(2)}) copy-start(f32[256]{0:T(256)S(1)} %add_rsqrt_fusion.3) | copy-start | bytes 3076
  195.2 157.4 %reduce-scatter.20.cloned.1.call-start = ((), (), s32[]{:S(2)}) async-start(), calls=%async_computation.20 | async-start | bytes 2621440 | tf_op jit(solution)/shard_map/reduce_scatter | solution.py:72
  251.3 48.5 %copy-start.30 = (bf16[1,8,128,256]{3,2,0,1:T(8,128)(2,1)}, bf16[1,8,128,256]{3,2,0,1:T(8,128)(2,1)S(1)}, u32[]{:S(2)}) copy-start(bf16[1,8,128,256]{3,2,0,1:T(8,128)(2,1)S(1)} %get-tuple-element.72) | copy-start | bytes 1572868
  251.3 48.5 %copy-start.32 = (bf16[1,8,128,256]{3,2,0,1:T(8,128)(2,1)}, bf16[1,8,128,256]{3,2,0,1:T(8,128)(2,1)S(1)}, u32[]{:S(2)}) copy-start(bf16[1,8,128,256]{3,2,0,1:T(8,128)(2,1)S(1)} %get-tuple-element.71) | copy-start | bytes 1572868
  251.3 51.8 %copy-start.28 = (bf16[1,8,128,256]{3,2,0,1:T(8,128)(2,1)}, bf16[1,8,128,256]{3,2,0,1:T(8,128)(2,1)S(1)}, u32[]{:S(2)}) copy-start(bf16[1,8,128,256]{3,2,0,1:T(8,128)(2,1)S(1)} %get-tuple-element.73) | copy-start | bytes 1572868
  251.3 149.9 %copy-start.24 = (bf16[1,8,128,256]{3,2,0,1:T(8,128)(2,1)}, bf16[1,8,128,256]{3,2,0,1:T(8,128)(2,1)S(1)}, u32[]{:S(2)}) copy-start(bf16[1,8,128,256]{3,2,0,1:T(8,128)(2,1)S(1)} %get-tuple-element.69) | copy-start | bytes 1572868
  251.4 152.4 %copy-start.34 = (bf16[1,8,128,256]{3,2,0,1:T(8,128)(2,1)}, bf16[1,8,128,256]{3,2,0,1:T(8,128)(2,1)S(1)}, u32[]{:S(2)}) copy-start(bf16[1,8,128,256]{3,2,0,1:T(8,128)(2,1)S(1)} %get-tuple-element.70) | copy-start | bytes 1572868
  307.8 44.8 %copy-start.5 = (bf16[1,256,1024]{2,1,0:T(8,128)(2,1)S(1)}, bf16[1,256,1024]{2,1,0:T(8,128)(2,1)}, u32[]{:S(2)}) copy-start(bf16[1,256,1024]{2,1,0:T(8,128)(2,1)} %reduce-scatter.18.cloned.1.call-done) | copy-start | bytes 1572868
  309.8 91.4 %all-gather.26.cloned.1.call-start = ((), (), s32[]{:S(2)}) async-start(), calls=%async_computation.21 | async-start | bytes 2621440 | tf_op jit(solution)/shard_map/all_gather | solution.py:68
  355.9 95.7 %reduce-scatter.22.cloned.1.call-start = ((), (), s32[]{:S(2)}) async-start(), calls=%async_computation.22 | async-start | bytes 2621440 | tf_op jit(solution)/shard_map/reduce_scatter | solution.py:72
  356.2 49.6 %copy-start.118 = (f32[1,256]{1,0:T(1,128)}, f32[1,256]{1,0:T(1,128)S(1)}, u32[]{:S(2)}) copy-start(f32[1,256]{1,0:T(1,128)S(1)} %get-tuple-element.105) | copy-start | bytes 3076
  408.8 44.3 %copy-start.109 = (f32[1,1024]{1,0:T(1,128)S(1)}, f32[1,1024]{1,0:T(1,128)}, u32[]{:S(2)}) copy-start(f32[1,1024]{1,0:T(1,128)} %get-tuple-element.92) | copy-start | bytes 12292
  408.8 90.7 %all-gather.28.cloned.1.call-start = ((), (), s32[]{:S(2)}) async-start(), calls=%async_computation.23 | async-start | bytes 2621440 | tf_op jit(solution)/shard_map/all_gather | solution.py:68
  454.1 98.6 %reduce-scatter.24.cloned.1.call-start = ((), (), s32[]{:S(2)}) async-start(), calls=%async_computation.24 | async-start | bytes 2621440 | tf_op jit(solution)/shard_map/reduce_scatter | solution.py:72
  510.0 92.8 %all-gather.30.cloned.1.call-start = ((), (), s32[]{:S(2)}) async-start(), calls=%async_computation.25 | async-start | bytes 2621440 | tf_op jit(solution)/shard_map/all_gather | solution.py:78
  557.4 100.0 %reduce-scatter.26.cloned.1.call-start = ((), (), s32[]{:S(2)}) async-start(), calls=%async_computation.26 | async-start | bytes 2621440 | tf_op jit(solution)/shard_map/reduce_scatter | solution.py:82
  602.8 8.1 copy-start.58
  614.6 44.4 %copy-start.110 = (f32[1,1024]{1,0:T(1,128)S(1)}, f32[1,1024]{1,0:T(1,128)}, u32[]{:S(2)}) copy-start(f32[1,1024]{1,0:T(1,128)} %get-tuple-element.90) | copy-start | bytes 12292
  614.6 93.3 %all-gather.32.cloned.1.call-start = ((), (), s32[]{:S(2)}) async-start(), calls=%async_computation.27 | async-start | bytes 2621440 | tf_op jit(solution)/shard_map/all_gather | solution.py:78
  658.9 49.0 %copy-start.119 = (f32[1,256]{1,0:T(1,128)S(1)}, f32[1,256]{1,0:T(1,128)}, u32[]{:S(2)}) copy-start(f32[1,256]{1,0:T(1,128)} %copy-done.118) | copy-start | bytes 3076
  662.5 51.5 %copy-start.7 = (f32[1024,256]{1,0:T(8,128)S(1)}, f32[1024,256]{1,0:T(8,128)}, u32[]{:S(2)}) copy-start(f32[1024,256]{1,0:T(8,128)} %copy-done.6) | copy-start | bytes 3145732
  662.5 99.5 %reduce-scatter.28.cloned.1.call-start = ((), (), s32[]{:S(2)}) async-start(), calls=%async_computation.28 | async-start | bytes 2621440 | tf_op jit(solution)/shard_map/reduce_scatter | solution.py:82
  717.2 44.8 %copy-start.106 = (f32[256]{0:T(256)S(1)}, f32[256]{0:T(256)}, u32[]{:S(2)}) copy-start(f32[256]{0:T(256)} %copy-done.105) | copy-start | bytes 3076
  717.2 44.8 %copy-start.114 = (f32[256]{0:T(256)S(1)}, f32[256]{0:T(256)}, u32[]{:S(2)}) copy-start(f32[256]{0:T(256)} %copy-done.113) | copy-start | bytes 3076
  719.2 44.4 %copy-start.19 = (f32[1,256,1024]{2,1,0:T(8,128)S(1)}, f32[1,256,1024]{2,1,0:T(8,128)}, u32[]{:S(2)}) copy-start(f32[1,256,1024]{2,1,0:T(8,128)} %get-tuple-element.60) | copy-start | bytes 3145732
  719.3 92.4 %all-gather.34.cloned.1.call-start = ((), (), s32[]{:S(2)}) async-start(), calls=%async_computation.29 | async-start | bytes 2621440 | tf_op jit(solution)/shard_map/all_gather | solution.py:78
  766.3 110.5 %reduce-scatter.30.cloned.1.call-start = ((), (), s32[]{:S(2)}) async-start(), calls=%async_computation.30 | async-start | bytes 2621440 | tf_op jit(solution)/shard_map/reduce_scatter | solution.py:82
  814.1 10.6 slice-start
  819.2 12.5 copy-start.61
  832.0 44.8 %copy-start.104 = (f32[256]{0:T(256)S(1)}, f32[256]{0:T(256)}, u32[]{:S(2)}) copy-start(f32[256]{0:T(256)} %copy-done.103) | copy-start | bytes 3076
  832.0 44.8 %copy-start.112 = (f32[256]{0:T(256)S(1)}, f32[256]{0:T(256)}, u32[]{:S(2)}) copy-start(f32[256]{0:T(256)} %copy-done.111) | copy-start | bytes 3076
  834.0 44.4 %copy-start.20 = (f32[1,256,1024]{2,1,0:T(8,128)S(1)}, f32[1,256,1024]{2,1,0:T(8,128)}, u32[]{:S(2)}) copy-start(f32[1,256,1024]{2,1,0:T(8,128)} %get-tuple-element.56) | copy-start | bytes 3145732
  834.1 92.6 %all-gather.36.cloned.1.call-start = ((), (), s32[]{:S(2)}) async-start(), calls=%async_computation.31 | async-start | bytes 2621440 | tf_op jit(solution)/shard_map/all_gather | solution.py:78
  881.2 53.4 %copy-start.57 = (bf16[1,8,128,1024]{3,2,0,1:T(8,128)(2,1)S(1)}, bf16[1,8,128,1024]{3,2,0,1:T(8,128)(2,1)}, u32[]{:S(2)}) copy-start(bf16[1,8,128,1024]{3,2,0,1:T(8,128)(2,1)} %copy-done.56) | copy-start | bytes 6291460
  881.3 160.4 %reduce-scatter.32.cloned.1.call-start = ((), (), s32[]{:S(2)}) async-start(), calls=%async_computation.32 | async-start | bytes 2621440 | tf_op jit(solution)/shard_map/reduce_scatter | solution.py:82
  938.4 131.5 %reduce-scatter.38.cloned.1.call-start = ((), (), s32[]{:S(2)}) async-start(), calls=%async_computation.35 | async-start | bytes 1179648 | tf_op jit(solution)/shard_map/reduce_scatter | solution.py:386
  961.0 113.6 %reduce-scatter.34.cloned.1.call-start = ((), (), s32[]{:S(2)}) async-start(), calls=%async_computation.33 | async-start | bytes 2949120 | tf_op jit(solution)/shard_map/reduce_scatter | solution.py:372
  975.8 228.5 %reduce-scatter.42.cloned.1.call-start = ((), (), s32[]{:S(2)}) async-start(), calls=%async_computation.37 | async-start | bytes 540672
  1044.5 211.4 %reduce-scatter.40.cloned.1.call-start = ((), (), s32[]{:S(2)}) async-start(), calls=%async_computation.36 | async-start | bytes 4718592
  1069.1 241.4 %reduce-scatter.36.cloned.1.call-start = ((), (), s32[]{:S(2)}) async-start(), calls=%async_computation.34 | async-start | bytes 4718592 | tf_op jit(solution)/shard_map/reduce_scatter | solution.py:380
  1078.9 126.2 %copy-start.95 = (f32[17,32]{1,0:T(8,128)S(1)}, f32[17,32]{1,0:T(8,128)}, u32[]{:S(2)}) copy-start(f32[17,32]{1,0:T(8,128)} %param.50) | copy-start | bytes 6532
  1078.9 126.1 %copy-start.115 = (f32[17,32]{1,0:T(8,128)S(1)}, f32[17,32]{1,0:T(8,128)}, u32[]{:S(2)}) copy-start(f32[17,32]{1,0:T(8,128)} %param.53) | copy-start | bytes 6532
  1078.9 126.1 %copy-start.116 = (f32[17,32]{1,0:T(8,128)S(1)}, f32[17,32]{1,0:T(8,128)}, u32[]{:S(2)}) copy-start(f32[17,32]{1,0:T(8,128)} %param.52) | copy-start | bytes 6532
  1078.9 126.1 %copy-start.117 = (f32[17,32]{1,0:T(8,128)S(1)}, f32[17,32]{1,0:T(8,128)}, u32[]{:S(2)}) copy-start(f32[17,32]{1,0:T(8,128)} %param.51) | copy-start | bytes 6532
  1263.9 8.0 copy-start.15
  1263.9 8.0 copy-start.16
  1264.1 7.8 copy-start.71
  1312.3 9.3 copy-start.13
  1312.3 9.3 copy-start.63
  1319.3 11.6 copy-start.64
  1319.3 11.6 copy-start.65
  (90 other events, 263.1 us)
Sparse Core Ops, SparseCore 0:
  10.6 39.6 all-gather.17
  52.7 36.9 all-gather.15
  91.8 45.9 all-gather.13
  147.8 42.5 reduce-scatter.17
  192.9 22.8 all-gather.23
  218.2 30.0 all-gather.21
  250.6 45.9 all-gather.19
  310.0 42.5 reduce-scatter.19
  356.0 45.2 all-gather.25
  408.9 42.5 reduce-scatter.21
  454.3 45.2 all-gather.27
  510.1 42.5 reduce-scatter.23
  557.5 45.2 all-gather.29
  614.7 42.5 reduce-scatter.25
  662.6 45.2 all-gather.31
  719.4 42.5 reduce-scatter.27
  766.4 45.2 all-gather.33
  834.2 42.5 reduce-scatter.29
  881.4 45.2 all-gather.35
  938.6 42.5 reduce-scatter.31
  984.9 35.3 reduce-scatter.37
  1023.6 43.6 reduce-scatter.33
  1070.1 134.0 reduce-scatter.41
  1207.8 47.9 reduce-scatter.39
  1259.2 51.2 reduce-scatter.35
where the time goes:
time: 1350 us; the launch traced here: 1340 us
  waiting for transfers between devices  885 us (66%)
  matrix products  162 us (12%)
  local copies, waits for them, and re-layouts  135 us (10%)
  blocking collectives  72 us (5%)
  other arithmetic  64.9 us (5%)
  between operations  16.2 us (1%)
    all_gather x4, waiting for transfers between devices, spread_back(): return lax.all_gather(local_rows, 'mp', axis=1, tiled=True)  181 us
    unnamed x27, waiting for transfers between devices  173 us
    reduce_scatter x4, waiting for transfers between devices, collect(): lax.psum_scatter(partial_sum.astype(jnp.bfloat16), 'mp', scatter_dimensio...  169 us
    all_gather x4, waiting for transfers between devices, spread(): return lax.all_gather(local_rows, 'mp', axis=1, tiled=True)  152 us
    reduce_scatter x4, waiting for transfers between devices, collect_back(): lax.psum_scatter(partial_sum.astype(jnp.bfloat16), 'mp', scatter_dimensio...  128 us
    all_gather x1, blocking collectives, shards(): lax.all_gather(small_weight.astype(jnp.bfloat16), ('dp', 'mp'), axis=1, t...  72 us
    gather x13, local copies, waits for them, and re-layouts, arrange(): jnp.take(stored.reshape(blocked), order, axis=block_axis).reshape(layout)  46 us
    unnamed x265, local copies, waits for them, and re-layouts  41.7 us
  transfers between devices with their start and end apart: 25, of which 20 were waited for; matrix products, arithmetic and copies ran while one was open for 16% of the time, Pallas kernels for 0%

commit v1 on v0

v1 whole, which is shorter than its diff:
```python
import math
from functools import partial

import jax
import jax.numpy as jnp
from jax import lax
from jax.sharding import PartitionSpec as P

HEAD_DIM = 128
KERNEL = 5
STEP = 10


NORM_EPS = 1e-05
MASKED = -1e30
BETA_ONE = 0.9
BETA_TWO = 0.95
ADAM_EPS = 1e-08
DECAY = 0.01
EMA_DECAY = 0.7
RATE_INNER = 0.03
RATE_EXPAND = 0.03
RATE_OUTPUT = 0.25
RATE_SHRINK = 0.015
RATE_SMALL = 0.5
AXES = ("dp", "mp")
F32 = jnp.float32
BF16 = jnp.bfloat16


def dot(left, right, contract):
    return lax.dot_general(left, right, (contract, ((), ())), preferred_element_type=F32)


def mm(left, right):
    return dot(left, right, ((1,), (0,)))


def mm_nt(left, right):
    return dot(left, right, ((1,), (1,)))


def mm_tn(left, right):
    return dot(left, right, ((0,), (0,)))


class Plan:
    def __init__(self, n_dp, n_mp):
        self.n_dp, self.n_mp, self.half = n_dp, n_mp, n_mp // 2
        self.chips = n_dp // 2
        side = math.isqrt(self.chips)
        if side * side == self.chips and side % 2 == 0:
            order = [(0, x) for x in range(side)]
            for y in range(1, side):
                xs = range(side - 1, 0, -1) if y % 2 else range(1, side)
                order += [(y, x) for x in xs]
            order += [(y, 0) for y in range(side - 1, 0, -1)]
            self.ring = [y * side + x for y, x in order]
        else:
            self.ring = list(range(self.chips))
        self.place = {chip: at for at, chip in enumerate(self.ring)}
        reach = self.chips // 2
        self.offsets = [0]
        for hop in range(1, reach):
            self.offsets += [-hop, hop]
        self.offsets.append(reach)
        self.to_next = self.perm(lambda chip, core, z: (self.beside(chip, 1), core, z))
        self.to_last = self.perm(lambda chip, core, z: (self.beside(chip, -1), core, z))
        self.swap_core = self.perm(lambda chip, core, z: (chip, 1 - core, z))
        self.swap_rows = self.perm(
            lambda chip, core, z: (chip, 1 - core, z ^ self.half) if core != z // self.half else None
        )
        self.table = [
            [2 * self.beside(chip, offset) + core for offset in self.offsets for core in (0, 1)]
            for chip in range(self.chips)
        ]

    def beside(self, chip, offset):
        return self.ring[(self.place[chip] + offset) % self.chips]

    def perm(self, target):
        pairs = []
        for chip in range(self.chips):
            for core in (0, 1):
                for z in range(self.n_mp):
                    to = target(chip, core, z)
                    if to is not None:
                        source = (2 * chip + core) * self.n_mp + z
                        pairs.append((source, (2 * to[0] + to[1]) * self.n_mp + to[2]))
        return pairs

    def swap_z(self, bit):
        return self.perm(lambda chip, core, z: (chip, core, z ^ bit))

    def swap_any(self, bit):
        return [(me, me ^ bit) for me in range(self.n_dp * self.n_mp)]

    def z_bits(self):
        bits, bit = [], self.half
        while bit:
            bits.append(bit)
            bit //= 2
        return bits


def send(value, pairs):
    return lax.ppermute(value, AXES, pairs)


def pin(*values):
    return lax.optimization_barrier(values)


def ring_gather(plan, shard):
    cut = shard.shape[0] // 2
    reach = plan.chips // 2
    from_last, from_next = shard, shard
    found = [shard]
    for _ in range(1, reach):
        from_last, from_next = send(from_last, plan.to_next), send(from_next, plan.to_last)
        found += [from_last, from_next]
    far = [send(from_last[:cut], plan.to_next), send(from_next[cut:], plan.to_last)]
    return found + [jnp.concatenate(far, axis=0)]


def ring_scatter(plan, pieces):
    cut = pieces[0].shape[0] // 2
    ahead, behind = pieces[-1][:cut], pieces[-1][cut:]
    for hop in range(plan.chips // 2 - 1, 0, -1):
        ahead, behind = send(ahead, plan.to_next), send(behind, plan.to_last)
        to_ahead, to_behind = pieces[2 * hop], pieces[2 * hop - 1]
        if ahead.shape[0] == cut:
            ahead = jnp.concatenate([to_ahead[:cut] + ahead, to_ahead[cut:]], axis=0)
            behind = jnp.concatenate([to_behind[:cut], to_behind[cut:] + behind], axis=0)
        else:
            ahead, behind = to_ahead + ahead, to_behind + behind
    ahead, behind = send(ahead, plan.to_next), send(behind, plan.to_last)
    return (pieces[0].astype(F32) + ahead.astype(F32) + behind.astype(F32)).astype(BF16)


def norm_forward(stream, gain, bias):
    centre = jnp.mean(stream, axis=-1, keepdims=True)
    centred = stream - centre
    inverse = lax.rsqrt(jnp.mean(centred * centred, axis=-1, keepdims=True) + NORM_EPS)
    unit_rows = centred * inverse
    return (unit_rows * gain + bias, unit_rows, inverse)


def norm_backward(upstream, unit_rows, inverse, gain):
    scaled = upstream * gain
    through = inverse * (
        scaled
        - jnp.mean(scaled, axis=-1, keepdims=True)
        - unit_rows * jnp.mean(scaled * unit_rows, axis=-1, keepdims=True)
    )
    return (through, jnp.sum(upstream * unit_rows, axis=0), jnp.sum(upstream, axis=0))


def rotate_entry(gradients, left, right):
    turned = jnp.einsum("src,rx->sxc", gradients, left)
    return jnp.einsum("sxc,cy->sxy", turned, right)


def restore_entry(steps, left, right):
    turned = jnp.einsum("sxy,rx->sry", steps, left)
    return jnp.einsum("sry,cy->src", turned, right)


def rotate_exit(gradients, left, right):
    turned = jnp.einsum("src,cy->sry", gradients, right)
    return jnp.einsum("sry,rx->syx", turned, left)


def restore_exit(steps, left, right):
    turned = jnp.einsum("syx,cy->scx", steps, right)
    return jnp.einsum("scx,rx->scr", turned, left)


def adam_update(turned, weight, first, second, average, rate, restore):
    first_new = BETA_ONE * first + (1.0 - BETA_ONE) * turned
    second_new = BETA_TWO * second + (1.0 - BETA_TWO) * turned * turned
    normal_step = (
        first_new
        / (1.0 - BETA_ONE**STEP)
        / (jnp.sqrt(second_new / (1.0 - BETA_TWO**STEP)) + ADAM_EPS)
    )
    weight_new = weight - rate * (restore(normal_step) + DECAY * weight)
    average_new = EMA_DECAY * average + (1.0 - EMA_DECAY) * weight_new
    return (first_new, second_new, weight_new, average_new)


def layer(
    plan,
    frames,
    cotangent,
    segment_ids,
    owners,
    rot_model,
    rot_hidden,
    rot_inner,
    inner_weight,
    inner_first,
    inner_second,
    inner_average,
    expand_weight,
    expand_first,
    expand_second,
    expand_average,
    output_weight,
    output_first,
    output_second,
    output_average,
    shrink_weight,
    shrink_first,
    shrink_second,
    shrink_average,
    small_weight,
    small_first,
    small_second,
    small_average,
):
    n_dp, n_mp, half = plan.n_dp, plan.n_mp, plan.half
    dp, z = lax.axis_index("dp"), lax.axis_index("mp")
    chip, core = dp // 2, dp % 2
    high, z_low = z // half, z % half
    on_zero, on_low = core == 0, high == 0
    me = dp * n_mp + z
    devices = n_dp * n_mp
    frames, cotangent, segment_ids = frames[0], cotangent[0], segment_ids[0]
    chunk, width = frames.shape
    share = width // n_dp
    hidden = expand_weight.shape[2]
    inner = inner_weight.shape[2]

    slots = jnp.arange(n_dp, dtype=jnp.int32)
    holds = jnp.sum(jnp.where(owners[None, :] == slots[:, None], slots[None, :], 0), axis=1)
    here = jnp.asarray(plan.table, jnp.int32)[chip]
    to_here = holds[here]
    from_here = jnp.sum(jnp.where(to_here[None, :] == slots[:, None], slots[None, :], 0), axis=1)

    def reorder(rows, order):
        return jnp.take(rows.reshape(rows.shape[0], n_dp, share), order, axis=1).reshape(rows.shape)

    moved = core != high

    def trade_rows(rows):
        return jnp.where(moved, send(rows, plan.swap_rows), rows)

    def by_core(mine, other):
        return jnp.where(on_zero, mine, other), jnp.where(on_zero, other, mine)

    def pack(slot):
        both = jnp.stack([expand_weight[slot].astype(BF16), shrink_weight[slot].astype(BF16).T])
        low, up = both[..., : hidden // 2], both[..., hidden // 2 :]
        keep, give = by_core(low, up)
        first, second = by_core(keep, send(give, plan.swap_core))
        return jnp.concatenate([first, second], axis=1)[None]

    def double(shard):
        for bit in plan.z_bits():
            shard = jnp.concatenate([shard, send(shard, plan.swap_z(bit))], axis=0)
        return shard

    def unpack(parts):
        return jnp.concatenate(parts, axis=2)

    def pack_narrow():
        mine = jnp.concatenate(
            [inner_weight.astype(BF16), jnp.swapaxes(output_weight.astype(BF16), 1, 2)], axis=0
        )
        other = send(mine, plan.swap_z(half))
        low, up = jnp.where(on_low, mine, other), jnp.where(on_low, other, mine)
        keep, give = by_core(low, up)
        first, second = by_core(keep, send(give, plan.swap_core))
        both = jnp.concatenate([first, second], axis=1)
        return jnp.concatenate([both[:3], both[5:6], both[3:5], both[6:7]], axis=0)

    early_shard = pack(0)
    narrow_shard = pack_narrow()
    late_shard = pack(1)

    rows = trade_rows(reorder(frames, to_here))
    other_segments = send(segment_ids, plan.swap_core)
    segments = jnp.where(moved, other_segments, segment_ids)

    small_rows = small_weight.shape[0]
    small_cut = small_weight.shape[1]
    tile = 8 * 128
    flat = jnp.pad(small_weight.astype(BF16).reshape(-1), (0, tile - small_rows * small_cut))
    spread_small = flat.reshape(1, 8, 128)
    bit = 1
    while bit < devices:
        spread_small = jnp.concatenate(
            [spread_small, send(spread_small, plan.swap_any(bit))], axis=0
        )
        bit *= 2
    relative = jnp.bitwise_xor(me, jnp.arange(devices, dtype=jnp.int32))
    small = jnp.take(spread_small, relative, axis=0).reshape(devices, tile)
    small = small[:, : small_rows * small_cut].reshape(devices, small_rows, small_cut)
    small = jnp.swapaxes(small, 0, 1).reshape(small_rows, width).astype(F32)
    gains = reorder(small[:10], to_here)
    block = z_low + half * core
    depthwise = lax.dynamic_slice_in_dim(small[10:], block * inner, inner, axis=1)

    early = unpack(ring_gather(plan, double(early_shard)))
    early, narrow_shard = pin(early, narrow_shard)
    narrow_parts = ring_gather(plan, narrow_shard)
    narrow = jnp.concatenate(narrow_parts, axis=1)
    narrow, late_shard = pin(narrow, late_shard)
    late = unpack(ring_gather(plan, double(late_shard)))

    def both_cores(own):
        return jnp.concatenate([own, send(own, plan.swap_core)], axis=0)

    def fold_cores(partial_sum):
        away = send(partial_sum[chunk:].astype(BF16), plan.swap_core)
        return partial_sum[:chunk] + away.astype(F32)

    def row_gather(own):
        got = own
        for bit in plan.z_bits()[1:]:
            got = jnp.concatenate([got, send(got, plan.swap_z(bit))], axis=0)
        return jnp.concatenate([got, send(got, plan.swap_core)], axis=0)

    def row_scatter(partial_sum):
        cut = partial_sum.shape[0] // 2
        away = send(partial_sum[cut:].astype(BF16), plan.swap_core)
        total = partial_sum[:cut] + away.astype(F32)
        for bit in plan.z_bits()[1:][::-1]:
            cut //= 2
            total = total[:cut] + send(total[cut:].astype(BF16), plan.swap_z(bit)).astype(F32)
        return total

    steps = jnp.arange(n_mp, dtype=jnp.int32)
    z_order = [0]
    for bit in plan.z_bits()[1:]:
        z_order = z_order + [at ^ bit for at in z_order]
    z_order = jnp.asarray(z_order, jnp.int32)
    chunk_of = jnp.concatenate(
        [core * half + jnp.bitwise_xor(z_low, z_order), (1 - core) * half + jnp.bitwise_xor(z_low, z_order)]
    )
    place_of = jnp.sum(jnp.where(chunk_of[None, :] == steps[:, None], steps[None, :], 0), axis=1)

    def rechunk(values, order):
        tall = values.reshape((n_mp, chunk) + values.shape[1:])
        return jnp.take(tall, order, axis=0).reshape(values.shape)

    mixed_segments = rechunk(segments, chunk_of)
    matching = mixed_segments[:, None] == mixed_segments[None, :]
    radius = KERNEL // 2
    padded_ids = jnp.pad(segments, (radius, radius), constant_values=-1)
    length = segments.shape[0]
    windows = [
        (padded_ids[tap : tap + length] == segments).astype(F32)[:, None] for tap in range(KERNEL)
    ]

    def shift(values, offset):
        padded = jnp.pad(values, ((radius, radius), (0, 0)))
        return lax.slice_in_dim(padded, radius + offset, radius + offset + length, axis=0)

    def feed_forward(stream, at, weights):
        normed, unit_rows, inverse = norm_forward(stream, gains[at], gains[at + 1])
        full = both_cores(normed.astype(BF16))
        preacts, total = [], 0.0
        for piece in range(n_mp):
            preact = mm(full, weights[piece, 0])
            preacts.append(preact)
            total = total + mm_nt(jax.nn.silu(preact).astype(BF16), weights[piece, 1])
        return stream + 0.5 * fold_cores(total), (full, unit_rows, inverse, preacts)

    def feed_back(gradient, state, at, weights):
        full, unit_rows, inverse, preacts = state
        incoming = both_cores((0.5 * gradient).astype(BF16))
        grads, total = [], 0.0
        for piece in range(n_mp):
            preact = preacts[piece]
            gate = jax.nn.sigmoid(preact)
            kept = (preact * gate).astype(BF16)
            grad_pre = (
                mm(incoming, weights[piece, 1]) * gate * (1.0 + preact * (1.0 - gate))
            ).astype(BF16)
            total = total + mm_nt(grad_pre, weights[piece, 0])
            grads.append(
                jnp.stack([mm_tn(full, grad_pre).astype(BF16), mm_tn(incoming, kept).astype(BF16)])
            )
        through, gain_row, bias_row = norm_backward(
            fold_cores(total), unit_rows, inverse, gains[at]
        )
        return gradient + through, jnp.stack(grads), [gain_row, bias_row]

    heads = inner // HEAD_DIM
    factor = HEAD_DIM**-0.5

    def split(values):
        return values.astype(BF16).reshape(length, heads, HEAD_DIM)

    def score(queries, keyset):
        scores = jnp.einsum("qhd,khd->hqk", queries, keyset, preferred_element_type=F32) * factor
        return jnp.where(matching[None], scores, MASKED)

    def attention(stream):
        normed, unit_rows, inverse = norm_forward(stream, gains[2], gains[3])
        full = row_gather(normed.astype(BF16))
        queries, keyset, values = [split(mm(full, narrow[which])) for which in range(3)]
        scores = score(queries, keyset)
        row_max = jnp.max(scores, axis=-1, keepdims=True)
        weights = jnp.exp(scores - row_max)
        totals = jnp.sum(weights, axis=-1, keepdims=True)
        log_total = row_max + jnp.log(totals)
        attended = (weights / totals).astype(BF16)
        mixture = jnp.einsum("hqk,khd->qhd", attended, values, preferred_element_type=F32)
        mixture = mixture.astype(BF16).reshape(length, inner)
        branch = row_scatter(mm_nt(mixture, narrow[3]))
        return stream + branch, (full, unit_rows, inverse, queries, keyset, values, mixture, log_total)

    def attention_back(gradient, state):
        full, unit_rows, inverse, queries, keyset, values, mixture, log_total = state
        incoming = row_gather(gradient.astype(BF16))
        grad_out = mm_tn(incoming, mixture)
        grad_mix = split(mm(incoming, narrow[3]))
        attended = jnp.exp(score(queries, keyset) - log_total)
        grad_values = jnp.einsum(
            "hqk,qhd->khd", attended.astype(BF16), grad_mix, preferred_element_type=F32
        )
        grad_attended = jnp.einsum("qhd,khd->hqk", grad_mix, values, preferred_element_type=F32)
        grad_scores = (
            attended * (grad_attended - jnp.sum(grad_attended * attended, axis=-1, keepdims=True))
        ).astype(BF16)
        grad_queries = factor * jnp.einsum(
            "hqk,khd->qhd", grad_scores, keyset, preferred_element_type=F32
        )
        grad_keyset = factor * jnp.einsum(
            "hqk,qhd->khd", grad_scores, queries, preferred_element_type=F32
        )
        pieces = [
            member.astype(BF16).reshape(length, inner)
            for member in (grad_queries, grad_keyset, grad_values)
        ]
        total = sum(mm_nt(pieces[which], narrow[which]) for which in range(3))
        grads = jnp.stack([mm_tn(full, member).astype(BF16) for member in pieces] + [grad_out.astype(BF16)])
        through, gain_row, bias_row = norm_backward(
            row_scatter(total), unit_rows, inverse, gains[2]
        )
        return gradient + through, grads, [gain_row, bias_row]

    def convolve(stream):
        normed, unit_rows, inverse = norm_forward(stream, gains[4], gains[5])
        full = rechunk(row_gather(normed.astype(BF16)), place_of)
        content, opening = mm(full, narrow[4]), mm(full, narrow[5])
        gated = content * jax.nn.sigmoid(opening)
        summed = sum(shift(gated, tap - radius) * windows[tap] * depthwise[tap] for tap in range(KERNEL))
        normal_conv = summed * depthwise[KERNEL] + depthwise[KERNEL + 1]
        activated = jax.nn.silu(normal_conv).astype(BF16)
        branch = row_scatter(rechunk(mm_nt(activated, narrow[6]).astype(BF16), chunk_of))
        return stream + branch, (full, unit_rows, inverse, content, opening, summed)

    def convolve_back(gradient, state):
        full, unit_rows, inverse, content, opening, summed = state
        incoming = rechunk(row_gather(gradient.astype(BF16)), place_of)
        normal_conv = summed * depthwise[KERNEL] + depthwise[KERNEL + 1]
        gate_conv = jax.nn.sigmoid(normal_conv)
        activated = (normal_conv * gate_conv).astype(BF16)
        grad_out = mm_tn(incoming, activated)
        grad_normal = mm(incoming, narrow[6]) * gate_conv * (1.0 + normal_conv * (1.0 - gate_conv))
        grad_summed = grad_normal * depthwise[KERNEL]
        gate_open = jax.nn.sigmoid(opening)
        gated = content * gate_open
        depth_rows, grad_gated = [], 0.0
        for tap in range(KERNEL):
            masked = grad_summed * windows[tap]
            depth_rows.append(jnp.sum(masked * shift(gated, tap - radius), axis=0))
            grad_gated = grad_gated + shift(masked * depthwise[tap], radius - tap)
        depth_rows.append(jnp.sum(grad_normal * summed, axis=0))
        depth_rows.append(jnp.sum(grad_normal, axis=0))
        grad_content = (grad_gated * gate_open).astype(BF16)
        grad_opening = (grad_gated * content * gate_open * (1.0 - gate_open)).astype(BF16)
        total = mm_nt(grad_content, narrow[4]) + mm_nt(grad_opening, narrow[5])
        grads = jnp.stack(
            [
                mm_tn(full, grad_content).astype(BF16),
                mm_tn(full, grad_opening).astype(BF16),
                grad_out.astype(BF16),
            ]
        )
        through, gain_row, bias_row = norm_backward(
            row_scatter(rechunk(total.astype(BF16), chunk_of)), unit_rows, inverse, gains[4]
        )
        return gradient + through, grads, [gain_row, bias_row], depth_rows

    piece_rows = 2 * share

    def collect_wide(grads):
        pieces = [
            grads[:, :, at * piece_rows : (at + 1) * piece_rows] for at in range(len(plan.offsets))
        ]
        total = ring_scatter(plan, pieces)
        for bit in plan.z_bits()[::-1]:
            cut = total.shape[0] // 2
            total = total[:cut] + send(total[cut:], plan.swap_z(bit))
        first, second = total[0, :, :share], total[0, :, share:]
        keep, give = by_core(first, second)
        low, up = by_core(keep, send(give, plan.swap_core))
        return jnp.concatenate([low, up], axis=2).astype(F32)

    def collect_narrow(grads):
        pieces = [
            grads[:, at * piece_rows : (at + 1) * piece_rows] for at in range(len(plan.offsets))
        ]
        total = ring_scatter(plan, pieces)
        first, second = total[:, :share], total[:, share:]
        keep, give = by_core(first, second)
        low, up = by_core(keep, send(give, plan.swap_core))
        own, away = jnp.where(on_low, low, up), jnp.where(on_low, up, low)
        return own.astype(F32) + send(away, plan.swap_z(half)).astype(F32)

    stream = rows.astype(F32)
    stream, early_state = feed_forward(stream, 0, early)
    stream, attend_state = attention(stream)
    stream, conv_state = convolve(stream)
    stream, late_state = feed_forward(stream, 6, late)
    result, unit_final, inverse_final = norm_forward(stream, gains[8], gains[9])
    block_output = reorder(trade_rows(result.astype(BF16)), from_here)[None]
    upstream = trade_rows(reorder(cotangent, to_here)).astype(F32)
    gradient, *final_rows = norm_backward(upstream, unit_final, inverse_final, gains[8])
    gradient, late_grads, late_rows = feed_back(gradient, late_state, 6, late)
    late_sum = collect_wide(late_grads)
    gradient, conv_grads, conv_rows, depth_rows = convolve_back(gradient, conv_state)
    gradient, attend_grads, attend_rows = attention_back(gradient, attend_state)
    narrow_sum = collect_narrow(jnp.concatenate([attend_grads, conv_grads], axis=0))
    gradient, early_grads, early_rows = feed_back(gradient, early_state, 0, early)
    early_sum = collect_wide(early_grads)
    input_grad = reorder(trade_rows(gradient.astype(BF16)), from_here)[None]

    norm_rows = reorder(
        jnp.stack(early_rows + attend_rows + conv_rows + late_rows + final_rows), from_here
    )
    depth_rows = lax.dynamic_update_slice_in_dim(
        jnp.zeros((KERNEL + 2, width), F32), jnp.stack(depth_rows), block * inner, axis=1
    )
    small_grad = jnp.concatenate([norm_rows, depth_rows], axis=0)
    small_grad = jnp.swapaxes(small_grad.reshape(small_rows, devices, small_cut), 0, 1)
    small_grad = small_grad.reshape(devices, small_rows * small_cut)
    small_grad = jnp.pad(small_grad, ((0, 0), (0, tile - small_rows * small_cut)))
    small_grad = jnp.take(small_grad.reshape(devices, 8, 128), relative, axis=0)
    while small_grad.shape[0] > 1:
        cut = small_grad.shape[0] // 2
        small_grad = small_grad[:cut] + send(small_grad[cut:], plan.swap_any(cut))
    small_grad = small_grad.reshape(-1)[: small_rows * small_cut].reshape(small_rows, small_cut)

    new_inner = adam_update(
        rotate_entry(jnp.concatenate([narrow_sum[:3], narrow_sum[4:6]]), rot_model, rot_inner),
        inner_weight,
        inner_first,
        inner_second,
        inner_average,
        RATE_INNER,
        partial(restore_entry, left=rot_model, right=rot_inner),
    )
    new_expand = adam_update(
        rotate_entry(jnp.stack([early_sum[0], late_sum[0]]), rot_model, rot_hidden),
        expand_weight,
        expand_first,
        expand_second,
        expand_average,
        RATE_EXPAND,
        partial(restore_entry, left=rot_model, right=rot_hidden),
    )
    new_output = adam_update(
        rotate_exit(jnp.stack([narrow_sum[3], narrow_sum[6]]), rot_model, rot_inner),
        output_weight,
        output_first,
        output_second,
        output_average,
        RATE_OUTPUT,
        partial(restore_exit, left=rot_model, right=rot_inner),
    )
    new_shrink = adam_update(
        rotate_exit(jnp.stack([early_sum[1], late_sum[1]]), rot_model, rot_hidden),
        shrink_weight,
        shrink_first,
        shrink_second,
        shrink_average,
        RATE_SHRINK,
        partial(restore_exit, left=rot_model, right=rot_hidden),
    )
    new_small = adam_update(
        small_grad, small_weight, small_first, small_second, small_average, RATE_SMALL, lambda step: step
    )
    return (block_output, input_grad) + new_inner + new_expand + new_output + new_shrink + new_small


def solution(mesh):
    plan = Plan(mesh.shape["dp"], mesh.shape["mp"])
    row = P("dp", "mp", None)
    entry = (P(None, "dp", "mp"),) * 4
    exit_ = (P(None, "mp", "dp"),) * 4
    small = (P(None, ("dp", "mp")),) * 4
    states = entry + entry + exit_ + exit_ + small
    return jax.shard_map(
        partial(layer, plan),
        mesh=mesh,
        in_specs=(row, row, P("dp", None), P(), P("dp", None), P("mp", None), P("mp", None)) + states,
        out_specs=(row, row) + states,
        check_vma=False,
    )
```

time: 1350 us -> 849 us (0.63)
  waiting for transfers between devices: 885 us -> 445 us
  starting transfers between devices: 2.88 us -> 86.5 us
  blocking collectives: 72 us -> 0 us
  local copies, waits for them, and re-layouts: 135 us -> 84.5 us
  matrix products: 162 us -> 117 us
  other arithmetic: 64.9 us -> 101 us
    ppermute x0 -> x79, waiting for transfers between devices: none -> 445 us  [send(): return lax.ppermute(value, AXES, pairs)]
    all_gather x12 -> x0, waiting for transfers between devices: 380 us -> none  [the longest x4 181 us: spread_back(): return lax.all_gather(local_rows, 'mp', axis=1, tiled=True)]
    reduce_scatter x11 -> x0, waiting for transfers between devices: 332 us -> none  [the longest x4 169 us: collect(): lax.psum_scatter(partial_sum.astype(jnp.bfloat16), 'mp', scatter_dimensio...]
    unnamed x27 -> x0, waiting for transfers between devices: 173 us -> none
    ppermute x0 -> x79, starting transfers between devices: none -> 86.5 us  [send(): return lax.ppermute(value, AXES, pairs)]
    all_gather x1 -> x0, blocking collectives: 72 us -> none  [shards(): lax.all_gather(small_weight.astype(jnp.bfloat16), ('dp', 'mp'), axis=1, t...]
    dot_general x55 -> x83, matrix products: 162 us -> 117 us  [the longest x69 76 us: dot(): lax.dot_general(left, right, (contract, ((), ())), preferred_element_type...]
    concatenate x0 -> x29, other arithmetic: none -> 28.3 us  [the longest x2 7.28 us: unpack(): return jnp.concatenate(parts, axis=2)]
  transfers between devices with their start and end apart: 25 -> 79, of which waited for: 20 -> 41; matrix products, arithmetic and copies ran while one was open for 16% -> 28% of each run, Pallas kernels for 0% -> 0%
where the time goes in v1:
time: 849 us; the launch traced here: 838 us
  waiting for transfers between devices  445 us (52%)
  matrix products  117 us (14%)
  other arithmetic  101 us (12%)
  starting transfers between devices  86.5 us (10%)
  local copies, waits for them, and re-layouts  84.5 us (10%)
    ppermute x79, waiting for transfers between devices, send(): return lax.ppermute(value, AXES, pairs)  445 us
    ppermute x79, starting transfers between devices, send(): return lax.ppermute(value, AXES, pairs)  86.5 us
    dot_general x69, matrix products, dot(): lax.dot_general(left, right, (contract, ((), ())), preferred_element_type...  76 us
    unnamed x310, local copies, waits for them, and re-layouts  27 us
  transfers between devices with their start and end apart: 79, of which 41 were waited for; matrix products, arithmetic and copies ran while one was open for 28% of the time, Pallas kernels for 0%

profile of v1, /device:TPU:0, one launch (start us, length us, event | category | flops | bytes accessed | tf_op | source)
XLA Modules:
  0.0 838.2 jit_solution(14960226253884340942)
XLA Ops:
  10.1 2.5 gather_fusion.9
  17.1 2.6 collective-permute-start.1
  22.0 3.5 collective-permute-start.8
  28.0 42.3 %collective-permute-done.8 = bf16[1,2,256,512]{2,3,1,0:T(8,128)(2,1)S(1)} collective-permute-done((bf16[1,2,256,512]{2,3,1,0:T(8,128)(2,1)S(1)}, bf16[1,2,256,512]{2,3,1,0:T(8,128)(2,1)S(1)}, u32[]{:S(2)}, u32[]{:S(2)}) %collective-permute-start.8) | collective-permute-done | bytes 524320 | tf_op jit(solution)/shard_map/ppermute | solution.py:107
  74.8 20.0 %collective-permute-done.2 = bf16[2,8,128]{2,1,0:T(8,128)(2,1)S(1)} collective-permute-done((bf16[2,8,128]{2,1,0:T(8,128)(2,1)S(1)}, bf16[2,8,128]{2,1,0:T(8,128)(2,1)S(1)}, u32[]{:S(2)}, u32[]{:S(2)}) %collective-permute-start.2) | collective-permute-done | bytes 4128 | tf_op jit(solution)/shard_map/ppermute | solution.py:107
  105.4 43.6 %collective-permute-done.5 = bf16[16,8,128]{2,1,0:T(8,128)(2,1)S(1)} collective-permute-done((bf16[16,8,128]{2,1,0:T(8,128)(2,1)S(1)}, bf16[16,8,128]{2,1,0:T(8,128)(2,1)S(1)}, u32[]{:S(2)}, u32[]{:S(2)}) %collective-permute-start.5) | collective-permute-done | bytes 32800 | tf_op jit(solution)/shard_map/ppermute | solution.py:107
  162.5 3.0 collective-permute-start.12
  169.7 18.9 %collective-permute-done.12 = bf16[2,2,256,512]{2,3,1,0:T(8,128)(2,1)S(1)} collective-permute-done((bf16[2,2,256,512]{2,3,1,0:T(8,128)(2,1)S(1)}, bf16[2,2,256,512]{2,3,1,0:T(8,128)(2,1)S(1)}, u32[]{:S(2)}, u32[]{:S(2)}) %collective-permute-start.12) | collective-permute-done | bytes 1048608 | tf_op jit(solution)/shard_map/ppermute | solution.py:107
  188.6 4.0 collective-permute-done.13
  192.6 3.4 maximum_maximum_fusion
  206.8 2.5 collective-permute-start.19
  212.7 17.1 %collective-permute-done.20 = bf16[7,256,256]{2,1,0:T(8,128)(2,1)S(1)} collective-permute-done((bf16[7,256,256]{2,1,0:T(8,128)(2,1)}, bf16[7,256,256]{2,1,0:T(8,128)(2,1)S(1)}, u32[]{:S(2)}, u32[]{:S(2)}) %collective-permute-start.20) | collective-permute-done | bytes 917536 | tf_op jit(solution)/shard_map/ppermute | solution.py:107
  236.3 5.7 collective-permute-done.21
  245.3 2.8 convolution_convert_fusion.25
  253.4 2.7 convolution_convert_fusion.27
  258.9 2.6 collective-permute-done.25
  265.1 22.0 %collective-permute-done.26 = bf16[256,1024]{1,0:T(8,128)(2,1)S(1)} collective-permute-done((bf16[256,1024]{1,0:T(8,128)(2,1)S(1)}, bf16[256,1024]{1,0:T(8,128)(2,1)S(1)}, u32[]{:S(2)}, u32[]{:S(2)}) %collective-permute-start.26) | collective-permute-done | bytes 524320 | tf_op jit(solution)/shard_map/ppermute | solution.py:107
  291.2 11.7 %collective-permute-done.27 = bf16[256,1024]{1,0:T(8,128)(2,1)S(1)} collective-permute-done((bf16[256,1024]{1,0:T(8,128)(2,1)S(1)}, bf16[256,1024]{1,0:T(8,128)(2,1)S(1)}, u32[]{:S(2)}, u32[]{:S(2)}) %collective-permute-start.27) | collective-permute-done | bytes 524320 | tf_op jit(solution)/shard_map/ppermute | solution.py:107
  310.1 13.7 %collective-permute-done.33 = bf16[2,2,256,512]{2,3,1,0:T(8,128)(2,1)} collective-permute-done((bf16[2,2,256,512]{2,3,1,0:T(8,128)(2,1)}, bf16[2,2,256,512]{2,3,1,0:T(8,128)(2,1)}, u32[]{:S(2)}, u32[]{:S(2)}) %collective-permute-start.33) | collective-permute-done | bytes 1048608 | tf_op jit(solution)/shard_map/ppermute | solution.py:107
  329.6 2.3 gather_fusion.6
  335.9 3.1 fusion.437
  341.1 3.5 convolution_convert_fusion
  344.6 2.4 gather_fusion.7
  347.5 2.6 collective-permute-done.29
  351.1 21.1 %collective-permute-done.34 = bf16[4,2,256,512]{2,3,1,0:T(8,128)(2,1)} collective-permute-done((bf16[4,2,256,512]{2,3,1,0:T(8,128)(2,1)}, bf16[4,2,256,512]{2,3,1,0:T(8,128)(2,1)}, u32[]{:S(2)}, u32[]{:S(2)}) %collective-permute-start.34) | collective-permute-done | bytes 2097184 | tf_op jit(solution)/shard_map/ppermute | solution.py:107
  377.8 18.2 %collective-permute-done.36 = bf16[2,2,256,512]{2,3,1,0:T(8,128)(2,1)S(1)} collective-permute-done((bf16[2,2,256,512]{2,3,1,0:T(8,128)(2,1)S(1)}, bf16[2,2,256,512]{2,3,1,0:T(8,128)(2,1)S(1)}, u32[]{:S(2)}, u32[]{:S(2)}) %collective-permute-start.36) | collective-permute-done | bytes 1048608 | tf_op jit(solution)/shard_map/ppermute | solution.py:107
  397.5 3.9 maximum_maximum_fusion.1
  411.7 15.2 %collective-permute-start.41 = (bf16[256,1024]{1,0:T(8,128)(2,1)S(1)}, bf16[256,1024]{1,0:T(8,128)(2,1)S(1)}, u32[]{:S(2)}, u32[]{:S(2)}) collective-permute-start(bf16[256,1024]{1,0:T(8,128)(2,1)S(1)} %multiply_convert_fusion.4), channel_id=1, source_target_pairs={{0,4},{1,5},{2,6},{3,7},{4,0},{5,1},{6,2},{7,3},{8,12},{9,13},{10,... | collective-permute-start | bytes 1572872 | tf_op jit(solution)/shard_map/ppermute | solution.py:107
  448.6 12.7 %collective-permute-done.43 = bf16[256,1024]{1,0:T(8,128)(2,1)S(1)} collective-permute-done((bf16[256,1024]{1,0:T(8,128)(2,1)S(1)}, bf16[256,1024]{1,0:T(8,128)(2,1)S(1)}, u32[]{:S(2)}, u32[]{:S(2)}) %collective-permute-start.43) | collective-permute-done | bytes 524320 | tf_op jit(solution)/shard_map/ppermute | solution.py:107
  461.5 3.4 collective-permute-done.67
  468.3 4.7 collective-permute-done.69
  477.5 3.7 gather_fusion.10
  483.4 3.6 multiply_reduce_fusion.2
  489.9 3.1 add_convert_fusion.2
  493.0 3.7 gather_fusion.11
  498.8 2.6 collective-permute-done.45
  503.8 10.2 %collective-permute-done.68 = bf16[4,2,256,512]{2,3,1,0:T(8,128)(2,1)} collective-permute-done((bf16[4,2,256,512]{2,3,1,0:T(8,128)(2,1)}, bf16[4,2,256,512]{2,3,1,0:T(8,128)(2,1)}, u32[]{:S(2)}, u32[]{:S(2)}) %collective-permute-start.68) | collective-permute-done | bytes 2097184 | tf_op jit(solution)/shard_map/ppermute | solution.py:107
  514.0 8.3 collective-permute-done.70
  522.3 2.7 add_convert_fusion
  528.9 28.1 %collective-permute-done.71 = bf16[2,2,256,512]{2,3,1,0:T(8,128)(2,1)S(1)} collective-permute-done((bf16[2,2,256,512]{2,3,1,0:T(8,128)(2,1)S(1)}, bf16[2,2,256,512]{2,3,1,0:T(8,128)(2,1)S(1)}, u32[]{:S(2)}, u32[]{:S(2)}) %collective-permute-start.71) | collective-permute-done | bytes 1048608 | tf_op jit(solution)/shard_map/ppermute | solution.py:107
  557.2 9.3 %collective-permute-done.47 = bf16[256,1024]{1,0:T(8,128)(2,1)S(1)} collective-permute-done((bf16[256,1024]{1,0:T(8,128)(2,1)S(1)}, bf16[256,1024]{1,0:T(8,128)(2,1)S(1)}, u32[]{:S(2)}, u32[]{:S(2)}) %collective-permute-start.47) | collective-permute-done | bytes 524320 | tf_op jit(solution)/shard_map/ppermute | solution.py:107
  567.7 14.7 %collective-permute-done.72 = bf16[1,2,256,512]{2,3,1,0:T(8,128)(2,1)S(1)} collective-permute-done((bf16[1,2,256,512]{2,3,1,0:T(8,128)(2,1)S(1)}, bf16[1,2,256,512]{2,3,1,0:T(8,128)(2,1)S(1)}, u32[]{:S(2)}, u32[]{:S(2)}) %collective-permute-start.72) | collective-permute-done | bytes 524320 | tf_op jit(solution)/shard_map/ppermute | solution.py:107
  588.5 2.5 multiply_convert_fusion
  615.5 7.0 collective-permute-done.56
  630.2 3.3 collective-permute-start.50
  633.4 3.7 collective-permute-done.55
  637.1 7.8 collective-permute-done.57
  677.2 3.1 fusion.225
  680.3 12.0 %collective-permute-done.60 = bf16[2,2,256,512]{2,3,1,0:T(8,128)(2,1)} collective-permute-done((bf16[2,2,256,512]{2,3,1,0:T(8,128)(2,1)}, bf16[2,2,256,512]{2,3,1,0:T(8,128)(2,1)}, u32[]{:S(2)}, u32[]{:S(2)}) %collective-permute-start.60) | collective-permute-done | bytes 1048608 | tf_op jit(solution)/shard_map/ppermute | solution.py:107
  697.0 3.0 collective-permute-done.62
  705.9 2.4 multiply_add_fusion.11
  708.3 3.5 multiply_add_fusion.9
  711.9 2.5 fusion.124
  727.2 22.4 %collective-permute-done.74 = f32[16,8,128]{2,1,0:T(8,128)S(1)} collective-permute-done((f32[16,8,128]{2,1,0:T(8,128)S(1)}, f32[16,8,128]{2,1,0:T(8,128)S(1)}, u32[]{:S(2)}, u32[]{:S(2)}) %collective-permute-start.74) | collective-permute-done | bytes 65568 | tf_op jit(solution)/shard_map/ppermute | solution.py:107
  749.6 2.5 collective-permute-start.75
  752.2 3.1 add_convert_fusion.1
  755.4 5.7 collective-permute-start.64
  765.8 19.1 %collective-permute-done.77 = f32[2,8,128]{2,1,0:T(8,128)S(1)} collective-permute-done((f32[2,8,128]{2,1,0:T(8,128)S(1)}, f32[2,8,128]{2,1,0:T(8,128)S(1)}, u32[]{:S(2)}, u32[]{:S(2)}) %collective-permute-start.77) | collective-permute-done | bytes 8224 | tf_op jit(solution)/shard_map/ppermute | solution.py:107
  785.0 3.1 collective-permute-done.64
  791.3 21.1 %collective-permute-done.65 = bf16[1,2,256,512]{2,3,1,0:T(8,128)(2,1)} collective-permute-done((bf16[1,2,256,512]{2,3,1,0:T(8,128)(2,1)}, bf16[1,2,256,512]{2,3,1,0:T(8,128)(2,1)}, u32[]{:S(2)}, u32[]{:S(2)}) %collective-permute-start.65) | collective-permute-done | bytes 524320 | tf_op jit(solution)/shard_map/ppermute | solution.py:107
  817.3 3.9 fusion.131
  821.2 6.3 multiply_add_fusion
  827.6 4.0 fusion.130
  831.6 6.4 multiply_add_fusion.2
  (743 shorter events, 277.9 us)
Async XLA Ops:
  4.0 16.8 %collective-permute-start.7 = (bf16[2,128,512]{1,2,0:T(8,128)(2,1)}, bf16[2,128,512]{1,2,0:T(8,128)(2,1)}, u32[]{:S(2)}, u32[]{:S(2)}) collective-permute-start(bf16[2,128,512]{1,2,0:T(8,128)(2,1)} %broadcast_select_fusion.25), channel_id=1, source_target_pairs={{0,4},{1,5},{2,6},{3,7},{4,0},{5,1},{6,2},{7,3},{8,12},{9,13},{10,... | collective-permute-start | bytes 786440 | tf_op jit(solution)/shard_map/ppermute | solution.py:107
  15.5 145.0 %collective-permute-start = (bf16[256,1024]{1,0:T(8,128)(2,1)}, bf16[256,1024]{1,0:T(8,128)(2,1)}, u32[]{:S(2)}, u32[]{:S(2)}) collective-permute-start(bf16[256,1024]{1,0:T(8,128)(2,1)} %bitcast.579), channel_id=1, source_target_pairs={{2,4},{3,5},{4,2},{5,3},{10,12},{11,13},{12,10},{13,11},{18,20},{1... | collective-permute-start | bytes 1572872 | tf_op jit(solution)/shard_map/ppermute | solution.py:107
  17.1 57.0 %collective-permute-start.1 = (bf16[1,8,128]{2,1,0:T(8,128)(2,1)S(1)}, bf16[1,8,128]{2,1,0:T(8,128)(2,1)S(1)}, u32[]{:S(2)}, u32[]{:S(2)}) collective-permute-start(bf16[1,8,128]{2,1,0:T(8,128)(2,1)S(1)} %pad_bitcast_fusion.1), channel_id=1, source_target_pairs={{0,1},{1,0},{2,3},{3,2},{4,5},{5,4},{6,7},{7,6},{8,9},{9,8},{10,11... | collective-permute-start | bytes 6152 | tf_op jit(solution)/shard_map/ppermute | solution.py:107
  22.0 48.2 %collective-permute-start.8 = (bf16[1,2,256,512]{2,3,1,0:T(8,128)(2,1)S(1)}, bf16[1,2,256,512]{2,3,1,0:T(8,128)(2,1)S(1)}, u32[]{:S(2)}, u32[]{:S(2)}) collective-permute-start(bf16[1,2,256,512]{2,3,1,0:T(8,128)(2,1)S(1)} %maximum_bitcast_fusion.8), channel_id=1, source_target_pairs={{0,2},{1,3},{2,0},{3,1},{4,6},{5,7},{6,4},{7,5},{8,10},{9,11},{10,... | collective-permute-start | bytes 1572872 | tf_op jit(solution)/shard_map/ppermute | solution.py:107
  26.4 132.5 %collective-permute-start.14 = (bf16[7,128,256]{2,1,0:T(8,128)(2,1)}, bf16[7,128,256]{2,1,0:T(8,128)(2,1)}, u32[]{:S(2)}, u32[]{:S(2)}) collective-permute-start(bf16[7,128,256]{2,1,0:T(8,128)(2,1)} %pad_maximum_fusion.39), channel_id=1, source_target_pairs={{0,2},{1,3},{2,0},{3,1},{4,6},{5,7},{6,4},{7,5},{8,10},{9,11},{10,... | collective-permute-start | bytes 1376264 | tf_op jit(solution)/shard_map/ppermute | solution.py:107
  71.3 27.7 %collective-permute-start.9 = (bf16[2,2,256,512]{2,3,1,0:T(8,128)(2,1)}, bf16[2,2,256,512]{2,3,1,0:T(8,128)(2,1)S(1)}, u32[]{:S(2)}, u32[]{:S(2)}) collective-permute-start(bf16[2,2,256,512]{2,3,1,0:T(8,128)(2,1)} %pad_maximum_fusion.20), channel_id=1, source_target_pairs={{0,1},{1,0},{2,3},{3,2},{4,5},{5,4},{6,7},{7,6},{8,9},{9,8},{10,11... | collective-permute-start | bytes 3145736 | tf_op jit(solution)/shard_map/ppermute | solution.py:107
  74.1 20.7 %collective-permute-start.2 = (bf16[2,8,128]{2,1,0:T(8,128)(2,1)S(1)}, bf16[2,8,128]{2,1,0:T(8,128)(2,1)S(1)}, u32[]{:S(2)}, u32[]{:S(2)}) collective-permute-start(bf16[2,8,128]{2,1,0:T(8,128)(2,1)S(1)} %pad_maximum_fusion.45), channel_id=1, source_target_pairs={{0,2},{1,3},{2,0},{3,1},{4,6},{5,7},{6,4},{7,5},{8,10},{9,11},{10,... | collective-permute-start | bytes 12296 | tf_op jit(solution)/shard_map/ppermute | solution.py:107
  100.7 60.5 %collective-permute-start.10 = (bf16[4,2,256,512]{2,3,1,0:T(8,128)(2,1)}, bf16[4,2,256,512]{2,3,1,0:T(8,128)(2,1)}, u32[]{:S(2)}, u32[]{:S(2)}) collective-permute-start(bf16[4,2,256,512]{2,3,1,0:T(8,128)(2,1)} %pad_maximum_fusion.10), channel_id=1, source_target_pairs={{0,8},{1,9},{2,10},{3,11},{4,12},{5,13},{6,14},{7,15},{8,24},{9,25... | collective-permute-start | bytes 6291464 | tf_op jit(solution)/shard_map/ppermute | solution.py:107
  102.2 63.3 %collective-permute-start.11 = (bf16[4,2,256,512]{2,3,1,0:T(8,128)(2,1)}, bf16[4,2,256,512]{2,3,1,0:T(8,128)(2,1)}, u32[]{:S(2)}, u32[]{:S(2)}) collective-permute-start(bf16[4,2,256,512]{2,3,1,0:T(8,128)(2,1)} %pad_maximum_fusion.10), channel_id=1, source_target_pairs={{0,16},{1,17},{2,18},{3,19},{4,20},{5,21},{6,22},{7,23},{8,0},{9,1... | collective-permute-start | bytes 6291464 | tf_op jit(solution)/shard_map/ppermute | solution.py:107
  103.3 45.6 %collective-permute-start.5 = (bf16[16,8,128]{2,1,0:T(8,128)(2,1)S(1)}, bf16[16,8,128]{2,1,0:T(8,128)(2,1)S(1)}, u32[]{:S(2)}, u32[]{:S(2)}) collective-permute-start(bf16[16,8,128]{2,1,0:T(8,128)(2,1)S(1)} %get-tuple-element.186), channel_id=1, source_target_pairs={{0,16},{1,17},{2,18},{3,19},{4,20},{5,21},{6,22},{7,23},{8,24},{9,... | collective-permute-start | bytes 98312 | tf_op jit(solution)/shard_map/ppermute | solution.py:107
  149.0 86.2 %collective-permute-start.23 = (bf16[2,128,512]{1,2,0:T(8,128)(2,1)}, bf16[2,128,512]{1,2,0:T(8,128)(2,1)}, u32[]{:S(2)}, u32[]{:S(2)}) collective-permute-start(bf16[2,128,512]{1,2,0:T(8,128)(2,1)} %broadcast_select_fusion.21), channel_id=1, source_target_pairs={{0,4},{1,5},{2,6},{3,7},{4,0},{5,1},{6,2},{7,3},{8,12},{9,13},{10,... | collective-permute-start | bytes 786440 | tf_op jit(solution)/shard_map/ppermute | solution.py:107
  158.8 53.1 %collective-permute-start.24 = (s32[1024]{0:T(1024)}, s32[1024]{0:T(1024)S(1)}, u32[]{:S(2)}, u32[]{:S(2)}) collective-permute-start(s32[1024]{0:T(1024)} %bitcast.670), channel_id=1, source_target_pairs={{0,4},{1,5},{2,6},{3,7},{4,0},{5,1},{6,2},{7,3},{8,12},{9,13},{10,... | collective-permute-start | bytes 12296 | tf_op jit(solution)/shard_map/ppermute | solution.py:107
  162.5 26.1 %collective-permute-start.12 = (bf16[2,2,256,512]{2,3,1,0:T(8,128)(2,1)S(1)}, bf16[2,2,256,512]{2,3,1,0:T(8,128)(2,1)S(1)}, u32[]{:S(2)}, u32[]{:S(2)}) collective-permute-start(bf16[2,2,256,512]{2,3,1,0:T(8,128)(2,1)S(1)} %slice.772), channel_id=1, source_target_pairs={{0,8},{1,9},{2,10},{3,11},{4,12},{5,13},{6,14},{7,15},{8,24},{9,25... | collective-permute-start | bytes 3145736 | tf_op jit(solution)/shard_map/ppermute | solution.py:107
  166.8 25.8 %collective-permute-start.13 = (bf16[2,2,256,512]{2,3,1,0:T(8,128)(2,1)S(1)}, bf16[2,2,256,512]{2,3,1,0:T(8,128)(2,1)S(1)}, u32[]{:S(2)}, u32[]{:S(2)}) collective-permute-start(bf16[2,2,256,512]{2,3,1,0:T(8,128)(2,1)S(1)} %slice.773), channel_id=1, source_target_pairs={{0,16},{1,17},{2,18},{3,19},{4,20},{5,21},{6,22},{7,23},{8,0},{9,1... | collective-permute-start | bytes 3145736 | tf_op jit(solution)/shard_map/ppermute | solution.py:107
  167.2 28.8 %collective-permute-start.6 = (bf16[256,1024]{1,0:T(8,128)(2,1)S(1)}, bf16[256,1024]{1,0:T(8,128)(2,1)S(1)}, u32[]{:S(2)}, u32[]{:S(2)}) collective-permute-start(bf16[256,1024]{1,0:T(8,128)(2,1)S(1)} %fusion.118), channel_id=1, source_target_pairs={{0,4},{1,5},{2,6},{3,7},{4,0},{5,1},{6,2},{7,3},{8,12},{9,13},{10,... | collective-permute-start | bytes 1572872 | tf_op jit(solution)/shard_map/ppermute | solution.py:107
  206.8 22.9 %collective-permute-start.20 = (bf16[7,256,256]{2,1,0:T(8,128)(2,1)}, bf16[7,256,256]{2,1,0:T(8,128)(2,1)S(1)}, u32[]{:S(2)}, u32[]{:S(2)}) collective-permute-start(bf16[7,256,256]{2,1,0:T(8,128)(2,1)} %fusion.222), channel_id=1, source_target_pairs={{0,16},{1,17},{2,18},{3,19},{4,20},{5,21},{6,22},{7,23},{8,0},{9,1... | collective-permute-start | bytes 2752520 | tf_op jit(solution)/shard_map/ppermute | solution.py:107
  206.8 23.4 %collective-permute-start.19 = (bf16[7,256,256]{2,1,0:T(8,128)(2,1)}, bf16[7,256,256]{2,1,0:T(8,128)(2,1)}, u32[]{:S(2)}, u32[]{:S(2)}) collective-permute-start(bf16[7,256,256]{2,1,0:T(8,128)(2,1)} %fusion.222), channel_id=1, source_target_pairs={{0,8},{1,9},{2,10},{3,11},{4,12},{5,13},{6,14},{7,15},{8,24},{9,25... | collective-permute-start | bytes 2752520 | tf_op jit(solution)/shard_map/ppermute | solution.py:107
  211.0 22.1 %collective-permute-start.17 = (bf16[256,1024]{1,0:T(8,128)(2,1)}, bf16[256,1024]{1,0:T(8,128)(2,1)}, u32[]{:S(2)}, u32[]{:S(2)}) collective-permute-start(bf16[256,1024]{1,0:T(8,128)(2,1)} %add_convert_fusion.7), channel_id=1, source_target_pairs={{0,1},{1,0},{2,3},{3,2},{4,5},{5,4},{6,7},{7,6},{8,9},{9,8},{10,11... | collective-permute-start | bytes 1572872 | tf_op jit(solution)/shard_map/ppermute | solution.py:107
  229.8 13.6 %collective-permute-start.22 = (bf16[4,256,256]{2,1,0:T(8,128)(2,1)S(1)}, bf16[4,256,256]{2,1,0:T(8,128)(2,1)S(1)}, u32[]{:S(2)}, u32[]{:S(2)}) collective-permute-start(bf16[4,256,256]{2,1,0:T(8,128)(2,1)S(1)} %slice.785), channel_id=1, source_target_pairs={{0,16},{1,17},{2,18},{3,19},{4,20},{5,21},{6,22},{7,23},{8,0},{9,1... | collective-permute-start | bytes 1572872 | tf_op jit(solution)/shard_map/ppermute | solution.py:107
  231.3 10.7 %collective-permute-start.21 = (bf16[3,256,256]{2,1,0:T(8,128)(2,1)S(1)}, bf16[3,256,256]{2,1,0:T(8,128)(2,1)S(1)}, u32[]{:S(2)}, u32[]{:S(2)}) collective-permute-start(bf16[3,256,256]{2,1,0:T(8,128)(2,1)S(1)} %slice.784), channel_id=1, source_target_pairs={{0,8},{1,9},{2,10},{3,11},{4,12},{5,13},{6,14},{7,15},{8,24},{9,25... | collective-permute-start | bytes 1179656 | tf_op jit(solution)/shard_map/ppermute | solution.py:107
  234.4 10.9 %collective-permute-start.18 = (bf16[512,1024]{1,0:T(8,128)(2,1)S(1)}, bf16[512,1024]{1,0:T(8,128)(2,1)S(1)}, u32[]{:S(2)}, u32[]{:S(2)}) collective-permute-start(bf16[512,1024]{1,0:T(8,128)(2,1)S(1)} %pad_maximum_fusion.21), channel_id=1, source_target_pairs={{0,4},{1,5},{2,6},{3,7},{4,0},{5,1},{6,2},{7,3},{8,12},{9,13},{10,... | collective-permute-start | bytes 3145736 | tf_op jit(solution)/shard_map/ppermute | solution.py:107
  262.1 25.0 %collective-permute-start.26 = (bf16[256,1024]{1,0:T(8,128)(2,1)S(1)}, bf16[256,1024]{1,0:T(8,128)(2,1)S(1)}, u32[]{:S(2)}, u32[]{:S(2)}) collective-permute-start(bf16[256,1024]{1,0:T(8,128)(2,1)S(1)} %slice.1249), channel_id=1, source_target_pairs={{0,1},{1,0},{2,3},{3,2},{4,5},{5,4},{6,7},{7,6},{8,9},{9,8},{10,11... | collective-permute-start | bytes 1572872 | tf_op jit(solution)/shard_map/ppermute | solution.py:107
  263.0 25.9 %collective-permute-start.32 = (bf16[1,2,256,512]{2,3,1,0:T(8,128)(2,1)S(1)}, bf16[1,2,256,512]{2,3,1,0:T(8,128)(2,1)S(1)}, u32[]{:S(2)}, u32[]{:S(2)}) collective-permute-start(bf16[1,2,256,512]{2,3,1,0:T(8,128)(2,1)S(1)} %maximum_bitcast_fusion.9), channel_id=1, source_target_pairs={{0,2},{1,3},{2,0},{3,1},{4,6},{5,7},{6,4},{7,5},{8,10},{9,11},{10,... | collective-permute-start | bytes 1572872 | tf_op jit(solution)/shard_map/ppermute | solution.py:107
  287.9 14.9 %collective-permute-start.27 = (bf16[256,1024]{1,0:T(8,128)(2,1)S(1)}, bf16[256,1024]{1,0:T(8,128)(2,1)S(1)}, u32[]{:S(2)}, u32[]{:S(2)}) collective-permute-start(bf16[256,1024]{1,0:T(8,128)(2,1)S(1)} %add_convert_fusion.6), channel_id=1, source_target_pairs={{0,1},{1,0},{2,3},{3,2},{4,5},{5,4},{6,7},{7,6},{8,9},{9,8},{10,11... | collective-permute-start | bytes 1572872 | tf_op jit(solution)/shard_map/ppermute | solution.py:107
  290.0 33.7 %collective-permute-start.33 = (bf16[2,2,256,512]{2,3,1,0:T(8,128)(2,1)}, bf16[2,2,256,512]{2,3,1,0:T(8,128)(2,1)}, u32[]{:S(2)}, u32[]{:S(2)}) collective-permute-start(bf16[2,2,256,512]{2,3,1,0:T(8,128)(2,1)} %pad_maximum_fusion.24), channel_id=1, source_target_pairs={{0,1},{1,0},{2,3},{3,2},{4,5},{5,4},{6,7},{7,6},{8,9},{9,8},{10,11... | collective-permute-start | bytes 3145736 | tf_op jit(solution)/shard_map/ppermute | solution.py:107
  303.0 25.2 %collective-permute-start.28 = (bf16[512,1024]{1,0:T(8,128)(2,1)S(1)}, bf16[512,1024]{1,0:T(8,128)(2,1)}, u32[]{:S(2)}, u32[]{:S(2)}) collective-permute-start(bf16[512,1024]{1,0:T(8,128)(2,1)S(1)} %pad_maximum_fusion.22), channel_id=1, source_target_pairs={{0,4},{1,5},{2,6},{3,7},{4,0},{5,1},{6,2},{7,3},{8,12},{9,13},{10,... | collective-permute-start | bytes 3145736 | tf_op jit(solution)/shard_map/ppermute | solution.py:107
  326.0 46.2 %collective-permute-start.34 = (bf16[4,2,256,512]{2,3,1,0:T(8,128)(2,1)}, bf16[4,2,256,512]{2,3,1,0:T(8,128)(2,1)}, u32[]{:S(2)}, u32[]{:S(2)}) collective-permute-start(bf16[4,2,256,512]{2,3,1,0:T(8,128)(2,1)} %constant_dynamic-update-slice_fusion.11), channel_id=1, source_target_pairs={{0,8},{1,9},{2,10},{3,11},{4,12},{5,13},{6,14},{7,15},{8,24},{9,25... | collective-permute-start | bytes 6291464 | tf_op jit(solution)/shard_map/ppermute | solution.py:107
  326.2 47.7 %collective-permute-start.35 = (bf16[4,2,256,512]{2,3,1,0:T(8,128)(2,1)}, bf16[4,2,256,512]{2,3,1,0:T(8,128)(2,1)}, u32[]{:S(2)}, u32[]{:S(2)}) collective-permute-start(bf16[4,2,256,512]{2,3,1,0:T(8,128)(2,1)} %constant_dynamic-update-slice_fusion.11), channel_id=1, source_target_pairs={{0,16},{1,17},{2,18},{3,19},{4,20},{5,21},{6,22},{7,23},{8,0},{9,1... | collective-permute-start | bytes 6291464 | tf_op jit(solution)/shard_map/ppermute | solution.py:107
  350.7 26.2 %collective-permute-start.30 = (bf16[256,1024]{1,0:T(8,128)(2,1)S(1)}, bf16[256,1024]{1,0:T(8,128)(2,1)S(1)}, u32[]{:S(2)}, u32[]{:S(2)}) collective-permute-start(bf16[256,1024]{1,0:T(8,128)(2,1)S(1)} %slice.1248), channel_id=1, source_target_pairs={{0,1},{1,0},{2,3},{3,2},{4,5},{5,4},{6,7},{7,6},{8,9},{9,8},{10,11... | collective-permute-start | bytes 1572872 | tf_op jit(solution)/shard_map/ppermute | solution.py:107
  373.5 22.6 %collective-permute-start.36 = (bf16[2,2,256,512]{2,3,1,0:T(8,128)(2,1)S(1)}, bf16[2,2,256,512]{2,3,1,0:T(8,128)(2,1)S(1)}, u32[]{:S(2)}, u32[]{:S(2)}) collective-permute-start(bf16[2,2,256,512]{2,3,1,0:T(8,128)(2,1)S(1)} %slice.803), channel_id=1, source_target_pairs={{0,8},{1,9},{2,10},{3,11},{4,12},{5,13},{6,14},{7,15},{8,24},{9,25... | collective-permute-start | bytes 3145736 | tf_op jit(solution)/shard_map/ppermute | solution.py:107
  375.1 22.4 %collective-permute-start.37 = (bf16[2,2,256,512]{2,3,1,0:T(8,128)(2,1)S(1)}, bf16[2,2,256,512]{2,3,1,0:T(8,128)(2,1)S(1)}, u32[]{:S(2)}, u32[]{:S(2)}) collective-permute-start(bf16[2,2,256,512]{2,3,1,0:T(8,128)(2,1)S(1)} %slice.804), channel_id=1, source_target_pairs={{0,16},{1,17},{2,18},{3,19},{4,20},{5,21},{6,22},{7,23},{8,0},{9,1... | collective-permute-start | bytes 3145736 | tf_op jit(solution)/shard_map/ppermute | solution.py:107
  377.8 23.7 %collective-permute-start.31 = (bf16[256,1024]{1,0:T(8,128)(2,1)S(1)}, bf16[256,1024]{1,0:T(8,128)(2,1)S(1)}, u32[]{:S(2)}, u32[]{:S(2)}) collective-permute-start(bf16[256,1024]{1,0:T(8,128)(2,1)S(1)} %add_convert_fusion.5), channel_id=1, source_target_pairs={{0,4},{1,5},{2,6},{3,7},{4,0},{5,1},{6,2},{7,3},{8,12},{9,13},{10,... | collective-permute-start | bytes 1572872 | tf_op jit(solution)/shard_map/ppermute | solution.py:107
  411.7 16.8 %collective-permute-start.41 = (bf16[256,1024]{1,0:T(8,128)(2,1)S(1)}, bf16[256,1024]{1,0:T(8,128)(2,1)S(1)}, u32[]{:S(2)}, u32[]{:S(2)}) collective-permute-start(bf16[256,1024]{1,0:T(8,128)(2,1)S(1)} %multiply_convert_fusion.4), channel_id=1, source_target_pairs={{0,4},{1,5},{2,6},{3,7},{4,0},{5,1},{6,2},{7,3},{8,12},{9,13},{10,... | collective-permute-start | bytes 1572872 | tf_op jit(solution)/shard_map/ppermute | solution.py:107
  439.4 25.5 %collective-permute-start.67 = (bf16[2,2,256,512]{2,3,1,0:T(8,128)(2,1)S(1)}, bf16[2,2,256,512]{2,3,1,0:T(8,128)(2,1)S(1)}, u32[]{:S(2)}, u32[]{:S(2)}) collective-permute-start(bf16[2,2,256,512]{2,3,1,0:T(8,128)(2,1)S(1)} %pad_maximum_fusion.16), channel_id=1, source_target_pairs={{0,8},{1,9},{2,10},{3,11},{4,12},{5,13},{6,14},{7,15},{8,24},{9,25... | collective-permute-start | bytes 3145736 | tf_op jit(solution)/shard_map/ppermute | solution.py:107
  447.7 13.7 %collective-permute-start.43 = (bf16[256,1024]{1,0:T(8,128)(2,1)S(1)}, bf16[256,1024]{1,0:T(8,128)(2,1)S(1)}, u32[]{:S(2)}, u32[]{:S(2)}) collective-permute-start(bf16[256,1024]{1,0:T(8,128)(2,1)S(1)} %get-tuple-element.114), channel_id=1, source_target_pairs={{0,1},{1,0},{2,3},{3,2},{4,5},{5,4},{6,7},{7,6},{8,9},{9,8},{10,11... | collective-permute-start | bytes 1572872 | tf_op jit(solution)/shard_map/ppermute | solution.py:107
  448.0 25.0 %collective-permute-start.69 = (bf16[2,2,256,512]{2,3,1,0:T(8,128)(2,1)S(1)}, bf16[2,2,256,512]{2,3,1,0:T(8,128)(2,1)S(1)}, u32[]{:S(2)}, u32[]{:S(2)}) collective-permute-start(bf16[2,2,256,512]{2,3,1,0:T(8,128)(2,1)S(1)} %pad_maximum_fusion.15), channel_id=1, source_target_pairs={{0,16},{1,17},{2,18},{3,19},{4,20},{5,21},{6,22},{7,23},{8,0},{9,1... | collective-permute-start | bytes 3145736 | tf_op jit(solution)/shard_map/ppermute | solution.py:107
  461.4 14.5 %collective-permute-start.44 = (bf16[512,1024]{1,0:T(8,128)(2,1)S(1)}, bf16[512,1024]{1,0:T(8,128)(2,1)S(1)}, u32[]{:S(2)}, u32[]{:S(2)}) collective-permute-start(bf16[512,1024]{1,0:T(8,128)(2,1)S(1)} %pad_maximum_fusion.26), channel_id=1, source_target_pairs={{0,4},{1,5},{2,6},{3,7},{4,0},{5,1},{6,2},{7,3},{8,12},{9,13},{10,... | collective-permute-start | bytes 3145736 | tf_op jit(solution)/shard_map/ppermute | solution.py:107
  466.8 47.2 %collective-permute-start.68 = (bf16[4,2,256,512]{2,3,1,0:T(8,128)(2,1)}, bf16[4,2,256,512]{2,3,1,0:T(8,128)(2,1)}, u32[]{:S(2)}, u32[]{:S(2)}) collective-permute-start(bf16[4,2,256,512]{2,3,1,0:T(8,128)(2,1)} %fusion.15), channel_id=1, source_target_pairs={{0,8},{1,9},{2,10},{3,11},{4,12},{5,13},{6,14},{7,15},{8,24},{9,25... | collective-permute-start | bytes 6291464 | tf_op jit(solution)/shard_map/ppermute | solution.py:107
  474.9 47.4 %collective-permute-start.70 = (bf16[4,2,256,512]{2,3,1,0:T(8,128)(2,1)}, bf16[4,2,256,512]{2,3,1,0:T(8,128)(2,1)}, u32[]{:S(2)}, u32[]{:S(2)}) collective-permute-start(bf16[4,2,256,512]{2,3,1,0:T(8,128)(2,1)} %fusion.14), channel_id=1, source_target_pairs={{0,16},{1,17},{2,18},{3,19},{4,20},{5,21},{6,22},{7,23},{8,0},{9,1... | collective-permute-start | bytes 6291464 | tf_op jit(solution)/shard_map/ppermute | solution.py:107
  502.0 24.7 %collective-permute-start.46 = (bf16[256,1024]{1,0:T(8,128)(2,1)S(1)}, bf16[256,1024]{1,0:T(8,128)(2,1)S(1)}, u32[]{:S(2)}, u32[]{:S(2)}) collective-permute-start(bf16[256,1024]{1,0:T(8,128)(2,1)S(1)} %slice.1245), channel_id=1, source_target_pairs={{0,1},{1,0},{2,3},{3,2},{4,5},{5,4},{6,7},{7,6},{8,9},{9,8},{10,11... | collective-permute-start | bytes 1572872 | tf_op jit(solution)/shard_map/ppermute | solution.py:107
  525.2 31.8 %collective-permute-start.71 = (bf16[2,2,256,512]{2,3,1,0:T(8,128)(2,1)S(1)}, bf16[2,2,256,512]{2,3,1,0:T(8,128)(2,1)S(1)}, u32[]{:S(2)}, u32[]{:S(2)}) collective-permute-start(bf16[2,2,256,512]{2,3,1,0:T(8,128)(2,1)S(1)} %slice.842), channel_id=1, source_target_pairs={{0,1},{1,0},{2,3},{3,2},{4,5},{5,4},{6,7},{7,6},{8,9},{9,8},{10,11... | collective-permute-start | bytes 3145736 | tf_op jit(solution)/shard_map/ppermute | solution.py:107
  528.2 38.3 %collective-permute-start.47 = (bf16[256,1024]{1,0:T(8,128)(2,1)S(1)}, bf16[256,1024]{1,0:T(8,128)(2,1)S(1)}, u32[]{:S(2)}, u32[]{:S(2)}) collective-permute-start(bf16[256,1024]{1,0:T(8,128)(2,1)S(1)} %get-tuple-element.110), channel_id=1, source_target_pairs={{0,1},{1,0},{2,3},{3,2},{4,5},{5,4},{6,7},{7,6},{8,9},{9,8},{10,11... | collective-permute-start | bytes 1572872 | tf_op jit(solution)/shard_map/ppermute | solution.py:107
  557.2 25.2 %collective-permute-start.72 = (bf16[1,2,256,512]{2,3,1,0:T(8,128)(2,1)S(1)}, bf16[1,2,256,512]{2,3,1,0:T(8,128)(2,1)S(1)}, u32[]{:S(2)}, u32[]{:S(2)}) collective-permute-start(bf16[1,2,256,512]{2,3,1,0:T(8,128)(2,1)S(1)} %slice.844), channel_id=1, source_target_pairs={{0,2},{1,3},{2,0},{3,1},{4,6},{5,7},{6,4},{7,5},{8,10},{9,11},{10,... | collective-permute-start | bytes 1572872 | tf_op jit(solution)/shard_map/ppermute | solution.py:107
  566.6 16.5 %collective-permute-start.48 = (bf16[512,1024]{1,0:T(8,128)(2,1)S(1)}, bf16[512,1024]{1,0:T(8,128)(2,1)S(1)}, u32[]{:S(2)}, u32[]{:S(2)}) collective-permute-start(bf16[512,1024]{1,0:T(8,128)(2,1)S(1)} %pad_maximum_fusion.27), channel_id=1, source_target_pairs={{0,4},{1,5},{2,6},{3,7},{4,0},{5,1},{6,2},{7,3},{8,12},{9,13},{10,... | collective-permute-start | bytes 3145736 | tf_op jit(solution)/shard_map/ppermute | solution.py:107
  566.8 58.5 %collective-permute-start.39 = (bf16[256,1024]{1,0:T(8,128)(2,1)S(1)}, bf16[256,1024]{1,0:T(8,128)(2,1)S(1)}, u32[]{:S(2)}, u32[]{:S(2)}) collective-permute-start(bf16[256,1024]{1,0:T(8,128)(2,1)S(1)} %copy-done.52), channel_id=1, source_target_pairs={{2,4},{3,5},{4,2},{5,3},{10,12},{11,13},{12,10},{13,11},{18,20},{1... | collective-permute-start | bytes 1572872 | tf_op jit(solution)/shard_map/ppermute | solution.py:107
  583.1 43.8 %collective-permute-start.73 = (bf16[2,128,512]{1,2,0:T(8,128)(2,1)}, bf16[2,128,512]{1,2,0:T(8,128)(2,1)}, u32[]{:S(2)}, u32[]{:S(2)}) collective-permute-start(bf16[2,128,512]{1,2,0:T(8,128)(2,1)} %select_bitcast_fusion.6), channel_id=1, source_target_pairs={{0,4},{1,5},{2,6},{3,7},{4,0},{5,1},{6,2},{7,3},{8,12},{9,13},{10,... | collective-permute-start | bytes 786440 | tf_op jit(solution)/shard_map/ppermute | solution.py:107
  601.4 11.5 %collective-permute-start.54 = (bf16[3,256,256]{2,1,0:T(8,128)(2,1)S(1)}, bf16[3,256,256]{2,1,0:T(8,128)(2,1)S(1)}, u32[]{:S(2)}, u32[]{:S(2)}) collective-permute-start(bf16[3,256,256]{2,1,0:T(8,128)(2,1)S(1)} %pad_maximum_fusion.40), channel_id=1, source_target_pairs={{0,8},{1,9},{2,10},{3,11},{4,12},{5,13},{6,14},{7,15},{8,24},{9,25... | collective-permute-start | bytes 1179656 | tf_op jit(solution)/shard_map/ppermute | solution.py:107
  609.3 13.1 %collective-permute-start.56 = (bf16[4,256,256]{2,1,0:T(8,128)(2,1)S(1)}, bf16[4,256,256]{2,1,0:T(8,128)(2,1)S(1)}, u32[]{:S(2)}, u32[]{:S(2)}) collective-permute-start(bf16[4,256,256]{2,1,0:T(8,128)(2,1)S(1)} %pad_maximum_fusion.36), channel_id=1, source_target_pairs={{0,16},{1,17},{2,18},{3,19},{4,20},{5,21},{6,22},{7,23},{8,0},{9,1... | collective-permute-start | bytes 1572872 | tf_op jit(solution)/shard_map/ppermute | solution.py:107
  612.9 15.0 %collective-permute-start.49 = (bf16[512,1024]{1,0:T(8,128)(2,1)}, bf16[512,1024]{1,0:T(8,128)(2,1)}, u32[]{:S(2)}, u32[]{:S(2)}) collective-permute-start(bf16[512,1024]{1,0:T(8,128)(2,1)} %slice.1241), channel_id=1, source_target_pairs={{0,4},{1,5},{2,6},{3,7},{4,0},{5,1},{6,2},{7,3},{8,12},{9,13},{10,... | collective-permute-start | bytes 3145736 | tf_op jit(solution)/shard_map/ppermute | solution.py:107
  614.9 22.1 %collective-permute-start.55 = (bf16[7,256,256]{2,1,0:T(8,128)(2,1)}, bf16[7,256,256]{2,1,0:T(8,128)(2,1)}, u32[]{:S(2)}, u32[]{:S(2)}) collective-permute-start(bf16[7,256,256]{2,1,0:T(8,128)(2,1)} %fusion.224), channel_id=1, source_target_pairs={{0,8},{1,9},{2,10},{3,11},{4,12},{5,13},{6,14},{7,15},{8,24},{9,25... | collective-permute-start | bytes 2752520 | tf_op jit(solution)/shard_map/ppermute | solution.py:107
  623.6 21.3 %collective-permute-start.57 = (bf16[7,256,256]{2,1,0:T(8,128)(2,1)}, bf16[7,256,256]{2,1,0:T(8,128)(2,1)}, u32[]{:S(2)}, u32[]{:S(2)}) collective-permute-start(bf16[7,256,256]{2,1,0:T(8,128)(2,1)} %fusion.223), channel_id=1, source_target_pairs={{0,16},{1,17},{2,18},{3,19},{4,20},{5,21},{6,22},{7,23},{8,0},{9,1... | collective-permute-start | bytes 2752520 | tf_op jit(solution)/shard_map/ppermute | solution.py:107
  630.2 17.1 %collective-permute-start.50 = (bf16[256,1024]{1,0:T(8,128)(2,1)S(1)}, bf16[256,1024]{1,0:T(8,128)(2,1)S(1)}, u32[]{:S(2)}, u32[]{:S(2)}) collective-permute-start(bf16[256,1024]{1,0:T(8,128)(2,1)S(1)} %slice.1244), channel_id=1, source_target_pairs={{0,1},{1,0},{2,3},{3,2},{4,5},{5,4},{6,7},{7,6},{8,9},{9,8},{10,11... | collective-permute-start | bytes 1572872 | tf_op jit(solution)/shard_map/ppermute | solution.py:107
  650.8 24.2 %collective-permute-start.59 = (bf16[7,128,256]{2,1,0:T(8,128)(2,1)S(1)}, bf16[7,128,256]{2,1,0:T(8,128)(2,1)S(1)}, u32[]{:S(2)}, u32[]{:S(2)}) collective-permute-start(bf16[7,128,256]{2,1,0:T(8,128)(2,1)S(1)} %broadcast_select_fusion.6), channel_id=1, source_target_pairs={{0,2},{1,3},{2,0},{3,1},{4,6},{5,7},{6,4},{7,5},{8,10},{9,11},{10,... | collective-permute-start | bytes 1376264 | tf_op jit(solution)/shard_map/ppermute | solution.py:107
  660.5 51.3 %collective-permute-start.52 = (bf16[256,1024]{1,0:T(8,128)(2,1)}, bf16[256,1024]{1,0:T(8,128)(2,1)}, u32[]{:S(2)}, u32[]{:S(2)}) collective-permute-start(bf16[256,1024]{1,0:T(8,128)(2,1)} %slice.1243), channel_id=1, source_target_pairs={{0,4},{1,5},{2,6},{3,7},{4,0},{5,1},{6,2},{7,3},{8,12},{9,13},{10,... | collective-permute-start | bytes 1572872 | tf_op jit(solution)/shard_map/ppermute | solution.py:107
  666.2 26.1 %collective-permute-start.60 = (bf16[2,2,256,512]{2,3,1,0:T(8,128)(2,1)}, bf16[2,2,256,512]{2,3,1,0:T(8,128)(2,1)}, u32[]{:S(2)}, u32[]{:S(2)}) collective-permute-start(bf16[2,2,256,512]{2,3,1,0:T(8,128)(2,1)} %pad_maximum_fusion.18), channel_id=1, source_target_pairs={{0,8},{1,9},{2,10},{3,11},{4,12},{5,13},{6,14},{7,15},{8,24},{9,25... | collective-permute-start | bytes 3145736 | tf_op jit(solution)/shard_map/ppermute | solution.py:107
  674.5 25.5 %collective-permute-start.62 = (bf16[2,2,256,512]{2,3,1,0:T(8,128)(2,1)}, bf16[2,2,256,512]{2,3,1,0:T(8,128)(2,1)}, u32[]{:S(2)}, u32[]{:S(2)}) collective-permute-start(bf16[2,2,256,512]{2,3,1,0:T(8,128)(2,1)} %pad_maximum_fusion.17), channel_id=1, source_target_pairs={{0,16},{1,17},{2,18},{3,19},{4,20},{5,21},{6,22},{7,23},{8,0},{9,1... | collective-permute-start | bytes 3145736 | tf_op jit(solution)/shard_map/ppermute | solution.py:107
  695.5 56.7 %collective-permute-start.61 = (bf16[4,2,256,512]{2,3,1,0:T(8,128)(2,1)}, bf16[4,2,256,512]{2,3,1,0:T(8,128)(2,1)}, u32[]{:S(2)}, u32[]{:S(2)}) collective-permute-start(bf16[4,2,256,512]{2,3,1,0:T(8,128)(2,1)} %fusion.17), channel_id=1, source_target_pairs={{0,8},{1,9},{2,10},{3,11},{4,12},{5,13},{6,14},{7,15},{8,24},{9,25... | collective-permute-start | bytes 6291464 | tf_op jit(solution)/shard_map/ppermute | solution.py:107
  703.2 49.0 %collective-permute-start.63 = (bf16[4,2,256,512]{2,3,1,0:T(8,128)(2,1)}, bf16[4,2,256,512]{2,3,1,0:T(8,128)(2,1)}, u32[]{:S(2)}, u32[]{:S(2)}) collective-permute-start(bf16[4,2,256,512]{2,3,1,0:T(8,128)(2,1)} %fusion.16), channel_id=1, source_target_pairs={{0,16},{1,17},{2,18},{3,19},{4,20},{5,21},{6,22},{7,23},{8,0},{9,1... | collective-permute-start | bytes 6291464 | tf_op jit(solution)/shard_map/ppermute | solution.py:107
  725.0 24.6 %collective-permute-start.74 = (f32[16,8,128]{2,1,0:T(8,128)S(1)}, f32[16,8,128]{2,1,0:T(8,128)S(1)}, u32[]{:S(2)}, u32[]{:S(2)}) collective-permute-start(f32[16,8,128]{2,1,0:T(8,128)S(1)} %slice.853), channel_id=1, source_target_pairs={{0,16},{1,17},{2,18},{3,19},{4,20},{5,21},{6,22},{7,23},{8,24},{9,... | collective-permute-start | bytes 196616 | tf_op jit(solution)/shard_map/ppermute | solution.py:107
  749.6 11.5 %collective-permute-start.75 = (f32[8,8,128]{2,1,0:T(8,128)S(1)}, f32[8,8,128]{2,1,0:T(8,128)S(1)}, u32[]{:S(2)}, u32[]{:S(2)}) collective-permute-start(f32[8,8,128]{2,1,0:T(8,128)S(1)} %slice.855), channel_id=1, source_target_pairs={{0,8},{1,9},{2,10},{3,11},{4,12},{5,13},{6,14},{7,15},{8,0},{9,1},... | collective-permute-start | bytes 98312 | tf_op jit(solution)/shard_map/ppermute | solution.py:107
  755.4 32.7 %collective-permute-start.64 = (bf16[2,2,256,512]{2,3,1,0:T(8,128)(2,1)S(1)}, bf16[2,2,256,512]{2,3,1,0:T(8,128)(2,1)S(1)}, u32[]{:S(2)}, u32[]{:S(2)}) collective-permute-start(bf16[2,2,256,512]{2,3,1,0:T(8,128)(2,1)S(1)} %slice.835), channel_id=1, source_target_pairs={{0,1},{1,0},{2,3},{3,2},{4,5},{5,4},{6,7},{7,6},{8,9},{9,8},{10,11... | collective-permute-start | bytes 3145736 | tf_op jit(solution)/shard_map/ppermute | solution.py:107
  762.4 22.5 %collective-permute-start.77 = (f32[2,8,128]{2,1,0:T(8,128)S(1)}, f32[2,8,128]{2,1,0:T(8,128)S(1)}, u32[]{:S(2)}, u32[]{:S(2)}) collective-permute-start(f32[2,8,128]{2,1,0:T(8,128)S(1)} %slice.859), channel_id=1, source_target_pairs={{0,2},{1,3},{2,0},{3,1},{4,6},{5,7},{6,4},{7,5},{8,10},{9,11},{10,... | collective-permute-start | bytes 24584 | tf_op jit(solution)/shard_map/ppermute | solution.py:107
  764.9 25.4 %collective-permute-start.53 = (bf16[256,1024]{1,0:T(8,128)(2,1)S(1)}, bf16[256,1024]{1,0:T(8,128)(2,1)S(1)}, u32[]{:S(2)}, u32[]{:S(2)}) collective-permute-start(bf16[256,1024]{1,0:T(8,128)(2,1)S(1)} %fusion.123), channel_id=1, source_target_pairs={{2,4},{3,5},{4,2},{5,3},{10,12},{11,13},{12,10},{13,11},{18,20},{1... | collective-permute-start | bytes 1572872 | tf_op jit(solution)/shard_map/ppermute | solution.py:107
  789.1 23.2 %collective-permute-start.65 = (bf16[1,2,256,512]{2,3,1,0:T(8,128)(2,1)}, bf16[1,2,256,512]{2,3,1,0:T(8,128)(2,1)}, u32[]{:S(2)}, u32[]{:S(2)}) collective-permute-start(bf16[1,2,256,512]{2,3,1,0:T(8,128)(2,1)} %slice.837), channel_id=1, source_target_pairs={{0,2},{1,3},{2,0},{3,1},{4,6},{5,7},{6,4},{7,5},{8,10},{9,11},{10,... | collective-permute-start | bytes 1572872 | tf_op jit(solution)/shard_map/ppermute | solution.py:107
  (162 other events, 2069.9 us)

commit v2 on v1

v2 whole, which is shorter than its diff:
```python
import math
from functools import partial

import jax
import jax.numpy as jnp
from jax import lax
from jax.experimental import pallas as pl
from jax.experimental.pallas import tpu as pltpu
from jax.sharding import PartitionSpec as P

HEAD_DIM = 128
KERNEL = 5
STEP = 10


NORM_EPS = 1e-05
MASKED = -1e30
BETA_ONE = 0.9
BETA_TWO = 0.95
ADAM_EPS = 1e-08
DECAY = 0.01
EMA_DECAY = 0.7
RATE_INNER = 0.03
RATE_EXPAND = 0.03
RATE_OUTPUT = 0.25
RATE_SHRINK = 0.015
RATE_SMALL = 0.5
AXES = ("dp", "mp")
F32 = jnp.float32
BF16 = jnp.bfloat16


def dot(left, right, contract):
    return lax.dot_general(left, right, (contract, ((), ())), preferred_element_type=F32)


def mm(left, right):
    return dot(left, right, ((1,), (0,)))


def mm_nt(left, right):
    return dot(left, right, ((1,), (1,)))


def mm_tn(left, right):
    return dot(left, right, ((0,), (0,)))


def reorder_kernel(blocks, order, source, target):
    share = source.shape[1] // blocks
    for at in range(blocks):
        columns = pl.ds(pl.multiple_of(order[at] * share, share), share)
        target[:, at * share : (at + 1) * share] = source[:, columns]


def reorder_blocks(rows, order):
    height, width = rows.shape
    blocks = order.shape[0]
    share = width // blocks
    if share % 128:
        return jnp.take(rows.reshape(height, blocks, share), order, axis=1).reshape(rows.shape)
    return pl.pallas_call(
        partial(reorder_kernel, blocks),
        out_shape=jax.ShapeDtypeStruct(rows.shape, rows.dtype),
        in_specs=[
            pl.BlockSpec(memory_space=pltpu.SMEM),
            pl.BlockSpec(memory_space=pltpu.VMEM),
        ],
        out_specs=pl.BlockSpec(memory_space=pltpu.VMEM),
        name="reorder_blocks",
    )(order, rows)


class Plan:
    def __init__(self, n_dp, n_mp):
        self.n_dp, self.n_mp, self.half = n_dp, n_mp, n_mp // 2
        self.chips = n_dp // 2
        side = math.isqrt(self.chips)
        if side * side == self.chips and side % 2 == 0:
            order = [(0, x) for x in range(side)]
            for y in range(1, side):
                xs = range(side - 1, 0, -1) if y % 2 else range(1, side)
                order += [(y, x) for x in xs]
            order += [(y, 0) for y in range(side - 1, 0, -1)]
            self.ring = [y * side + x for y, x in order]
        else:
            self.ring = list(range(self.chips))
        self.place = {chip: at for at, chip in enumerate(self.ring)}
        reach = self.chips // 2
        self.offsets = [0]
        for hop in range(1, reach):
            self.offsets += [-hop, hop]
        self.offsets.append(reach)
        self.to_next = self.perm(lambda chip, core, z: (self.beside(chip, 1), core, z))
        self.to_last = self.perm(lambda chip, core, z: (self.beside(chip, -1), core, z))
        self.swap_core = self.perm(lambda chip, core, z: (chip, 1 - core, z))
        self.swap_rows = self.perm(
            lambda chip, core, z: (chip, 1 - core, z ^ self.half) if core != z // self.half else None
        )
        self.to_chunk_above = self.perm(lambda chip, core, z: self.chunk_beside(chip, core, z, 1))
        self.to_chunk_below = self.perm(lambda chip, core, z: self.chunk_beside(chip, core, z, -1))
        self.table = [
            [2 * self.beside(chip, offset) + core for offset in self.offsets for core in (0, 1)]
            for chip in range(self.chips)
        ]

    def beside(self, chip, offset):
        return self.ring[(self.place[chip] + offset) % self.chips]

    def chunk_beside(self, chip, core, z, step):
        at = core * self.half + z % self.half + step
        if not 0 <= at < self.n_mp:
            return None
        return chip, at // self.half, z // self.half * self.half + at % self.half

    def perm(self, target):
        pairs = []
        for chip in range(self.chips):
            for core in (0, 1):
                for z in range(self.n_mp):
                    to = target(chip, core, z)
                    if to is not None:
                        source = (2 * chip + core) * self.n_mp + z
                        pairs.append((source, (2 * to[0] + to[1]) * self.n_mp + to[2]))
        return pairs

    def swap_z(self, bit):
        return self.perm(lambda chip, core, z: (chip, core, z ^ bit))

    def z_bits(self):
        bits, bit = [], self.half
        while bit:
            bits.append(bit)
            bit //= 2
        return bits

    def z_order(self, bits):
        order = [0]
        for bit in bits:
            order = order + [at ^ bit for at in order]
        return order


def send(value, pairs):
    return lax.ppermute(value, AXES, pairs)


def after(value, *earlier):
    return lax.optimization_barrier((value,) + earlier)[0]


def together(*values):
    return lax.optimization_barrier(values)


def gather_hops(plan, shard):
    from_last, from_next = shard, shard
    found = [shard]
    for _ in range(1, plan.chips // 2):
        from_last, from_next = send(from_last, plan.to_next), send(from_next, plan.to_last)
        found += [from_last, from_next]
    return found


def gather_end(plan, found, *earlier):
    cut = found[0].shape[0] // 2
    from_last, from_next = found[-2], found[-1]
    if earlier:
        from_last, from_next, *_ = together(from_last, from_next, *earlier)
    return [send(from_last[:cut], plan.to_next), send(from_next[cut:], plan.to_last)]


def gathered(found, ends, height=None):
    height = height or found[0].shape[0]
    cut = ends[0].shape[0]
    whole = jnp.concatenate(
        [part[:height] for part in found] + [ends[0], ends[1][: height - cut]], axis=0
    )
    return whole, [part[height:] for part in found] + [ends[1][height - cut :]]


def scatter_start(plan, pieces, *earlier):
    ahead, behind = pieces[-1]
    if earlier:
        ahead, behind, *_ = together(ahead, behind, *earlier)
    return send(ahead, plan.to_next), send(behind, plan.to_last)


def scatter_end(plan, pieces, ahead, behind):
    cut = pieces[0].shape[0] // 2
    for hop in range(plan.chips // 2 - 1, 0, -1):
        to_ahead, to_behind = pieces[2 * hop], pieces[2 * hop - 1]
        if ahead.shape[0] == cut:
            ahead = jnp.concatenate([to_ahead[:cut] + ahead, to_ahead[cut:]], axis=0)
            behind = jnp.concatenate([to_behind[:cut], to_behind[cut:] + behind], axis=0)
        else:
            ahead, behind = to_ahead + ahead, to_behind + behind
        ahead, behind = send(ahead, plan.to_next), send(behind, plan.to_last)
    return ahead, behind


def scatter_sum(pieces, ahead, behind):
    return (pieces[0].astype(F32) + ahead.astype(F32) + behind.astype(F32)).astype(BF16)


VMEM = pltpu.VMEM
PARAMS = pltpu.CompilerParams(vmem_limit_bytes=56 * 1024 * 1024)


def shape_of(shape, kind):
    return jax.ShapeDtypeStruct(shape, kind)


def cost(flops, *arrays):
    size = sum(math.prod(array.shape) * array.dtype.itemsize for array in arrays)
    return pl.CostEstimate(flops=int(flops), bytes_accessed=int(size), transcendentals=0)


def in_place(kernel, outs, args, name, flops=0, scratch=()):
    return pl.pallas_call(
        kernel,
        out_shape=outs,
        in_specs=[pl.BlockSpec(memory_space=VMEM)] * len(args),
        out_specs=[pl.BlockSpec(memory_space=VMEM)] * len(outs),
        scratch_shapes=scratch,
        compiler_params=PARAMS,
        cost_estimate=cost(flops, *args, *outs),
        name=name,
    )(*args)


def part_out(last, total, near, away):
    half = near.shape[0]

    @pl.when(last)
    def _():
        near[...] = total[:half, :]
        away[...] = total[half:, :].astype(BF16)


def parts_of(rows, width):
    return [shape_of((rows // 2, width), F32), shape_of((rows // 2, width), BF16)]


def hidden_blocks(weights):
    if weights[0].ndim == 4:
        return weights[0].shape[3] // 2, weights[0].shape[1]
    middle = weights[0].shape[1] // 2
    block = min(512, middle)
    return block, middle // block


def weight_specs(weights, block, each):
    specs = []
    for at, weight in enumerate(weights):
        for side in (0, 1):
            if weight.ndim == 4:
                shape = (weight.shape[0], 1, weight.shape[2], block)
                specs.append(pl.BlockSpec(shape, lambda step, side=side: (0, step, 0, side)))
            else:
                specs.append(
                    pl.BlockSpec(
                        (weight.shape[0], block),
                        lambda step, at=at, side=side: (
                            0,
                            side * each + jnp.clip(step - at * each, 0, each - 1),
                        ),
                    )
                )
    return specs


def flat(ref):
    values = ref[...]
    return values.reshape(-1, values.shape[-1])


def whole_specs(chunks):
    return [pl.BlockSpec(chunk.shape, lambda step: (0, 0)) for chunk in chunks]


def join(first, chunks, joined):
    @pl.when(first)
    def _():
        at = 0
        for chunk in chunks:
            joined[at : at + chunk.shape[0], :] = chunk[...]
            at += chunk.shape[0]


def expand_shrink_kernel(count, each, full, *refs):
    preact, near, away, total = refs[2 * count :]
    step = pl.program_id(0)
    for at in range(count):

        @pl.when(step // each == at)
        def _(at=at):
            values = mm(full[...], flat(refs[2 * at]))
            preact[...] = values
            kept = (values * jax.nn.sigmoid(values)).astype(BF16)
            added = mm_nt(kept, flat(refs[2 * at + 1]))

            @pl.when(step == 0)
            def _():
                total[...] = added

            @pl.when(step > 0)
            def _():
                total[...] += added

    part_out(step == pl.num_programs(0) - 1, total, near, away)


def expand_shrink(full, weights):
    block, each = hidden_blocks(weights)
    rows, width = full.shape
    steps = each * len(weights)
    outs = [shape_of((rows, steps * block), F32)] + parts_of(rows, width)
    part = pl.BlockSpec((rows // 2, width), lambda step: (0, 0))
    return pl.pallas_call(
        partial(expand_shrink_kernel, len(weights), each),
        grid=(steps,),
        out_shape=outs,
        in_specs=[pl.BlockSpec((rows, width), lambda step: (0, 0))] + weight_specs(weights, block, each),
        out_specs=[
            pl.BlockSpec((rows, block), lambda step: (0, step)),
            part,
            part,
        ],
        scratch_shapes=[pltpu.VMEM((rows, width), F32)],
        compiler_params=PARAMS,
        cost_estimate=cost(4 * rows * width * steps * block, full, *weights, *outs),
        name="expand_shrink",
    )(full, *[weight for weight in weights for _ in (0, 1)])


def expand_shrink_back_kernel(count, each, parts, *refs):
    chunks, preact, refs = refs[:parts], refs[parts], refs[parts + 1 :]
    back, kept, near, away, total, incoming = refs[2 * count :]
    step = pl.program_id(0)
    join(step == 0, chunks, incoming)
    for at in range(count):

        @pl.when(step // each == at)
        def _(at=at):
            values = preact[...]
            gate = jax.nn.sigmoid(values)
            kept[...] = (values * gate).astype(BF16)
            grad = mm(incoming[...], flat(refs[2 * at + 1]))
            grad = (grad * gate * (1.0 + values * (1.0 - gate))).astype(BF16)
            back[...] = grad
            added = mm_nt(grad, flat(refs[2 * at]))

            @pl.when(step == 0)
            def _():
                total[...] = added

            @pl.when(step > 0)
            def _():
                total[...] += added

    part_out(step == pl.num_programs(0) - 1, total, near, away)


def expand_shrink_back(incoming, preact, weights):
    block, each = hidden_blocks(weights)
    rows, width = preact.shape[0], incoming[0].shape[1]
    steps = each * len(weights)
    hidden = shape_of((rows, steps * block), BF16)
    outs = [hidden, hidden] + parts_of(rows, width)
    part = pl.BlockSpec((rows // 2, width), lambda step: (0, 0))
    by_step = pl.BlockSpec((rows, block), lambda step: (0, step))
    return pl.pallas_call(
        partial(expand_shrink_back_kernel, len(weights), each, len(incoming)),
        grid=(steps,),
        out_shape=outs,
        in_specs=whole_specs(incoming) + [by_step] + weight_specs(weights, block, each),
        out_specs=[by_step, by_step, part, part],
        scratch_shapes=[pltpu.VMEM((rows, width), F32), pltpu.VMEM((rows, width), BF16)],
        compiler_params=PARAMS,
        cost_estimate=cost(4 * rows * width * steps * block, *incoming, preact, *weights, *outs),
        name="expand_shrink_back",
    )(*incoming, preact, *[weight for weight in weights for _ in (0, 1)])


def pair_grad_kernel(each, cuts, parts, other_parts, *refs):
    chunks, right, refs = refs[:parts], refs[parts], refs[parts + 1 :]
    other_chunks, other_right, refs = refs[:other_parts], refs[other_parts], refs[other_parts + 1 :]
    outs, left = refs[:-1], refs[-1]
    step = pl.program_id(0)
    join(step == 0, chunks, left)
    join(step == each, other_chunks, left)

    def put(values):
        at = 0
        for out, height in zip(outs, cuts):
            out[...] = values[at : at + height].astype(BF16).reshape(out.shape)
            at += height

    @pl.when(step < each)
    def _():
        put(mm_tn(left[...], right[...]))

    @pl.when(step >= each)
    def _():
        put(mm_tn(left[...], other_right[...]))


def pair_grad(left, right, other_left, other_right, cuts, block=512, columns=None, first=0, blocked=None):
    rows, width = right.shape[0], left[0].shape[1]
    columns = columns or right.shape[1]
    other_columns = other_right.shape[1] if columns == right.shape[1] else columns
    block = blocked[3] // 2 if blocked else min(block, columns, other_columns)
    each, other_each = columns // block, other_columns // block
    start = first // block
    if blocked:
        outs = [shape_of(blocked, BF16)]
        shape = (blocked[0], 1, blocked[2], block)
        out_specs = [pl.BlockSpec(shape, lambda step: (0, step % each, 0, step // each))]
    else:
        outs = [shape_of((height, columns + other_columns), BF16) for height in cuts]
        out_specs = [pl.BlockSpec((height, block), lambda step: (0, step)) for height in cuts]
    return pl.pallas_call(
        partial(pair_grad_kernel, each, cuts, len(left), len(other_left)),
        grid=(each + other_each,),
        out_shape=outs,
        in_specs=whole_specs(left)
        + [pl.BlockSpec((rows, block), lambda step: (0, start + jnp.clip(step, 0, each - 1)))]
        + whole_specs(other_left)
        + [
            pl.BlockSpec(
                (rows, block), lambda step: (0, start + jnp.clip(step - each, 0, other_each - 1))
            )
        ],
        out_specs=out_specs,
        scratch_shapes=[pltpu.VMEM((rows, width), BF16)],
        compiler_params=PARAMS,
        cost_estimate=cost(2 * rows * width * (columns + other_columns), *left, right, *other_left, *outs),
        name="pair_grad",
    )(*left, right, *other_left, other_right)


def masked_scores(queries, keyset, marks, mark_row):
    scores = mm_nt(queries, keyset) * HEAD_DIM**-0.5
    return jnp.where(marks == mark_row, scores, MASKED)


def attention_kernel(inner, parts, *refs):
    chunks, refs = refs[:parts], refs[parts:]
    weights, mark_rows, mark_columns, narrow, mixture, log_total, near, away, full = refs
    length = full.shape[0]
    join(True, chunks, full)
    block = min(256, length)
    narrow[...] = mm(full[...], weights[:, : 3 * inner]).astype(BF16)
    for head in range(inner // HEAD_DIM):
        at = head * HEAD_DIM
        for first in range(0, length, block):
            rows = slice(first, first + block)
            scores = masked_scores(
                narrow[rows, at : at + HEAD_DIM],
                narrow[:, inner + at : inner + at + HEAD_DIM],
                mark_columns[rows, :1],
                mark_rows[:1, :],
            )
            row_max = jnp.max(scores, axis=-1, keepdims=True)
            weighted = jnp.exp(scores - row_max)
            sums = jnp.sum(weighted, axis=-1, keepdims=True)
            attended = (weighted / sums).astype(BF16)
            values = narrow[:, 2 * inner + at : 2 * inner + at + HEAD_DIM]
            mixture[rows, at : at + HEAD_DIM] = mm(attended, values).astype(BF16)
            log_total[rows, at : at + HEAD_DIM] = jnp.broadcast_to(
                row_max + jnp.log(sums), (block, HEAD_DIM)
            )
    away[...] = mm_nt(mixture[length // 2 :, :], weights[:, 3 * inner :]).astype(BF16)
    near[...] = mm_nt(mixture[: length // 2, :], weights[:, 3 * inner :])


def attention_step(chunks, weights, marks):
    length, width = marks.shape[0], chunks[0].shape[1]
    inner = weights.shape[1] // 4
    mark_rows = jnp.broadcast_to(marks[None, :], (8, length))
    mark_columns = jnp.broadcast_to(marks[:, None], (length, 128))
    outs = [
        shape_of((length, 3 * inner), BF16),
        shape_of((length, inner), BF16),
        shape_of((length, inner), F32),
    ] + parts_of(length, width)
    flops = 8 * length * width * inner + 4 * length * length * inner
    results = in_place(
        partial(attention_kernel, inner, len(chunks)),
        outs,
        (*chunks, weights, mark_rows, mark_columns),
        "attention",
        flops,
        [pltpu.VMEM((length, width), BF16)],
    )
    return results, (mark_rows, mark_columns)


def attention_back_kernel(inner, parts, *refs):
    chunks, refs = refs[:parts], refs[parts:]
    weights, mark_rows, mark_columns, narrow, log_total, back, near, away = refs[:8]
    grad_mix, keys, values_sum, incoming = refs[8:]
    join(True, chunks, incoming)
    length = incoming.shape[0]
    block = min(256, length)
    grad_mix[...] = mm(incoming[...], weights[:, 3 * inner :]).astype(BF16)
    factor = HEAD_DIM**-0.5
    for head in range(inner // HEAD_DIM):
        at = head * HEAD_DIM
        here = slice(at, at + HEAD_DIM)
        keyset = narrow[:, inner + at : inner + at + HEAD_DIM]
        values = narrow[:, 2 * inner + at : 2 * inner + at + HEAD_DIM]
        for first in range(0, length, block):
            rows = slice(first, first + block)
            queries = narrow[rows, here]
            mixed = grad_mix[rows, here]
            scores = masked_scores(queries, keyset, mark_columns[rows, :1], mark_rows[:1, :])
            attended = jnp.exp(scores - log_total[rows, at : at + 1])
            added = mm_tn(attended.astype(BF16), mixed)
            grad = mm_nt(mixed, values)
            grad = attended * (grad - jnp.sum(grad * attended, axis=-1, keepdims=True))
            grad = grad.astype(BF16)
            back[rows, here] = (mm(grad, keyset) * factor).astype(BF16)
            key_added = mm_tn(grad, queries)
            if first == 0:
                values_sum[...] = added
                keys[...] = key_added
            else:
                values_sum[...] += added
                keys[...] += key_added
        back[:, inner + at : inner + at + HEAD_DIM] = (keys[...] * factor).astype(BF16)
        back[:, 2 * inner + at : 2 * inner + at + HEAD_DIM] = values_sum[...].astype(BF16)
    away[...] = mm_nt(back[length // 2 :, :], weights[:, : 3 * inner]).astype(BF16)
    near[...] = mm_nt(back[: length // 2, :], weights[:, : 3 * inner])


def attention_back_step(chunks, weights, marks, narrow, log_total):
    length, width = narrow.shape[0], chunks[0].shape[1]
    inner = weights.shape[1] // 4
    outs = [shape_of((length, 3 * inner), BF16)] + parts_of(length, width)
    flops = 8 * length * width * inner + 10 * length * length * inner
    return in_place(
        partial(attention_back_kernel, inner, len(chunks)),
        outs,
        (*chunks, weights, *marks, narrow, log_total),
        "attention_back",
        flops,
        [
            pltpu.VMEM((length, inner), BF16),
            pltpu.VMEM((length, HEAD_DIM), F32),
            pltpu.VMEM((length, HEAD_DIM), F32),
            pltpu.VMEM((length, width), BF16),
        ],
    )


def move_blocks(values, order, blocks):
    share = values.shape[1] // blocks
    return [values[:, pl.ds(pl.multiple_of(order[at] * share, share), share)] for at in range(blocks)]


def unit_of(stream):
    centred = stream - jnp.mean(stream, axis=-1, keepdims=True)
    inverse = lax.rsqrt(jnp.mean(centred * centred, axis=-1, keepdims=True) + NORM_EPS)
    return centred * inverse, inverse


def add_norm_kernel(scale, at, blocks, *refs):
    order = refs[0] if blocks else None
    base, own, got, gains, stream, normed = refs[1 if blocks else 0 :][:6]
    values = base[...] + scale * (own[...] + got[...].astype(F32))
    if blocks:
        moved = refs[-1]
        moved[...] = values
        share = moved.shape[1] // blocks
        for to, part in enumerate(move_blocks(moved, order, blocks)):
            stream[:, to * share : (to + 1) * share] = part
        values = stream[...]
    else:
        stream[...] = values
    unit, _ = unit_of(values)
    normed[...] = (unit * gains[at : at + 1, :] + gains[at + 1 : at + 2, :]).astype(BF16)


def add_norm(base, own, got, scale, gains, at, order=None):
    rows, width = base.shape
    blocks = 0 if order is None else order.shape[0]
    if blocks and width // blocks % 128:
        stream = jnp.take(
            (base + scale * (own + got.astype(F32))).reshape(rows, blocks, -1), order, axis=1
        ).reshape(rows, width)
        zero = jnp.zeros_like(stream)
        return add_norm(stream, zero, zero.astype(BF16), 1.0, gains, at)
    args = (base, own, got, gains)
    outs = [shape_of((rows, width), F32), shape_of((rows, width), BF16)]
    return pl.pallas_call(
        partial(add_norm_kernel, scale, at, blocks),
        out_shape=outs,
        in_specs=[pl.BlockSpec(memory_space=pltpu.SMEM)] * (1 if blocks else 0)
        + [pl.BlockSpec(memory_space=VMEM)] * 4,
        out_specs=[pl.BlockSpec(memory_space=VMEM)] * 2,
        scratch_shapes=[pltpu.VMEM((rows, width), F32)] if blocks else [],
        compiler_params=PARAMS,
        cost_estimate=cost(20 * rows * width, *args, *outs),
        name="add_norm",
    )(*((order,) if blocks else ()), *args)


def norm_back_kernel(scale, at, blocks, chained, *refs):
    order = refs[0] if blocks else None
    refs = refs[1 if blocks else 0 :]
    if chained:
        gradient, own, got, stream, gains, summed, sent, rows_out = refs[:8]
        upstream = own[...] + got[...].astype(F32)
    else:
        own, stream, gains, summed, sent, rows_out = refs[:6]
        upstream = own[...].astype(F32)
    unit, inverse = unit_of(stream[...])
    rows_out[0:1, :] = jnp.sum(upstream * unit, axis=0, keepdims=True)
    rows_out[1:2, :] = jnp.sum(upstream, axis=0, keepdims=True)
    rows_out[2:, :] = jnp.zeros((rows_out.shape[0] - 2, rows_out.shape[1]), F32)
    scaled = upstream * gains[at : at + 1, :]
    through = inverse * (
        scaled
        - jnp.mean(scaled, axis=-1, keepdims=True)
        - unit * jnp.mean(scaled * unit, axis=-1, keepdims=True)
    )
    values = gradient[...] + through if chained else through
    if blocks:
        moved = refs[-1]
        moved[...] = values
        share = moved.shape[1] // blocks
        for to, part in enumerate(move_blocks(moved, order, blocks)):
            summed[:, to * share : (to + 1) * share] = part
        values = summed[...]
    else:
        summed[...] = values
    sent[...] = (scale * values).astype(BF16)


def norm_back(gradient, own, got, stream, gains, at, scale, order=None):
    rows, width = stream.shape
    blocks = 0 if order is None else order.shape[0]
    chained = gradient is not None
    late_order = None
    if blocks and width // blocks % 128:
        late_order, blocks = order, 0
    args = ((gradient, own, got) if chained else (own,)) + (stream, gains)
    outs = [shape_of((rows, width), F32), shape_of((rows, width), BF16), shape_of((8, width), F32)]
    results = pl.pallas_call(
        partial(norm_back_kernel, scale, at, blocks, chained),
        out_shape=outs,
        in_specs=[pl.BlockSpec(memory_space=pltpu.SMEM)] * (1 if blocks else 0)
        + [pl.BlockSpec(memory_space=VMEM)] * len(args),
        out_specs=[pl.BlockSpec(memory_space=VMEM)] * 3,
        scratch_shapes=[pltpu.VMEM((rows, width), F32)] if blocks else [],
        compiler_params=PARAMS,
        cost_estimate=cost(30 * rows * width, *args, *outs),
        name="norm_back",
    )(*((order,) if blocks else ()), *args)
    if late_order is not None:
        results = [reorder_blocks(part, late_order) for part in results[:2]] + [results[2]]
    return results


def norm_kernel(at, chunks, *refs):
    gains, normed = refs[chunks:]
    first = 0
    for chunk in refs[:chunks]:
        unit, _ = unit_of(chunk[...].astype(F32))
        rows = slice(first, first + chunk.shape[0])
        normed[rows, :] = (unit * gains[at : at + 1, :] + gains[at + 1 : at + 2, :]).astype(BF16)
        first += chunk.shape[0]


def norm_of(chunks, gains, at):
    rows, width = sum(chunk.shape[0] for chunk in chunks), chunks[0].shape[1]
    return in_place(
        partial(norm_kernel, at, len(chunks)),
        [shape_of((rows, width), BF16)],
        (*chunks, gains),
        "norm",
        10 * rows * width,
    )[0]


def adam_terms(turned, first, second):
    first_new = BETA_ONE * first + (1.0 - BETA_ONE) * turned
    second_new = BETA_TWO * second + (1.0 - BETA_TWO) * turned * turned
    normal_step = (
        first_new
        / (1.0 - BETA_ONE**STEP)
        / (jnp.sqrt(second_new / (1.0 - BETA_TWO**STEP)) + ADAM_EPS)
    )
    return first_new, second_new, normal_step


def adam_weight(step, weight, average, rate):
    weight_new = weight - rate * (step + DECAY * weight)
    return weight_new, EMA_DECAY * average + (1.0 - EMA_DECAY) * weight_new


def adam_kernel(turn, rate, grad, left, right, weight, first, second, average, *rest):
    first_out, second_out, weight_out, average_out = rest[-4:]
    left = left[...].astype(BF16)
    turned = mm(mm_tn(left, grad[0].astype(BF16)).astype(BF16), right[...])
    if turn:
        turned = turned.T
    first_new, second_new, step = adam_terms(turned, first[0], second[0])
    first_out[0] = first_new
    second_out[0] = second_new
    if turn:
        step = step.T
    step = mm(left, mm_nt(step.astype(BF16), right[...]).astype(BF16))
    if turn:
        step = step.T
    weight_out[0], average_out[0] = adam_weight(step, weight[0], average[0], rate)


def rotated_adam(grads, left, right, states, rate, turn, slot=0, partly=()):
    count, share, other = grads.shape
    block = (1, other, share) if turn else (1, share, other)
    whole = lambda at: (0, 0)
    here = lambda at: (at + slot, 0, 0)
    return tuple(
        pl.pallas_call(
            partial(adam_kernel, turn, rate),
            grid=(count,),
            out_shape=[jax.ShapeDtypeStruct(part.shape, F32) for part in states],
            in_specs=[
                pl.BlockSpec((1, share, other), lambda at: (at, 0, 0)),
                pl.BlockSpec(left.shape, whole),
                pl.BlockSpec(right.shape, whole),
            ]
            + [pl.BlockSpec(block, here)] * 4
            + [pl.BlockSpec(memory_space=pl.ANY)] * len(partly),
            out_specs=[pl.BlockSpec(block, here)] * 4,
            input_output_aliases={7 + at: at for at in range(len(partly))},
            compiler_params=pltpu.CompilerParams(vmem_limit_bytes=48 * 1024 * 1024),
            cost_estimate=pl.CostEstimate(
                flops=4 * count * share * other * (share + other),
                bytes_accessed=count * share * other * 36 + other * other * 2,
                transcendentals=count * share * other,
            ),
            name="rotated_adam",
        )(grads, left, right, *states, *partly)
    )


def layer(
    plan,
    frames,
    cotangent,
    segment_ids,
    owners,
    rot_model,
    rot_hidden,
    rot_inner,
    inner_weight,
    inner_first,
    inner_second,
    inner_average,
    expand_weight,
    expand_first,
    expand_second,
    expand_average,
    output_weight,
    output_first,
    output_second,
    output_average,
    shrink_weight,
    shrink_first,
    shrink_second,
    shrink_average,
    small_weight,
    small_first,
    small_second,
    small_average,
):
    n_dp, n_mp, half = plan.n_dp, plan.n_mp, plan.half
    dp, z = lax.axis_index("dp"), lax.axis_index("mp")
    chip, core = dp // 2, dp % 2
    high, z_low = z // half, z % half
    on_zero, on_low = core == 0, high == 0
    frames, cotangent, segment_ids = frames[0], cotangent[0], segment_ids[0]
    chunk, width = frames.shape
    share = width // n_dp
    hidden = expand_weight.shape[2]
    inner = inner_weight.shape[2]
    bits = plan.z_bits()
    near_bits = bits[1:]
    piece_rows = 2 * share
    lanes = hidden
    row_lanes = n_mp * small_weight.shape[1]

    def by_core(mine, other):
        return jnp.where(on_zero, mine, other), jnp.where(on_zero, other, mine)

    def over_cores(keep, give):
        return jnp.concatenate(by_core(keep, send(give, plan.swap_core)), axis=0)

    def back_to_cores(rows):
        keep, give = by_core(rows[:share], rows[share:])
        return by_core(keep, send(give, plan.swap_core))

    def halves(matrix):
        middle = matrix.shape[-1] // 2
        return by_core(matrix[..., :middle], matrix[..., middle:])

    def pack(slot, hold=lambda *values: values):
        entry, exit_ = hold(expand_weight, shrink_weight)
        keep_in, give_in = halves(entry[slot].astype(BF16))
        keep_out, give_out = halves(exit_[slot].astype(BF16).T)
        return over_cores(
            jnp.concatenate([keep_in, keep_out], axis=1), jnp.concatenate([give_in, give_out], axis=1)
        )

    small_rows, small_cut = small_weight.shape
    place = jnp.where(jnp.arange(row_lanes) // small_cut == z, 1.0, 0.0).astype(BF16)
    small_own = jnp.tile(small_weight.astype(BF16), (1, n_mp)) * place
    small_here = small_own
    for step in range(1, n_mp):
        small_here = small_here + send(small_own, plan.swap_z(step))

    early_shard = after(pack(0), small_here)

    def behind(*values):
        held = lax.optimization_barrier(values + (early_shard,))[:-1]
        return held if len(values) > 1 else held[0]

    owners, segment_ids, cotangent = behind(owners, segment_ids, cotangent)
    early_far = early_far_raw = send(early_shard, plan.swap_z(half))
    early_found = gather_hops(plan, early_shard)

    slots = jnp.arange(n_dp, dtype=jnp.int32)

    def inverse_of(order):
        return jnp.sum(jnp.where(order[None, :] == slots[:, None], slots[None, :], 0), axis=1)

    here = jnp.asarray(plan.table, jnp.int32)[chip]
    holds = inverse_of(owners)
    to_here = jnp.sum(jnp.where(here[:, None] == slots[None, :], holds[None, :], 0), axis=1)
    from_here = inverse_of(to_here)
    here_back = inverse_of(here)

    moved = core != high

    def trade_rows(rows):
        return jnp.where(moved, send(rows, plan.swap_rows), rows)

    late_own = pack(1, behind)
    rows = trade_rows(after(reorder_blocks(frames, to_here), early_far))

    def fold_small(values):
        extra = jnp.pad(values[16:], ((0, 16 - (small_rows - 16)), (0, lanes - 2 * values.shape[1])))
        return jnp.concatenate([values[:16], extra], axis=1)

    def unfold_small(values, count):
        return jnp.concatenate([values[:, :count], values[: small_rows - 16, count : 2 * count]], axis=0)

    early_ends = gather_end(plan, early_found, early_far)
    small_here = jnp.concatenate(by_core(small_here, send(small_here, plan.swap_core)), axis=1)
    early_far = jnp.concatenate([early_far, fold_small(small_here)], axis=0)
    far_found = gather_hops(plan, early_far)
    far_ends = gather_end(plan, far_found, rows)
    early_near, _ = gathered(early_found, early_ends)
    early_far, small_parts = gathered(far_found, far_ends, piece_rows)
    early = [early_near, early_far]

    entry, exit_ = behind(inner_weight, output_weight)
    mine = jnp.concatenate(
        [entry[at].astype(BF16) for at in range(3)] + [exit_[0].astype(BF16).T], axis=1
    )
    other = send(after(mine, far_found[-1]), plan.swap_z(half))
    low, up = jnp.where(on_low, mine, other), jnp.where(on_low, other, mine)
    attend_shard = over_cores(*by_core(low, up))

    z_steps = plan.z_order(bits)

    def side_by_side(pieces, count):
        columns = pieces[0].shape[1] // count
        return jnp.concatenate(
            [piece[:, at * columns : (at + 1) * columns] for at in range(count) for piece in pieces],
            axis=1,
        )

    same_core = [[2 * at + core_at for at in range(plan.chips)] for core_at in (0, 1)]
    late_own = after(late_own, early_far_raw)
    late_beside = lax.all_gather(late_own, "mp", axis=0, tiled=False)
    late = lax.all_gather(late_beside, "dp", axis=0, tiled=False, axis_index_groups=same_core)

    pairs = [halves(entry[at].astype(BF16)) for at in (3, 4)]
    pairs.append(halves(exit_[1].astype(BF16).T))
    conv_shard = over_cores(
        jnp.concatenate([keep for keep, _ in pairs], axis=1),
        jnp.concatenate([give for _, give in pairs], axis=1),
    )

    other_segments = send(segment_ids, plan.swap_core)
    segments = jnp.where(moved, other_segments, segment_ids)

    count = 2 * row_lanes
    small = jnp.concatenate([unfold_small(part, count) for part in small_parts], axis=1).astype(F32)
    gain_order = jnp.sum(jnp.where(here[None, :] == to_here[:, None], slots[None, :], 0), axis=1)
    small = jnp.pad(small, ((0, 24 - small_rows), (0, 0)))
    gains = reorder_blocks(small, gain_order)
    depth_small = reorder_blocks(small, here_back)
    z_order = jnp.asarray(plan.z_order(bits), jnp.int32)
    place_z = [0] * n_mp
    for at, value in enumerate(plan.z_order(bits)):
        place_z[value] = at
    z_blocks = jnp.bitwise_xor(z, z_order)
    z_places = jnp.asarray(place_z, jnp.int32)[jnp.bitwise_xor(z, jnp.arange(n_mp, dtype=jnp.int32))]
    by_block = depth_small[10:small_rows].reshape(KERNEL + 2, n_mp, 2, inner // 2)
    depthwise = jnp.take(jnp.where(on_zero, by_block[:, :, 0], by_block[:, :, 1]), z_blocks, axis=1)
    depthwise = depthwise.reshape(KERNEL + 2, -1)

    def both_cores(own):
        return [own, send(own, plan.swap_core)]

    def row_gather(own, work=lambda: []):
        beside = send(own, plan.swap_core)
        far, done = [own], []
        for bit in near_bits:
            got = [send(part, plan.swap_z(bit)) for part in far]
            if not done:
                done = work()
                got[0], *done = together(got[0], *done)
            far = far + got
        far_beside = [send(part, plan.swap_core) for part in far[1:]]
        return far + [beside] + far_beside, done

    def row_scatter(near, away, work=lambda hold: []):
        total = near + send(away, plan.swap_core).astype(F32)
        done = work(lambda value: after(value, total))
        for at, bit in enumerate(near_bits[::-1]):
            cut = total.shape[0] // 2
            got = send(total[cut:].astype(BF16), plan.swap_z(bit))
            if at == 0:
                got, *done = together(got, *done)
            own = total[:cut]
            total = own + got.astype(F32)
        return own, got, done

    near_z = jnp.bitwise_xor(z_low, jnp.asarray(plan.z_order(near_bits), jnp.int32))
    chunk_of = jnp.concatenate([core * half + near_z, (1 - core) * half + near_z])
    length = segments.shape[0]
    mixed_segments = jnp.take(segments.reshape(n_mp, chunk), chunk_of, axis=0).reshape(-1)

    radius = KERNEL // 2
    reach = 2 * radius
    padded_ids = jnp.pad(segments, (reach, reach), constant_values=-1)
    ids = jnp.stack(
        [
            lax.dynamic_slice_in_dim(padded_ids, (at * half + z_low) * chunk, chunk + 2 * reach)
            for at in (0, 1)
        ]
    )

    def same(first, second, count):
        return (ids[:, first : first + count] == ids[:, second : second + count])[:, :, None].astype(F32)

    def with_halo(own, count, work=lambda: []):
        low, up = by_core(own, send(own, plan.swap_core))
        above = send(own[-count:], plan.to_chunk_above)
        below = send(own[:count], plan.to_chunk_below)
        above, *done = together(above, *work())
        around = jnp.concatenate([above, below], axis=0)
        low_around, up_around = by_core(around, send(around, plan.swap_core))
        return (
            jnp.concatenate([low, up], axis=0),
            jnp.concatenate([low_around, up_around], axis=0),
            done,
        )

    def extend(main, around, count):
        main = main.reshape(2, chunk, main.shape[1])
        around = around.reshape(2, 2 * count, around.shape[1])
        return jnp.concatenate([around[:, :count], main, around[:, count:]], axis=1)

    channels = n_mp * inner // 2

    def convolve(full, around):
        content, opening = mm(full, conv[:, :channels]), mm(full, conv[:, channels : 2 * channels])
        beside = mm(around, conv[:, : 2 * channels])
        gated = extend(
            content * jax.nn.sigmoid(opening),
            beside[:, :channels] * jax.nn.sigmoid(beside[:, channels:]),
            reach,
        )
        count = chunk + 2 * radius
        summed = sum(
            gated[:, tap : tap + count] * same(tap, radius, count) * depthwise[tap]
            for tap in range(KERNEL)
        )
        normal_conv = summed * depthwise[KERNEL] + depthwise[KERNEL + 1]
        activated = jax.nn.silu(normal_conv[:, radius : radius + chunk]).astype(BF16)
        total = mm_nt(activated.reshape(2 * chunk, -1), conv[:, 2 * channels :])
        return fold_chunks(total), (content, opening, gated, summed)

    def fold_chunks(total):
        keep, give = by_core(total[:chunk], total[chunk:])
        return keep, send(give.astype(BF16), plan.swap_core)

    def convolve_back(incoming, around, state):
        content, opening, gated, summed = state
        normal_conv = summed * depthwise[KERNEL] + depthwise[KERNEL + 1]
        gate_conv = jax.nn.sigmoid(normal_conv)
        activated = (normal_conv * gate_conv)[:, radius : radius + chunk].astype(BF16)
        activated = activated.reshape(2 * chunk, -1)
        grad_active = extend(
            mm(incoming, conv[:, 2 * channels :]), mm(around, conv[:, 2 * channels :]), radius
        )
        grad_normal = grad_active * gate_conv * (1.0 + normal_conv * (1.0 - gate_conv))
        grad_summed = grad_normal * depthwise[KERNEL]
        own = slice(radius, radius + chunk)
        depth_rows, grad_gated = [], 0.0
        for tap in range(KERNEL):
            masked = grad_summed[:, own] * same(reach, radius + tap, chunk)
            source = gated[:, radius + tap : radius + tap + chunk]
            depth_rows.append(jnp.sum(masked * source, axis=(0, 1)))
            back = reach - tap
            grad_gated = grad_gated + (
                grad_summed[:, back : back + chunk] * same(reach, radius + back, chunk) * depthwise[tap]
            )
        depth_rows.append(jnp.sum(grad_normal[:, own] * summed[:, own], axis=(0, 1)))
        depth_rows.append(jnp.sum(grad_normal[:, own], axis=(0, 1)))
        grad_gated = grad_gated.reshape(2 * chunk, -1)
        gate_open = jax.nn.sigmoid(opening)
        grad_content = (grad_gated * gate_open).astype(BF16)
        grad_opening = (grad_gated * content * gate_open * (1.0 - gate_open)).astype(BF16)
        total = mm_nt(grad_content, conv[:, :channels]) + mm_nt(
            grad_opening, conv[:, channels : 2 * channels]
        )
        return total, grad_content, grad_opening, activated, depth_rows

    def undouble(total, count):
        columns = total.shape[1] // count // n_mp
        pieces = [
            jnp.concatenate(
                [
                    total[:, (group * n_mp + at) * columns : (group * n_mp + at + 1) * columns]
                    for group in range(count)
                ],
                axis=1,
            )
            for at in range(n_mp)
        ]
        return [pieces[0]] + [
            send(piece, plan.swap_z(step)) for piece, step in zip(pieces[1:], z_steps[1:])
        ]

    def sum_of(pieces):
        return sum(piece.astype(F32) for piece in pieces).astype(BF16)

    def unpack(total, count):
        low, up = back_to_cores(total)
        columns = total.shape[1] // count
        return jnp.stack(
            [
                jnp.concatenate(
                    [part[:, at * columns : (at + 1) * columns] for part in (low, up)], axis=1
                )
                for at in range(count)
            ]
        )

    ring_cuts = [piece_rows] * (plan.chips - 1)
    half_cuts = ring_cuts + [share, share]

    def ring_pieces(parts):
        return list(parts[:-2]) + [(parts[-2], parts[-1])]

    early_full = norm_of(row_gather(rows)[0], gains, 0)
    attend_found = gather_hops(plan, after(attend_shard, early_full))
    early_preact, near, away = expand_shrink(early_full, early)
    own, got, _ = row_scatter(near, away)
    early_stream = rows.astype(F32)
    attend_stream, normed = add_norm(early_stream, own, got, 0.5, gains, 2)
    normed, *attend_found = together(normed, *attend_found)
    attend_ends = gather_end(plan, attend_found)
    attend_full, _ = row_gather(normed)
    narrow, _ = gathered(attend_found, attend_ends)
    conv_shard = after(conv_shard, attend_full[1])
    conv_shard = side_by_side(
        [conv_shard] + [send(conv_shard, plan.swap_z(step)) for step in z_steps[1:]], 3
    )
    upstream = trade_rows(after(reorder_blocks(cotangent, holds), attend_full[1]))
    (attend_narrow, mixture, log_total, near, away), marks = attention_step(
        attend_full, narrow, mixed_segments
    )
    near, away, conv_shard = together(near, away, conv_shard)
    conv_found = gather_hops(plan, conv_shard)
    own, got, _ = row_scatter(near, away)
    got, upstream, *conv_found = together(got, upstream, *conv_found)
    conv_ends = gather_end(plan, conv_found)
    conv_stream, normed = add_norm(attend_stream, own, got, 1.0, gains, 4)
    conv_full, around, _ = with_halo(normed, reach)
    conv, _ = gathered(conv_found, conv_ends)
    (own, got), conv_state = convolve(conv_full, around)
    late_gains = reorder_blocks(gains, here_back)
    late_stream, normed = add_norm(conv_stream, own, got, 1.0, late_gains, 6, here_back)
    late_full = jnp.concatenate(both_cores(normed), axis=0)
    late_preact, near, away = expand_shrink(late_full, [late])
    final_stream, result = add_norm(
        late_stream, near, send(away, plan.swap_core), 0.5, late_gains, 8
    )

    gradient, sent, final_rows = norm_back(None, upstream, None, final_stream, late_gains, 8, 0.5)
    incoming_late = both_cores(sent)
    back_late, kept_late, near, away = expand_shrink_back(incoming_late, late_preact, [late])
    gradient, sent, late_rows = norm_back(
        gradient, near, send(away, plan.swap_core), late_stream, late_gains, 6, 1.0, here
    )

    def late_work():
        return pair_grad(
            [late_full], back_late, incoming_late, kept_late, [width], blocked=late.shape
        )

    incoming_conv, around, (late_grads,) = with_halo(sent, radius, late_work)
    late_sum = lax.psum_scatter(
        late_grads, "dp", scatter_dimension=0, tiled=False, axis_index_groups=same_core
    )
    total, grad_content, grad_opening, activated, depth_rows = convolve_back(
        incoming_conv, around, conv_state
    )
    gradient, sent, conv_rows = norm_back(
        gradient, *fold_chunks(total), conv_stream, gains, 4, 1.0
    )

    def conv_work():
        columns = jnp.concatenate([grad_content, grad_opening], axis=1)
        return pair_grad([conv_full], columns, [incoming_conv], activated, half_cuts)

    incoming_attend, conv_pieces = row_gather(sent, conv_work)
    conv_pieces = ring_pieces(conv_pieces)
    conv_moving = scatter_start(plan, conv_pieces, incoming_attend[1])
    block_output = trade_rows(after(reorder_blocks(result, owners), incoming_attend[1]))
    back_attend, near, away = attention_back_step(
        incoming_attend, narrow, marks, attend_narrow, log_total
    )
    away, *conv_moving = together(away, *conv_moving)
    conv_moving = scatter_end(plan, conv_pieces, *conv_moving)

    def attend_work(hold):
        return pair_grad(attend_full, hold(back_attend), incoming_attend, mixture, half_cuts)

    own, got, attend_pieces = row_scatter(near, away, attend_work)
    gradient, sent, attend_rows = norm_back(gradient, own, got, attend_stream, gains, 2, 0.5)
    attend_pieces = ring_pieces(attend_pieces)
    sent, *conv_moving = together(sent, *conv_moving)
    attend_moving = scatter_start(plan, attend_pieces)
    conv_sum = scatter_sum(conv_pieces, *conv_moving)
    incoming_early, _ = row_gather(sent)
    incoming_early[1], late_sum, conv_sum, *attend_moving = together(
        incoming_early[1], late_sum, conv_sum, *attend_moving
    )
    attend_moving = scatter_end(plan, attend_pieces, *attend_moving)
    late_sum = lax.psum_scatter(late_sum, "mp", scatter_dimension=0, tiled=False)
    conv_sum = undouble(conv_sum, 3)
    back_early, kept_early, near, away = expand_shrink_back(incoming_early, early_preact, early)

    def early_grad(left, right, cuts, first):
        return pair_grad(
            [early_full], left, incoming_early, right, cuts, columns=hidden // 2, first=first * hidden // 2
        )

    far_pieces = ring_pieces(early_grad(back_early, kept_early, half_cuts, 1))
    far_moving = scatter_start(plan, far_pieces)

    def early_work(hold):
        grads = early_grad(hold(back_early), kept_early, half_cuts, 0)
        return [*grads, *attend_moving]

    own, got, done = row_scatter(near, away, early_work)
    near_pieces, attend_moving = ring_pieces(done[:-2]), done[-2:]
    far_moving = scatter_end(plan, far_pieces, *far_moving)
    near_moving = list(scatter_start(plan, near_pieces))
    attend_sum = scatter_sum(attend_pieces, *attend_moving)
    _, sent, early_rows = norm_back(gradient, own, got, early_stream, gains, 0, 1.0)

    hidden_turn, inner_turn = rot_hidden.astype(BF16), rot_inner.astype(BF16)
    expand_states = (expand_weight, expand_first, expand_second, expand_average)
    shrink_states = (shrink_weight, shrink_first, shrink_second, shrink_average)
    inner_states = (inner_weight, inner_first, inner_second, inner_average)
    output_states = (output_weight, output_first, output_second, output_average)

    def wide(total, slot, states, rate, turn, partly=()):
        return rotated_adam(total[None], rot_model, hidden_turn, states, rate, turn, slot, partly)

    def narrow_step(totals, slot, states, rate, turn, partly=()):
        return rotated_adam(totals, rot_model, inner_turn, states, rate, turn, slot, partly)

    far_sum = send(scatter_sum(far_pieces, *far_moving), plan.swap_z(half))
    near_moving[0], attend_sum, late_sum, *conv_sum = together(
        near_moving[0], attend_sum, late_sum, *conv_sum
    )
    late_sum, conv_sum = unpack(late_sum, 2), unpack(sum_of(conv_sum), 3)
    low, up = back_to_cores(attend_sum)
    own, away = jnp.where(on_low, low, up), jnp.where(on_low, up, low)
    attend_sum = own.astype(F32) + send(away, plan.swap_z(half)).astype(F32)
    attend_sum = jnp.stack([attend_sum[:, at * inner : (at + 1) * inner] for at in range(4)])

    def late_adam():
        new_expand = wide(late_sum[0], 1, expand_states, RATE_EXPAND, False)
        new_shrink = wide(late_sum[1], 1, shrink_states, RATE_SHRINK, True)
        new_inner = narrow_step(conv_sum[:2], 3, inner_states, RATE_INNER, False)
        new_output = narrow_step(conv_sum[2:], 1, output_states, RATE_OUTPUT, True)
        new_inner = narrow_step(attend_sum[:3], 0, inner_states, RATE_INNER, False, new_inner)
        new_output = narrow_step(attend_sum[3:], 0, output_states, RATE_OUTPUT, True, new_output)
        return new_expand, new_shrink, new_inner, new_output

    home = jnp.sum(jnp.where(here[:, None] == slots[None, :], from_here[None, :], 0), axis=1)
    late_norms = reorder_blocks(jnp.concatenate([late_rows[:2], final_rows[:6]], axis=0), here)[:4]
    norm_rows = jnp.concatenate([attend_rows[:2], conv_rows[:2], late_norms], axis=0)
    norm_rows = reorder_blocks(norm_rows, home)
    depth_rows = jnp.stack(depth_rows).reshape(KERNEL + 2, n_mp, 1, inner // 2)
    depth_rows = jnp.take(depth_rows, z_places, axis=1)
    empty = jnp.zeros_like(depth_rows)
    depth_rows = jnp.concatenate(
        [jnp.where(on_zero, depth_rows, empty), jnp.where(on_zero, empty, depth_rows)], axis=2
    )
    depth_rows = jnp.pad(depth_rows.reshape(KERNEL + 2, width), ((0, 1), (0, 0)))
    depth_rows = reorder_blocks(depth_rows, here)[: KERNEL + 2]
    early_rows = reorder_blocks(early_rows, home)[:2]
    small_grad = jnp.concatenate([early_rows, norm_rows, depth_rows], axis=0)
    small_pieces = [small_grad[:, at * count : (at + 1) * count] for at in range(plan.chips)]
    small_moving = [send(small_pieces[-1], plan.to_next), jnp.zeros_like(small_pieces[-1])]
    for hop in range(plan.chips // 2 - 1, 0, -1):
        small_moving = [
            send(small_pieces[2 * hop] + small_moving[0], plan.to_next),
            send(small_pieces[2 * hop - 1] + small_moving[1], plan.to_last),
        ]

    ahead, behind_, *small_moving = together(*near_moving, *small_moving)
    near_moving = scatter_end(plan, near_pieces, ahead, behind_)
    new_expand, new_shrink, new_inner, new_output = late_adam()
    small_grad = small_pieces[0] + small_moving[0] + small_moving[1]
    keep, give = by_core(small_grad[:, :row_lanes], small_grad[:, row_lanes:])
    small_grad = keep + send(give, plan.swap_core)
    small_grad = small_grad + sum(send(small_grad, plan.swap_z(step)) for step in range(1, n_mp))
    small_grad = lax.dynamic_slice_in_dim(small_grad, z * small_cut, small_cut, axis=1)
    first_new, second_new, step = adam_terms(small_grad, small_first, small_second)
    weight_new, average_new = adam_weight(step, small_weight, small_average, RATE_SMALL)
    new_small = (first_new, second_new, weight_new, average_new)
    input_grad = trade_rows(reorder_blocks(sent, from_here))[None]

    far_sum, *_ = together(
        far_sum, new_expand[0], new_shrink[0], new_inner[0], new_output[0], weight_new, input_grad
    )
    near_sum = scatter_sum(near_pieces, *near_moving)
    early_sum = unpack(near_sum + far_sum, 2)
    new_expand = wide(early_sum[0], 0, expand_states, RATE_EXPAND, False, new_expand)
    new_shrink = wide(early_sum[1], 0, shrink_states, RATE_SHRINK, True, new_shrink)
    return (block_output[None], input_grad) + new_inner + new_expand + new_output + new_shrink + new_small


def solution(mesh):
    plan = Plan(mesh.shape["dp"], mesh.shape["mp"])
    row = P("dp", "mp", None)
    entry = (P(None, "dp", "mp"),) * 4
    exit_ = (P(None, "mp", "dp"),) * 4
    small = (P(None, ("dp", "mp")),) * 4
    states = entry + entry + exit_ + exit_ + small
    return jax.shard_map(
        partial(layer, plan),
        mesh=mesh,
        in_specs=(row, row, P("dp", None), P(), P("dp", None), P("mp", None), P("mp", None)) + states,
        out_specs=(row, row) + states,
        check_vma=False,
    )
```

time: 849 us -> 681 us (0.80)
  waiting for transfers between devices: 445 us -> 190 us
  Pallas kernels: 0 us -> 189 us
  matrix products: 117 us -> 9.6 us
  other arithmetic: 101 us -> 73.8 us
  starting transfers between devices: 86.5 us -> 111 us
  between operations: 4.04 us -> 16.6 us
    ppermute x79 -> x100, waiting for transfers between devices: 445 us -> 190 us  [send(): return lax.ppermute(value, AXES, pairs)]
    pallas_call x0 -> x40, Pallas kernels: none -> 189 us  [the longest x5 37.9 us: pair_grad(): pl.pallas_call(partial(pair_grad_kernel, each, cuts, len(left), len(other...]
    dot_general x69 -> x8, matrix products: 76 us -> 9.6 us  [dot(): lax.dot_general(left, right, (contract, ((), ())), preferred_element_type...]
    dot_general x14 -> x0, matrix products: 41.1 us -> none  [the longest x2 9.82 us: restore_entry(): return jnp.einsum('sry,cy->src', turned, right)]
    ppermute x79 -> x100, starting transfers between devices: 86.5 us -> 111 us  [send(): return lax.ppermute(value, AXES, pairs)]
    gather x14 -> x4, local copies, waits for them, and re-layouts: 24.4 us -> 2.42 us  [the longest x1 0.68 us: layer(): jnp.take(segments.reshape(n_mp, chunk), chunk_of, axis=0).reshape(-1)]
    concatenate x29 -> x36, other arithmetic: 28.3 us -> 13.8 us  [the longest x4 2.14 us: undouble(): jnp.concatenate([total[:, (group * n_mp + at) * columns:(group * n_mp + a...]
    slice x41 -> x44, local copies, waits for them, and re-layouts: 18.5 us -> 26.3 us  [the longest x4 5.44 us: row_scatter(): own = total[:cut]]
  transfers between devices with their start and end apart: 79 -> 104, of which waited for: 41 -> 34; matrix products, arithmetic and copies ran while one was open for 28% -> 22% of each run, Pallas kernels for 0% -> 20%
where the time goes in v2:
time: 681 us; the launch traced here: 669 us
  waiting for transfers between devices  190 us (28%)
  Pallas kernels  189 us (28%)
  starting transfers between devices  111 us (16%)
  local copies, waits for them, and re-layouts  79 us (12%)
  other arithmetic  73.8 us (11%)
  between operations  16.6 us (2%)
  matrix products  9.6 us (1%)
    ppermute x100, waiting for transfers between devices, send(): return lax.ppermute(value, AXES, pairs)  190 us
    ppermute x100, starting transfers between devices, send(): return lax.ppermute(value, AXES, pairs)  111 us
    pallas_call x5, Pallas kernels, pair_grad(): pl.pallas_call(partial(pair_grad_kernel, each, cuts, len(left), len(other...  37.9 us
    unnamed x298, local copies, waits for them, and re-layouts  34.6 us
    pallas_call x3, Pallas kernels, in_place(): pl.pallas_call(kernel, out_shape=outs, in_specs=[pl.BlockSpec(memory_spac...  31.8 us
    pallas_call x8, Pallas kernels, rotated_adam(): pl.pallas_call(partial(adam_kernel, turn, rate), grid=(count,), out_shape...  25.7 us
    pallas_call x2, Pallas kernels, expand_shrink_back(): pl.pallas_call(partial(expand_shrink_back_kernel, len(weights), each, len...  23 us
    pallas_call x2, Pallas kernels, expand_shrink(): pl.pallas_call(partial(expand_shrink_kernel, len(weights), each), grid=(s...  20.6 us
  transfers between devices with their start and end apart: 104, of which 34 were waited for; matrix products, arithmetic and copies ran while one was open for 22% of the time, Pallas kernels for 20%

profile of v2, /device:TPU:0, one launch (start us, length us, event | category | flops | bytes accessed | tf_op | source)
XLA Modules:
  0.0 669.0 jit_solution(9220996543767061198)
XLA Ops:
  8.1 5.1 collective-permute-start.3
  22.6 2.3 collective-permute-start.4
  43.4 5.7 collective-permute-done.4
  63.5 7.2 %collective-permute-done.15 = bf16[128,1024]{1,0:T(8,128)(2,1)} collective-permute-done((bf16[128,1024]{1,0:T(8,128)(2,1)}, bf16[128,1024]{1,0:T(8,128)(2,1)}, u32[]{:S(2)}, u32[]{:S(2)}) %collective-permute-start.15) | collective-permute-done | bytes 262176 | tf_op jit(solution)/shard_map/ppermute | solution.py:145
  87.1 3.4 collective-permute-start.20
  90.5 30.0 %collective-permute-done.6.refs_1_ = bf16[256,1024]{1,0:T(8,128)(2,1)} collective-permute-done((bf16[256,1024]{1,0:T(8,128)(2,1)S(1)}, bf16[256,1024]{1,0:T(8,128)(2,1)}, u32[]{:S(2)}, u32[]{:S(2)}) %collective-permute-start.6) | collective-permute-done | bytes 524320 | tf_op jit(solution)/shard_map/ppermute | solution.py:145
  126.4 4.4 norm.1.full.refs_0_
  130.9 10.7 %expand_shrink.2 = (f32[1024,1024]{1,0:T(8,128)}, f32[512,1024]{1,0:T(8,128)}, bf16[512,1024]{1,0:T(8,128)(2,1)}) custom-call(bf16[1024,1024]{1,0:T(8,128)(2,1)} %norm.1.full.refs_0_, bf16[1024,1024]{1,0:T(8,128)(2,1)} %constant_dynamic-update-slice_fusion.5.refs_0_.refs_1_.refs_5_.refs_6_, ...), custom_call_target="tpu_custom_call" | custom-call | flops 4294967296 | bytes 13631488 | tf_op jit(solution)/shard_map/expand_shrink/pallas_call | solution.py:320
  155.5 2.3 slice.845.refs_1_
  157.8 9.8 %collective-permute-done.19.refs_2_ = bf16[256,1024]{1,0:T(8,128)(2,1)} collective-permute-done((bf16[256,1024]{1,0:T(8,128)(2,1)}, bf16[256,1024]{1,0:T(8,128)(2,1)}, u32[]{:S(2)}, u32[]{:S(2)}) %collective-permute-start.19) | collective-permute-done | bytes 524320 | tf_op jit(solution)/shard_map/ppermute | solution.py:145
  167.6 3.0 add_norm.4
  177.3 9.4 %collective-permute-done.27 = bf16[128,1024]{1,0:T(8,128)(2,1)S(1)} collective-permute-done((bf16[128,1024]{1,0:T(8,128)(2,1)S(1)}, bf16[128,1024]{1,0:T(8,128)(2,1)S(1)}, u32[]{:S(2)}, u32[]{:S(2)}) %collective-permute-start.27) | collective-permute-done | bytes 262176 | tf_op jit(solution)/shard_map/ppermute | solution.py:145
  186.7 2.5 collective-permute-done.28
  189.3 2.7 collective-permute-start.31
  194.4 7.8 %collective-permute-done.31 = bf16[256,384]{1,0:T(8,128)(2,1)S(1)} collective-permute-done((bf16[256,384]{1,0:T(8,128)(2,1)S(1)}, bf16[256,384]{1,0:T(8,128)(2,1)S(1)}, u32[]{:S(2)}, u32[]{:S(2)}) %collective-permute-start.31) | collective-permute-done | bytes 196640 | tf_op jit(solution)/shard_map/ppermute | solution.py:145
  203.5 3.7 collective-permute-done.33
  214.6 12.4 %attention.1 = (bf16[1024,768]{1,0:T(8,128)(2,1)}, bf16[1024,256]{1,0:T(8,128)(2,1)}, f32[1024,256]{1,0:T(8,128)}, f32[512,1024]{1,0:T(8,128)}, bf16[512,1024]{1,0:T(8,128)(2,1)}) custom-call(bf16[256,1024]{1,0:T(8,128)(2,1)} %get-tuple-element.213.refs_0_, bf16[256,1024]{1,0:T(8,128)(2,1)} %copy-done.130, bf16[256,1024]{1,0:T(8,128)(2,1)} %copy-done.131, ...), custom_call_target="tpu_custom_call" | custom-call | flops 3221225472 | bytes 11042816 | tf_op jit(solution)/shard_map/attention/pallas_call | solution.py:220
  238.7 3.6 collective-permute-start.35
  244.4 12.5 %collective-permute-done.35.refs_2_ = bf16[256,1024]{1,0:T(8,128)(2,1)S(1)} collective-permute-done((bf16[256,1024]{1,0:T(8,128)(2,1)S(1)}, bf16[256,1024]{1,0:T(8,128)(2,1)S(1)}, u32[]{:S(2)}, u32[]{:S(2)}) %collective-permute-start.35) | collective-permute-done | bytes 524320 | tf_op jit(solution)/shard_map/ppermute | solution.py:145
  256.9 6.1 collective-permute-done.37
  263.1 3.0 add_norm.5
  269.4 4.5 collective-permute-start.39
  278.6 7.5 %collective-permute-done.42 = bf16[128,1536]{1,0:T(8,128)(2,1)S(1)} collective-permute-done((bf16[128,1536]{1,0:T(8,128)(2,1)S(1)}, bf16[128,1536]{1,0:T(8,128)(2,1)S(1)}, u32[]{:S(2)}, u32[]{:S(2)}) %collective-permute-start.42) | collective-permute-done | bytes 393248 | tf_op jit(solution)/shard_map/ppermute | solution.py:145
  286.1 2.6 collective-permute-done.43
  300.8 2.7 slice_select_fusion.1.refs_2_
  303.5 3.2 add_norm.6
  309.9 9.9 %expand_shrink.3 = (f32[512,2048]{1,0:T(8,128)}, f32[256,1024]{1,0:T(8,128)}, bf16[256,1024]{1,0:T(8,128)(2,1)}) custom-call(bf16[512,1024]{1,0:T(8,128)(2,1)} %constant_dynamic-update-slice_fusion.34.full.refs_0_, bf16[4,4,256,1024]{3,2,1,0:T(8,128)(2,1)} %bitcast.132, bf16[4,4,256,1024]{3,2,1,0:T(8,128)(2,1)} %bitcast.133), custom_call_target="tpu_custom_call" | custom-call | flops 4294967296 | bytes 15204352 | tf_op jit(solution)/shard_map/expand_shrink/pallas_call | solution.py:320
  322.8 3.0 add_norm.7
  325.8 3.3 norm_back.5
  332.0 11.2 %expand_shrink_back.2 = (bf16[512,2048]{1,0:T(8,128)(2,1)}, bf16[512,2048]{1,0:T(8,128)(2,1)}, f32[256,1024]{1,0:T(8,128)}, bf16[256,1024]{1,0:T(8,128)(2,1)}) custom-call(bf16[256,1024]{1,0:T(8,128)(2,1)} %get-tuple-element.243.refs_0_.refs_2_, bf16[256,1024]{1,0:T(8,128)(2,1)} %copy-done.64, f32[512,2048]{1,0:T(8,128)} %get-tuple-element.244.refs_2_, ...), custom_call_target="tpu_custom_call" | custom-call | flops 4294967296 | bytes 19398656 | tf_op jit(solution)/shard_map/expand_shrink_back/pallas_call | solution.py:373
  346.2 4.2 norm_back.6
  351.7 3.8 collective-permute-start.51
  355.5 11.2 %pair_grad.5 = bf16[4,4,256,1024]{3,2,1,0:T(8,128)(2,1)} custom-call(bf16[512,1024]{1,0:T(8,128)(2,1)} %constant_dynamic-update-slice_fusion.34.full.refs_0_, bf16[512,2048]{1,0:T(8,128)(2,1)} %get-tuple-element.249.refs_1_, bf16[256,1024]{1,0:T(8,128)(2,1)} %get-tuple-element.243.refs_0_.refs_2_, bf16[256,1024]{1,0:T(8,128)(2,1)} %copy-done.64, ...), custom_call_target="tpu_custom_call" | custom-call | flops 4294967296 | bytes 12582912 | tf_op jit(solution)/shard_map/pair_grad/pallas_call | solution.py:423
  369.8 2.8 collective-permute-done.52
  381.5 2.4 fusion.48
  393.7 4.0 norm_back.7
  401.3 5.6 pair_grad.6
  407.0 5.1 collective-permute-done.56.refs_1_.refs_6_
  421.1 15.0 %attention_back.1 = (bf16[1024,768]{1,0:T(8,128)(2,1)}, f32[512,1024]{1,0:T(8,128)}, bf16[512,1024]{1,0:T(8,128)(2,1)}) custom-call(bf16[256,1024]{1,0:T(8,128)(2,1)} %get-tuple-element.252.refs_0_.refs_5_, bf16[256,1024]{1,0:T(8,128)(2,1)} %collective-permute-done.56.refs_1_.refs_6_, bf16[256,1024]{1,0:T(8,128)(2,1)} %collective-permute-done.58.refs_2_.refs_7_, ...), custom_call_target="tpu_custom_call" | custom-call | flops 4831838208 | bytes 12091392 | tf_op jit(solution)/shard_map/attention_back/pallas_call | solution.py:220
  442.8 7.2 %pair_grad.7 = (bf16[256,1024]{1,0:T(8,128)(2,1)}, bf16[256,1024]{1,0:T(8,128)(2,1)}, bf16[256,1024]{1,0:T(8,128)(2,1)}, bf16[128,1024]{1,0:T(8,128)(2,1)}, bf16[128,1024]{1,0:T(8,128)(2,1)}) custom-call(bf16[256,1024]{1,0:T(8,128)(2,1)} %get-tuple-element.213.refs_0_, bf16[256,1024]{1,0:T(8,128)(2,1)} %copy-done.130, bf16[256,1024]{1,0:T(8,128)(2,1)} %copy-done.131, ...), custom_call_target="tpu_custom_call" | custom-call | flops 2147483648 | bytes 7864320 | tf_op jit(solution)/shard_map/pair_grad/pallas_call | solution.py:423
  450.1 4.5 collective-permute-done.63.refs_2_
  454.6 4.0 norm_back.8
  458.6 11.1 %collective-permute-done.64 = bf16[256,1536]{1,0:T(8,128)(2,1)S(1)} collective-permute-done((bf16[256,1536]{1,0:T(8,128)(2,1)S(1)}, bf16[256,1536]{1,0:T(8,128)(2,1)S(1)}, u32[]{:S(2)}, u32[]{:S(2)}) %collective-permute-start.64) | collective-permute-done | bytes 786464 | tf_op jit(solution)/shard_map/ppermute | solution.py:145
  477.1 7.9 %collective-permute-done.66.refs_1_.refs_3_ = bf16[256,1024]{1,0:T(8,128)(2,1)} collective-permute-done((bf16[256,1024]{1,0:T(8,128)(2,1)}, bf16[256,1024]{1,0:T(8,128)(2,1)}, u32[]{:S(2)}, u32[]{:S(2)}) %collective-permute-start.66) | collective-permute-done | bytes 524320 | tf_op jit(solution)/shard_map/ppermute | solution.py:145
  484.9 2.8 add_convert_fusion
  490.5 11.8 %expand_shrink_back.3 = (bf16[1024,1024]{1,0:T(8,128)(2,1)}, bf16[1024,1024]{1,0:T(8,128)(2,1)}, f32[512,1024]{1,0:T(8,128)}, bf16[512,1024]{1,0:T(8,128)(2,1)}) custom-call(bf16[256,1024]{1,0:T(8,128)(2,1)} %get-tuple-element.285.refs_0_.refs_2_, bf16[256,1024]{1,0:T(8,128)(2,1)} %collective-permute-done.66.refs_1_.refs_3_, ...), custom_call_target="tpu_custom_call" | custom-call | flops 4294967296 | bytes 17825792 | tf_op jit(solution)/shard_map/expand_shrink_back/pallas_call | solution.py:373
  506.7 7.1 %pair_grad.9 = (bf16[256,1024]{1,0:T(8,128)(2,1)}, bf16[256,1024]{1,0:T(8,128)(2,1)}, bf16[256,1024]{1,0:T(8,128)(2,1)}, bf16[128,1024]{1,0:T(8,128)(2,1)}, bf16[128,1024]{1,0:T(8,128)(2,1)}) custom-call(bf16[1024,1024]{1,0:T(8,128)(2,1)} %norm.1.full.refs_0_, bf16[1024,1024]{1,0:T(8,128)(2,1)} %get-tuple-element.297.refs_1_, ...), custom_call_target="tpu_custom_call" | custom-call | flops 2147483648 | bytes 8388608 | tf_op jit(solution)/shard_map/pair_grad/pallas_call | solution.py:423
  516.8 8.0 %collective-permute-done.91 = bf16[128,1024]{1,0:T(8,128)(2,1)S(1)} collective-permute-done((bf16[128,1024]{1,0:T(8,128)(2,1)}, bf16[128,1024]{1,0:T(8,128)(2,1)S(1)}, u32[]{:S(2)}, u32[]{:S(2)}) %collective-permute-start.91) | collective-permute-done | bytes 262176 | tf_op jit(solution)/shard_map/ppermute | solution.py:145
  530.7 7.0 %collective-permute-done.92 = bf16[256,1024]{1,0:T(8,128)(2,1)S(1)} collective-permute-done((bf16[256,1024]{1,0:T(8,128)(2,1)S(1)}, bf16[256,1024]{1,0:T(8,128)(2,1)S(1)}, u32[]{:S(2)}, u32[]{:S(2)}) %collective-permute-start.92) | collective-permute-done | bytes 524320 | tf_op jit(solution)/shard_map/ppermute | solution.py:145
  539.2 3.1 collective-permute-start.77
  544.3 6.7 pair_grad.8
  551.3 14.2 %collective-permute-done.72.refs_2_ = bf16[256,1024]{1,0:T(8,128)(2,1)S(1)} collective-permute-done((bf16[256,1024]{1,0:T(8,128)(2,1)S(1)}, bf16[256,1024]{1,0:T(8,128)(2,1)S(1)}, u32[]{:S(2)}, u32[]{:S(2)}) %collective-permute-start.72) | collective-permute-done | bytes 524320 | tf_op jit(solution)/shard_map/ppermute | solution.py:145
  566.4 4.0 norm_back.9
  577.6 2.4 add_convert_fusion.3
  580.1 3.0 collective-permute-start.79
  585.4 12.8 %collective-permute-start.93 = (bf16[256,1024]{1,0:T(8,128)(2,1)}, bf16[256,1024]{1,0:T(8,128)(2,1)}, u32[]{:S(2)}, u32[]{:S(2)}) collective-permute-start(bf16[256,1024]{1,0:T(8,128)(2,1)} %add_convert_fusion.1), channel_id=1, source_target_pairs={{0,2},{1,3},{2,0},{3,1},{4,6},{5,7},{6,4},{7,5},{8,10},{9,11},{10,... | collective-permute-start | bytes 1572872 | tf_op jit(solution)/shard_map/ppermute | solution.py:145
  603.3 3.9 collective-permute-done.86
  615.1 7.0 %collective-permute-done.97 = f32[17,128]{1,0:T(8,128)S(1)} collective-permute-done((f32[17,128]{1,0:T(8,128)S(1)}, f32[17,128]{1,0:T(8,128)S(1)}, u32[]{:S(2)}, u32[]{:S(2)}) %collective-permute-start.97) | collective-permute-done | bytes 8736 | tf_op jit(solution)/shard_map/ppermute | solution.py:145
  632.1 4.4 rotated_adam.10
  636.6 4.5 rotated_adam.11
  641.1 4.1 collective-permute-done.81
  646.9 2.8 rotated_adam.9
  653.3 4.3 rotated_adam.14
  657.6 4.4 rotated_adam.15
  (713 shorter events, 250.0 us)
Async XLA Ops:
  7.2 146.5 %all-gather.5.cloned.1.call-start = ((), (), s32[]{:S(2)}) async-start(), calls=%async_computation.3 | async-start | bytes 2621440 | tf_op jit(solution)/shard_map/all_gather | solution.py:890
  22.6 26.5 %collective-permute-start.4 = (bf16[256,1024]{1,0:T(8,128)(2,1)}, bf16[256,1024]{1,0:T(8,128)(2,1)S(1)}, u32[]{:S(2)}, u32[]{:S(2)}) collective-permute-start(bf16[256,1024]{1,0:T(8,128)(2,1)} %pad_maximum_fusion.8), channel_id=1, source_target_pairs={{0,2},{1,3},{2,0},{3,1},{4,6},{5,7},{6,4},{7,5},{8,10},{9,11},{10,... | collective-permute-start | bytes 1572872 | tf_op jit(solution)/shard_map/ppermute | solution.py:145
  26.8 27.4 %collective-permute-start.13 = (bf16[256,1024]{1,0:T(8,128)(2,1)}, bf16[256,1024]{1,0:T(8,128)(2,1)}, u32[]{:S(2)}, u32[]{:S(2)}) collective-permute-start(bf16[256,1024]{1,0:T(8,128)(2,1)} %pad_maximum_fusion.8), channel_id=1, source_target_pairs={{0,8},{1,9},{2,10},{3,11},{4,12},{5,13},{6,14},{7,15},{8,24},{9,25... | collective-permute-start | bytes 1572872 | tf_op jit(solution)/shard_map/ppermute | solution.py:145
  28.3 25.9 %collective-permute-start.14 = (bf16[256,1024]{1,0:T(8,128)(2,1)}, bf16[256,1024]{1,0:T(8,128)(2,1)}, u32[]{:S(2)}, u32[]{:S(2)}) collective-permute-start(bf16[256,1024]{1,0:T(8,128)(2,1)} %pad_maximum_fusion.8), channel_id=1, source_target_pairs={{0,16},{1,17},{2,18},{3,19},{4,20},{5,21},{6,22},{7,23},{8,0},{9,1... | collective-permute-start | bytes 1572872 | tf_op jit(solution)/shard_map/ppermute | solution.py:145
  50.7 26.7 %collective-permute-start.10 = (bf16[272,1024]{1,0:T(8,128)(2,1)}, bf16[272,1024]{1,0:T(8,128)(2,1)}, u32[]{:S(2)}, u32[]{:S(2)}) collective-permute-start(bf16[272,1024]{1,0:T(8,128)(2,1)} %maximum_maximum_fusion), channel_id=1, source_target_pairs={{0,8},{1,9},{2,10},{3,11},{4,12},{5,13},{6,14},{7,15},{8,24},{9,25... | collective-permute-start | bytes 1671176 | tf_op jit(solution)/shard_map/ppermute | solution.py:145
  52.3 25.1 %collective-permute-start.11 = (bf16[272,1024]{1,0:T(8,128)(2,1)}, bf16[272,1024]{1,0:T(8,128)(2,1)}, u32[]{:S(2)}, u32[]{:S(2)}) collective-permute-start(bf16[272,1024]{1,0:T(8,128)(2,1)} %maximum_maximum_fusion), channel_id=1, source_target_pairs={{0,16},{1,17},{2,18},{3,19},{4,20},{5,21},{6,22},{7,23},{8,0},{9,1... | collective-permute-start | bytes 1671176 | tf_op jit(solution)/shard_map/ppermute | solution.py:145
  52.7 21.3 %collective-permute-start.5 = (bf16[256,1024]{1,0:T(8,128)(2,1)}, bf16[256,1024]{1,0:T(8,128)(2,1)}, u32[]{:S(2)}, u32[]{:S(2)}) collective-permute-start(bf16[256,1024]{1,0:T(8,128)(2,1)} %reorder_blocks.11), channel_id=1, source_target_pairs={{2,4},{3,5},{4,2},{5,3},{10,12},{11,13},{12,10},{13,11},{18,20},{1... | collective-permute-start | bytes 1572872 | tf_op jit(solution)/shard_map/ppermute | solution.py:145
  55.8 14.9 %collective-permute-start.15 = (bf16[128,1024]{1,0:T(8,128)(2,1)}, bf16[128,1024]{1,0:T(8,128)(2,1)}, u32[]{:S(2)}, u32[]{:S(2)}) collective-permute-start(bf16[128,1024]{1,0:T(8,128)(2,1)} %slice.650), channel_id=1, source_target_pairs={{0,8},{1,9},{2,10},{3,11},{4,12},{5,13},{6,14},{7,15},{8,24},{9,25... | collective-permute-start | bytes 786440 | tf_op jit(solution)/shard_map/ppermute | solution.py:145
  59.1 13.2 %collective-permute-start.16 = (bf16[128,1024]{1,0:T(8,128)(2,1)}, bf16[128,1024]{1,0:T(8,128)(2,1)}, u32[]{:S(2)}, u32[]{:S(2)}) collective-permute-start(bf16[128,1024]{1,0:T(8,128)(2,1)} %slice.651), channel_id=1, source_target_pairs={{0,16},{1,17},{2,18},{3,19},{4,20},{5,21},{6,22},{7,23},{8,0},{9,1... | collective-permute-start | bytes 786440 | tf_op jit(solution)/shard_map/ppermute | solution.py:145
  59.5 250.4 %all-gather.7.cloned.1.call-start = ((), (), s32[]{:S(2)}) async-start(), calls=%async_computation.4 | async-start | bytes 10485760 | tf_op jit(solution)/shard_map/all_gather | solution.py:891
  70.7 74.7 %collective-permute-start.29 = (s32[1024]{0:T(1024)S(1)}, s32[1024]{0:T(1024)S(1)}, u32[]{:S(2)}, u32[]{:S(2)}) collective-permute-start(s32[1024]{0:T(1024)S(1)} %bitcast.174), channel_id=1, source_target_pairs={{0,4},{1,5},{2,6},{3,7},{4,0},{5,1},{6,2},{7,3},{8,12},{9,13},{10,... | collective-permute-start | bytes 12296 | tf_op jit(solution)/shard_map/ppermute | solution.py:145
  75.1 45.4 %collective-permute-start.6 = (bf16[256,1024]{1,0:T(8,128)(2,1)S(1)}, bf16[256,1024]{1,0:T(8,128)(2,1)}, u32[]{:S(2)}, u32[]{:S(2)}) collective-permute-start(bf16[256,1024]{1,0:T(8,128)(2,1)S(1)} %get-tuple-element.409.refs_0_), channel_id=1, source_target_pairs={{0,1},{1,0},{2,3},{3,2},{4,5},{5,4},{6,7},{7,6},{8,9},{9,8},{10,11... | collective-permute-start | bytes 1572872 | tf_op jit(solution)/shard_map/ppermute | solution.py:145
  76.1 50.3 %collective-permute-start.7 = (bf16[256,1024]{1,0:T(8,128)(2,1)S(1)}, bf16[256,1024]{1,0:T(8,128)(2,1)}, u32[]{:S(2)}, u32[]{:S(2)}) collective-permute-start(bf16[256,1024]{1,0:T(8,128)(2,1)S(1)} %get-tuple-element.409.refs_0_), channel_id=1, source_target_pairs={{0,4},{1,5},{2,6},{3,7},{4,0},{5,1},{6,2},{7,3},{8,12},{9,13},{10,... | collective-permute-start | bytes 1572872 | tf_op jit(solution)/shard_map/ppermute | solution.py:145
  81.6 41.5 %collective-permute-start.17 = (bf16[136,1024]{1,0:T(8,128)(2,1)}, bf16[136,1024]{1,0:T(8,128)(2,1)}, u32[]{:S(2)}, u32[]{:S(2)}) collective-permute-start(bf16[136,1024]{1,0:T(8,128)(2,1)} %slice.654), channel_id=1, source_target_pairs={{0,8},{1,9},{2,10},{3,11},{4,12},{5,13},{6,14},{7,15},{8,24},{9,25... | collective-permute-start | bytes 835592 | tf_op jit(solution)/shard_map/ppermute | solution.py:145
  87.1 55.2 %collective-permute-start.20 = (bf16[128,1024]{1,0:T(8,128)(2,1)}, bf16[128,1024]{1,0:T(8,128)(2,1)}, u32[]{:S(2)}, u32[]{:S(2)}) collective-permute-start(bf16[128,1024]{1,0:T(8,128)(2,1)} %pad_maximum_fusion.20), channel_id=1, source_target_pairs={{0,2},{1,3},{2,0},{3,1},{4,6},{5,7},{6,4},{7,5},{8,10},{9,11},{10,... | collective-permute-start | bytes 786440 | tf_op jit(solution)/shard_map/ppermute | solution.py:145
  147.3 23.3 %collective-permute-start.22 = (bf16[256,1024]{1,0:T(8,128)(2,1)S(1)}, bf16[256,1024]{1,0:T(8,128)(2,1)}, u32[]{:S(2)}, u32[]{:S(2)}) collective-permute-start(bf16[256,1024]{1,0:T(8,128)(2,1)S(1)} %pad_maximum_fusion.9), channel_id=1, source_target_pairs={{0,8},{1,9},{2,10},{3,11},{4,12},{5,13},{6,14},{7,15},{8,24},{9,25... | collective-permute-start | bytes 1572872 | tf_op jit(solution)/shard_map/ppermute | solution.py:145
  148.8 21.8 %collective-permute-start.23 = (bf16[256,1024]{1,0:T(8,128)(2,1)S(1)}, bf16[256,1024]{1,0:T(8,128)(2,1)}, u32[]{:S(2)}, u32[]{:S(2)}) collective-permute-start(bf16[256,1024]{1,0:T(8,128)(2,1)S(1)} %pad_maximum_fusion.9), channel_id=1, source_target_pairs={{0,16},{1,17},{2,18},{3,19},{4,20},{5,21},{6,22},{7,23},{8,0},{9,1... | collective-permute-start | bytes 1572872 | tf_op jit(solution)/shard_map/ppermute | solution.py:145
  153.7 13.9 %collective-permute-start.19 = (bf16[256,1024]{1,0:T(8,128)(2,1)}, bf16[256,1024]{1,0:T(8,128)(2,1)}, u32[]{:S(2)}, u32[]{:S(2)}) collective-permute-start(bf16[256,1024]{1,0:T(8,128)(2,1)} %slice.1306), channel_id=1, source_target_pairs={{0,1},{1,0},{2,3},{3,2},{4,5},{5,4},{6,7},{7,6},{8,9},{9,8},{10,11... | collective-permute-start | bytes 1572872 | tf_op jit(solution)/shard_map/ppermute | solution.py:145
  153.7 336.8 %reduce-scatter.7.cloned.1.call-start = ((), (), s32[]{:S(2)}) async-start(), calls=%async_computation.5 | async-start | bytes 10485760
  170.6 18.6 %collective-permute-start.24 = (bf16[256,1024]{1,0:T(8,128)(2,1)}, bf16[256,1024]{1,0:T(8,128)(2,1)S(1)}, u32[]{:S(2)}, u32[]{:S(2)}) collective-permute-start(bf16[256,1024]{1,0:T(8,128)(2,1)} %get-tuple-element.213.refs_0_), channel_id=1, source_target_pairs={{0,1},{1,0},{2,3},{3,2},{4,5},{5,4},{6,7},{7,6},{8,9},{9,8},{10,11... | collective-permute-start | bytes 1572872 | tf_op jit(solution)/shard_map/ppermute | solution.py:145
  171.1 41.9 %collective-permute-start.25 = (bf16[256,1024]{1,0:T(8,128)(2,1)}, bf16[256,1024]{1,0:T(8,128)(2,1)S(1)}, u32[]{:S(2)}, u32[]{:S(2)}) collective-permute-start(bf16[256,1024]{1,0:T(8,128)(2,1)} %get-tuple-element.213.refs_0_), channel_id=1, source_target_pairs={{0,4},{1,5},{2,6},{3,7},{4,0},{5,1},{6,2},{7,3},{8,12},{9,13},{10,... | collective-permute-start | bytes 1572872 | tf_op jit(solution)/shard_map/ppermute | solution.py:145
  172.0 14.7 %collective-permute-start.27 = (bf16[128,1024]{1,0:T(8,128)(2,1)S(1)}, bf16[128,1024]{1,0:T(8,128)(2,1)S(1)}, u32[]{:S(2)}, u32[]{:S(2)}) collective-permute-start(bf16[128,1024]{1,0:T(8,128)(2,1)S(1)} %slice.662), channel_id=1, source_target_pairs={{0,8},{1,9},{2,10},{3,11},{4,12},{5,13},{6,14},{7,15},{8,24},{9,25... | collective-permute-start | bytes 786440 | tf_op jit(solution)/shard_map/ppermute | solution.py:145
  174.6 14.6 %collective-permute-start.28 = (bf16[128,1024]{1,0:T(8,128)(2,1)S(1)}, bf16[128,1024]{1,0:T(8,128)(2,1)S(1)}, u32[]{:S(2)}, u32[]{:S(2)}) collective-permute-start(bf16[128,1024]{1,0:T(8,128)(2,1)S(1)} %slice.663), channel_id=1, source_target_pairs={{0,16},{1,17},{2,18},{3,19},{4,20},{5,21},{6,22},{7,23},{8,0},{9,1... | collective-permute-start | bytes 786440 | tf_op jit(solution)/shard_map/ppermute | solution.py:145
  189.3 23.7 %collective-permute-start.26 = (bf16[256,1024]{1,0:T(8,128)(2,1)S(1)}, bf16[256,1024]{1,0:T(8,128)(2,1)S(1)}, u32[]{:S(2)}, u32[]{:S(2)}) collective-permute-start(bf16[256,1024]{1,0:T(8,128)(2,1)S(1)} %collective-permute-done.24.refs_1_), channel_id=1, source_target_pairs={{0,4},{1,5},{2,6},{3,7},{4,0},{5,1},{6,2},{7,3},{8,12},{9,13},{10,... | collective-permute-start | bytes 1572872 | tf_op jit(solution)/shard_map/ppermute | solution.py:145
  189.3 12.9 %collective-permute-start.31 = (bf16[256,384]{1,0:T(8,128)(2,1)S(1)}, bf16[256,384]{1,0:T(8,128)(2,1)S(1)}, u32[]{:S(2)}, u32[]{:S(2)}) collective-permute-start(bf16[256,384]{1,0:T(8,128)(2,1)S(1)} %pad_maximum_fusion.23), channel_id=1, source_target_pairs={{0,2},{1,3},{2,0},{3,1},{4,6},{5,7},{6,4},{7,5},{8,10},{9,11},{10,... | collective-permute-start | bytes 589832 | tf_op jit(solution)/shard_map/ppermute | solution.py:145
  192.0 10.8 %collective-permute-start.32 = (bf16[256,384]{1,0:T(8,128)(2,1)S(1)}, bf16[256,384]{1,0:T(8,128)(2,1)S(1)}, u32[]{:S(2)}, u32[]{:S(2)}) collective-permute-start(bf16[256,384]{1,0:T(8,128)(2,1)S(1)} %pad_maximum_fusion.23), channel_id=1, source_target_pairs={{0,1},{1,0},{2,3},{3,2},{4,5},{5,4},{6,7},{7,6},{8,9},{9,8},{10,11... | collective-permute-start | bytes 589832 | tf_op jit(solution)/shard_map/ppermute | solution.py:145
  192.4 14.9 %collective-permute-start.33 = (bf16[256,384]{1,0:T(8,128)(2,1)S(1)}, bf16[256,384]{1,0:T(8,128)(2,1)S(1)}, u32[]{:S(2)}, u32[]{:S(2)}) collective-permute-start(bf16[256,384]{1,0:T(8,128)(2,1)S(1)} %pad_maximum_fusion.23), channel_id=1, source_target_pairs={{0,3},{1,2},{2,1},{3,0},{4,7},{5,6},{6,5},{7,4},{8,11},{9,10},{10,... | collective-permute-start | bytes 589832 | tf_op jit(solution)/shard_map/ppermute | solution.py:145
  234.4 28.6 %collective-permute-start.37 = (bf16[256,1536]{1,0:T(8,128)(2,1)}, bf16[256,1536]{1,0:T(8,128)(2,1)S(1)}, u32[]{:S(2)}, u32[]{:S(2)}) collective-permute-start(bf16[256,1536]{1,0:T(8,128)(2,1)} %constant_dynamic-update-slice_fusion.17), channel_id=1, source_target_pairs={{0,8},{1,9},{2,10},{3,11},{4,12},{5,13},{6,14},{7,15},{8,24},{9,25... | collective-permute-start | bytes 2359304 | tf_op jit(solution)/shard_map/ppermute | solution.py:145
  235.9 27.1 %collective-permute-start.38 = (bf16[256,1536]{1,0:T(8,128)(2,1)}, bf16[256,1536]{1,0:T(8,128)(2,1)S(1)}, u32[]{:S(2)}, u32[]{:S(2)}) collective-permute-start(bf16[256,1536]{1,0:T(8,128)(2,1)} %constant_dynamic-update-slice_fusion.17), channel_id=1, source_target_pairs={{0,16},{1,17},{2,18},{3,19},{4,20},{5,21},{6,22},{7,23},{8,0},{9,1... | collective-permute-start | bytes 2359304 | tf_op jit(solution)/shard_map/ppermute | solution.py:145
  238.7 18.2 %collective-permute-start.35 = (bf16[256,1024]{1,0:T(8,128)(2,1)S(1)}, bf16[256,1024]{1,0:T(8,128)(2,1)S(1)}, u32[]{:S(2)}, u32[]{:S(2)}) collective-permute-start(bf16[256,1024]{1,0:T(8,128)(2,1)S(1)} %slice.1305), channel_id=1, source_target_pairs={{0,1},{1,0},{2,3},{3,2},{4,5},{5,4},{6,7},{7,6},{8,9},{9,8},{10,11... | collective-permute-start | bytes 1572872 | tf_op jit(solution)/shard_map/ppermute | solution.py:145
  266.0 23.2 %collective-permute-start.44 = (bf16[256,1024]{1,0:T(8,128)(2,1)}, bf16[256,1024]{1,0:T(8,128)(2,1)S(1)}, u32[]{:S(2)}, u32[]{:S(2)}) collective-permute-start(bf16[256,1024]{1,0:T(8,128)(2,1)} %get-tuple-element.228), channel_id=1, source_target_pairs={{0,4},{1,5},{2,6},{3,7},{4,0},{5,1},{6,2},{7,3},{8,12},{9,13},{10,... | collective-permute-start | bytes 1572872 | tf_op jit(solution)/shard_map/ppermute | solution.py:145
  277.0 11.7 %collective-permute-start.43 = (bf16[128,1536]{1,0:T(8,128)(2,1)S(1)}, bf16[128,1536]{1,0:T(8,128)(2,1)S(1)}, u32[]{:S(2)}, u32[]{:S(2)}) collective-permute-start(bf16[128,1536]{1,0:T(8,128)(2,1)S(1)} %slice.690), channel_id=1, source_target_pairs={{0,16},{1,17},{2,18},{3,19},{4,20},{5,21},{6,22},{7,23},{8,0},{9,1... | collective-permute-start | bytes 1179656 | tf_op jit(solution)/shard_map/ppermute | solution.py:145
  351.7 15.0 %collective-permute-start.51 = (bf16[2,1024]{1,0:T(2,128)(2,1)}, bf16[2,1024]{1,0:T(2,128)(2,1)}, u32[]{:S(2)}, u32[]{:S(2)}) collective-permute-start(bf16[2,1024]{1,0:T(2,128)(2,1)} %get-tuple-element.456), channel_id=1, source_target_pairs={{0,1},{1,4},{2,3},{3,6},{4,5},{6,7},{8,9},{9,12},{10,11},{11,14},{... | collective-permute-start | bytes 12296 | tf_op jit(solution)/shard_map/ppermute | solution.py:145
  366.8 234.0 %reduce-scatter.5.cloned.1.call-start = ((), (), s32[]{:S(2)}) async-start(), calls=%async_computation.2 | async-start | bytes 2621440 | tf_op jit(solution)/shard_map/reduce_scatter | solution.py:1161
  397.7 14.4 %collective-permute-start.56 = (bf16[256,1024]{1,0:T(8,128)(2,1)}, bf16[256,1024]{1,0:T(8,128)(2,1)}, u32[]{:S(2)}, u32[]{:S(2)}) collective-permute-start(bf16[256,1024]{1,0:T(8,128)(2,1)} %get-tuple-element.252.refs_0_.refs_5_), channel_id=1, source_target_pairs={{0,1},{1,0},{2,3},{3,2},{4,5},{5,4},{6,7},{7,6},{8,9},{9,8},{10,11... | collective-permute-start | bytes 1572872 | tf_op jit(solution)/shard_map/ppermute | solution.py:145
  407.0 14.1 %collective-permute-start.58 = (bf16[256,1024]{1,0:T(8,128)(2,1)}, bf16[256,1024]{1,0:T(8,128)(2,1)}, u32[]{:S(2)}, u32[]{:S(2)}) collective-permute-start(bf16[256,1024]{1,0:T(8,128)(2,1)} %get-tuple-element.252.refs_0_.refs_5_), channel_id=1, source_target_pairs={{0,4},{1,5},{2,6},{3,7},{4,0},{5,1},{6,2},{7,3},{8,12},{9,13},{10,... | collective-permute-start | bytes 1572872 | tf_op jit(solution)/shard_map/ppermute | solution.py:145
  418.6 17.4 %collective-permute-start.60 = (bf16[128,1536]{1,0:T(8,128)(2,1)}, bf16[128,1536]{1,0:T(8,128)(2,1)S(1)}, u32[]{:S(2)}, u32[]{:S(2)}) collective-permute-start(bf16[128,1536]{1,0:T(8,128)(2,1)} %get-tuple-element.267), channel_id=1, source_target_pairs={{0,8},{1,9},{2,10},{3,11},{4,12},{5,13},{6,14},{7,15},{8,24},{9,25... | collective-permute-start | bytes 1179656 | tf_op jit(solution)/shard_map/ppermute | solution.py:145
  419.7 16.4 %collective-permute-start.61 = (bf16[128,1536]{1,0:T(8,128)(2,1)}, bf16[128,1536]{1,0:T(8,128)(2,1)S(1)}, u32[]{:S(2)}, u32[]{:S(2)}) collective-permute-start(bf16[128,1536]{1,0:T(8,128)(2,1)} %get-tuple-element.268), channel_id=1, source_target_pairs={{0,16},{1,17},{2,18},{3,19},{4,20},{5,21},{6,22},{7,23},{8,0},{9,1... | collective-permute-start | bytes 1179656 | tf_op jit(solution)/shard_map/ppermute | solution.py:145
  436.3 33.5 %collective-permute-start.64 = (bf16[256,1536]{1,0:T(8,128)(2,1)S(1)}, bf16[256,1536]{1,0:T(8,128)(2,1)S(1)}, u32[]{:S(2)}, u32[]{:S(2)}) collective-permute-start(bf16[256,1536]{1,0:T(8,128)(2,1)S(1)} %pad_maximum_fusion.6), channel_id=1, source_target_pairs={{0,8},{1,9},{2,10},{3,11},{4,12},{5,13},{6,14},{7,15},{8,24},{9,25... | collective-permute-start | bytes 2359304 | tf_op jit(solution)/shard_map/ppermute | solution.py:145
  437.5 33.4 %collective-permute-start.65 = (bf16[256,1536]{1,0:T(8,128)(2,1)S(1)}, bf16[256,1536]{1,0:T(8,128)(2,1)}, u32[]{:S(2)}, u32[]{:S(2)}) collective-permute-start(bf16[256,1536]{1,0:T(8,128)(2,1)S(1)} %pad_maximum_fusion.7), channel_id=1, source_target_pairs={{0,16},{1,17},{2,18},{3,19},{4,20},{5,21},{6,22},{7,23},{8,0},{9,1... | collective-permute-start | bytes 2359304 | tf_op jit(solution)/shard_map/ppermute | solution.py:145
  440.3 14.3 %collective-permute-start.63 = (bf16[256,1024]{1,0:T(8,128)(2,1)}, bf16[256,1024]{1,0:T(8,128)(2,1)}, u32[]{:S(2)}, u32[]{:S(2)}) collective-permute-start(bf16[256,1024]{1,0:T(8,128)(2,1)} %slice.1304), channel_id=1, source_target_pairs={{0,1},{1,0},{2,3},{3,2},{4,5},{5,4},{6,7},{7,6},{8,9},{9,8},{10,11... | collective-permute-start | bytes 1572872 | tf_op jit(solution)/shard_map/ppermute | solution.py:145
  470.9 14.0 %collective-permute-start.66 = (bf16[256,1024]{1,0:T(8,128)(2,1)}, bf16[256,1024]{1,0:T(8,128)(2,1)}, u32[]{:S(2)}, u32[]{:S(2)}) collective-permute-start(bf16[256,1024]{1,0:T(8,128)(2,1)} %get-tuple-element.285.refs_0_.refs_2_), channel_id=1, source_target_pairs={{0,1},{1,0},{2,3},{3,2},{4,5},{5,4},{6,7},{7,6},{8,9},{9,8},{10,11... | collective-permute-start | bytes 1572872 | tf_op jit(solution)/shard_map/ppermute | solution.py:145
  475.1 15.5 %collective-permute-start.69 = (bf16[256,1024]{1,0:T(8,128)(2,1)}, bf16[256,1024]{1,0:T(8,128)(2,1)}, u32[]{:S(2)}, u32[]{:S(2)}) collective-permute-start(bf16[256,1024]{1,0:T(8,128)(2,1)} %get-tuple-element.285.refs_0_.refs_2_), channel_id=1, source_target_pairs={{0,4},{1,5},{2,6},{3,7},{4,0},{5,1},{6,2},{7,3},{8,12},{9,13},{10,... | collective-permute-start | bytes 1572872 | tf_op jit(solution)/shard_map/ppermute | solution.py:145
  475.1 15.4 %collective-permute-start.67 = (bf16[128,1024]{1,0:T(8,128)(2,1)}, bf16[128,1024]{1,0:T(8,128)(2,1)}, u32[]{:S(2)}, u32[]{:S(2)}) collective-permute-start(bf16[128,1024]{1,0:T(8,128)(2,1)} %get-tuple-element.290), channel_id=1, source_target_pairs={{0,8},{1,9},{2,10},{3,11},{4,12},{5,13},{6,14},{7,15},{8,24},{9,25... | collective-permute-start | bytes 786440 | tf_op jit(solution)/shard_map/ppermute | solution.py:145
  476.0 14.5 %collective-permute-start.68 = (bf16[128,1024]{1,0:T(8,128)(2,1)}, bf16[128,1024]{1,0:T(8,128)(2,1)S(1)}, u32[]{:S(2)}, u32[]{:S(2)}) collective-permute-start(bf16[128,1024]{1,0:T(8,128)(2,1)} %get-tuple-element.291), channel_id=1, source_target_pairs={{0,16},{1,17},{2,18},{3,19},{4,20},{5,21},{6,22},{7,23},{8,0},{9,1... | collective-permute-start | bytes 786440 | tf_op jit(solution)/shard_map/ppermute | solution.py:145
  502.3 25.5 %collective-permute-start.71 = (bf16[512,1024]{1,0:T(8,128)(2,1)}, bf16[512,1024]{1,0:T(8,128)(2,1)}, u32[]{:S(2)}, u32[]{:S(2)}) collective-permute-start(bf16[512,1024]{1,0:T(8,128)(2,1)} %get-tuple-element.295), channel_id=1, source_target_pairs={{0,4},{1,5},{2,6},{3,7},{4,0},{5,1},{6,2},{7,3},{8,12},{9,13},{10,... | collective-permute-start | bytes 3145736 | tf_op jit(solution)/shard_map/ppermute | solution.py:145
  504.2 46.8 %collective-permute-start.73 = (bf16[256,1024]{1,0:T(8,128)(2,1)S(1)}, bf16[256,1024]{1,0:T(8,128)(2,1)S(1)}, u32[]{:S(2)}, u32[]{:S(2)}) collective-permute-start(bf16[256,1024]{1,0:T(8,128)(2,1)S(1)} %pad_maximum_fusion.11), channel_id=1, source_target_pairs={{0,8},{1,9},{2,10},{3,11},{4,12},{5,13},{6,14},{7,15},{8,24},{9,25... | collective-permute-start | bytes 1572872 | tf_op jit(solution)/shard_map/ppermute | solution.py:145
  505.3 46.0 %collective-permute-start.74 = (bf16[256,1024]{1,0:T(8,128)(2,1)S(1)}, bf16[256,1024]{1,0:T(8,128)(2,1)S(1)}, u32[]{:S(2)}, u32[]{:S(2)}) collective-permute-start(bf16[256,1024]{1,0:T(8,128)(2,1)S(1)} %pad_maximum_fusion.12), channel_id=1, source_target_pairs={{0,16},{1,17},{2,18},{3,19},{4,20},{5,21},{6,22},{7,23},{8,0},{9,1... | collective-permute-start | bytes 1572872 | tf_op jit(solution)/shard_map/ppermute | solution.py:145
  513.8 11.0 %collective-permute-start.91 = (bf16[128,1024]{1,0:T(8,128)(2,1)}, bf16[128,1024]{1,0:T(8,128)(2,1)S(1)}, u32[]{:S(2)}, u32[]{:S(2)}) collective-permute-start(bf16[128,1024]{1,0:T(8,128)(2,1)} %get-tuple-element.345), channel_id=1, source_target_pairs={{0,16},{1,17},{2,18},{3,19},{4,20},{5,21},{6,22},{7,23},{8,0},{9,1... | collective-permute-start | bytes 786440 | tf_op jit(solution)/shard_map/ppermute | solution.py:145
  514.9 11.1 %collective-permute-start.89 = (bf16[128,1024]{1,0:T(8,128)(2,1)}, bf16[128,1024]{1,0:T(8,128)(2,1)S(1)}, u32[]{:S(2)}, u32[]{:S(2)}) collective-permute-start(bf16[128,1024]{1,0:T(8,128)(2,1)} %get-tuple-element.343), channel_id=1, source_target_pairs={{0,8},{1,9},{2,10},{3,11},{4,12},{5,13},{6,14},{7,15},{8,24},{9,25... | collective-permute-start | bytes 786440 | tf_op jit(solution)/shard_map/ppermute | solution.py:145
  524.9 12.8 %collective-permute-start.92 = (bf16[256,1024]{1,0:T(8,128)(2,1)S(1)}, bf16[256,1024]{1,0:T(8,128)(2,1)S(1)}, u32[]{:S(2)}, u32[]{:S(2)}) collective-permute-start(bf16[256,1024]{1,0:T(8,128)(2,1)S(1)} %pad_maximum_fusion.16), channel_id=1, source_target_pairs={{0,16},{1,17},{2,18},{3,19},{4,20},{5,21},{6,22},{7,23},{8,0},{9,1... | collective-permute-start | bytes 1572872 | tf_op jit(solution)/shard_map/ppermute | solution.py:145
  526.1 13.1 %collective-permute-start.90 = (bf16[256,1024]{1,0:T(8,128)(2,1)S(1)}, bf16[256,1024]{1,0:T(8,128)(2,1)S(1)}, u32[]{:S(2)}, u32[]{:S(2)}) collective-permute-start(bf16[256,1024]{1,0:T(8,128)(2,1)S(1)} %pad_maximum_fusion.15), channel_id=1, source_target_pairs={{0,8},{1,9},{2,10},{3,11},{4,12},{5,13},{6,14},{7,15},{8,24},{9,25... | collective-permute-start | bytes 1572872 | tf_op jit(solution)/shard_map/ppermute | solution.py:145
  529.6 35.9 %collective-permute-start.72 = (bf16[256,1024]{1,0:T(8,128)(2,1)S(1)}, bf16[256,1024]{1,0:T(8,128)(2,1)S(1)}, u32[]{:S(2)}, u32[]{:S(2)}) collective-permute-start(bf16[256,1024]{1,0:T(8,128)(2,1)S(1)} %slice.1303), channel_id=1, source_target_pairs={{0,1},{1,0},{2,3},{3,2},{4,5},{5,4},{6,7},{7,6},{8,9},{9,8},{10,11... | collective-permute-start | bytes 1572872 | tf_op jit(solution)/shard_map/ppermute | solution.py:145
  537.7 113.5 %collective-permute-start.57 = (bf16[256,1024]{1,0:T(8,128)(2,1)}, bf16[256,1024]{1,0:T(8,128)(2,1)}, u32[]{:S(2)}, u32[]{:S(2)}) collective-permute-start(bf16[256,1024]{1,0:T(8,128)(2,1)} %reorder_blocks.16), channel_id=1, source_target_pairs={{2,4},{3,5},{4,2},{5,3},{10,12},{11,13},{12,10},{13,11},{18,20},{1... | collective-permute-start | bytes 1572872 | tf_op jit(solution)/shard_map/ppermute | solution.py:145
  539.2 46.2 %collective-permute-start.77 = (bf16[256,384]{1,0:T(8,128)(2,1)}, bf16[256,384]{1,0:T(8,128)(2,1)}, u32[]{:S(2)}, u32[]{:S(2)}) collective-permute-start(bf16[256,384]{1,0:T(8,128)(2,1)} %pad_maximum_fusion.25), channel_id=1, source_target_pairs={{0,2},{1,3},{2,0},{3,1},{4,6},{5,7},{6,4},{7,5},{8,10},{9,11},{10,... | collective-permute-start | bytes 589832 | tf_op jit(solution)/shard_map/ppermute | solution.py:145
  551.0 47.2 %collective-permute-start.78 = (bf16[256,384]{1,0:T(8,128)(2,1)}, bf16[256,384]{1,0:T(8,128)(2,1)}, u32[]{:S(2)}, u32[]{:S(2)}) collective-permute-start(bf16[256,384]{1,0:T(8,128)(2,1)} %pad_maximum_fusion.26), channel_id=1, source_target_pairs={{0,1},{1,0},{2,3},{3,2},{4,5},{5,4},{6,7},{7,6},{8,9},{9,8},{10,11... | collective-permute-start | bytes 589832 | tf_op jit(solution)/shard_map/ppermute | solution.py:145
  580.1 18.7 %collective-permute-start.79 = (bf16[256,384]{1,0:T(8,128)(2,1)}, bf16[256,384]{1,0:T(8,128)(2,1)}, u32[]{:S(2)}, u32[]{:S(2)}) collective-permute-start(bf16[256,384]{1,0:T(8,128)(2,1)} %pad_maximum_fusion.27), channel_id=1, source_target_pairs={{0,3},{1,2},{2,1},{3,0},{4,7},{5,6},{6,5},{7,4},{8,11},{9,10},{10,... | collective-permute-start | bytes 589832 | tf_op jit(solution)/shard_map/ppermute | solution.py:145
  583.1 17.1 %collective-permute-start.76 = (bf16[128,1024]{1,0:T(8,128)(2,1)S(1)}, bf16[128,1024]{1,0:T(8,128)(2,1)}, u32[]{:S(2)}, u32[]{:S(2)}) collective-permute-start(bf16[128,1024]{1,0:T(8,128)(2,1)S(1)} %copy-done.133), channel_id=1, source_target_pairs={{0,8},{1,9},{2,10},{3,11},{4,12},{5,13},{6,14},{7,15},{8,24},{9,25... | collective-permute-start | bytes 786440 | tf_op jit(solution)/shard_map/ppermute | solution.py:145
  585.4 64.3 %collective-permute-start.93 = (bf16[256,1024]{1,0:T(8,128)(2,1)}, bf16[256,1024]{1,0:T(8,128)(2,1)}, u32[]{:S(2)}, u32[]{:S(2)}) collective-permute-start(bf16[256,1024]{1,0:T(8,128)(2,1)} %add_convert_fusion.1), channel_id=1, source_target_pairs={{0,2},{1,3},{2,0},{3,1},{4,6},{5,7},{6,4},{7,5},{8,10},{9,11},{10,... | collective-permute-start | bytes 1572872 | tf_op jit(solution)/shard_map/ppermute | solution.py:145
  612.2 11.1 %collective-permute-start.96 = (f32[17,128]{1,0:T(8,128)S(1)}, f32[17,128]{1,0:T(8,128)S(1)}, u32[]{:S(2)}, u32[]{:S(2)}) collective-permute-start(f32[17,128]{1,0:T(8,128)S(1)} %select_add_fusion), channel_id=1, source_target_pairs={{0,1},{1,0},{2,3},{3,2},{4,5},{5,4},{6,7},{7,6},{8,9},{9,8},{10,11... | collective-permute-start | bytes 26120 | tf_op jit(solution)/shard_map/ppermute | solution.py:145
  615.1 13.6 %collective-permute-start.80 = (bf16[128,1024]{1,0:T(8,128)(2,1)S(1)}, bf16[128,1024]{1,0:T(8,128)(2,1)S(1)}, u32[]{:S(2)}, u32[]{:S(2)}) collective-permute-start(bf16[128,1024]{1,0:T(8,128)(2,1)S(1)} %broadcast_select_fusion.19), channel_id=1, source_target_pairs={{0,4},{1,5},{2,6},{3,7},{4,0},{5,1},{6,2},{7,3},{8,12},{9,13},{10,... | collective-permute-start | bytes 786440 | tf_op jit(solution)/shard_map/ppermute | solution.py:145
  624.2 25.5 %collective-permute-start.88 = (bf16[256,1024]{1,0:T(8,128)(2,1)S(1)}, bf16[256,1024]{1,0:T(8,128)(2,1)S(1)}, u32[]{:S(2)}, u32[]{:S(2)}) collective-permute-start(bf16[256,1024]{1,0:T(8,128)(2,1)S(1)} %pad_maximum_fusion.14), channel_id=1, source_target_pairs={{0,16},{1,17},{2,18},{3,19},{4,20},{5,21},{6,22},{7,23},{8,0},{9,1... | collective-permute-start | bytes 1572872 | tf_op jit(solution)/shard_map/ppermute | solution.py:145
  628.7 21.0 %collective-permute-start.87 = (bf16[256,1024]{1,0:T(8,128)(2,1)S(1)}, bf16[256,1024]{1,0:T(8,128)(2,1)S(1)}, u32[]{:S(2)}, u32[]{:S(2)}) collective-permute-start(bf16[256,1024]{1,0:T(8,128)(2,1)S(1)} %pad_maximum_fusion.13), channel_id=1, source_target_pairs={{0,8},{1,9},{2,10},{3,11},{4,12},{5,13},{6,14},{7,15},{8,24},{9,25... | collective-permute-start | bytes 1572872 | tf_op jit(solution)/shard_map/ppermute | solution.py:145
  630.6 14.6 %collective-permute-start.81 = (bf16[128,1024]{1,0:T(8,128)(2,1)S(1)}, bf16[128,1024]{1,0:T(8,128)(2,1)S(1)}, u32[]{:S(2)}, u32[]{:S(2)}) collective-permute-start(bf16[128,1024]{1,0:T(8,128)(2,1)S(1)} %broadcast_select_fusion.6), channel_id=1, source_target_pairs={{0,2},{1,3},{2,0},{3,1},{4,6},{5,7},{6,4},{7,5},{8,10},{9,11},{10,... | collective-permute-start | bytes 786440 | tf_op jit(solution)/shard_map/ppermute | solution.py:145
  (175 other events, 1517.8 us)
Sparse Core Ops, SparseCore 0:
  59.7 62.6 all-gather.4
  153.8 102.3 all-gather.6
  366.9 101.7 reduce-scatter.6
  503.1 57.5 reduce-scatter.4

commit v3 on v2

--- a/solution.py
+++ b/solution.py
@@ -69,6 +69,63 @@
         out_specs=pl.BlockSpec(memory_space=pltpu.VMEM),
         name="reorder_blocks",
     )(order, rows)
+
+
+def merge_kernel(count, *refs):
+    pieces, merged = refs[:-1], refs[-1]
+    columns = merged.shape[1] // count // len(pieces)
+    for group in range(count):
+        for at, piece in enumerate(pieces):
+            first = (group * len(pieces) + at) * columns
+            merged[:, first : first + columns] = piece[:, group * columns : (group + 1) * columns]
+
+
+def side_by_side(pieces, count):
+    rows, lanes = pieces[0].shape
+    columns = lanes // count
+    if columns % 128:
+        return jnp.concatenate(
+            [piece[:, at * columns : (at + 1) * columns] for at in range(count) for piece in pieces],
+            axis=1,
+        )
+    return pl.pallas_call(
+        partial(merge_kernel, count),
+        out_shape=jax.ShapeDtypeStruct((rows, lanes * len(pieces)), pieces[0].dtype),
+        in_specs=[pl.BlockSpec(memory_space=pltpu.VMEM)] * len(pieces),
+        out_specs=pl.BlockSpec(memory_space=pltpu.VMEM),
+        name="side_by_side",
+    )(*pieces)
+
+
+def apart_kernel(count, merged, *pieces):
+    columns = merged.shape[1] // count // len(pieces)
+    for group in range(count):
+        for at, piece in enumerate(pieces):
+            first = (group * len(pieces) + at) * columns
+            piece[:, group * columns : (group + 1) * columns] = merged[:, first : first + columns]
+
+
+def apart(merged, count, parts):
+    rows, lanes = merged.shape
+    columns = lanes // count // parts
+    if columns % 128:
+        return [
+            jnp.concatenate(
+                [
+                    merged[:, (group * parts + at) * columns : (group * parts + at + 1) * columns]
+                    for group in range(count)
+                ],
+                axis=1,
+            )
+            for at in range(parts)
+        ]
+    return pl.pallas_call(
+        partial(apart_kernel, count),
+        out_shape=[jax.ShapeDtypeStruct((rows, lanes // parts), merged.dtype)] * parts,
+        in_specs=[pl.BlockSpec(memory_space=pltpu.VMEM)],
+        out_specs=[pl.BlockSpec(memory_space=pltpu.VMEM)] * parts,
+        name="apart",
+    )(merged)
 
 
 class Plan:
@@ -167,7 +224,7 @@
     from_last, from_next = found[-2], found[-1]
     if earlier:
         from_last, from_next, *_ = together(from_last, from_next, *earlier)
-    return [send(from_last[:cut], plan.to_next), send(from_next[cut:], plan.to_last)]
+    return send(from_last[:cut], plan.to_next), send(from_next[cut:], plan.to_last)
 
 
 def gathered(found, ends, height=None):
@@ -177,30 +234,6 @@
         [part[:height] for part in found] + [ends[0], ends[1][: height - cut]], axis=0
     )
     return whole, [part[height:] for part in found] + [ends[1][height - cut :]]
-
-
-def scatter_start(plan, pieces, *earlier):
-    ahead, behind = pieces[-1]
-    if earlier:
-        ahead, behind, *_ = together(ahead, behind, *earlier)
-    return send(ahead, plan.to_next), send(behind, plan.to_last)
-
-
-def scatter_end(plan, pieces, ahead, behind):
-    cut = pieces[0].shape[0] // 2
-    for hop in range(plan.chips // 2 - 1, 0, -1):
-        to_ahead, to_behind = pieces[2 * hop], pieces[2 * hop - 1]
-        if ahead.shape[0] == cut:
-            ahead = jnp.concatenate([to_ahead[:cut] + ahead, to_ahead[cut:]], axis=0)
-            behind = jnp.concatenate([to_behind[:cut], to_behind[cut:] + behind], axis=0)
-        else:
-            ahead, behind = to_ahead + ahead, to_behind + behind
-        ahead, behind = send(ahead, plan.to_next), send(behind, plan.to_last)
-    return ahead, behind
-
-
-def scatter_sum(pieces, ahead, behind):
-    return (pieces[0].astype(F32) + ahead.astype(F32) + behind.astype(F32)).astype(BF16)
 
 
 VMEM = pltpu.VMEM
@@ -243,36 +276,27 @@
 
 
 def hidden_blocks(weights):
-    if weights[0].ndim == 4:
-        return weights[0].shape[3] // 2, weights[0].shape[1]
-    middle = weights[0].shape[1] // 2
+    middle = weights[0][2] // 2
     block = min(512, middle)
     return block, middle // block
 
 
 def weight_specs(weights, block, each):
     specs = []
-    for at, weight in enumerate(weights):
+    for at, (weight, first, _) in enumerate(weights):
         for side in (0, 1):
-            if weight.ndim == 4:
-                shape = (weight.shape[0], 1, weight.shape[2], block)
-                specs.append(pl.BlockSpec(shape, lambda step, side=side: (0, step, 0, side)))
-            else:
-                specs.append(
-                    pl.BlockSpec(
-                        (weight.shape[0], block),
-                        lambda step, at=at, side=side: (
-                            0,
-                            side * each + jnp.clip(step - at * each, 0, each - 1),
-                        ),
-                    )
+            start = first // block + side * each
+            specs.append(
+                pl.BlockSpec(
+                    (weight.shape[0], block),
+                    lambda step, at=at, start=start: (0, start + jnp.clip(step - at * each, 0, each - 1)),
                 )
+            )
     return specs
 
 
-def flat(ref):
-    values = ref[...]
-    return values.reshape(-1, values.shape[-1])
+def weight_args(weights):
+    return [weight for weight, _, _ in weights for _ in (0, 1)]
 
 
 def whole_specs(chunks):
@@ -288,17 +312,19 @@
             at += chunk.shape[0]
 
 
-def expand_shrink_kernel(count, each, full, *refs):
-    preact, near, away, total = refs[2 * count :]
+def expand_shrink_kernel(count, each, parts, *refs):
+    chunks, refs = refs[:parts], refs[parts:]
+    preact, near, away, total, full = refs[2 * count :]
     step = pl.program_id(0)
+    join(step == 0, chunks, full)
     for at in range(count):
 
         @pl.when(step // each == at)
         def _(at=at):
-            values = mm(full[...], flat(refs[2 * at]))
+            values = mm(full[...], refs[2 * at][...])
             preact[...] = values
             kept = (values * jax.nn.sigmoid(values)).astype(BF16)
-            added = mm_nt(kept, flat(refs[2 * at + 1]))
+            added = mm_nt(kept, refs[2 * at + 1][...])
 
             @pl.when(step == 0)
             def _():
@@ -313,25 +339,21 @@
 
 def expand_shrink(full, weights):
     block, each = hidden_blocks(weights)
-    rows, width = full.shape
+    rows, width = sum(chunk.shape[0] for chunk in full), full[0].shape[1]
     steps = each * len(weights)
     outs = [shape_of((rows, steps * block), F32)] + parts_of(rows, width)
     part = pl.BlockSpec((rows // 2, width), lambda step: (0, 0))
     return pl.pallas_call(
-        partial(expand_shrink_kernel, len(weights), each),
+        partial(expand_shrink_kernel, len(weights), each, len(full)),
         grid=(steps,),
         out_shape=outs,
-        in_specs=[pl.BlockSpec((rows, width), lambda step: (0, 0))] + weight_specs(weights, block, each),
-        out_specs=[
-            pl.BlockSpec((rows, block), lambda step: (0, step)),
-            part,
-            part,
-        ],
-        scratch_shapes=[pltpu.VMEM((rows, width), F32)],
+        in_specs=whole_specs(full) + weight_specs(weights, block, each),
+        out_specs=[pl.BlockSpec((rows, block), lambda step: (0, step)), part, part],
+        scratch_shapes=[pltpu.VMEM((rows, width), F32), pltpu.VMEM((rows, width), BF16)],
         compiler_params=PARAMS,
-        cost_estimate=cost(4 * rows * width * steps * block, full, *weights, *outs),
+        cost_estimate=cost(4 * rows * width * steps * block, *full, *outs),
         name="expand_shrink",
-    )(full, *[weight for weight in weights for _ in (0, 1)])
+    )(*full, *weight_args(weights))
 
 
 def expand_shrink_back_kernel(count, each, parts, *refs):
@@ -346,10 +368,10 @@
             values = preact[...]
             gate = jax.nn.sigmoid(values)
             kept[...] = (values * gate).astype(BF16)
-            grad = mm(incoming[...], flat(refs[2 * at + 1]))
+            grad = mm(incoming[...], refs[2 * at + 1][...])
             grad = (grad * gate * (1.0 + values * (1.0 - gate))).astype(BF16)
             back[...] = grad
-            added = mm_nt(grad, flat(refs[2 * at]))
+            added = mm_nt(grad, refs[2 * at][...])
 
             @pl.when(step == 0)
             def _():
@@ -378,24 +400,28 @@
         out_specs=[by_step, by_step, part, part],
         scratch_shapes=[pltpu.VMEM((rows, width), F32), pltpu.VMEM((rows, width), BF16)],
         compiler_params=PARAMS,
-        cost_estimate=cost(4 * rows * width * steps * block, *incoming, preact, *weights, *outs),
+        cost_estimate=cost(4 * rows * width * steps * block, *incoming, preact, *outs),
         name="expand_shrink_back",
-    )(*incoming, preact, *[weight for weight in weights for _ in (0, 1)])
-
-
-def pair_grad_kernel(each, cuts, parts, other_parts, *refs):
+    )(*incoming, preact, *weight_args(weights))
+
+
+def pair_grad_kernel(each, parts, other_parts, ordered, *refs):
+    order, refs = (refs[0], refs[1:]) if ordered else (None, refs)
     chunks, right, refs = refs[:parts], refs[parts], refs[parts + 1 :]
     other_chunks, other_right, refs = refs[:other_parts], refs[other_parts], refs[other_parts + 1 :]
-    outs, left = refs[:-1], refs[-1]
+    out, left = refs
     step = pl.program_id(0)
     join(step == 0, chunks, left)
     join(step == each, other_chunks, left)
 
     def put(values):
-        at = 0
-        for out, height in zip(outs, cuts):
-            out[...] = values[at : at + height].astype(BF16).reshape(out.shape)
-            at += height
+        if not ordered:
+            out[...] = values.astype(BF16)
+            return
+        height = out.shape[0] // ordered
+        for at in range(ordered):
+            rows = pl.ds(pl.multiple_of(order[at] * height, height), height)
+            out[rows, :] = values[at * height : (at + 1) * height].astype(BF16)
 
     @pl.when(step < each)
     def _():
@@ -406,25 +432,21 @@
         put(mm_tn(left[...], other_right[...]))
 
 
-def pair_grad(left, right, other_left, other_right, cuts, block=512, columns=None, first=0, blocked=None):
+def pair_grad(left, right, other_left, other_right, block=512, columns=None, first=0, order=None):
     rows, width = right.shape[0], left[0].shape[1]
     columns = columns or right.shape[1]
     other_columns = other_right.shape[1] if columns == right.shape[1] else columns
-    block = blocked[3] // 2 if blocked else min(block, columns, other_columns)
+    block = min(block, columns, other_columns)
     each, other_each = columns // block, other_columns // block
     start = first // block
-    if blocked:
-        outs = [shape_of(blocked, BF16)]
-        shape = (blocked[0], 1, blocked[2], block)
-        out_specs = [pl.BlockSpec(shape, lambda step: (0, step % each, 0, step // each))]
-    else:
-        outs = [shape_of((height, columns + other_columns), BF16) for height in cuts]
-        out_specs = [pl.BlockSpec((height, block), lambda step: (0, step)) for height in cuts]
+    out = shape_of((width, columns + other_columns), BF16)
+    ordered = 0 if order is None else order.shape[0]
     return pl.pallas_call(
-        partial(pair_grad_kernel, each, cuts, len(left), len(other_left)),
+        partial(pair_grad_kernel, each, len(left), len(other_left), ordered),
         grid=(each + other_each,),
-        out_shape=outs,
-        in_specs=whole_specs(left)
+        out_shape=out,
+        in_specs=[pl.BlockSpec(memory_space=pltpu.SMEM)] * (1 if ordered else 0)
+        + whole_specs(left)
         + [pl.BlockSpec((rows, block), lambda step: (0, start + jnp.clip(step, 0, each - 1)))]
         + whole_specs(other_left)
         + [
@@ -432,12 +454,12 @@
                 (rows, block), lambda step: (0, start + jnp.clip(step - each, 0, other_each - 1))
             )
         ],
-        out_specs=out_specs,
+        out_specs=pl.BlockSpec((width, block), lambda step: (0, step)),
         scratch_shapes=[pltpu.VMEM((rows, width), BF16)],
         compiler_params=PARAMS,
-        cost_estimate=cost(2 * rows * width * (columns + other_columns), *left, right, *other_left, *outs),
+        cost_estimate=cost(2 * rows * width * (columns + other_columns), *left, right, *other_left, out),
         name="pair_grad",
-    )(*left, right, *other_left, other_right)
+    )(*((order,) if ordered else ()), *left, right, *other_left, other_right)
 
 
 def masked_scores(queries, keyset, marks, mark_row):
@@ -830,8 +852,17 @@
         return held if len(values) > 1 else held[0]
 
     owners, segment_ids, cotangent = behind(owners, segment_ids, cotangent)
-    early_far = early_far_raw = send(early_shard, plan.swap_z(half))
-    early_found = gather_hops(plan, early_shard)
+    early_far = send(early_shard, plan.swap_z(half))
+    small_here = jnp.concatenate(by_core(small_here, send(small_here, plan.swap_core)), axis=1)
+
+    def fold_small(values):
+        extra = jnp.pad(values[16:], ((0, 16 - (small_rows - 16)), (0, lanes - 2 * values.shape[1])))
+        return jnp.concatenate([values[:16], extra], axis=1)
+
+    def unfold_small(values, count):
+        return jnp.concatenate([values[:, :count], values[: small_rows - 16, count : 2 * count]], axis=0)
+
+    early_found = gather_hops(plan, jnp.concatenate([early_shard, fold_small(small_here)], axis=0))
 
     slots = jnp.arange(n_dp, dtype=jnp.int32)
 
@@ -850,45 +881,13 @@
         return jnp.where(moved, send(rows, plan.swap_rows), rows)
 
     late_own = pack(1, behind)
-    rows = trade_rows(after(reorder_blocks(frames, to_here), early_far))
-
-    def fold_small(values):
-        extra = jnp.pad(values[16:], ((0, 16 - (small_rows - 16)), (0, lanes - 2 * values.shape[1])))
-        return jnp.concatenate([values[:16], extra], axis=1)
-
-    def unfold_small(values, count):
-        return jnp.concatenate([values[:, :count], values[: small_rows - 16, count : 2 * count]], axis=0)
-
-    early_ends = gather_end(plan, early_found, early_far)
-    small_here = jnp.concatenate(by_core(small_here, send(small_here, plan.swap_core)), axis=1)
-    early_far = jnp.concatenate([early_far, fold_small(small_here)], axis=0)
-    far_found = gather_hops(plan, early_far)
-    far_ends = gather_end(plan, far_found, rows)
-    early_near, _ = gathered(early_found, early_ends)
-    early_far, small_parts = gathered(far_found, far_ends, piece_rows)
-    early = [early_near, early_far]
+    rows = reorder_blocks(frames, to_here)
+    rows, late_own, *early_found[1:] = together(rows, late_own, *early_found[1:])
 
     entry, exit_ = behind(inner_weight, output_weight)
-    mine = jnp.concatenate(
+    attend_own = jnp.concatenate(
         [entry[at].astype(BF16) for at in range(3)] + [exit_[0].astype(BF16).T], axis=1
     )
-    other = send(after(mine, far_found[-1]), plan.swap_z(half))
-    low, up = jnp.where(on_low, mine, other), jnp.where(on_low, other, mine)
-    attend_shard = over_cores(*by_core(low, up))
-
-    z_steps = plan.z_order(bits)
-
-    def side_by_side(pieces, count):
-        columns = pieces[0].shape[1] // count
-        return jnp.concatenate(
-            [piece[:, at * columns : (at + 1) * columns] for at in range(count) for piece in pieces],
-            axis=1,
-        )
-
-    same_core = [[2 * at + core_at for at in range(plan.chips)] for core_at in (0, 1)]
-    late_own = after(late_own, early_far_raw)
-    late_beside = lax.all_gather(late_own, "mp", axis=0, tiled=False)
-    late = lax.all_gather(late_beside, "dp", axis=0, tiled=False, axis_index_groups=same_core)
 
     pairs = [halves(entry[at].astype(BF16)) for at in (3, 4)]
     pairs.append(halves(exit_[1].astype(BF16).T))
@@ -896,25 +895,18 @@
         jnp.concatenate([keep for keep, _ in pairs], axis=1),
         jnp.concatenate([give for _, give in pairs], axis=1),
     )
-
+    hidden_turn, inner_turn = [part.astype(BF16) for part in behind(rot_hidden, rot_inner)]
+    attend_own, conv_shard, rows, early_far, hidden_turn, inner_turn = together(
+        attend_own, conv_shard, rows, early_far, hidden_turn, inner_turn
+    )
+    swapped = send(rows, plan.swap_rows)
+
+    early_ends = gather_end(plan, early_found, early_far)
+    far_found = gather_hops(plan, early_far)
+    swapped, *early_ends = together(swapped, *early_ends)
+    rows = jnp.where(moved, swapped, rows)
     other_segments = send(segment_ids, plan.swap_core)
     segments = jnp.where(moved, other_segments, segment_ids)
-
-    count = 2 * row_lanes
-    small = jnp.concatenate([unfold_small(part, count) for part in small_parts], axis=1).astype(F32)
-    gain_order = jnp.sum(jnp.where(here[None, :] == to_here[:, None], slots[None, :], 0), axis=1)
-    small = jnp.pad(small, ((0, 24 - small_rows), (0, 0)))
-    gains = reorder_blocks(small, gain_order)
-    depth_small = reorder_blocks(small, here_back)
-    z_order = jnp.asarray(plan.z_order(bits), jnp.int32)
-    place_z = [0] * n_mp
-    for at, value in enumerate(plan.z_order(bits)):
-        place_z[value] = at
-    z_blocks = jnp.bitwise_xor(z, z_order)
-    z_places = jnp.asarray(place_z, jnp.int32)[jnp.bitwise_xor(z, jnp.arange(n_mp, dtype=jnp.int32))]
-    by_block = depth_small[10:small_rows].reshape(KERNEL + 2, n_mp, 2, inner // 2)
-    depthwise = jnp.take(jnp.where(on_zero, by_block[:, :, 0], by_block[:, :, 1]), z_blocks, axis=1)
-    depthwise = depthwise.reshape(KERNEL + 2, -1)
 
     def both_cores(own):
         return [own, send(own, plan.swap_core)]
@@ -933,13 +925,15 @@
 
     def row_scatter(near, away, work=lambda hold: []):
         total = near + send(away, plan.swap_core).astype(F32)
-        done = work(lambda value: after(value, total))
-        for at, bit in enumerate(near_bits[::-1]):
+        done = None
+        for bit in near_bits[::-1]:
             cut = total.shape[0] // 2
-            got = send(total[cut:].astype(BF16), plan.swap_z(bit))
-            if at == 0:
+            own, outgoing = total[:cut], total[cut:].astype(BF16)
+            if done is None:
+                done = work(lambda value: after(value, outgoing))
+            got = send(outgoing, plan.swap_z(bit))
+            if done:
                 got, *done = together(got, *done)
-            own = total[:cut]
             total = own + got.astype(F32)
         return own, got, done
 
@@ -1035,22 +1029,6 @@
         )
         return total, grad_content, grad_opening, activated, depth_rows
 
-    def undouble(total, count):
-        columns = total.shape[1] // count // n_mp
-        pieces = [
-            jnp.concatenate(
-                [
-                    total[:, (group * n_mp + at) * columns : (group * n_mp + at + 1) * columns]
-                    for group in range(count)
-                ],
-                axis=1,
-            )
-            for at in range(n_mp)
-        ]
-        return [pieces[0]] + [
-            send(piece, plan.swap_z(step)) for piece, step in zip(pieces[1:], z_steps[1:])
-        ]
-
     def sum_of(pieces):
         return sum(piece.astype(F32) for piece in pieces).astype(BF16)
 
@@ -1066,122 +1044,183 @@
             ]
         )
 
-    ring_cuts = [piece_rows] * (plan.chips - 1)
-    half_cuts = ring_cuts + [share, share]
-
-    def ring_pieces(parts):
-        return list(parts[:-2]) + [(parts[-2], parts[-1])]
-
-    early_full = norm_of(row_gather(rows)[0], gains, 0)
-    attend_found = gather_hops(plan, after(attend_shard, early_full))
-    early_preact, near, away = expand_shrink(early_full, early)
+    same_core = [[2 * at + core_at for at in range(plan.chips)] for core_at in (0, 1)]
+
+    def chips_gather(shard):
+        return lax.all_gather(shard, "dp", axis=0, tiled=True, axis_index_groups=same_core)
+
+    def chips_scatter(grads):
+        return lax.psum_scatter(
+            grads, "dp", scatter_dimension=0, tiled=True, axis_index_groups=same_core
+        )
+
+    row_parts, far_found[1:] = row_gather(rows, lambda: far_found[1:])
+    far_ends = gather_end(plan, far_found)
+    other = send(after(attend_own, row_parts[1]), plan.swap_z(half))
+    other, *far_ends = together(other, *far_ends)
+    early_near, small_parts = gathered(early_found, early_ends, piece_rows)
+    early_far, _ = gathered(far_found, far_ends)
+    early = [(early_near, 0, lanes), (early_far, 0, lanes)]
+
+    low, up = jnp.where(on_low, attend_own, other), jnp.where(on_low, other, attend_own)
+    attend_shard = over_cores(*by_core(low, up))
+
+    z_steps = plan.z_order(bits)
+
+    count = 2 * row_lanes
+    small = jnp.concatenate([unfold_small(part, count) for part in small_parts], axis=1).astype(F32)
+    gain_order = jnp.sum(jnp.where(here[None, :] == to_here[:, None], slots[None, :], 0), axis=1)
+    small = jnp.pad(small, ((0, 24 - small_rows), (0, 0)))
+    gains = reorder_blocks(small, gain_order)
+    depth_small = reorder_blocks(small, here_back)
+    z_order = jnp.asarray(plan.z_order(bits), jnp.int32)
+    place_z = [0] * n_mp
+    for at, value in enumerate(plan.z_order(bits)):
+        place_z[value] = at
+    z_blocks = jnp.bitwise_xor(z, z_order)
+    z_places = jnp.asarray(place_z, jnp.int32)[jnp.bitwise_xor(z, jnp.arange(n_mp, dtype=jnp.int32))]
+    by_block = depth_small[10:small_rows].reshape(KERNEL + 2, n_mp, 2, inner // 2)
+    depthwise = jnp.take(jnp.where(on_zero, by_block[:, :, 0], by_block[:, :, 1]), z_blocks, axis=1)
+    depthwise = depthwise.reshape(KERNEL + 2, -1)
+
+    conv_shard = after(conv_shard, row_parts[1])
+    conv_parts = [conv_shard] + [send(conv_shard, plan.swap_z(step)) for step in z_steps[1:]]
+    early_full = norm_of(row_parts, gains, 0)
+    early_full, attend_shard = together(early_full, attend_shard)
+    narrow = chips_gather(attend_shard)
+    late_gains = reorder_blocks(gains, here_back)
+    early_preact, near, away = expand_shrink([early_full], early)
+    near, *conv_parts[1:] = together(near, *conv_parts[1:])
+    conv = chips_gather(side_by_side(conv_parts, 3))
+    late_far = send(after(late_own, near), plan.swap_z(half))
     own, got, _ = row_scatter(near, away)
     early_stream = rows.astype(F32)
-    attend_stream, normed = add_norm(early_stream, own, got, 0.5, gains, 2)
-    normed, *attend_found = together(normed, *attend_found)
-    attend_ends = gather_end(plan, attend_found)
-    attend_full, _ = row_gather(normed)
-    narrow, _ = gathered(attend_found, attend_ends)
-    conv_shard = after(conv_shard, attend_full[1])
-    conv_shard = side_by_side(
-        [conv_shard] + [send(conv_shard, plan.swap_z(step)) for step in z_steps[1:]], 3
-    )
-    upstream = trade_rows(after(reorder_blocks(cotangent, holds), attend_full[1]))
+    attend_stream, normed = add_norm(early_stream, own, got, 0.5, late_gains, 2, here_back)
+    attend_full, (late_far,) = row_gather(normed, lambda: [late_far])
+    late = chips_gather(jnp.concatenate([late_own, late_far], axis=1))
+    late = [(late, 0, lanes), (late, lanes, lanes)]
     (attend_narrow, mixture, log_total, near, away), marks = attention_step(
         attend_full, narrow, mixed_segments
     )
-    near, away, conv_shard = together(near, away, conv_shard)
-    conv_found = gather_hops(plan, conv_shard)
     own, got, _ = row_scatter(near, away)
-    got, upstream, *conv_found = together(got, upstream, *conv_found)
-    conv_ends = gather_end(plan, conv_found)
-    conv_stream, normed = add_norm(attend_stream, own, got, 1.0, gains, 4)
+    conv_stream, normed = add_norm(attend_stream, own, got, 1.0, late_gains, 4)
     conv_full, around, _ = with_halo(normed, reach)
-    conv, _ = gathered(conv_found, conv_ends)
+    upstream = trade_rows(after(reorder_blocks(cotangent, holds), around))
     (own, got), conv_state = convolve(conv_full, around)
-    late_gains = reorder_blocks(gains, here_back)
-    late_stream, normed = add_norm(conv_stream, own, got, 1.0, late_gains, 6, here_back)
-    late_full = jnp.concatenate(both_cores(normed), axis=0)
-    late_preact, near, away = expand_shrink(late_full, [late])
-    final_stream, result = add_norm(
-        late_stream, near, send(away, plan.swap_core), 0.5, late_gains, 8
-    )
+    got, upstream = together(got, upstream)
+    late_stream, normed = add_norm(conv_stream, own, got, 1.0, late_gains, 6)
+    late_full, _ = row_gather(normed)
+    late_preact, near, away = expand_shrink(late_full, late)
+    own, got, _ = row_scatter(near, away)
+    final_stream, result = add_norm(late_stream, own, got, 0.5, late_gains, 8)
 
     gradient, sent, final_rows = norm_back(None, upstream, None, final_stream, late_gains, 8, 0.5)
-    incoming_late = both_cores(sent)
-    back_late, kept_late, near, away = expand_shrink_back(incoming_late, late_preact, [late])
-    gradient, sent, late_rows = norm_back(
-        gradient, near, send(away, plan.swap_core), late_stream, late_gains, 6, 1.0, here
-    )
-
-    def late_work():
-        return pair_grad(
-            [late_full], back_late, incoming_late, kept_late, [width], blocked=late.shape
-        )
-
-    incoming_conv, around, (late_grads,) = with_halo(sent, radius, late_work)
-    late_sum = lax.psum_scatter(
-        late_grads, "dp", scatter_dimension=0, tiled=False, axis_index_groups=same_core
-    )
-    total, grad_content, grad_opening, activated, depth_rows = convolve_back(
+    incoming_late, _ = row_gather(sent)
+    back_late, kept_late, near, away = expand_shrink_back(incoming_late, late_preact, late)
+
+    def late_work(hold):
+        return [pair_grad(late_full, hold(back_late), incoming_late, kept_late)]
+
+    own, got, (late_grads,) = row_scatter(near, away, late_work)
+    late_sum = chips_scatter(late_grads)
+    gradient, sent, late_rows = norm_back(gradient, own, got, late_stream, late_gains, 6, 1.0)
+    incoming_conv, around, _ = with_halo(sent, radius)
+    block_output = trade_rows(after(reorder_blocks(result, owners), around))
+    total, grad_content, grad_opening, activated, tap_rows = convolve_back(
         incoming_conv, around, conv_state
     )
-    gradient, sent, conv_rows = norm_back(
-        gradient, *fold_chunks(total), conv_stream, gains, 4, 1.0
-    )
+    own, got = fold_chunks(total)
+    got, block_output = together(got, block_output)
+    gradient, sent, conv_rows = norm_back(gradient, own, got, conv_stream, late_gains, 4, 1.0)
 
     def conv_work():
         columns = jnp.concatenate([grad_content, grad_opening], axis=1)
-        return pair_grad([conv_full], columns, [incoming_conv], activated, half_cuts)
-
-    incoming_attend, conv_pieces = row_gather(sent, conv_work)
-    conv_pieces = ring_pieces(conv_pieces)
-    conv_moving = scatter_start(plan, conv_pieces, incoming_attend[1])
-    block_output = trade_rows(after(reorder_blocks(result, owners), incoming_attend[1]))
+        return [pair_grad([conv_full], columns, [incoming_conv], activated)]
+
+    incoming_attend, (conv_grads,) = row_gather(sent, conv_work)
+    conv_sum = chips_scatter(conv_grads)
+    incoming_attend[1], late_sum = together(incoming_attend[1], late_sum)
+    middle = lanes // 2
+    late_sum, late_away = [
+        jnp.concatenate([late_sum[:, at : at + middle], late_sum[:, lanes + at : lanes + at + middle]], axis=1)
+        for at in (0, middle)
+    ]
+    late_away = send(late_away, plan.swap_z(half))
     back_attend, near, away = attention_back_step(
         incoming_attend, narrow, marks, attend_narrow, log_total
     )
-    away, *conv_moving = together(away, *conv_moving)
-    conv_moving = scatter_end(plan, conv_pieces, *conv_moving)
+    near, away, late_away = together(near, away, late_away)
 
     def attend_work(hold):
-        return pair_grad(attend_full, hold(back_attend), incoming_attend, mixture, half_cuts)
-
-    own, got, attend_pieces = row_scatter(near, away, attend_work)
-    gradient, sent, attend_rows = norm_back(gradient, own, got, attend_stream, gains, 2, 0.5)
-    attend_pieces = ring_pieces(attend_pieces)
-    sent, *conv_moving = together(sent, *conv_moving)
-    attend_moving = scatter_start(plan, attend_pieces)
-    conv_sum = scatter_sum(conv_pieces, *conv_moving)
-    incoming_early, _ = row_gather(sent)
-    incoming_early[1], late_sum, conv_sum, *attend_moving = together(
-        incoming_early[1], late_sum, conv_sum, *attend_moving
-    )
-    attend_moving = scatter_end(plan, attend_pieces, *attend_moving)
-    late_sum = lax.psum_scatter(late_sum, "mp", scatter_dimension=0, tiled=False)
-    conv_sum = undouble(conv_sum, 3)
+        return [pair_grad(attend_full, hold(back_attend), incoming_attend, mixture)]
+
+    own, got, (attend_grads,) = row_scatter(near, away, attend_work)
+    got, conv_sum = together(got, conv_sum)
+    conv_sum = apart(conv_sum, 3, n_mp)
+    conv_sum = [conv_sum[0]] + [
+        send(piece, plan.swap_z(step)) for piece, step in zip(conv_sum[1:], z_steps[1:])
+    ]
+    attend_sum = chips_scatter(attend_grads)
+    gradient, sent, attend_rows = norm_back(
+        gradient, own, got, attend_stream, late_gains, 2, 0.5, here
+    )
+
+    def small_work():
+        owned = jnp.sum(jnp.where(here[:, None] == slots[None, :], owners[None, :], 0), axis=1)
+        norm_rows = jnp.concatenate([attend_rows[:2], conv_rows[:2], late_rows[:2], final_rows[:2]], axis=0)
+        norm_rows = reorder_blocks(norm_rows, owned)
+        depth_rows = jnp.stack(tap_rows).reshape(KERNEL + 2, n_mp, 1, inner // 2)
+        depth_rows = jnp.take(depth_rows, z_places, axis=1)
+        empty = jnp.zeros_like(depth_rows)
+        depth_rows = jnp.concatenate(
+            [jnp.where(on_zero, depth_rows, empty), jnp.where(on_zero, empty, depth_rows)], axis=2
+        )
+        depth_rows = jnp.pad(depth_rows.reshape(KERNEL + 2, width), ((0, 1), (0, 0)))
+        depth_rows = reorder_blocks(depth_rows, here)[: KERNEL + 2]
+        return [conv_sum, norm_rows, depth_rows]
+
+    incoming_early, (conv_sum, norm_rows, depth_rows) = row_gather(sent, small_work)
     back_early, kept_early, near, away = expand_shrink_back(incoming_early, early_preact, early)
 
-    def early_grad(left, right, cuts, first):
+    def early_grad(left, right, first):
         return pair_grad(
-            [early_full], left, incoming_early, right, cuts, columns=hidden // 2, first=first * hidden // 2
+            [early_full],
+            left,
+            incoming_early,
+            right,
+            columns=hidden // 2,
+            first=first * hidden // 2,
+            order=here[0::2] // 2,
         )
 
-    far_pieces = ring_pieces(early_grad(back_early, kept_early, half_cuts, 1))
-    far_moving = scatter_start(plan, far_pieces)
-
-    def early_work(hold):
-        grads = early_grad(hold(back_early), kept_early, half_cuts, 0)
-        return [*grads, *attend_moving]
-
-    own, got, done = row_scatter(near, away, early_work)
-    near_pieces, attend_moving = ring_pieces(done[:-2]), done[-2:]
-    far_moving = scatter_end(plan, far_pieces, *far_moving)
-    near_moving = list(scatter_start(plan, near_pieces))
-    attend_sum = scatter_sum(attend_pieces, *attend_moving)
+    got, back_early, far_grads, attend_sum = together(
+        send(away, plan.swap_core), back_early, early_grad(back_early, kept_early, 1), attend_sum
+    )
+    low, up = back_to_cores(attend_sum)
+    attend_own, away = jnp.where(on_low, low, up), jnp.where(on_low, up, low)
+    attend_away = send(away, plan.swap_z(half))
+    far_sum = chips_scatter(far_grads)
+    total = near + got.astype(F32)
+    cut = total.shape[0] // 2
+    own, outgoing = total[:cut], total[cut:].astype(BF16)
+    got, near_grads = together(
+        send(outgoing, plan.swap_z(near_bits[-1])),
+        early_grad(after(back_early, outgoing), kept_early, 0),
+    )
+    near_sum = chips_scatter(near_grads)
+    for bit in near_bits[:-1][::-1]:
+        total = own + got.astype(F32)
+        cut //= 2
+        own, got = total[:cut], send(total[cut:].astype(BF16), plan.swap_z(bit))
     _, sent, early_rows = norm_back(gradient, own, got, early_stream, gains, 0, 1.0)
-
-    hidden_turn, inner_turn = rot_hidden.astype(BF16), rot_inner.astype(BF16)
+    sent, early_rows, far_sum, attend_away, late_sum, late_away, conv_sum = together(
+        sent, early_rows, far_sum, attend_away, late_sum, late_away, conv_sum
+    )
+    far_sum = send(far_sum, plan.swap_z(half))
+    attend_sum = attend_own.astype(F32) + attend_away.astype(F32)
+    attend_sum = jnp.stack([attend_sum[:, at * inner : (at + 1) * inner] for at in range(4)])
+    late_sum = unpack(late_sum + late_away, 2)
+
     expand_states = (expand_weight, expand_first, expand_second, expand_average)
     shrink_states = (shrink_weight, shrink_first, shrink_second, shrink_average)
     inner_states = (inner_weight, inner_first, inner_second, inner_average)
@@ -1193,37 +1232,17 @@
     def narrow_step(totals, slot, states, rate, turn, partly=()):
         return rotated_adam(totals, rot_model, inner_turn, states, rate, turn, slot, partly)
 
-    far_sum = send(scatter_sum(far_pieces, *far_moving), plan.swap_z(half))
-    near_moving[0], attend_sum, late_sum, *conv_sum = together(
-        near_moving[0], attend_sum, late_sum, *conv_sum
-    )
-    late_sum, conv_sum = unpack(late_sum, 2), unpack(sum_of(conv_sum), 3)
-    low, up = back_to_cores(attend_sum)
-    own, away = jnp.where(on_low, low, up), jnp.where(on_low, up, low)
-    attend_sum = own.astype(F32) + send(away, plan.swap_z(half)).astype(F32)
-    attend_sum = jnp.stack([attend_sum[:, at * inner : (at + 1) * inner] for at in range(4)])
-
-    def late_adam():
-        new_expand = wide(late_sum[0], 1, expand_states, RATE_EXPAND, False)
-        new_shrink = wide(late_sum[1], 1, shrink_states, RATE_SHRINK, True)
-        new_inner = narrow_step(conv_sum[:2], 3, inner_states, RATE_INNER, False)
-        new_output = narrow_step(conv_sum[2:], 1, output_states, RATE_OUTPUT, True)
-        new_inner = narrow_step(attend_sum[:3], 0, inner_states, RATE_INNER, False, new_inner)
-        new_output = narrow_step(attend_sum[3:], 0, output_states, RATE_OUTPUT, True, new_output)
-        return new_expand, new_shrink, new_inner, new_output
+    new_expand = wide(late_sum[0], 1, expand_states, RATE_EXPAND, False)
+    new_shrink = wide(late_sum[1], 1, shrink_states, RATE_SHRINK, True)
+    sent, early_rows, new_expand, new_shrink = together(sent, early_rows, new_expand, new_shrink)
+    conv_sum = unpack(sum_of(conv_sum), 3)
+    new_inner = narrow_step(conv_sum[:2], 3, inner_states, RATE_INNER, False)
+    new_output = narrow_step(conv_sum[2:], 1, output_states, RATE_OUTPUT, True)
+    new_inner = narrow_step(attend_sum[:3], 0, inner_states, RATE_INNER, False, new_inner)
+    new_output = narrow_step(attend_sum[3:], 0, output_states, RATE_OUTPUT, True, new_output)
+    far_sum, new_inner, new_output = together(far_sum, new_inner, new_output)
 
     home = jnp.sum(jnp.where(here[:, None] == slots[None, :], from_here[None, :], 0), axis=1)
-    late_norms = reorder_blocks(jnp.concatenate([late_rows[:2], final_rows[:6]], axis=0), here)[:4]
-    norm_rows = jnp.concatenate([attend_rows[:2], conv_rows[:2], late_norms], axis=0)
-    norm_rows = reorder_blocks(norm_rows, home)
-    depth_rows = jnp.stack(depth_rows).reshape(KERNEL + 2, n_mp, 1, inner // 2)
-    depth_rows = jnp.take(depth_rows, z_places, axis=1)
-    empty = jnp.zeros_like(depth_rows)
-    depth_rows = jnp.concatenate(
-        [jnp.where(on_zero, depth_rows, empty), jnp.where(on_zero, empty, depth_rows)], axis=2
-    )
-    depth_rows = jnp.pad(depth_rows.reshape(KERNEL + 2, width), ((0, 1), (0, 0)))
-    depth_rows = reorder_blocks(depth_rows, here)[: KERNEL + 2]
     early_rows = reorder_blocks(early_rows, home)[:2]
     small_grad = jnp.concatenate([early_rows, norm_rows, depth_rows], axis=0)
     small_pieces = [small_grad[:, at * count : (at + 1) * count] for at in range(plan.chips)]
@@ -1233,10 +1252,6 @@
             send(small_pieces[2 * hop] + small_moving[0], plan.to_next),
             send(small_pieces[2 * hop - 1] + small_moving[1], plan.to_last),
         ]
-
-    ahead, behind_, *small_moving = together(*near_moving, *small_moving)
-    near_moving = scatter_end(plan, near_pieces, ahead, behind_)
-    new_expand, new_shrink, new_inner, new_output = late_adam()
     small_grad = small_pieces[0] + small_moving[0] + small_moving[1]
     keep, give = by_core(small_grad[:, :row_lanes], small_grad[:, row_lanes:])
     small_grad = keep + send(give, plan.swap_core)
@@ -1247,14 +1262,18 @@
     new_small = (first_new, second_new, weight_new, average_new)
     input_grad = trade_rows(reorder_blocks(sent, from_here))[None]
 
-    far_sum, *_ = together(
-        far_sum, new_expand[0], new_shrink[0], new_inner[0], new_output[0], weight_new, input_grad
-    )
-    near_sum = scatter_sum(near_pieces, *near_moving)
+    near_sum, new_small, input_grad = together(near_sum, new_small, input_grad)
     early_sum = unpack(near_sum + far_sum, 2)
     new_expand = wide(early_sum[0], 0, expand_states, RATE_EXPAND, False, new_expand)
     new_shrink = wide(early_sum[1], 0, shrink_states, RATE_SHRINK, True, new_shrink)
-    return (block_output[None], input_grad) + new_inner + new_expand + new_output + new_shrink + new_small
+    return (
+        (block_output[None], input_grad)
+        + tuple(new_inner)
+        + tuple(new_expand)
+        + tuple(new_output)
+        + tuple(new_shrink)
+        + tuple(new_small)
+    )
 
 
 def solution(mesh):

time: 681 us -> 656 us (0.963)
  starting transfers between devices: 111 us -> 71.7 us
    ppermute x100 -> x84, starting transfers between devices: 111 us -> 70.8 us  [send(): return lax.ppermute(value, AXES, pairs)]
    slice x14 -> x18, local copies, waits for them, and re-layouts: 9.73 us -> 21.1 us  [the longest x10 12.7 us: row_scatter(): own, outgoing = (total[:cut], total[cut:].astype(BF16))]
    pallas_call x7 -> x9, Pallas kernels: 58.5 us -> 61.8 us  [the longest x5 36.3 us: pair_grad(): pl.pallas_call(partial(pair_grad_kernel, each, len(left), len(other_left)...]
    unnamed x298 -> x194, local copies, waits for them, and re-layouts: 34.6 us -> 31.6 us
    ppermute x100 -> x84, waiting for transfers between devices: 190 us -> 188 us  [send(): return lax.ppermute(value, AXES, pairs)]
    pallas_call x11 -> x10, Pallas kernels: 18.2 us -> 16.8 us  [reorder_blocks(): pl.pallas_call(partial(reorder_kernel, blocks), out_shape=jax.ShapeDtypeS...]
  transfers between devices with their start and end apart: 104 -> 92, of which waited for: 34 -> 40; matrix products, arithmetic and copies ran while one was open for 22% -> 21% of each run, Pallas kernels for 20% -> 23%
where the time goes in v3:
time: 656 us; the launch traced here: 643 us
  waiting for transfers between devices  193 us (29%)
  Pallas kernels  192 us (29%)
  local copies, waits for them, and re-layouts  81.6 us (12%)
  other arithmetic  78.1 us (12%)
  starting transfers between devices  71.7 us (11%)
  between operations  16.3 us (2%)
  matrix products  10.4 us (2%)
    ppermute x84, waiting for transfers between devices, send(): return lax.ppermute(value, AXES, pairs)  188 us
    ppermute x84, starting transfers between devices, send(): return lax.ppermute(value, AXES, pairs)  70.8 us
    pallas_call x5, Pallas kernels, pair_grad(): pl.pallas_call(partial(pair_grad_kernel, each, len(left), len(other_left)...  36.3 us
    pallas_call x3, Pallas kernels, in_place(): pl.pallas_call(kernel, out_shape=outs, in_specs=[pl.BlockSpec(memory_spac...  31.8 us
    unnamed x194, local copies, waits for them, and re-layouts  31.6 us
    pallas_call x8, Pallas kernels, rotated_adam(): pl.pallas_call(partial(adam_kernel, turn, rate), grid=(count,), out_shape...  26 us
    pallas_call x2, Pallas kernels, expand_shrink_back(): pl.pallas_call(partial(expand_shrink_back_kernel, len(weights), each, len...  23.8 us
    pallas_call x2, Pallas kernels, expand_shrink(): pl.pallas_call(partial(expand_shrink_kernel, len(weights), each, len(full...  21.1 us
  transfers between devices with their start and end apart: 92, of which 40 were waited for; matrix products, arithmetic and copies ran while one was open for 21% of the time, Pallas kernels for 23%

profile of v3, /device:TPU:0, one launch (start us, length us, event | category | flops | bytes accessed | tf_op | source)
XLA Modules:
  0.0 643.3 jit_solution(8353964319000916544)
XLA Ops:
  8.1 4.1 collective-permute-start.2
  34.3 3.8 convert_element_type.189.right
  56.4 5.8 collective-permute-done.12
  63.7 2.3 fusion.95
  66.0 6.7 %collective-permute-done.15 = bf16[256,1024]{1,0:T(8,128)(2,1)} collective-permute-done((bf16[256,1024]{1,0:T(8,128)(2,1)}, bf16[256,1024]{1,0:T(8,128)(2,1)}, u32[]{:S(2)}, u32[]{:S(2)}) %collective-permute-start.15) | collective-permute-done | bytes 524320 | tf_op jit(solution)/shard_map/ppermute | solution.py:202
  73.9 6.8 %collective-permute-done.13.refs_1_ = bf16[256,1024]{1,0:T(8,128)(2,1)} collective-permute-done((bf16[256,1024]{1,0:T(8,128)(2,1)}, bf16[256,1024]{1,0:T(8,128)(2,1)}, u32[]{:S(2)}, u32[]{:S(2)}) %collective-permute-start.13) | collective-permute-done | bytes 524320 | tf_op jit(solution)/shard_map/ppermute | solution.py:202
  88.4 2.4 collective-permute-done.20
  92.0 6.6 %collective-permute-done.18 = bf16[128,1024]{1,0:T(8,128)(2,1)S(1)} collective-permute-done((bf16[128,1024]{1,0:T(8,128)(2,1)S(1)}, bf16[128,1024]{1,0:T(8,128)(2,1)S(1)}, u32[]{:S(2)}, u32[]{:S(2)}) %collective-permute-start.18) | collective-permute-done | bytes 262176 | tf_op jit(solution)/shard_map/ppermute | solution.py:202
  106.3 4.4 norm.1.refs_0_.refs_1_
  117.5 4.2 collective-permute-start.22
  125.4 10.6 %expand_shrink.2 = (f32[1024,1024]{1,0:T(8,128)}, f32[512,1024]{1,0:T(8,128)}, bf16[512,1024]{1,0:T(8,128)(2,1)}) custom-call(bf16[1024,1024]{1,0:T(8,128)(2,1)} %norm.1.refs_0_.refs_1_, bf16[1024,1024]{1,0:T(8,128)(2,1)} %copy-done.78, bf16[1024,1024]{1,0:T(8,128)(2,1)} %copy-done.78, bf16[1024,1024]{1,0:T(8,128)(2,1)} %copy-done.77, ...), custom_call_target="tpu_custom_call" | custom-call | flops 4294967296 | bytes 9437184 | tf_op jit(solution)/shard_map/expand_shrink/pallas_call | solution.py:346
  140.0 2.9 collective-permute-done.25
  150.9 2.3 slice.714.refs_2_
  153.2 15.7 %collective-permute-done.26.refs_3_ = bf16[256,1024]{1,0:T(8,128)(2,1)} collective-permute-done((bf16[256,1024]{1,0:T(8,128)(2,1)}, bf16[256,1024]{1,0:T(8,128)(2,1)}, u32[]{:S(2)}, u32[]{:S(2)}) %collective-permute-start.26) | collective-permute-done | bytes 524320 | tf_op jit(solution)/shard_map/ppermute | solution.py:202
  169.0 3.2 add_norm.4
  172.9 3.0 collective-permute-done.28
  175.9 11.1 %collective-permute-done.27.refs_1_ = bf16[256,1024]{1,0:T(8,128)(2,1)} collective-permute-done((bf16[256,1024]{1,0:T(8,128)(2,1)}, bf16[256,1024]{1,0:T(8,128)(2,1)}, u32[]{:S(2)}, u32[]{:S(2)}) %collective-permute-start.27) | collective-permute-done | bytes 524320 | tf_op jit(solution)/shard_map/ppermute | solution.py:202
  190.9 12.4 %attention.1 = (bf16[1024,768]{1,0:T(8,128)(2,1)}, bf16[1024,256]{1,0:T(8,128)(2,1)}, f32[1024,256]{1,0:T(8,128)}, f32[512,1024]{1,0:T(8,128)}, bf16[512,1024]{1,0:T(8,128)(2,1)}) custom-call(bf16[256,1024]{1,0:T(8,128)(2,1)} %get-tuple-element.247.refs_0_, bf16[256,1024]{1,0:T(8,128)(2,1)} %collective-permute-done.27.refs_1_, ...), custom_call_target="tpu_custom_call" | custom-call | flops 3221225472 | bytes 11042816 | tf_op jit(solution)/shard_map/attention/pallas_call | solution.py:253
  217.1 2.4 slice.716.refs_1_
  219.5 14.1 %collective-permute-done.33.refs_2_ = bf16[256,1024]{1,0:T(8,128)(2,1)} collective-permute-done((bf16[256,1024]{1,0:T(8,128)(2,1)}, bf16[256,1024]{1,0:T(8,128)(2,1)}, u32[]{:S(2)}, u32[]{:S(2)}) %collective-permute-start.33) | collective-permute-done | bytes 524320 | tf_op jit(solution)/shard_map/ppermute | solution.py:202
  233.6 3.0 add_norm.5
  240.6 3.9 collective-permute-done.35
  259.1 3.0 add_norm.6
  264.6 12.1 %collective-permute-done.40.refs_1_ = bf16[256,1024]{1,0:T(8,128)(2,1)S(1)} collective-permute-done((bf16[256,1024]{1,0:T(8,128)(2,1)}, bf16[256,1024]{1,0:T(8,128)(2,1)S(1)}, u32[]{:S(2)}, u32[]{:S(2)}) %collective-permute-start.40) | collective-permute-done | bytes 524320 | tf_op jit(solution)/shard_map/ppermute | solution.py:202
  279.6 10.6 %expand_shrink.3 = (f32[1024,1024]{1,0:T(8,128)}, f32[512,1024]{1,0:T(8,128)}, bf16[512,1024]{1,0:T(8,128)(2,1)}) custom-call(bf16[256,1024]{1,0:T(8,128)(2,1)} %get-tuple-element.265.refs_0_, bf16[256,1024]{1,0:T(8,128)(2,1)} %copy-done.60, bf16[256,1024]{1,0:T(8,128)(2,1)} %collective-permute-done.41.refs_2_, ...), custom_call_target="tpu_custom_call" | custom-call | flops 4294967296 | bytes 9437184 | tf_op jit(solution)/shard_map/expand_shrink/pallas_call | solution.py:346
  290.4 2.7 collective-permute-done.43
  297.7 11.5 %collective-permute-done.44.refs_2_ = bf16[256,1024]{1,0:T(8,128)(2,1)S(1)} collective-permute-done((bf16[256,1024]{1,0:T(8,128)(2,1)S(1)}, bf16[256,1024]{1,0:T(8,128)(2,1)S(1)}, u32[]{:S(2)}, u32[]{:S(2)}) %collective-permute-start.44) | collective-permute-done | bytes 524320 | tf_op jit(solution)/shard_map/ppermute | solution.py:202
  310.0 3.0 add_norm.7
  313.0 3.3 norm_back.5
  317.7 11.9 %collective-permute-done.45.refs_1_.refs_6_ = bf16[256,1024]{1,0:T(8,128)(2,1)S(1)} collective-permute-done((bf16[256,1024]{1,0:T(8,128)(2,1)}, bf16[256,1024]{1,0:T(8,128)(2,1)S(1)}, u32[]{:S(2)}, u32[]{:S(2)}) %collective-permute-start.45) | collective-permute-done | bytes 524320 | tf_op jit(solution)/shard_map/ppermute | solution.py:202
  332.4 12.0 %expand_shrink_back.2 = (bf16[1024,1024]{1,0:T(8,128)(2,1)}, bf16[1024,1024]{1,0:T(8,128)(2,1)}, f32[512,1024]{1,0:T(8,128)}, bf16[512,1024]{1,0:T(8,128)(2,1)}) custom-call(bf16[256,1024]{1,0:T(8,128)(2,1)} %get-tuple-element.271.refs_0_.refs_5_, bf16[256,1024]{1,0:T(8,128)(2,1)} %copy-done.61, bf16[256,1024]{1,0:T(8,128)(2,1)} %copy-done.62, ...), custom_call_target="tpu_custom_call" | custom-call | flops 4294967296 | bytes 13631488 | tf_op jit(solution)/shard_map/expand_shrink_back/pallas_call | solution.py:395
  344.6 2.8 collective-permute-done.48
  353.0 9.5 %pair_grad.5 = bf16[1024,2048]{1,0:T(8,128)(2,1)} custom-call(bf16[256,1024]{1,0:T(8,128)(2,1)} %get-tuple-element.265.refs_0_, bf16[256,1024]{1,0:T(8,128)(2,1)} %copy-done.60, bf16[256,1024]{1,0:T(8,128)(2,1)} %collective-permute-done.41.refs_2_, bf16[256,1024]{1,0:T(8,128)(2,1)} %collective-permute-done.42.refs_3_, ...), custom_call_target="tpu_custom_call" | custom-call | flops 4294967296 | bytes 10485760 | tf_op jit(solution)/shard_map/pair_grad/pallas_call | solution.py:444
  362.5 3.3 collective-permute-done.49.refs_2_
  365.9 2.3 slice.754.refs_1_
  368.2 4.0 norm_back.6
  372.9 3.3 collective-permute-start.50
  377.7 4.1 collective-permute-done.51
  402.5 4.2 norm_back.7
  409.9 5.5 pair_grad.6
  415.5 5.4 collective-permute-done.56.refs_1_.refs_6_
  424.4 2.4 collective-permute-start.59
  426.8 15.0 %attention_back.1 = (bf16[1024,768]{1,0:T(8,128)(2,1)}, f32[512,1024]{1,0:T(8,128)}, bf16[512,1024]{1,0:T(8,128)(2,1)}) custom-call(bf16[256,1024]{1,0:T(8,128)(2,1)} %get-tuple-element.286.refs_0_.refs_5_, bf16[256,1024]{1,0:T(8,128)(2,1)} %collective-permute-done.56.refs_1_.refs_6_, bf16[256,1024]{1,0:T(8,128)(2,1)} %collective-permute-done.57.refs_2_.refs_7_, ...), custom_call_target="tpu_custom_call" | custom-call | flops 4831838208 | bytes 12091392 | tf_op jit(solution)/shard_map/attention_back/pallas_call | solution.py:253
  441.8 8.5 %collective-permute-done.59 = bf16[256,1024]{1,0:T(8,128)(2,1)S(1)} collective-permute-done((bf16[256,1024]{1,0:T(8,128)(2,1)S(1)}, bf16[256,1024]{1,0:T(8,128)(2,1)S(1)}, u32[]{:S(2)}, u32[]{:S(2)}) %collective-permute-start.59) | collective-permute-done | bytes 524320 | tf_op jit(solution)/shard_map/ppermute | solution.py:202
  450.4 2.8 collective-permute-done.60
  457.3 7.3 %pair_grad.7 = bf16[1024,1024]{1,0:T(8,128)(2,1)} custom-call(bf16[256,1024]{1,0:T(8,128)(2,1)} %get-tuple-element.247.refs_0_, bf16[256,1024]{1,0:T(8,128)(2,1)} %collective-permute-done.27.refs_1_, bf16[256,1024]{1,0:T(8,128)(2,1)} %collective-permute-done.29.refs_2_, bf16[256,1024]{1,0:T(8,128)(2,1)} %collective-permute-done.30.refs_3_, ...), custom_call_target="tpu_custom_call" | custom-call | flops 2147483648 | bytes 7864320 | tf_op jit(solution)/shard_map/pair_grad/pallas_call | solution.py:444
  464.6 6.9 %collective-permute-done.61.refs_3_ = bf16[256,1024]{1,0:T(8,128)(2,1)} collective-permute-done((bf16[256,1024]{1,0:T(8,128)(2,1)}, bf16[256,1024]{1,0:T(8,128)(2,1)}, u32[]{:S(2)}, u32[]{:S(2)}) %collective-permute-start.61) | collective-permute-done | bytes 524320 | tf_op jit(solution)/shard_map/ppermute | solution.py:202
  474.6 4.3 fusion.21
  480.0 4.3 norm_back.8
  488.4 3.0 collective-permute-start.63
  502.6 3.5 collective-permute-done.64
  506.1 5.7 collective-permute-done.65
  514.7 11.8 %expand_shrink_back.3 = (bf16[1024,1024]{1,0:T(8,128)(2,1)}, bf16[1024,1024]{1,0:T(8,128)(2,1)}, f32[512,1024]{1,0:T(8,128)}, bf16[512,1024]{1,0:T(8,128)(2,1)}) custom-call(bf16[256,1024]{1,0:T(8,128)(2,1)} %get-tuple-element.303.refs_0_.refs_3_, bf16[256,1024]{1,0:T(8,128)(2,1)} %collective-permute-done.62.refs_1_.refs_4_, ...), custom_call_target="tpu_custom_call" | custom-call | flops 4294967296 | bytes 13631488 | tf_op jit(solution)/shard_map/expand_shrink_back/pallas_call | solution.py:395
  527.4 6.7 %pair_grad.8 = bf16[1024,1024]{1,0:T(8,128)(2,1)} custom-call(s32[4]{0:T(128)} %and_select_fusion.refs_0_, bf16[1024,1024]{1,0:T(8,128)(2,1)} %norm.1.refs_0_.refs_1_, bf16[1024,1024]{1,0:T(8,128)(2,1)} %get-tuple-element.322.refs_2_, bf16[256,1024]{1,0:T(8,128)(2,1)} %get-tuple-element.303.refs_0_.refs_3_, ...), custom_call_target="tpu_custom_call" | custom-call | flops 2147483648 | bytes 8388608 | tf_op jit(solution)/shard_map/pair_grad/pallas_call | solution.py:444
  543.4 7.1 %pair_grad.9 = bf16[1024,1024]{1,0:T(8,128)(2,1)} custom-call(s32[4]{0:T(128)} %and_select_fusion.refs_0_, bf16[1024,1024]{1,0:T(8,128)(2,1)} %norm.1.refs_0_.refs_1_, bf16[1024,1024]{1,0:T(8,128)(2,1)} %get-tuple-element.322.refs_2_, bf16[256,1024]{1,0:T(8,128)(2,1)} %get-tuple-element.303.refs_0_.refs_3_, ...), custom_call_target="tpu_custom_call" | custom-call | flops 2147483648 | bytes 8388608 | tf_op jit(solution)/shard_map/pair_grad/pallas_call | solution.py:444
  550.6 8.2 %collective-permute-done.69.refs_2_ = bf16[256,1024]{1,0:T(8,128)(2,1)} collective-permute-done((bf16[256,1024]{1,0:T(8,128)(2,1)}, bf16[256,1024]{1,0:T(8,128)(2,1)}, u32[]{:S(2)}, u32[]{:S(2)}) %collective-permute-start.69) | collective-permute-done | bytes 524320 | tf_op jit(solution)/shard_map/ppermute | solution.py:202
  558.7 4.0 norm_back.9
  562.7 5.1 reduce-scatter.14.cloned.1.call-done
  571.4 2.4 collective-permute-start.81
  577.8 4.4 rotated_adam.8
  582.3 4.5 rotated_adam.9
  611.5 3.0 rotated_adam.11
  627.1 4.6 rotated_adam.15
  631.8 4.3 rotated_adam.14
  (569 shorter events, 250.9 us)
Async XLA Ops:
  7.2 182.1 %all-gather.4.cloned.1.call-start = ((), (), s32[]{:S(2)}) async-start(), calls=%async_computation.5 | async-start | bytes 2621440 | tf_op jit(solution)/shard_map/all_gather | solution.py:1050
  8.1 8.2 %collective-permute-start.2 = (bf16[17,128]{1,0:T(8,128)(2,1)S(1)}, bf16[17,128]{1,0:T(8,128)(2,1)S(1)}, u32[]{:S(2)}, u32[]{:S(2)}) collective-permute-start(bf16[17,128]{1,0:T(8,128)(2,1)S(1)} %broadcast_multiply_fusion.1), channel_id=1, source_target_pairs={{0,2},{1,3},{2,0},{3,1},{4,6},{5,7},{6,4},{7,5},{8,10},{9,11},{10,... | collective-permute-start | bytes 13064 | tf_op jit(solution)/shard_map/ppermute | solution.py:202
  21.0 26.4 %collective-permute-start.9 = (bf16[256,1024]{1,0:T(8,128)(2,1)}, bf16[256,1024]{1,0:T(8,128)(2,1)}, u32[]{:S(2)}, u32[]{:S(2)}) collective-permute-start(bf16[256,1024]{1,0:T(8,128)(2,1)} %pad_maximum_fusion.7), channel_id=1, source_target_pairs={{0,2},{1,3},{2,0},{3,1},{4,6},{5,7},{6,4},{7,5},{8,10},{9,11},{10,... | collective-permute-start | bytes 1572872 | tf_op jit(solution)/shard_map/ppermute | solution.py:202
  24.7 20.7 %collective-permute-start.8 = (bf16[272,1024]{1,0:T(8,128)(2,1)}, bf16[272,1024]{1,0:T(8,128)(2,1)}, u32[]{:S(2)}, u32[]{:S(2)}) collective-permute-start(bf16[272,1024]{1,0:T(8,128)(2,1)} %maximum_maximum_fusion), channel_id=1, source_target_pairs={{0,16},{1,17},{2,18},{3,19},{4,20},{5,21},{6,22},{7,23},{8,0},{9,1... | collective-permute-start | bytes 1671176 | tf_op jit(solution)/shard_map/ppermute | solution.py:202
  26.2 19.2 %collective-permute-start.7 = (bf16[272,1024]{1,0:T(8,128)(2,1)}, bf16[272,1024]{1,0:T(8,128)(2,1)}, u32[]{:S(2)}, u32[]{:S(2)}) collective-permute-start(bf16[272,1024]{1,0:T(8,128)(2,1)} %maximum_maximum_fusion), channel_id=1, source_target_pairs={{0,8},{1,9},{2,10},{3,11},{4,12},{5,13},{6,14},{7,15},{8,24},{9,25... | collective-permute-start | bytes 1671176 | tf_op jit(solution)/shard_map/ppermute | solution.py:202
  30.3 11.4 %collective-permute-start.4 = (bf16[128,384]{1,0:T(8,128)(2,1)}, bf16[128,384]{1,0:T(8,128)(2,1)}, u32[]{:S(2)}, u32[]{:S(2)}) collective-permute-start(bf16[128,384]{1,0:T(8,128)(2,1)} %pad_maximum_fusion.21), channel_id=1, source_target_pairs={{0,4},{1,5},{2,6},{3,7},{4,0},{5,1},{6,2},{7,3},{8,12},{9,13},{10,... | collective-permute-start | bytes 294920 | tf_op jit(solution)/shard_map/ppermute | solution.py:202
  33.7 9.8 %collective-permute-start.5 = (bf16[128,1024]{1,0:T(8,128)(2,1)}, bf16[128,1024]{1,0:T(8,128)(2,1)}, u32[]{:S(2)}, u32[]{:S(2)}) collective-permute-start(bf16[128,1024]{1,0:T(8,128)(2,1)} %pad_maximum_fusion.17), channel_id=1, source_target_pairs={{0,4},{1,5},{2,6},{3,7},{4,0},{5,1},{6,2},{7,3},{8,12},{9,13},{10,... | collective-permute-start | bytes 786440 | tf_op jit(solution)/shard_map/ppermute | solution.py:202
  47.5 16.2 %collective-permute-start.10 = (bf16[256,1024]{1,0:T(8,128)(2,1)}, bf16[256,1024]{1,0:T(8,128)(2,1)}, u32[]{:S(2)}, u32[]{:S(2)}) collective-permute-start(bf16[256,1024]{1,0:T(8,128)(2,1)} %reorder_blocks.10), channel_id=1, source_target_pairs={{2,4},{3,5},{4,2},{5,3},{10,12},{11,13},{12,10},{13,11},{18,20},{1... | collective-permute-start | bytes 1572872 | tf_op jit(solution)/shard_map/ppermute | solution.py:202
  52.3 9.8 %collective-permute-start.12 = (bf16[136,1024]{1,0:T(8,128)(2,1)}, bf16[136,1024]{1,0:T(8,128)(2,1)}, u32[]{:S(2)}, u32[]{:S(2)}) collective-permute-start(bf16[136,1024]{1,0:T(8,128)(2,1)} %slice.558), channel_id=1, source_target_pairs={{0,16},{1,17},{2,18},{3,19},{4,20},{5,21},{6,22},{7,23},{8,0},{9,1... | collective-permute-start | bytes 835592 | tf_op jit(solution)/shard_map/ppermute | solution.py:202
  53.9 9.8 %collective-permute-start.11 = (bf16[136,1024]{1,0:T(8,128)(2,1)}, bf16[136,1024]{1,0:T(8,128)(2,1)}, u32[]{:S(2)}, u32[]{:S(2)}) collective-permute-start(bf16[136,1024]{1,0:T(8,128)(2,1)} %slice.557), channel_id=1, source_target_pairs={{0,8},{1,9},{2,10},{3,11},{4,12},{5,13},{6,14},{7,15},{8,24},{9,25... | collective-permute-start | bytes 835592 | tf_op jit(solution)/shard_map/ppermute | solution.py:202
  54.4 18.3 %collective-permute-start.15 = (bf16[256,1024]{1,0:T(8,128)(2,1)}, bf16[256,1024]{1,0:T(8,128)(2,1)}, u32[]{:S(2)}, u32[]{:S(2)}) collective-permute-start(bf16[256,1024]{1,0:T(8,128)(2,1)} %collective-permute-done.9), channel_id=1, source_target_pairs={{0,16},{1,17},{2,18},{3,19},{4,20},{5,21},{6,22},{7,23},{8,0},{9,1... | collective-permute-start | bytes 1572872 | tf_op jit(solution)/shard_map/ppermute | solution.py:202
  55.9 18.0 %collective-permute-start.14 = (bf16[256,1024]{1,0:T(8,128)(2,1)}, bf16[256,1024]{1,0:T(8,128)(2,1)}, u32[]{:S(2)}, u32[]{:S(2)}) collective-permute-start(bf16[256,1024]{1,0:T(8,128)(2,1)} %collective-permute-done.9), channel_id=1, source_target_pairs={{0,8},{1,9},{2,10},{3,11},{4,12},{5,13},{6,14},{7,15},{8,24},{9,25... | collective-permute-start | bytes 1572872 | tf_op jit(solution)/shard_map/ppermute | solution.py:202
  66.0 14.8 %collective-permute-start.13 = (bf16[256,1024]{1,0:T(8,128)(2,1)}, bf16[256,1024]{1,0:T(8,128)(2,1)}, u32[]{:S(2)}, u32[]{:S(2)}) collective-permute-start(bf16[256,1024]{1,0:T(8,128)(2,1)} %get-tuple-element.435.refs_0_), channel_id=1, source_target_pairs={{0,1},{1,0},{2,3},{3,2},{4,5},{5,4},{6,7},{7,6},{8,9},{9,8},{10,11... | collective-permute-start | bytes 1572872 | tf_op jit(solution)/shard_map/ppermute | solution.py:202
  82.7 8.1 %collective-permute-start.20 = (bf16[128,1024]{1,0:T(8,128)(2,1)S(1)}, bf16[128,1024]{1,0:T(8,128)(2,1)S(1)}, u32[]{:S(2)}, u32[]{:S(2)}) collective-permute-start(bf16[128,1024]{1,0:T(8,128)(2,1)S(1)} %slice.566), channel_id=1, source_target_pairs={{0,16},{1,17},{2,18},{3,19},{4,20},{5,21},{6,22},{7,23},{8,0},{9,1... | collective-permute-start | bytes 786440 | tf_op jit(solution)/shard_map/ppermute | solution.py:202
  84.3 7.7 %collective-permute-start.19 = (bf16[128,1024]{1,0:T(8,128)(2,1)S(1)}, bf16[128,1024]{1,0:T(8,128)(2,1)S(1)}, u32[]{:S(2)}, u32[]{:S(2)}) collective-permute-start(bf16[128,1024]{1,0:T(8,128)(2,1)S(1)} %slice.565), channel_id=1, source_target_pairs={{0,8},{1,9},{2,10},{3,11},{4,12},{5,13},{6,14},{7,15},{8,24},{9,25... | collective-permute-start | bytes 786440 | tf_op jit(solution)/shard_map/ppermute | solution.py:202
  84.8 13.8 %collective-permute-start.18 = (bf16[128,1024]{1,0:T(8,128)(2,1)S(1)}, bf16[128,1024]{1,0:T(8,128)(2,1)S(1)}, u32[]{:S(2)}, u32[]{:S(2)}) collective-permute-start(bf16[128,1024]{1,0:T(8,128)(2,1)S(1)} %pad_maximum_fusion.15), channel_id=1, source_target_pairs={{0,2},{1,3},{2,0},{3,1},{4,6},{5,7},{6,4},{7,5},{8,10},{9,11},{10,... | collective-permute-start | bytes 786440 | tf_op jit(solution)/shard_map/ppermute | solution.py:202
  110.7 135.0 %all-gather.6.cloned.1.call-start = ((), (), s32[]{:S(2)}) async-start(), calls=%async_computation.6 | async-start | bytes 3932160 | tf_op jit(solution)/shard_map/all_gather | solution.py:1050
  117.3 18.7 %collective-permute-start.24 = (bf16[256,384]{1,0:T(8,128)(2,1)S(1)}, bf16[256,384]{1,0:T(8,128)(2,1)S(1)}, u32[]{:S(2)}, u32[]{:S(2)}) collective-permute-start(bf16[256,384]{1,0:T(8,128)(2,1)S(1)} %copy-done.57), channel_id=1, source_target_pairs={{0,3},{1,2},{2,1},{3,0},{4,7},{5,6},{6,5},{7,4},{8,11},{9,10},{10,... | collective-permute-start | bytes 589832 | tf_op jit(solution)/shard_map/ppermute | solution.py:202
  117.5 18.5 %collective-permute-start.23 = (bf16[256,384]{1,0:T(8,128)(2,1)S(1)}, bf16[256,384]{1,0:T(8,128)(2,1)S(1)}, u32[]{:S(2)}, u32[]{:S(2)}) collective-permute-start(bf16[256,384]{1,0:T(8,128)(2,1)S(1)} %copy-done.57), channel_id=1, source_target_pairs={{0,1},{1,0},{2,3},{3,2},{4,5},{5,4},{6,7},{7,6},{8,9},{9,8},{10,11... | collective-permute-start | bytes 589832 | tf_op jit(solution)/shard_map/ppermute | solution.py:202
  117.5 18.5 %collective-permute-start.22 = (bf16[256,384]{1,0:T(8,128)(2,1)S(1)}, bf16[256,384]{1,0:T(8,128)(2,1)S(1)}, u32[]{:S(2)}, u32[]{:S(2)}) collective-permute-start(bf16[256,384]{1,0:T(8,128)(2,1)S(1)} %copy-done.57), channel_id=1, source_target_pairs={{0,2},{1,3},{2,0},{3,1},{4,6},{5,7},{6,4},{7,5},{8,10},{9,11},{10,... | collective-permute-start | bytes 589832 | tf_op jit(solution)/shard_map/ppermute | solution.py:202
  139.7 139.9 %all-gather.8.cloned.1.call-start = ((), (), s32[]{:S(2)}) async-start(), calls=%async_computation.7 | async-start | bytes 5242880 | tf_op jit(solution)/shard_map/all_gather | solution.py:1050
  147.1 21.9 %collective-permute-start.26 = (bf16[256,1024]{1,0:T(8,128)(2,1)}, bf16[256,1024]{1,0:T(8,128)(2,1)}, u32[]{:S(2)}, u32[]{:S(2)}) collective-permute-start(bf16[256,1024]{1,0:T(8,128)(2,1)} %slice.1136), channel_id=1, source_target_pairs={{0,1},{1,0},{2,3},{3,2},{4,5},{5,4},{6,7},{7,6},{8,9},{9,8},{10,11... | collective-permute-start | bytes 1572872 | tf_op jit(solution)/shard_map/ppermute | solution.py:202
  149.3 26.6 %collective-permute-start.28 = (bf16[256,1024]{1,0:T(8,128)(2,1)}, bf16[256,1024]{1,0:T(8,128)(2,1)}, u32[]{:S(2)}, u32[]{:S(2)}) collective-permute-start(bf16[256,1024]{1,0:T(8,128)(2,1)} %pad_maximum_fusion.8), channel_id=1, source_target_pairs={{0,2},{1,3},{2,0},{3,1},{4,6},{5,7},{6,4},{7,5},{8,10},{9,11},{10,... | collective-permute-start | bytes 1572872 | tf_op jit(solution)/shard_map/ppermute | solution.py:202
  172.2 14.9 %collective-permute-start.27 = (bf16[256,1024]{1,0:T(8,128)(2,1)}, bf16[256,1024]{1,0:T(8,128)(2,1)}, u32[]{:S(2)}, u32[]{:S(2)}) collective-permute-start(bf16[256,1024]{1,0:T(8,128)(2,1)} %get-tuple-element.247.refs_0_), channel_id=1, source_target_pairs={{0,1},{1,0},{2,3},{3,2},{4,5},{5,4},{6,7},{7,6},{8,9},{9,8},{10,11... | collective-permute-start | bytes 1572872 | tf_op jit(solution)/shard_map/ppermute | solution.py:202
  172.3 14.7 %collective-permute-start.31 = (s32[1024]{0:T(1024)S(1)}, s32[1024]{0:T(1024)S(1)}, u32[]{:S(2)}, u32[]{:S(2)}) collective-permute-start(s32[1024]{0:T(1024)S(1)} %bitcast.159), channel_id=1, source_target_pairs={{0,4},{1,5},{2,6},{3,7},{4,0},{5,1},{6,2},{7,3},{8,12},{9,13},{10,... | collective-permute-start | bytes 12296 | tf_op jit(solution)/shard_map/ppermute | solution.py:202
  172.4 15.4 %collective-permute-start.29 = (bf16[256,1024]{1,0:T(8,128)(2,1)}, bf16[256,1024]{1,0:T(8,128)(2,1)}, u32[]{:S(2)}, u32[]{:S(2)}) collective-permute-start(bf16[256,1024]{1,0:T(8,128)(2,1)} %get-tuple-element.247.refs_0_), channel_id=1, source_target_pairs={{0,4},{1,5},{2,6},{3,7},{4,0},{5,1},{6,2},{7,3},{8,12},{9,13},{10,... | collective-permute-start | bytes 1572872 | tf_op jit(solution)/shard_map/ppermute | solution.py:202
  203.3 6.1 collective-permute-start.32
  205.5 50.9 %collective-permute-start.39 = (bf16[256,1024]{1,0:T(8,128)(2,1)}, bf16[256,1024]{1,0:T(8,128)(2,1)}, u32[]{:S(2)}, u32[]{:S(2)}) collective-permute-start(bf16[256,1024]{1,0:T(8,128)(2,1)} %reorder_blocks.14), channel_id=1, source_target_pairs={{2,4},{3,5},{4,2},{5,3},{10,12},{11,13},{12,10},{13,11},{18,20},{1... | collective-permute-start | bytes 1572872 | tf_op jit(solution)/shard_map/ppermute | solution.py:202
  209.4 212.9 %reduce-scatter.6.cloned.1.call-start = ((), (), s32[]{:S(2)}) async-start(), calls=%async_computation.8 | async-start | bytes 5242880 | tf_op jit(solution)/shard_map/reduce_scatter | solution.py:1053
  213.9 19.7 %collective-permute-start.33 = (bf16[256,1024]{1,0:T(8,128)(2,1)}, bf16[256,1024]{1,0:T(8,128)(2,1)}, u32[]{:S(2)}, u32[]{:S(2)}) collective-permute-start(bf16[256,1024]{1,0:T(8,128)(2,1)} %slice.1135), channel_id=1, source_target_pairs={{0,1},{1,0},{2,3},{3,2},{4,5},{5,4},{6,7},{7,6},{8,9},{9,8},{10,11... | collective-permute-start | bytes 1572872 | tf_op jit(solution)/shard_map/ppermute | solution.py:202
  238.7 5.7 collective-permute-start.35
  262.1 14.7 %collective-permute-start.40 = (bf16[256,1024]{1,0:T(8,128)(2,1)}, bf16[256,1024]{1,0:T(8,128)(2,1)S(1)}, u32[]{:S(2)}, u32[]{:S(2)}) collective-permute-start(bf16[256,1024]{1,0:T(8,128)(2,1)} %get-tuple-element.265.refs_0_), channel_id=1, source_target_pairs={{0,1},{1,0},{2,3},{3,2},{4,5},{5,4},{6,7},{7,6},{8,9},{9,8},{10,11... | collective-permute-start | bytes 1572872 | tf_op jit(solution)/shard_map/ppermute | solution.py:202
  263.5 14.2 %collective-permute-start.41 = (bf16[256,1024]{1,0:T(8,128)(2,1)}, bf16[256,1024]{1,0:T(8,128)(2,1)}, u32[]{:S(2)}, u32[]{:S(2)}) collective-permute-start(bf16[256,1024]{1,0:T(8,128)(2,1)} %get-tuple-element.265.refs_0_), channel_id=1, source_target_pairs={{0,4},{1,5},{2,6},{3,7},{4,0},{5,1},{6,2},{7,3},{8,12},{9,13},{10,... | collective-permute-start | bytes 1572872 | tf_op jit(solution)/shard_map/ppermute | solution.py:202
  295.1 14.1 %collective-permute-start.44 = (bf16[256,1024]{1,0:T(8,128)(2,1)S(1)}, bf16[256,1024]{1,0:T(8,128)(2,1)S(1)}, u32[]{:S(2)}, u32[]{:S(2)}) collective-permute-start(bf16[256,1024]{1,0:T(8,128)(2,1)S(1)} %slice.1134), channel_id=1, source_target_pairs={{0,1},{1,0},{2,3},{3,2},{4,5},{5,4},{6,7},{7,6},{8,9},{9,8},{10,11... | collective-permute-start | bytes 1572872 | tf_op jit(solution)/shard_map/ppermute | solution.py:202
  316.3 13.4 %collective-permute-start.45 = (bf16[256,1024]{1,0:T(8,128)(2,1)}, bf16[256,1024]{1,0:T(8,128)(2,1)S(1)}, u32[]{:S(2)}, u32[]{:S(2)}) collective-permute-start(bf16[256,1024]{1,0:T(8,128)(2,1)} %get-tuple-element.271.refs_0_.refs_5_), channel_id=1, source_target_pairs={{0,1},{1,0},{2,3},{3,2},{4,5},{5,4},{6,7},{7,6},{8,9},{9,8},{10,11... | collective-permute-start | bytes 1572872 | tf_op jit(solution)/shard_map/ppermute | solution.py:202
  317.7 11.9 %collective-permute-start.46 = (bf16[256,1024]{1,0:T(8,128)(2,1)}, bf16[256,1024]{1,0:T(8,128)(2,1)S(1)}, u32[]{:S(2)}, u32[]{:S(2)}) collective-permute-start(bf16[256,1024]{1,0:T(8,128)(2,1)} %get-tuple-element.271.refs_0_.refs_5_), channel_id=1, source_target_pairs={{0,4},{1,5},{2,6},{3,7},{4,0},{5,1},{6,2},{7,3},{8,12},{9,13},{10,... | collective-permute-start | bytes 1572872 | tf_op jit(solution)/shard_map/ppermute | solution.py:202
  351.6 14.3 %collective-permute-start.49 = (bf16[256,1024]{1,0:T(8,128)(2,1)}, bf16[256,1024]{1,0:T(8,128)(2,1)}, u32[]{:S(2)}, u32[]{:S(2)}) collective-permute-start(bf16[256,1024]{1,0:T(8,128)(2,1)} %slice.1133), channel_id=1, source_target_pairs={{0,1},{1,0},{2,3},{3,2},{4,5},{5,4},{6,7},{7,6},{8,9},{9,8},{10,11... | collective-permute-start | bytes 1572872 | tf_op jit(solution)/shard_map/ppermute | solution.py:202
  365.9 114.1 %reduce-scatter.8.cloned.1.call-start = ((), (), s32[]{:S(2)}) async-start(), calls=%async_computation.9 | async-start | bytes 3932160 | tf_op jit(solution)/shard_map/reduce_scatter | solution.py:1053
  376.3 5.5 collective-permute-start.51
  383.9 15.8 %collective-permute-start.55 = (bf16[256,1024]{1,0:T(8,128)(2,1)}, bf16[256,1024]{1,0:T(8,128)(2,1)}, u32[]{:S(2)}, u32[]{:S(2)}) collective-permute-start(bf16[256,1024]{1,0:T(8,128)(2,1)} %reorder_blocks.15), channel_id=1, source_target_pairs={{2,4},{3,5},{4,2},{5,3},{10,12},{11,13},{12,10},{13,11},{18,20},{1... | collective-permute-start | bytes 1572872 | tf_op jit(solution)/shard_map/ppermute | solution.py:202
  406.7 14.1 %collective-permute-start.56 = (bf16[256,1024]{1,0:T(8,128)(2,1)}, bf16[256,1024]{1,0:T(8,128)(2,1)}, u32[]{:S(2)}, u32[]{:S(2)}) collective-permute-start(bf16[256,1024]{1,0:T(8,128)(2,1)} %get-tuple-element.286.refs_0_.refs_5_), channel_id=1, source_target_pairs={{0,1},{1,0},{2,3},{3,2},{4,5},{5,4},{6,7},{7,6},{8,9},{9,8},{10,11... | collective-permute-start | bytes 1572872 | tf_op jit(solution)/shard_map/ppermute | solution.py:202
  420.9 113.3 %reduce-scatter.10.cloned.1.call-start = ((), (), s32[]{:S(2)}) async-start(), calls=%async_computation.10 | async-start | bytes 2621440 | tf_op jit(solution)/shard_map/reduce_scatter | solution.py:1053
  421.3 5.5 collective-permute-start.57
  424.4 25.9 %collective-permute-start.59 = (bf16[256,1024]{1,0:T(8,128)(2,1)S(1)}, bf16[256,1024]{1,0:T(8,128)(2,1)S(1)}, u32[]{:S(2)}, u32[]{:S(2)}) collective-permute-start(bf16[256,1024]{1,0:T(8,128)(2,1)S(1)} %pad_maximum_fusion.10), channel_id=1, source_target_pairs={{0,2},{1,3},{2,0},{3,1},{4,6},{5,7},{6,4},{7,5},{8,10},{9,11},{10,... | collective-permute-start | bytes 1572872 | tf_op jit(solution)/shard_map/ppermute | solution.py:202
  457.3 14.3 %collective-permute-start.61 = (bf16[256,1024]{1,0:T(8,128)(2,1)}, bf16[256,1024]{1,0:T(8,128)(2,1)}, u32[]{:S(2)}, u32[]{:S(2)}) collective-permute-start(bf16[256,1024]{1,0:T(8,128)(2,1)} %slice.1132), channel_id=1, source_target_pairs={{0,1},{1,0},{2,3},{3,2},{4,5},{5,4},{6,7},{7,6},{8,9},{9,8},{10,11... | collective-permute-start | bytes 1572872 | tf_op jit(solution)/shard_map/ppermute | solution.py:202
  471.6 96.3 %reduce-scatter.14.cloned.1.call-start = ((), (), s32[]{:S(2)}) async-start(), calls=%async_computation.12 | async-start | bytes 2621440 | tf_op jit(solution)/shard_map/reduce_scatter | solution.py:1053
  484.3 27.5 %collective-permute-start.62 = (bf16[256,1024]{1,0:T(8,128)(2,1)}, bf16[256,1024]{1,0:T(8,128)(2,1)}, u32[]{:S(2)}, u32[]{:S(2)}) collective-permute-start(bf16[256,1024]{1,0:T(8,128)(2,1)} %get-tuple-element.303.refs_0_.refs_3_), channel_id=1, source_target_pairs={{0,1},{1,0},{2,3},{3,2},{4,5},{5,4},{6,7},{7,6},{8,9},{9,8},{10,11... | collective-permute-start | bytes 1572872 | tf_op jit(solution)/shard_map/ppermute | solution.py:202
  488.4 14.2 %collective-permute-start.63 = (bf16[256,384]{1,0:T(8,128)(2,1)}, bf16[256,384]{1,0:T(8,128)(2,1)S(1)}, u32[]{:S(2)}, u32[]{:S(2)}) collective-permute-start(bf16[256,384]{1,0:T(8,128)(2,1)} %get-tuple-element.306), channel_id=1, source_target_pairs={{0,2},{1,3},{2,0},{3,1},{4,6},{5,7},{6,4},{7,5},{8,10},{9,11},{10,... | collective-permute-start | bytes 589832 | tf_op jit(solution)/shard_map/ppermute | solution.py:202
  491.3 14.8 %collective-permute-start.64 = (bf16[256,384]{1,0:T(8,128)(2,1)}, bf16[256,384]{1,0:T(8,128)(2,1)S(1)}, u32[]{:S(2)}, u32[]{:S(2)}) collective-permute-start(bf16[256,384]{1,0:T(8,128)(2,1)} %get-tuple-element.307), channel_id=1, source_target_pairs={{0,1},{1,0},{2,3},{3,2},{4,5},{5,4},{6,7},{7,6},{8,9},{9,8},{10,11... | collective-permute-start | bytes 589832 | tf_op jit(solution)/shard_map/ppermute | solution.py:202
  491.6 20.2 %collective-permute-start.65 = (bf16[256,384]{1,0:T(8,128)(2,1)}, bf16[256,384]{1,0:T(8,128)(2,1)}, u32[]{:S(2)}, u32[]{:S(2)}) collective-permute-start(bf16[256,384]{1,0:T(8,128)(2,1)} %get-tuple-element.308), channel_id=1, source_target_pairs={{0,3},{1,2},{2,1},{3,0},{4,7},{5,6},{6,5},{7,4},{8,11},{9,10},{10,... | collective-permute-start | bytes 589832 | tf_op jit(solution)/shard_map/ppermute | solution.py:202
  499.1 12.7 %collective-permute-start.66 = (bf16[256,1024]{1,0:T(8,128)(2,1)}, bf16[256,1024]{1,0:T(8,128)(2,1)}, u32[]{:S(2)}, u32[]{:S(2)}) collective-permute-start(bf16[256,1024]{1,0:T(8,128)(2,1)} %get-tuple-element.303.refs_0_.refs_3_), channel_id=1, source_target_pairs={{0,4},{1,5},{2,6},{3,7},{4,0},{5,1},{6,2},{7,3},{8,12},{9,13},{10,... | collective-permute-start | bytes 1572872 | tf_op jit(solution)/shard_map/ppermute | solution.py:202
  526.5 7.6 %collective-permute-start.68 = (bf16[512,1024]{1,0:T(8,128)(2,1)}, bf16[512,1024]{1,0:T(8,128)(2,1)}, u32[]{:S(2)}, u32[]{:S(2)}) collective-permute-start(bf16[512,1024]{1,0:T(8,128)(2,1)} %get-tuple-element.316), channel_id=1, source_target_pairs={{0,4},{1,5},{2,6},{3,7},{4,0},{5,1},{6,2},{7,3},{8,12},{9,13},{10,... | collective-permute-start | bytes 3145736 | tf_op jit(solution)/shard_map/ppermute | solution.py:202
  534.2 89.7 %reduce-scatter.12.cloned.1.call-start = ((), (), s32[]{:S(2)}) async-start(), calls=%async_computation.11 | async-start | bytes 2621440 | tf_op jit(solution)/shard_map/reduce_scatter | solution.py:1053
  538.8 19.9 %collective-permute-start.69 = (bf16[256,1024]{1,0:T(8,128)(2,1)}, bf16[256,1024]{1,0:T(8,128)(2,1)}, u32[]{:S(2)}, u32[]{:S(2)}) collective-permute-start(bf16[256,1024]{1,0:T(8,128)(2,1)} %slice.1131), channel_id=1, source_target_pairs={{0,1},{1,0},{2,3},{3,2},{4,5},{5,4},{6,7},{7,6},{8,9},{9,8},{10,11... | collective-permute-start | bytes 1572872 | tf_op jit(solution)/shard_map/ppermute | solution.py:202
  539.6 23.2 %collective-permute-start.71 = (bf16[128,1024]{1,0:T(8,128)(2,1)}, bf16[128,1024]{1,0:T(8,128)(2,1)}, u32[]{:S(2)}, u32[]{:S(2)}) collective-permute-start(bf16[128,1024]{1,0:T(8,128)(2,1)} %broadcast_select_fusion.7), channel_id=1, source_target_pairs={{0,2},{1,3},{2,0},{3,1},{4,6},{5,7},{6,4},{7,5},{8,10},{9,11},{10,... | collective-permute-start | bytes 786440 | tf_op jit(solution)/shard_map/ppermute | solution.py:202
  569.3 6.4 collective-permute-start.82
  570.8 6.8 %collective-permute-start.72 = (bf16[128,1024]{1,0:T(8,128)(2,1)S(1)}, bf16[128,1024]{1,0:T(8,128)(2,1)S(1)}, u32[]{:S(2)}, u32[]{:S(2)}) collective-permute-start(bf16[128,1024]{1,0:T(8,128)(2,1)S(1)} %broadcast_select_fusion.16), channel_id=1, source_target_pairs={{0,4},{1,5},{2,6},{3,7},{4,0},{5,1},{6,2},{7,3},{8,12},{9,13},{10,... | collective-permute-start | bytes 786440 | tf_op jit(solution)/shard_map/ppermute | solution.py:202
  571.4 51.6 %collective-permute-start.81 = (bf16[256,1024]{1,0:T(8,128)(2,1)}, bf16[256,1024]{1,0:T(8,128)(2,1)}, u32[]{:S(2)}, u32[]{:S(2)}) collective-permute-start(bf16[256,1024]{1,0:T(8,128)(2,1)} %reduce-scatter.14.cloned.1.call-done), channel_id=1, source_target_pairs={{0,2},{1,3},{2,0},{3,1},{4,6},{5,7},{6,4},{7,5},{8,10},{9,11},{10,... | collective-permute-start | bytes 1572872 | tf_op jit(solution)/shard_map/ppermute | solution.py:202
  594.3 11.0 %collective-permute-start.74 = (f32[17,256]{1,0:T(8,128)}, f32[17,256]{1,0:T(8,128)S(1)}, u32[]{:S(2)}, u32[]{:S(2)}) collective-permute-start(f32[17,256]{1,0:T(8,128)} %get-tuple-element.506), channel_id=1, source_target_pairs={{0,8},{1,9},{2,10},{3,11},{4,12},{5,13},{6,14},{7,15},{8,24},{9,25... | collective-permute-start | bytes 52232 | tf_op jit(solution)/shard_map/ppermute | solution.py:202
  595.7 9.6 %collective-permute-start.75 = (f32[17,256]{1,0:T(8,128)}, f32[17,256]{1,0:T(8,128)S(1)}, u32[]{:S(2)}, u32[]{:S(2)}) collective-permute-start(f32[17,256]{1,0:T(8,128)} %get-tuple-element.507), channel_id=1, source_target_pairs={{0,16},{1,17},{2,18},{3,19},{4,20},{5,21},{6,22},{7,23},{8,0},{9,1... | collective-permute-start | bytes 52232 | tf_op jit(solution)/shard_map/ppermute | solution.py:202
  604.6 18.4 %collective-permute-start.80 = (bf16[256,1024]{1,0:T(8,128)(2,1)}, bf16[256,1024]{1,0:T(8,128)(2,1)S(1)}, u32[]{:S(2)}, u32[]{:S(2)}) collective-permute-start(bf16[256,1024]{1,0:T(8,128)(2,1)} %reorder_blocks.19), channel_id=1, source_target_pairs={{2,4},{3,5},{4,2},{5,3},{10,12},{11,13},{12,10},{13,11},{18,20},{1... | collective-permute-start | bytes 1572872 | tf_op jit(solution)/shard_map/ppermute | solution.py:202
  605.3 9.3 %collective-permute-start.76 = (f32[17,128]{1,0:T(8,128)S(1)}, f32[17,128]{1,0:T(8,128)S(1)}, u32[]{:S(2)}, u32[]{:S(2)}) collective-permute-start(f32[17,128]{1,0:T(8,128)S(1)} %slice_select_fusion.2), channel_id=1, source_target_pairs={{0,4},{1,5},{2,6},{3,7},{4,0},{5,1},{6,2},{7,3},{8,12},{9,13},{10,... | collective-permute-start | bytes 26120 | tf_op jit(solution)/shard_map/ppermute | solution.py:202
  614.6 7.6 %collective-permute-start.79 = (f32[17,128]{1,0:T(8,128)S(1)}, f32[17,128]{1,0:T(8,128)S(1)}, u32[]{:S(2)}, u32[]{:S(2)}) collective-permute-start(f32[17,128]{1,0:T(8,128)S(1)} %select_add_fusion), channel_id=1, source_target_pairs={{0,3},{1,2},{2,1},{3,0},{4,7},{5,6},{6,5},{7,4},{8,11},{9,10},{10,... | collective-permute-start | bytes 26120 | tf_op jit(solution)/shard_map/ppermute | solution.py:202
  615.7 6.5 %collective-permute-start.78 = (f32[17,128]{1,0:T(8,128)S(1)}, f32[17,128]{1,0:T(8,128)S(1)}, u32[]{:S(2)}, u32[]{:S(2)}) collective-permute-start(f32[17,128]{1,0:T(8,128)S(1)} %select_add_fusion), channel_id=1, source_target_pairs={{0,2},{1,3},{2,0},{3,1},{4,6},{5,7},{6,4},{7,5},{8,10},{9,11},{10,... | collective-permute-start | bytes 26120 | tf_op jit(solution)/shard_map/ppermute | solution.py:202
  (120 other events, 706.4 us)
Sparse Core Ops, SparseCore 0:
  110.9 32.7 all-gather.3
  146.1 43.9 all-gather.5
  209.5 52.6 all-gather.7
  366.0 51.4 reduce-scatter.5
  421.0 43.5 reduce-scatter.7
  471.7 34.5 reduce-scatter.9
  534.3 33.5 reduce-scatter.13
  571.1 35.3 reduce-scatter.11

commit v4 on v3

--- a/solution.py
+++ b/solution.py
@@ -923,18 +923,21 @@
         far_beside = [send(part, plan.swap_core) for part in far[1:]]
         return far + [beside] + far_beside, done
 
+    def pass_on(own, got):
+        cut = own.shape[0] // 2
+        outgoing = (own[cut:] + got[cut:].astype(F32)).astype(BF16)
+        own, got, outgoing = together(own, got, outgoing)
+        return own[:cut] + got[:cut].astype(F32), outgoing
+
     def row_scatter(near, away, work=lambda hold: []):
-        total = near + send(away, plan.swap_core).astype(F32)
-        done = None
+        own, got, done = near, send(away, plan.swap_core), None
         for bit in near_bits[::-1]:
-            cut = total.shape[0] // 2
-            own, outgoing = total[:cut], total[cut:].astype(BF16)
+            own, outgoing = pass_on(own, got)
             if done is None:
                 done = work(lambda value: after(value, outgoing))
             got = send(outgoing, plan.swap_z(bit))
             if done:
                 got, *done = together(got, *done)
-            total = own + got.astype(F32)
         return own, got, done
 
     near_z = jnp.bitwise_xor(z_low, jnp.asarray(plan.z_order(near_bits), jnp.int32))
@@ -1057,8 +1060,8 @@
     row_parts, far_found[1:] = row_gather(rows, lambda: far_found[1:])
     far_ends = gather_end(plan, far_found)
     other = send(after(attend_own, row_parts[1]), plan.swap_z(half))
-    other, *far_ends = together(other, *far_ends)
     early_near, small_parts = gathered(early_found, early_ends, piece_rows)
+    other, early_near, *far_ends = together(other, early_near, *far_ends)
     early_far, _ = gathered(far_found, far_ends)
     early = [(early_near, 0, lanes), (early_far, 0, lanes)]
 
@@ -1177,10 +1180,11 @@
         )
         depth_rows = jnp.pad(depth_rows.reshape(KERNEL + 2, width), ((0, 1), (0, 0)))
         depth_rows = reorder_blocks(depth_rows, here)[: KERNEL + 2]
-        return [conv_sum, norm_rows, depth_rows]
-
-    incoming_early, (conv_sum, norm_rows, depth_rows) = row_gather(sent, small_work)
+        return [norm_rows, depth_rows]
+
+    incoming_early, (norm_rows, depth_rows) = row_gather(sent, small_work)
     back_early, kept_early, near, away = expand_shrink_back(incoming_early, early_preact, early)
+    near, away, back_early, conv_sum = together(near, away, back_early, conv_sum)
 
     def early_grad(left, right, first):
         return pair_grad(
@@ -1200,18 +1204,15 @@
     attend_own, away = jnp.where(on_low, low, up), jnp.where(on_low, up, low)
     attend_away = send(away, plan.swap_z(half))
     far_sum = chips_scatter(far_grads)
-    total = near + got.astype(F32)
-    cut = total.shape[0] // 2
-    own, outgoing = total[:cut], total[cut:].astype(BF16)
+    own, outgoing = pass_on(near, got)
     got, near_grads = together(
         send(outgoing, plan.swap_z(near_bits[-1])),
         early_grad(after(back_early, outgoing), kept_early, 0),
     )
     near_sum = chips_scatter(near_grads)
     for bit in near_bits[:-1][::-1]:
-        total = own + got.astype(F32)
-        cut //= 2
-        own, got = total[:cut], send(total[cut:].astype(BF16), plan.swap_z(bit))
+        own, outgoing = pass_on(own, got)
+        got = send(outgoing, plan.swap_z(bit))
     _, sent, early_rows = norm_back(gradient, own, got, early_stream, gains, 0, 1.0)
     sent, early_rows, far_sum, attend_away, late_sum, late_away, conv_sum = together(
         sent, early_rows, far_sum, attend_away, late_sum, late_away, conv_sum

time: 656 us -> 638 us (0.973)
  local copies, waits for them, and re-layouts: 81.6 us -> 50.9 us
  other arithmetic: 78.1 us -> 91.6 us
  starting transfers between devices: 71.7 us -> 78.6 us
    slice x12 -> x0, local copies, waits for them, and re-layouts: 14.6 us -> none  [the longest x10 12.7 us: row_scatter(): own, outgoing = (total[:cut], total[cut:].astype(BF16))]
    convert_element_type x0 -> x6, other arithmetic: none -> 12.7 us  [pass_on(): outgoing = (own[cut:] + got[cut:].astype(F32)).astype(BF16)]
    ppermute x84, starting transfers between devices: 70.8 us -> 77.5 us  [send(): return lax.ppermute(value, AXES, pairs)]
    unnamed x194 -> x190, local copies, waits for them, and re-layouts: 31.6 us -> 25.2 us
  transfers between devices with their start and end apart: 92 -> 92, of which waited for: 40 -> 41; matrix products, arithmetic and copies ran while one was open for 21% -> 20% of each run, Pallas kernels for 23% -> 24%
where the time goes in v4:
time: 638 us; the launch traced here: 629 us
  Pallas kernels  193 us (30%)
  waiting for transfers between devices  189 us (30%)
  other arithmetic  91.6 us (14%)
  starting transfers between devices  78.6 us (12%)
  local copies, waits for them, and re-layouts  50.9 us (8%)
  between operations  16.1 us (3%)
  matrix products  10.4 us (2%)
    ppermute x84, waiting for transfers between devices, send(): return lax.ppermute(value, AXES, pairs)  186 us
    ppermute x84, starting transfers between devices, send(): return lax.ppermute(value, AXES, pairs)  77.5 us
    pallas_call x5, Pallas kernels, pair_grad(): pl.pallas_call(partial(pair_grad_kernel, each, len(left), len(other_left)...  36.3 us
    pallas_call x3, Pallas kernels, in_place(): pl.pallas_call(kernel, out_shape=outs, in_specs=[pl.BlockSpec(memory_spac...  31.7 us
    pallas_call x8, Pallas kernels, rotated_adam(): pl.pallas_call(partial(adam_kernel, turn, rate), grid=(count,), out_shape...  26 us
    unnamed x190, local copies, waits for them, and re-layouts  25.2 us
    pallas_call x2, Pallas kernels, expand_shrink_back(): pl.pallas_call(partial(expand_shrink_back_kernel, len(weights), each, len...  23.9 us
    pallas_call x2, Pallas kernels, expand_shrink(): pl.pallas_call(partial(expand_shrink_kernel, len(weights), each, len(full...  21.5 us
  transfers between devices with their start and end apart: 92, of which 41 were waited for; matrix products, arithmetic and copies ran while one was open for 20% of the time, Pallas kernels for 24%

profile of v4, /device:TPU:0, one launch (start us, length us, event | category | flops | bytes accessed | tf_op | source)
XLA Modules:
  0.0 629.4 jit_solution(16857733423937877432)
XLA Ops:
  8.1 4.1 collective-permute-start.2
  34.3 3.8 convert_element_type.219.right
  67.8 3.2 collective-permute-done.15
  72.3 5.6 collective-permute-done.13.refs_1_
  80.1 6.8 %collective-permute-done.20 = bf16[128,1024]{1,0:T(8,128)(2,1)S(1)} collective-permute-done((bf16[128,1024]{1,0:T(8,128)(2,1)S(1)}, bf16[128,1024]{1,0:T(8,128)(2,1)S(1)}, u32[]{:S(2)}, u32[]{:S(2)}) %collective-permute-start.20) | collective-permute-done | bytes 262176 | tf_op jit(solution)/shard_map/ppermute | solution.py:202
  88.5 6.3 %collective-permute-done.18 = bf16[128,1024]{1,0:T(8,128)(2,1)S(1)} collective-permute-done((bf16[128,1024]{1,0:T(8,128)(2,1)S(1)}, bf16[128,1024]{1,0:T(8,128)(2,1)S(1)}, u32[]{:S(2)}, u32[]{:S(2)}) %collective-permute-start.18) | collective-permute-done | bytes 262176 | tf_op jit(solution)/shard_map/ppermute | solution.py:202
  101.4 4.4 norm.1.refs_0_.refs_1_
  109.8 11.0 %expand_shrink.2 = (f32[1024,1024]{1,0:T(8,128)}, f32[512,1024]{1,0:T(8,128)}, bf16[512,1024]{1,0:T(8,128)(2,1)}) custom-call(bf16[1024,1024]{1,0:T(8,128)(2,1)} %norm.1.refs_0_.refs_1_, bf16[1024,1024]{1,0:T(8,128)(2,1)} %copy-done.75, bf16[1024,1024]{1,0:T(8,128)(2,1)} %copy-done.75, bf16[1024,1024]{1,0:T(8,128)(2,1)} %copy-done.76, ...), custom_call_target="tpu_custom_call" | custom-call | flops 4294967296 | bytes 9437184 | tf_op jit(solution)/shard_map/expand_shrink/pallas_call | solution.py:346
  121.2 4.4 collective-permute-start.22
  125.6 5.3 collective-permute-done.24.refs_3_
  130.9 5.7 collective-permute-done.23.refs_2_
  146.8 2.5 collective-permute-start.28
  149.3 2.7 convert_add_fusion.5.refs_2_
  152.0 13.1 %collective-permute-done.26.refs_3_ = bf16[256,1024]{1,0:T(8,128)(2,1)} collective-permute-done((bf16[256,1024]{1,0:T(8,128)(2,1)}, bf16[256,1024]{1,0:T(8,128)(2,1)}, u32[]{:S(2)}, u32[]{:S(2)}) %collective-permute-start.26) | collective-permute-done | bytes 524320 | tf_op jit(solution)/shard_map/ppermute | solution.py:202
  165.1 3.7 add_norm.4
  169.5 2.7 collective-permute-done.28
  172.1 11.1 %collective-permute-done.27.refs_1_ = bf16[256,1024]{1,0:T(8,128)(2,1)} collective-permute-done((bf16[256,1024]{1,0:T(8,128)(2,1)}, bf16[256,1024]{1,0:T(8,128)(2,1)}, u32[]{:S(2)}, u32[]{:S(2)}) %collective-permute-start.27) | collective-permute-done | bytes 524320 | tf_op jit(solution)/shard_map/ppermute | solution.py:202
  187.1 12.4 %attention.1 = (bf16[1024,768]{1,0:T(8,128)(2,1)}, bf16[1024,256]{1,0:T(8,128)(2,1)}, f32[1024,256]{1,0:T(8,128)}, f32[512,1024]{1,0:T(8,128)}, bf16[512,1024]{1,0:T(8,128)(2,1)}) custom-call(bf16[256,1024]{1,0:T(8,128)(2,1)} %get-tuple-element.273.refs_0_, bf16[256,1024]{1,0:T(8,128)(2,1)} %collective-permute-done.27.refs_1_, ...), custom_call_target="tpu_custom_call" | custom-call | flops 3221225472 | bytes 11042816 | tf_op jit(solution)/shard_map/attention/pallas_call | solution.py:253
  211.0 2.5 convert_add_fusion.4.refs_1_
  213.5 15.0 %collective-permute-done.33.refs_2_ = bf16[256,1024]{1,0:T(8,128)(2,1)} collective-permute-done((bf16[256,1024]{1,0:T(8,128)(2,1)}, bf16[256,1024]{1,0:T(8,128)(2,1)}, u32[]{:S(2)}, u32[]{:S(2)}) %collective-permute-start.33) | collective-permute-done | bytes 524320 | tf_op jit(solution)/shard_map/ppermute | solution.py:202
  228.5 3.0 add_norm.5
  235.5 4.3 collective-permute-done.35
  254.4 3.0 add_norm.6
  259.9 12.1 %collective-permute-done.40.refs_1_ = bf16[256,1024]{1,0:T(8,128)(2,1)S(1)} collective-permute-done((bf16[256,1024]{1,0:T(8,128)(2,1)}, bf16[256,1024]{1,0:T(8,128)(2,1)S(1)}, u32[]{:S(2)}, u32[]{:S(2)}) %collective-permute-start.40) | collective-permute-done | bytes 524320 | tf_op jit(solution)/shard_map/ppermute | solution.py:202
  274.9 10.6 %expand_shrink.3 = (f32[1024,1024]{1,0:T(8,128)}, f32[512,1024]{1,0:T(8,128)}, bf16[512,1024]{1,0:T(8,128)(2,1)}) custom-call(bf16[256,1024]{1,0:T(8,128)(2,1)} %get-tuple-element.294.refs_0_, bf16[256,1024]{1,0:T(8,128)(2,1)} %copy-done.60, bf16[256,1024]{1,0:T(8,128)(2,1)} %collective-permute-done.41.refs_2_, ...), custom_call_target="tpu_custom_call" | custom-call | flops 4294967296 | bytes 9437184 | tf_op jit(solution)/shard_map/expand_shrink/pallas_call | solution.py:346
  285.7 2.7 collective-permute-done.43
  292.4 11.4 %collective-permute-done.44.refs_2_ = bf16[256,1024]{1,0:T(8,128)(2,1)S(1)} collective-permute-done((bf16[256,1024]{1,0:T(8,128)(2,1)S(1)}, bf16[256,1024]{1,0:T(8,128)(2,1)S(1)}, u32[]{:S(2)}, u32[]{:S(2)}) %collective-permute-start.44) | collective-permute-done | bytes 524320 | tf_op jit(solution)/shard_map/ppermute | solution.py:202
  304.7 3.0 add_norm.7
  307.7 3.3 norm_back.5
  312.4 11.9 %collective-permute-done.45.refs_1_.refs_6_ = bf16[256,1024]{1,0:T(8,128)(2,1)S(1)} collective-permute-done((bf16[256,1024]{1,0:T(8,128)(2,1)}, bf16[256,1024]{1,0:T(8,128)(2,1)S(1)}, u32[]{:S(2)}, u32[]{:S(2)}) %collective-permute-start.45) | collective-permute-done | bytes 524320 | tf_op jit(solution)/shard_map/ppermute | solution.py:202
  327.0 12.0 %expand_shrink_back.2 = (bf16[1024,1024]{1,0:T(8,128)(2,1)}, bf16[1024,1024]{1,0:T(8,128)(2,1)}, f32[512,1024]{1,0:T(8,128)}, bf16[512,1024]{1,0:T(8,128)(2,1)}) custom-call(bf16[256,1024]{1,0:T(8,128)(2,1)} %get-tuple-element.303.refs_0_.refs_5_, bf16[256,1024]{1,0:T(8,128)(2,1)} %copy-done.61, bf16[256,1024]{1,0:T(8,128)(2,1)} %copy-done.62, ...), custom_call_target="tpu_custom_call" | custom-call | flops 4294967296 | bytes 13631488 | tf_op jit(solution)/shard_map/expand_shrink_back/pallas_call | solution.py:395
  339.3 2.7 collective-permute-done.48
  346.6 9.6 %pair_grad.5 = bf16[1024,2048]{1,0:T(8,128)(2,1)} custom-call(bf16[256,1024]{1,0:T(8,128)(2,1)} %get-tuple-element.294.refs_0_, bf16[256,1024]{1,0:T(8,128)(2,1)} %copy-done.60, bf16[256,1024]{1,0:T(8,128)(2,1)} %collective-permute-done.41.refs_2_, bf16[256,1024]{1,0:T(8,128)(2,1)} %collective-permute-done.42.refs_3_, ...), custom_call_target="tpu_custom_call" | custom-call | flops 4294967296 | bytes 10485760 | tf_op jit(solution)/shard_map/pair_grad/pallas_call | solution.py:444
  356.1 3.3 collective-permute-done.49.refs_2_
  359.5 2.5 convert_add_fusion.2.refs_1_
  362.0 4.0 norm_back.6
  366.7 3.3 collective-permute-start.50
  371.5 4.1 collective-permute-done.51
  396.6 4.0 norm_back.7
  404.3 5.7 pair_grad.6
  410.0 4.7 collective-permute-done.56.refs_1_.refs_6_
  418.1 2.4 collective-permute-start.59
  420.6 15.0 %attention_back.1 = (bf16[1024,768]{1,0:T(8,128)(2,1)}, f32[512,1024]{1,0:T(8,128)}, bf16[512,1024]{1,0:T(8,128)(2,1)}) custom-call(bf16[256,1024]{1,0:T(8,128)(2,1)} %get-tuple-element.321.refs_0_.refs_5_, bf16[256,1024]{1,0:T(8,128)(2,1)} %collective-permute-done.56.refs_1_.refs_6_, bf16[256,1024]{1,0:T(8,128)(2,1)} %collective-permute-done.57.refs_2_.refs_7_, ...), custom_call_target="tpu_custom_call" | custom-call | flops 4831838208 | bytes 12091392 | tf_op jit(solution)/shard_map/attention_back/pallas_call | solution.py:253
  435.5 9.1 %collective-permute-done.59 = bf16[256,1024]{1,0:T(8,128)(2,1)S(1)} collective-permute-done((bf16[256,1024]{1,0:T(8,128)(2,1)S(1)}, bf16[256,1024]{1,0:T(8,128)(2,1)S(1)}, u32[]{:S(2)}, u32[]{:S(2)}) %collective-permute-start.59) | collective-permute-done | bytes 524320 | tf_op jit(solution)/shard_map/ppermute | solution.py:202
  444.7 2.8 collective-permute-done.60
  450.6 7.3 %pair_grad.7 = bf16[1024,1024]{1,0:T(8,128)(2,1)} custom-call(bf16[256,1024]{1,0:T(8,128)(2,1)} %get-tuple-element.273.refs_0_, bf16[256,1024]{1,0:T(8,128)(2,1)} %collective-permute-done.27.refs_1_, bf16[256,1024]{1,0:T(8,128)(2,1)} %collective-permute-done.29.refs_2_, bf16[256,1024]{1,0:T(8,128)(2,1)} %collective-permute-done.30.refs_3_, ...), custom_call_target="tpu_custom_call" | custom-call | flops 2147483648 | bytes 7864320 | tf_op jit(solution)/shard_map/pair_grad/pallas_call | solution.py:444
  457.9 6.9 %collective-permute-done.61.refs_3_ = bf16[256,1024]{1,0:T(8,128)(2,1)} collective-permute-done((bf16[256,1024]{1,0:T(8,128)(2,1)}, bf16[256,1024]{1,0:T(8,128)(2,1)}, u32[]{:S(2)}, u32[]{:S(2)}) %collective-permute-start.61) | collective-permute-done | bytes 524320 | tf_op jit(solution)/shard_map/ppermute | solution.py:202
  466.7 4.3 fusion.21
  472.1 4.3 norm_back.8
  483.3 6.6 %collective-permute-done.62.refs_1_.refs_4_ = bf16[256,1024]{1,0:T(8,128)(2,1)} collective-permute-done((bf16[256,1024]{1,0:T(8,128)(2,1)}, bf16[256,1024]{1,0:T(8,128)(2,1)}, u32[]{:S(2)}, u32[]{:S(2)}) %collective-permute-start.62) | collective-permute-done | bytes 524320 | tf_op jit(solution)/shard_map/ppermute | solution.py:202
  496.5 11.9 %expand_shrink_back.3 = (bf16[1024,1024]{1,0:T(8,128)(2,1)}, bf16[1024,1024]{1,0:T(8,128)(2,1)}, f32[512,1024]{1,0:T(8,128)}, bf16[512,1024]{1,0:T(8,128)(2,1)}) custom-call(bf16[256,1024]{1,0:T(8,128)(2,1)} %get-tuple-element.341.refs_0_.refs_3_, bf16[256,1024]{1,0:T(8,128)(2,1)} %collective-permute-done.62.refs_1_.refs_4_, ...), custom_call_target="tpu_custom_call" | custom-call | flops 4294967296 | bytes 13631488 | tf_op jit(solution)/shard_map/expand_shrink_back/pallas_call | solution.py:395
  509.9 6.7 %pair_grad.8 = bf16[1024,1024]{1,0:T(8,128)(2,1)} custom-call(s32[4]{0:T(128)} %and_select_fusion.refs_0_, bf16[1024,1024]{1,0:T(8,128)(2,1)} %norm.1.refs_0_.refs_1_, bf16[1024,1024]{1,0:T(8,128)(2,1)} %get-tuple-element.364.refs_2_, bf16[256,1024]{1,0:T(8,128)(2,1)} %get-tuple-element.341.refs_0_.refs_3_, ...), custom_call_target="tpu_custom_call" | custom-call | flops 2147483648 | bytes 8388608 | tf_op jit(solution)/shard_map/pair_grad/pallas_call | solution.py:444
  523.1 4.5 collective-permute-start.69
  527.6 6.9 %pair_grad.9 = bf16[1024,1024]{1,0:T(8,128)(2,1)} custom-call(s32[4]{0:T(128)} %and_select_fusion.refs_0_, bf16[1024,1024]{1,0:T(8,128)(2,1)} %norm.1.refs_0_.refs_1_, bf16[1024,1024]{1,0:T(8,128)(2,1)} %get-tuple-element.364.refs_2_, bf16[256,1024]{1,0:T(8,128)(2,1)} %get-tuple-element.341.refs_0_.refs_3_, ...), custom_call_target="tpu_custom_call" | custom-call | flops 2147483648 | bytes 8388608 | tf_op jit(solution)/shard_map/pair_grad/pallas_call | solution.py:444
  536.9 2.5 convert_add_fusion.refs_1_
  541.1 4.0 norm_back.9
  545.0 6.1 collective-permute-done.71
  551.1 3.0 reduce-scatter.14.cloned.1.call-done
  557.6 2.4 collective-permute-start.81
  564.1 4.4 rotated_adam.8
  568.6 4.5 rotated_adam.9
  597.8 3.0 rotated_adam.11
  613.4 4.6 rotated_adam.15
  618.0 4.3 rotated_adam.14
  (559 shorter events, 238.4 us)
Async XLA Ops:
  7.2 178.3 %all-gather.4.cloned.1.call-start = ((), (), s32[]{:S(2)}) async-start(), calls=%async_computation.5 | async-start | bytes 2621440 | tf_op jit(solution)/shard_map/all_gather | solution.py:1053
  8.1 8.2 %collective-permute-start.2 = (bf16[17,128]{1,0:T(8,128)(2,1)S(1)}, bf16[17,128]{1,0:T(8,128)(2,1)S(1)}, u32[]{:S(2)}, u32[]{:S(2)}) collective-permute-start(bf16[17,128]{1,0:T(8,128)(2,1)S(1)} %broadcast_multiply_fusion.1), channel_id=1, source_target_pairs={{0,2},{1,3},{2,0},{3,1},{4,6},{5,7},{6,4},{7,5},{8,10},{9,11},{10,... | collective-permute-start | bytes 13064 | tf_op jit(solution)/shard_map/ppermute | solution.py:202
  21.0 26.4 %collective-permute-start.9 = (bf16[256,1024]{1,0:T(8,128)(2,1)}, bf16[256,1024]{1,0:T(8,128)(2,1)}, u32[]{:S(2)}, u32[]{:S(2)}) collective-permute-start(bf16[256,1024]{1,0:T(8,128)(2,1)} %pad_maximum_fusion.7), channel_id=1, source_target_pairs={{0,2},{1,3},{2,0},{3,1},{4,6},{5,7},{6,4},{7,5},{8,10},{9,11},{10,... | collective-permute-start | bytes 1572872 | tf_op jit(solution)/shard_map/ppermute | solution.py:202
  24.7 20.7 %collective-permute-start.8 = (bf16[272,1024]{1,0:T(8,128)(2,1)}, bf16[272,1024]{1,0:T(8,128)(2,1)}, u32[]{:S(2)}, u32[]{:S(2)}) collective-permute-start(bf16[272,1024]{1,0:T(8,128)(2,1)} %maximum_maximum_fusion), channel_id=1, source_target_pairs={{0,16},{1,17},{2,18},{3,19},{4,20},{5,21},{6,22},{7,23},{8,0},{9,1... | collective-permute-start | bytes 1671176 | tf_op jit(solution)/shard_map/ppermute | solution.py:202
  26.2 19.2 %collective-permute-start.7 = (bf16[272,1024]{1,0:T(8,128)(2,1)}, bf16[272,1024]{1,0:T(8,128)(2,1)}, u32[]{:S(2)}, u32[]{:S(2)}) collective-permute-start(bf16[272,1024]{1,0:T(8,128)(2,1)} %maximum_maximum_fusion), channel_id=1, source_target_pairs={{0,8},{1,9},{2,10},{3,11},{4,12},{5,13},{6,14},{7,15},{8,24},{9,25... | collective-permute-start | bytes 1671176 | tf_op jit(solution)/shard_map/ppermute | solution.py:202
  30.3 11.4 %collective-permute-start.4 = (bf16[128,384]{1,0:T(8,128)(2,1)}, bf16[128,384]{1,0:T(8,128)(2,1)}, u32[]{:S(2)}, u32[]{:S(2)}) collective-permute-start(bf16[128,384]{1,0:T(8,128)(2,1)} %pad_maximum_fusion.21), channel_id=1, source_target_pairs={{0,4},{1,5},{2,6},{3,7},{4,0},{5,1},{6,2},{7,3},{8,12},{9,13},{10,... | collective-permute-start | bytes 294920 | tf_op jit(solution)/shard_map/ppermute | solution.py:202
  33.7 9.8 %collective-permute-start.5 = (bf16[128,1024]{1,0:T(8,128)(2,1)}, bf16[128,1024]{1,0:T(8,128)(2,1)}, u32[]{:S(2)}, u32[]{:S(2)}) collective-permute-start(bf16[128,1024]{1,0:T(8,128)(2,1)} %pad_maximum_fusion.17), channel_id=1, source_target_pairs={{0,4},{1,5},{2,6},{3,7},{4,0},{5,1},{6,2},{7,3},{8,12},{9,13},{10,... | collective-permute-start | bytes 786440 | tf_op jit(solution)/shard_map/ppermute | solution.py:202
  47.5 14.4 %collective-permute-start.10 = (bf16[256,1024]{1,0:T(8,128)(2,1)}, bf16[256,1024]{1,0:T(8,128)(2,1)}, u32[]{:S(2)}, u32[]{:S(2)}) collective-permute-start(bf16[256,1024]{1,0:T(8,128)(2,1)} %reorder_blocks.10), channel_id=1, source_target_pairs={{2,4},{3,5},{4,2},{5,3},{10,12},{11,13},{12,10},{13,11},{18,20},{1... | collective-permute-start | bytes 1572872 | tf_op jit(solution)/shard_map/ppermute | solution.py:202
  50.9 9.5 %collective-permute-start.12 = (bf16[136,1024]{1,0:T(8,128)(2,1)S(1)}, bf16[136,1024]{1,0:T(8,128)(2,1)S(1)}, u32[]{:S(2)}, u32[]{:S(2)}) collective-permute-start(bf16[136,1024]{1,0:T(8,128)(2,1)S(1)} %slice.588), channel_id=1, source_target_pairs={{0,16},{1,17},{2,18},{3,19},{4,20},{5,21},{6,22},{7,23},{8,0},{9,1... | collective-permute-start | bytes 835592 | tf_op jit(solution)/shard_map/ppermute | solution.py:202
  52.5 9.4 %collective-permute-start.11 = (bf16[136,1024]{1,0:T(8,128)(2,1)S(1)}, bf16[136,1024]{1,0:T(8,128)(2,1)S(1)}, u32[]{:S(2)}, u32[]{:S(2)}) collective-permute-start(bf16[136,1024]{1,0:T(8,128)(2,1)S(1)} %slice.587), channel_id=1, source_target_pairs={{0,8},{1,9},{2,10},{3,11},{4,12},{5,13},{6,14},{7,15},{8,24},{9,25... | collective-permute-start | bytes 835592 | tf_op jit(solution)/shard_map/ppermute | solution.py:202
  56.3 14.7 %collective-permute-start.15 = (bf16[256,1024]{1,0:T(8,128)(2,1)}, bf16[256,1024]{1,0:T(8,128)(2,1)S(1)}, u32[]{:S(2)}, u32[]{:S(2)}) collective-permute-start(bf16[256,1024]{1,0:T(8,128)(2,1)} %collective-permute-done.9), channel_id=1, source_target_pairs={{0,16},{1,17},{2,18},{3,19},{4,20},{5,21},{6,22},{7,23},{8,0},{9,1... | collective-permute-start | bytes 1572872 | tf_op jit(solution)/shard_map/ppermute | solution.py:202
  57.9 14.4 %collective-permute-start.14 = (bf16[256,1024]{1,0:T(8,128)(2,1)}, bf16[256,1024]{1,0:T(8,128)(2,1)S(1)}, u32[]{:S(2)}, u32[]{:S(2)}) collective-permute-start(bf16[256,1024]{1,0:T(8,128)(2,1)} %collective-permute-done.9), channel_id=1, source_target_pairs={{0,8},{1,9},{2,10},{3,11},{4,12},{5,13},{6,14},{7,15},{8,24},{9,25... | collective-permute-start | bytes 1572872 | tf_op jit(solution)/shard_map/ppermute | solution.py:202
  64.2 13.6 %collective-permute-start.13 = (bf16[256,1024]{1,0:T(8,128)(2,1)}, bf16[256,1024]{1,0:T(8,128)(2,1)}, u32[]{:S(2)}, u32[]{:S(2)}) collective-permute-start(bf16[256,1024]{1,0:T(8,128)(2,1)} %get-tuple-element.479.refs_0_), channel_id=1, source_target_pairs={{0,1},{1,0},{2,3},{3,2},{4,5},{5,4},{6,7},{7,6},{8,9},{9,8},{10,11... | collective-permute-start | bytes 1572872 | tf_op jit(solution)/shard_map/ppermute | solution.py:202
  77.9 8.9 %collective-permute-start.20 = (bf16[128,1024]{1,0:T(8,128)(2,1)S(1)}, bf16[128,1024]{1,0:T(8,128)(2,1)S(1)}, u32[]{:S(2)}, u32[]{:S(2)}) collective-permute-start(bf16[128,1024]{1,0:T(8,128)(2,1)S(1)} %slice.599), channel_id=1, source_target_pairs={{0,16},{1,17},{2,18},{3,19},{4,20},{5,21},{6,22},{7,23},{8,0},{9,1... | collective-permute-start | bytes 786440 | tf_op jit(solution)/shard_map/ppermute | solution.py:202
  79.4 9.1 %collective-permute-start.19 = (bf16[128,1024]{1,0:T(8,128)(2,1)S(1)}, bf16[128,1024]{1,0:T(8,128)(2,1)S(1)}, u32[]{:S(2)}, u32[]{:S(2)}) collective-permute-start(bf16[128,1024]{1,0:T(8,128)(2,1)S(1)} %slice.598), channel_id=1, source_target_pairs={{0,8},{1,9},{2,10},{3,11},{4,12},{5,13},{6,14},{7,15},{8,24},{9,25... | collective-permute-start | bytes 786440 | tf_op jit(solution)/shard_map/ppermute | solution.py:202
  80.0 14.8 %collective-permute-start.18 = (bf16[128,1024]{1,0:T(8,128)(2,1)S(1)}, bf16[128,1024]{1,0:T(8,128)(2,1)S(1)}, u32[]{:S(2)}, u32[]{:S(2)}) collective-permute-start(bf16[128,1024]{1,0:T(8,128)(2,1)S(1)} %pad_maximum_fusion.15), channel_id=1, source_target_pairs={{0,2},{1,3},{2,0},{3,1},{4,6},{5,7},{6,4},{7,5},{8,10},{9,11},{10,... | collective-permute-start | bytes 786440 | tf_op jit(solution)/shard_map/ppermute | solution.py:202
  105.8 135.3 %all-gather.6.cloned.1.call-start = ((), (), s32[]{:S(2)}) async-start(), calls=%async_computation.6 | async-start | bytes 3932160 | tf_op jit(solution)/shard_map/all_gather | solution.py:1053
  120.8 19.8 %collective-permute-start.25 = (bf16[512,1024]{1,0:T(8,128)(2,1)}, bf16[512,1024]{1,0:T(8,128)(2,1)}, u32[]{:S(2)}, u32[]{:S(2)}) collective-permute-start(bf16[512,1024]{1,0:T(8,128)(2,1)} %get-tuple-element.268), channel_id=1, source_target_pairs={{0,4},{1,5},{2,6},{3,7},{4,0},{5,1},{6,2},{7,3},{8,12},{9,13},{10,... | collective-permute-start | bytes 3145736 | tf_op jit(solution)/shard_map/ppermute | solution.py:202
  121.2 9.7 %collective-permute-start.24 = (bf16[256,384]{1,0:T(8,128)(2,1)S(1)}, bf16[256,384]{1,0:T(8,128)(2,1)S(1)}, u32[]{:S(2)}, u32[]{:S(2)}) collective-permute-start(bf16[256,384]{1,0:T(8,128)(2,1)S(1)} %copy-done.57), channel_id=1, source_target_pairs={{0,3},{1,2},{2,1},{3,0},{4,7},{5,6},{6,5},{7,4},{8,11},{9,10},{10,... | collective-permute-start | bytes 589832 | tf_op jit(solution)/shard_map/ppermute | solution.py:202
  121.2 15.4 %collective-permute-start.23 = (bf16[256,384]{1,0:T(8,128)(2,1)S(1)}, bf16[256,384]{1,0:T(8,128)(2,1)S(1)}, u32[]{:S(2)}, u32[]{:S(2)}) collective-permute-start(bf16[256,384]{1,0:T(8,128)(2,1)S(1)} %copy-done.57), channel_id=1, source_target_pairs={{0,1},{1,0},{2,3},{3,2},{4,5},{5,4},{6,7},{7,6},{8,9},{9,8},{10,11... | collective-permute-start | bytes 589832 | tf_op jit(solution)/shard_map/ppermute | solution.py:202
  121.2 15.4 %collective-permute-start.22 = (bf16[256,384]{1,0:T(8,128)(2,1)S(1)}, bf16[256,384]{1,0:T(8,128)(2,1)S(1)}, u32[]{:S(2)}, u32[]{:S(2)}) collective-permute-start(bf16[256,384]{1,0:T(8,128)(2,1)S(1)} %copy-done.57), channel_id=1, source_target_pairs={{0,2},{1,3},{2,0},{3,1},{4,6},{5,7},{6,4},{7,5},{8,10},{9,11},{10,... | collective-permute-start | bytes 589832 | tf_op jit(solution)/shard_map/ppermute | solution.py:202
  140.2 134.7 %all-gather.8.cloned.1.call-start = ((), (), s32[]{:S(2)}) async-start(), calls=%async_computation.7 | async-start | bytes 5242880 | tf_op jit(solution)/shard_map/all_gather | solution.py:1053
  142.8 22.2 %collective-permute-start.26 = (bf16[256,1024]{1,0:T(8,128)(2,1)}, bf16[256,1024]{1,0:T(8,128)(2,1)}, u32[]{:S(2)}, u32[]{:S(2)}) collective-permute-start(bf16[256,1024]{1,0:T(8,128)(2,1)} %add_convert_fusion.5), channel_id=1, source_target_pairs={{0,1},{1,0},{2,3},{3,2},{4,5},{5,4},{6,7},{7,6},{8,9},{9,8},{10,11... | collective-permute-start | bytes 1572872 | tf_op jit(solution)/shard_map/ppermute | solution.py:202
  146.8 25.4 %collective-permute-start.28 = (bf16[256,1024]{1,0:T(8,128)(2,1)}, bf16[256,1024]{1,0:T(8,128)(2,1)}, u32[]{:S(2)}, u32[]{:S(2)}) collective-permute-start(bf16[256,1024]{1,0:T(8,128)(2,1)} %pad_maximum_fusion.8), channel_id=1, source_target_pairs={{0,2},{1,3},{2,0},{3,1},{4,6},{5,7},{6,4},{7,5},{8,10},{9,11},{10,... | collective-permute-start | bytes 1572872 | tf_op jit(solution)/shard_map/ppermute | solution.py:202
  168.8 14.5 %collective-permute-start.27 = (bf16[256,1024]{1,0:T(8,128)(2,1)}, bf16[256,1024]{1,0:T(8,128)(2,1)}, u32[]{:S(2)}, u32[]{:S(2)}) collective-permute-start(bf16[256,1024]{1,0:T(8,128)(2,1)} %get-tuple-element.273.refs_0_), channel_id=1, source_target_pairs={{0,1},{1,0},{2,3},{3,2},{4,5},{5,4},{6,7},{7,6},{8,9},{9,8},{10,11... | collective-permute-start | bytes 1572872 | tf_op jit(solution)/shard_map/ppermute | solution.py:202
  168.9 14.3 %collective-permute-start.31 = (s32[1024]{0:T(1024)S(1)}, s32[1024]{0:T(1024)S(1)}, u32[]{:S(2)}, u32[]{:S(2)}) collective-permute-start(s32[1024]{0:T(1024)S(1)} %bitcast.159), channel_id=1, source_target_pairs={{0,4},{1,5},{2,6},{3,7},{4,0},{5,1},{6,2},{7,3},{8,12},{9,13},{10,... | collective-permute-start | bytes 12296 | tf_op jit(solution)/shard_map/ppermute | solution.py:202
  169.0 15.0 %collective-permute-start.29 = (bf16[256,1024]{1,0:T(8,128)(2,1)}, bf16[256,1024]{1,0:T(8,128)(2,1)}, u32[]{:S(2)}, u32[]{:S(2)}) collective-permute-start(bf16[256,1024]{1,0:T(8,128)(2,1)} %get-tuple-element.273.refs_0_), channel_id=1, source_target_pairs={{0,4},{1,5},{2,6},{3,7},{4,0},{5,1},{6,2},{7,3},{8,12},{9,13},{10,... | collective-permute-start | bytes 1572872 | tf_op jit(solution)/shard_map/ppermute | solution.py:202
  199.5 6.3 %collective-permute-start.32 = (bf16[512,1024]{1,0:T(8,128)(2,1)}, bf16[512,1024]{1,0:T(8,128)(2,1)}, u32[]{:S(2)}, u32[]{:S(2)}) collective-permute-start(bf16[512,1024]{1,0:T(8,128)(2,1)} %get-tuple-element.280), channel_id=1, source_target_pairs={{0,4},{1,5},{2,6},{3,7},{4,0},{5,1},{6,2},{7,3},{8,12},{9,13},{10,... | collective-permute-start | bytes 3145736 | tf_op jit(solution)/shard_map/ppermute | solution.py:202
  201.7 50.0 %collective-permute-start.39 = (bf16[256,1024]{1,0:T(8,128)(2,1)}, bf16[256,1024]{1,0:T(8,128)(2,1)}, u32[]{:S(2)}, u32[]{:S(2)}) collective-permute-start(bf16[256,1024]{1,0:T(8,128)(2,1)} %reorder_blocks.14), channel_id=1, source_target_pairs={{2,4},{3,5},{4,2},{5,3},{10,12},{11,13},{12,10},{13,11},{18,20},{1... | collective-permute-start | bytes 1572872 | tf_op jit(solution)/shard_map/ppermute | solution.py:202
  208.2 20.3 %collective-permute-start.33 = (bf16[256,1024]{1,0:T(8,128)(2,1)}, bf16[256,1024]{1,0:T(8,128)(2,1)}, u32[]{:S(2)}, u32[]{:S(2)}) collective-permute-start(bf16[256,1024]{1,0:T(8,128)(2,1)} %add_convert_fusion.4), channel_id=1, source_target_pairs={{0,1},{1,0},{2,3},{3,2},{4,5},{5,4},{6,7},{7,6},{8,9},{9,8},{10,11... | collective-permute-start | bytes 1572872 | tf_op jit(solution)/shard_map/ppermute | solution.py:202
  210.4 205.7 %reduce-scatter.6.cloned.1.call-start = ((), (), s32[]{:S(2)}) async-start(), calls=%async_computation.8 | async-start | bytes 5242880 | tf_op jit(solution)/shard_map/reduce_scatter | solution.py:1056
  257.4 14.7 %collective-permute-start.40 = (bf16[256,1024]{1,0:T(8,128)(2,1)}, bf16[256,1024]{1,0:T(8,128)(2,1)S(1)}, u32[]{:S(2)}, u32[]{:S(2)}) collective-permute-start(bf16[256,1024]{1,0:T(8,128)(2,1)} %get-tuple-element.294.refs_0_), channel_id=1, source_target_pairs={{0,1},{1,0},{2,3},{3,2},{4,5},{5,4},{6,7},{7,6},{8,9},{9,8},{10,11... | collective-permute-start | bytes 1572872 | tf_op jit(solution)/shard_map/ppermute | solution.py:202
  258.8 14.2 %collective-permute-start.41 = (bf16[256,1024]{1,0:T(8,128)(2,1)}, bf16[256,1024]{1,0:T(8,128)(2,1)}, u32[]{:S(2)}, u32[]{:S(2)}) collective-permute-start(bf16[256,1024]{1,0:T(8,128)(2,1)} %get-tuple-element.294.refs_0_), channel_id=1, source_target_pairs={{0,4},{1,5},{2,6},{3,7},{4,0},{5,1},{6,2},{7,3},{8,12},{9,13},{10,... | collective-permute-start | bytes 1572872 | tf_op jit(solution)/shard_map/ppermute | solution.py:202
  289.8 14.0 %collective-permute-start.44 = (bf16[256,1024]{1,0:T(8,128)(2,1)S(1)}, bf16[256,1024]{1,0:T(8,128)(2,1)S(1)}, u32[]{:S(2)}, u32[]{:S(2)}) collective-permute-start(bf16[256,1024]{1,0:T(8,128)(2,1)S(1)} %add_convert_fusion.3), channel_id=1, source_target_pairs={{0,1},{1,0},{2,3},{3,2},{4,5},{5,4},{6,7},{7,6},{8,9},{9,8},{10,11... | collective-permute-start | bytes 1572872 | tf_op jit(solution)/shard_map/ppermute | solution.py:202
  311.0 13.4 %collective-permute-start.45 = (bf16[256,1024]{1,0:T(8,128)(2,1)}, bf16[256,1024]{1,0:T(8,128)(2,1)S(1)}, u32[]{:S(2)}, u32[]{:S(2)}) collective-permute-start(bf16[256,1024]{1,0:T(8,128)(2,1)} %get-tuple-element.303.refs_0_.refs_5_), channel_id=1, source_target_pairs={{0,1},{1,0},{2,3},{3,2},{4,5},{5,4},{6,7},{7,6},{8,9},{9,8},{10,11... | collective-permute-start | bytes 1572872 | tf_op jit(solution)/shard_map/ppermute | solution.py:202
  312.4 11.9 %collective-permute-start.46 = (bf16[256,1024]{1,0:T(8,128)(2,1)}, bf16[256,1024]{1,0:T(8,128)(2,1)S(1)}, u32[]{:S(2)}, u32[]{:S(2)}) collective-permute-start(bf16[256,1024]{1,0:T(8,128)(2,1)} %get-tuple-element.303.refs_0_.refs_5_), channel_id=1, source_target_pairs={{0,4},{1,5},{2,6},{3,7},{4,0},{5,1},{6,2},{7,3},{8,12},{9,13},{10,... | collective-permute-start | bytes 1572872 | tf_op jit(solution)/shard_map/ppermute | solution.py:202
  345.1 14.3 %collective-permute-start.49 = (bf16[256,1024]{1,0:T(8,128)(2,1)}, bf16[256,1024]{1,0:T(8,128)(2,1)}, u32[]{:S(2)}, u32[]{:S(2)}) collective-permute-start(bf16[256,1024]{1,0:T(8,128)(2,1)} %add_convert_fusion.2), channel_id=1, source_target_pairs={{0,1},{1,0},{2,3},{3,2},{4,5},{5,4},{6,7},{7,6},{8,9},{9,8},{10,11... | collective-permute-start | bytes 1572872 | tf_op jit(solution)/shard_map/ppermute | solution.py:202
  359.4 112.7 %reduce-scatter.8.cloned.1.call-start = ((), (), s32[]{:S(2)}) async-start(), calls=%async_computation.9 | async-start | bytes 3932160 | tf_op jit(solution)/shard_map/reduce_scatter | solution.py:1056
  377.8 16.1 %collective-permute-start.55 = (bf16[256,1024]{1,0:T(8,128)(2,1)}, bf16[256,1024]{1,0:T(8,128)(2,1)}, u32[]{:S(2)}, u32[]{:S(2)}) collective-permute-start(bf16[256,1024]{1,0:T(8,128)(2,1)} %reorder_blocks.15), channel_id=1, source_target_pairs={{2,4},{3,5},{4,2},{5,3},{10,12},{11,13},{12,10},{13,11},{18,20},{1... | collective-permute-start | bytes 1572872 | tf_op jit(solution)/shard_map/ppermute | solution.py:202
  400.6 14.1 %collective-permute-start.56 = (bf16[256,1024]{1,0:T(8,128)(2,1)}, bf16[256,1024]{1,0:T(8,128)(2,1)}, u32[]{:S(2)}, u32[]{:S(2)}) collective-permute-start(bf16[256,1024]{1,0:T(8,128)(2,1)} %get-tuple-element.321.refs_0_.refs_5_), channel_id=1, source_target_pairs={{0,1},{1,0},{2,3},{3,2},{4,5},{5,4},{6,7},{7,6},{8,9},{9,8},{10,11... | collective-permute-start | bytes 1572872 | tf_op jit(solution)/shard_map/ppermute | solution.py:202
  414.7 102.0 %reduce-scatter.10.cloned.1.call-start = ((), (), s32[]{:S(2)}) async-start(), calls=%async_computation.10 | async-start | bytes 2621440 | tf_op jit(solution)/shard_map/reduce_scatter | solution.py:1056
  418.1 26.4 %collective-permute-start.59 = (bf16[256,1024]{1,0:T(8,128)(2,1)S(1)}, bf16[256,1024]{1,0:T(8,128)(2,1)S(1)}, u32[]{:S(2)}, u32[]{:S(2)}) collective-permute-start(bf16[256,1024]{1,0:T(8,128)(2,1)S(1)} %pad_maximum_fusion.10), channel_id=1, source_target_pairs={{0,2},{1,3},{2,0},{3,1},{4,6},{5,7},{6,4},{7,5},{8,10},{9,11},{10,... | collective-permute-start | bytes 1572872 | tf_op jit(solution)/shard_map/ppermute | solution.py:202
  450.6 14.3 %collective-permute-start.61 = (bf16[256,1024]{1,0:T(8,128)(2,1)}, bf16[256,1024]{1,0:T(8,128)(2,1)}, u32[]{:S(2)}, u32[]{:S(2)}) collective-permute-start(bf16[256,1024]{1,0:T(8,128)(2,1)} %add_convert_fusion.1), channel_id=1, source_target_pairs={{0,1},{1,0},{2,3},{3,2},{4,5},{5,4},{6,7},{7,6},{8,9},{9,8},{10,11... | collective-permute-start | bytes 1572872 | tf_op jit(solution)/shard_map/ppermute | solution.py:202
  464.9 89.2 %reduce-scatter.14.cloned.1.call-start = ((), (), s32[]{:S(2)}) async-start(), calls=%async_computation.12 | async-start | bytes 2621440 | tf_op jit(solution)/shard_map/reduce_scatter | solution.py:1056
  476.4 13.5 %collective-permute-start.62 = (bf16[256,1024]{1,0:T(8,128)(2,1)}, bf16[256,1024]{1,0:T(8,128)(2,1)}, u32[]{:S(2)}, u32[]{:S(2)}) collective-permute-start(bf16[256,1024]{1,0:T(8,128)(2,1)} %get-tuple-element.341.refs_0_.refs_3_), channel_id=1, source_target_pairs={{0,1},{1,0},{2,3},{3,2},{4,5},{5,4},{6,7},{7,6},{8,9},{9,8},{10,11... | collective-permute-start | bytes 1572872 | tf_op jit(solution)/shard_map/ppermute | solution.py:202
  480.5 15.9 %collective-permute-start.63 = (bf16[256,1024]{1,0:T(8,128)(2,1)}, bf16[256,1024]{1,0:T(8,128)(2,1)}, u32[]{:S(2)}, u32[]{:S(2)}) collective-permute-start(bf16[256,1024]{1,0:T(8,128)(2,1)} %get-tuple-element.341.refs_0_.refs_3_), channel_id=1, source_target_pairs={{0,4},{1,5},{2,6},{3,7},{4,0},{5,1},{6,2},{7,3},{8,12},{9,13},{10,... | collective-permute-start | bytes 1572872 | tf_op jit(solution)/shard_map/ppermute | solution.py:202
  489.9 6.5 %collective-permute-start.64 = (bf16[256,1024]{1,0:T(8,128)(2,1)}, bf16[256,1024]{1,0:T(8,128)(2,1)}, u32[]{:S(2)}, u32[]{:S(2)}) collective-permute-start(bf16[256,1024]{1,0:T(8,128)(2,1)} %collective-permute-done.62.refs_1_.refs_4_), channel_id=1, source_target_pairs={{0,4},{1,5},{2,6},{3,7},{4,0},{5,1},{6,2},{7,3},{8,12},{9,13},{10,... | collective-permute-start | bytes 1572872 | tf_op jit(solution)/shard_map/ppermute | solution.py:202
  492.1 16.3 %collective-permute-start.65 = (bf16[256,384]{1,0:T(8,128)(2,1)}, bf16[256,384]{1,0:T(8,128)(2,1)}, u32[]{:S(2)}, u32[]{:S(2)}) collective-permute-start(bf16[256,384]{1,0:T(8,128)(2,1)} %get-tuple-element.353), channel_id=1, source_target_pairs={{0,2},{1,3},{2,0},{3,1},{4,6},{5,7},{6,4},{7,5},{8,10},{9,11},{10,... | collective-permute-start | bytes 589832 | tf_op jit(solution)/shard_map/ppermute | solution.py:202
  493.2 15.2 %collective-permute-start.66 = (bf16[256,384]{1,0:T(8,128)(2,1)}, bf16[256,384]{1,0:T(8,128)(2,1)}, u32[]{:S(2)}, u32[]{:S(2)}) collective-permute-start(bf16[256,384]{1,0:T(8,128)(2,1)} %get-tuple-element.354), channel_id=1, source_target_pairs={{0,1},{1,0},{2,3},{3,2},{4,5},{5,4},{6,7},{7,6},{8,9},{9,8},{10,11... | collective-permute-start | bytes 589832 | tf_op jit(solution)/shard_map/ppermute | solution.py:202
  494.6 14.7 %collective-permute-start.67 = (bf16[256,384]{1,0:T(8,128)(2,1)}, bf16[256,384]{1,0:T(8,128)(2,1)}, u32[]{:S(2)}, u32[]{:S(2)}) collective-permute-start(bf16[256,384]{1,0:T(8,128)(2,1)} %get-tuple-element.355), channel_id=1, source_target_pairs={{0,3},{1,2},{2,1},{3,0},{4,7},{5,6},{6,5},{7,4},{8,11},{9,10},{10,... | collective-permute-start | bytes 589832 | tf_op jit(solution)/shard_map/ppermute | solution.py:202
  509.3 7.4 %collective-permute-start.68 = (bf16[512,1024]{1,0:T(8,128)(2,1)}, bf16[512,1024]{1,0:T(8,128)(2,1)}, u32[]{:S(2)}, u32[]{:S(2)}) collective-permute-start(bf16[512,1024]{1,0:T(8,128)(2,1)} %get-tuple-element.357), channel_id=1, source_target_pairs={{0,4},{1,5},{2,6},{3,7},{4,0},{5,1},{6,2},{7,3},{8,12},{9,13},{10,... | collective-permute-start | bytes 3145736 | tf_op jit(solution)/shard_map/ppermute | solution.py:202
  516.7 93.4 %reduce-scatter.12.cloned.1.call-start = ((), (), s32[]{:S(2)}) async-start(), calls=%async_computation.11 | async-start | bytes 2621440 | tf_op jit(solution)/shard_map/reduce_scatter | solution.py:1056
  520.3 14.2 %collective-permute-start.70 = (bf16[128,1024]{1,0:T(8,128)(2,1)}, bf16[128,1024]{1,0:T(8,128)(2,1)S(1)}, u32[]{:S(2)}, u32[]{:S(2)}) collective-permute-start(bf16[128,1024]{1,0:T(8,128)(2,1)} %broadcast_select_fusion.21), channel_id=1, source_target_pairs={{0,4},{1,5},{2,6},{3,7},{4,0},{5,1},{6,2},{7,3},{8,12},{9,13},{10,... | collective-permute-start | bytes 786440 | tf_op jit(solution)/shard_map/ppermute | solution.py:202
  523.1 17.9 %collective-permute-start.69 = (bf16[256,1024]{1,0:T(8,128)(2,1)}, bf16[256,1024]{1,0:T(8,128)(2,1)}, u32[]{:S(2)}, u32[]{:S(2)}) collective-permute-start(bf16[256,1024]{1,0:T(8,128)(2,1)} %add_convert_fusion), channel_id=1, source_target_pairs={{0,1},{1,0},{2,3},{3,2},{4,5},{5,4},{6,7},{7,6},{8,9},{9,8},{10,11... | collective-permute-start | bytes 1572872 | tf_op jit(solution)/shard_map/ppermute | solution.py:202
  536.3 14.8 %collective-permute-start.71 = (bf16[128,1024]{1,0:T(8,128)(2,1)}, bf16[128,1024]{1,0:T(8,128)(2,1)}, u32[]{:S(2)}, u32[]{:S(2)}) collective-permute-start(bf16[128,1024]{1,0:T(8,128)(2,1)} %broadcast_select_fusion.7), channel_id=1, source_target_pairs={{0,2},{1,3},{2,0},{3,1},{4,6},{5,7},{6,4},{7,5},{8,10},{9,11},{10,... | collective-permute-start | bytes 786440 | tf_op jit(solution)/shard_map/ppermute | solution.py:202
  555.5 6.4 %collective-permute-start.82 = (bf16[128,384]{1,0:T(8,128)(2,1)S(1)}, bf16[128,384]{1,0:T(8,128)(2,1)S(1)}, u32[]{:S(2)}, u32[]{:S(2)}) collective-permute-start(bf16[128,384]{1,0:T(8,128)(2,1)S(1)} %broadcast_select_fusion.40), channel_id=1, source_target_pairs={{0,4},{1,5},{2,6},{3,7},{4,0},{5,1},{6,2},{7,3},{8,12},{9,13},{10,... | collective-permute-start | bytes 294920 | tf_op jit(solution)/shard_map/ppermute | solution.py:202
  557.1 6.8 %collective-permute-start.72 = (bf16[128,1024]{1,0:T(8,128)(2,1)S(1)}, bf16[128,1024]{1,0:T(8,128)(2,1)S(1)}, u32[]{:S(2)}, u32[]{:S(2)}) collective-permute-start(bf16[128,1024]{1,0:T(8,128)(2,1)S(1)} %broadcast_select_fusion.16), channel_id=1, source_target_pairs={{0,4},{1,5},{2,6},{3,7},{4,0},{5,1},{6,2},{7,3},{8,12},{9,13},{10,... | collective-permute-start | bytes 786440 | tf_op jit(solution)/shard_map/ppermute | solution.py:202
  557.6 51.6 %collective-permute-start.81 = (bf16[256,1024]{1,0:T(8,128)(2,1)}, bf16[256,1024]{1,0:T(8,128)(2,1)}, u32[]{:S(2)}, u32[]{:S(2)}) collective-permute-start(bf16[256,1024]{1,0:T(8,128)(2,1)} %reduce-scatter.14.cloned.1.call-done), channel_id=1, source_target_pairs={{0,2},{1,3},{2,0},{3,1},{4,6},{5,7},{6,4},{7,5},{8,10},{9,11},{10,... | collective-permute-start | bytes 1572872 | tf_op jit(solution)/shard_map/ppermute | solution.py:202
  580.5 11.0 %collective-permute-start.74 = (f32[17,256]{1,0:T(8,128)}, f32[17,256]{1,0:T(8,128)S(1)}, u32[]{:S(2)}, u32[]{:S(2)}) collective-permute-start(f32[17,256]{1,0:T(8,128)} %get-tuple-element.550), channel_id=1, source_target_pairs={{0,8},{1,9},{2,10},{3,11},{4,12},{5,13},{6,14},{7,15},{8,24},{9,25... | collective-permute-start | bytes 52232 | tf_op jit(solution)/shard_map/ppermute | solution.py:202
  582.0 9.6 %collective-permute-start.75 = (f32[17,256]{1,0:T(8,128)}, f32[17,256]{1,0:T(8,128)S(1)}, u32[]{:S(2)}, u32[]{:S(2)}) collective-permute-start(f32[17,256]{1,0:T(8,128)} %get-tuple-element.551), channel_id=1, source_target_pairs={{0,16},{1,17},{2,18},{3,19},{4,20},{5,21},{6,22},{7,23},{8,0},{9,1... | collective-permute-start | bytes 52232 | tf_op jit(solution)/shard_map/ppermute | solution.py:202
  590.8 18.4 %collective-permute-start.80 = (bf16[256,1024]{1,0:T(8,128)(2,1)}, bf16[256,1024]{1,0:T(8,128)(2,1)S(1)}, u32[]{:S(2)}, u32[]{:S(2)}) collective-permute-start(bf16[256,1024]{1,0:T(8,128)(2,1)} %reorder_blocks.19), channel_id=1, source_target_pairs={{2,4},{3,5},{4,2},{5,3},{10,12},{11,13},{12,10},{13,11},{18,20},{1... | collective-permute-start | bytes 1572872 | tf_op jit(solution)/shard_map/ppermute | solution.py:202
  591.6 9.3 %collective-permute-start.76 = (f32[17,128]{1,0:T(8,128)S(1)}, f32[17,128]{1,0:T(8,128)S(1)}, u32[]{:S(2)}, u32[]{:S(2)}) collective-permute-start(f32[17,128]{1,0:T(8,128)S(1)} %slice_select_fusion.2), channel_id=1, source_target_pairs={{0,4},{1,5},{2,6},{3,7},{4,0},{5,1},{6,2},{7,3},{8,12},{9,13},{10,... | collective-permute-start | bytes 26120 | tf_op jit(solution)/shard_map/ppermute | solution.py:202
  600.8 7.6 %collective-permute-start.79 = (f32[17,128]{1,0:T(8,128)S(1)}, f32[17,128]{1,0:T(8,128)S(1)}, u32[]{:S(2)}, u32[]{:S(2)}) collective-permute-start(f32[17,128]{1,0:T(8,128)S(1)} %select_add_fusion), channel_id=1, source_target_pairs={{0,3},{1,2},{2,1},{3,0},{4,7},{5,6},{6,5},{7,4},{8,11},{9,10},{10,... | collective-permute-start | bytes 26120 | tf_op jit(solution)/shard_map/ppermute | solution.py:202
  602.0 6.5 %collective-permute-start.78 = (f32[17,128]{1,0:T(8,128)S(1)}, f32[17,128]{1,0:T(8,128)S(1)}, u32[]{:S(2)}, u32[]{:S(2)}) collective-permute-start(f32[17,128]{1,0:T(8,128)S(1)} %select_add_fusion), channel_id=1, source_target_pairs={{0,2},{1,3},{2,0},{3,1},{4,6},{5,7},{6,4},{7,5},{8,10},{9,11},{10,... | collective-permute-start | bytes 26120 | tf_op jit(solution)/shard_map/ppermute | solution.py:202
  (118 other events, 595.3 us)
Sparse Core Ops, SparseCore 0:
  105.9 32.6 all-gather.3
  141.0 43.9 all-gather.5
  210.5 54.2 all-gather.7
  359.6 51.4 reduce-scatter.5
  414.8 43.3 reduce-scatter.7
  465.0 33.7 reduce-scatter.9
  516.8 37.2 reduce-scatter.13
  557.4 35.4 reduce-scatter.11

commit v5 on v4

--- a/solution.py
+++ b/solution.py
@@ -936,8 +936,7 @@
             if done is None:
                 done = work(lambda value: after(value, outgoing))
             got = send(outgoing, plan.swap_z(bit))
-            if done:
-                got, *done = together(got, *done)
+            got, own, *done = together(got, own, *done)
         return own, got, done
 
     near_z = jnp.bitwise_xor(z_low, jnp.asarray(plan.z_order(near_bits), jnp.int32))
@@ -1159,10 +1158,6 @@
 
     own, got, (attend_grads,) = row_scatter(near, away, attend_work)
     got, conv_sum = together(got, conv_sum)
-    conv_sum = apart(conv_sum, 3, n_mp)
-    conv_sum = [conv_sum[0]] + [
-        send(piece, plan.swap_z(step)) for piece, step in zip(conv_sum[1:], z_steps[1:])
-    ]
     attend_sum = chips_scatter(attend_grads)
     gradient, sent, attend_rows = norm_back(
         gradient, own, got, attend_stream, late_gains, 2, 0.5, here
@@ -1172,7 +1167,7 @@
         owned = jnp.sum(jnp.where(here[:, None] == slots[None, :], owners[None, :], 0), axis=1)
         norm_rows = jnp.concatenate([attend_rows[:2], conv_rows[:2], late_rows[:2], final_rows[:2]], axis=0)
         norm_rows = reorder_blocks(norm_rows, owned)
-        depth_rows = jnp.stack(tap_rows).reshape(KERNEL + 2, n_mp, 1, inner // 2)
+        depth_rows = after(jnp.stack([after(row, sent) for row in tap_rows]), sent).reshape(KERNEL + 2, n_mp, 1, inner // 2)
         depth_rows = jnp.take(depth_rows, z_places, axis=1)
         empty = jnp.zeros_like(depth_rows)
         depth_rows = jnp.concatenate(
@@ -1180,9 +1175,12 @@
         )
         depth_rows = jnp.pad(depth_rows.reshape(KERNEL + 2, width), ((0, 1), (0, 0)))
         depth_rows = reorder_blocks(depth_rows, here)[: KERNEL + 2]
-        return [norm_rows, depth_rows]
-
-    incoming_early, (norm_rows, depth_rows) = row_gather(sent, small_work)
+        return [norm_rows, depth_rows, *apart(after(conv_sum, sent), 3, n_mp)]
+
+    incoming_early, (norm_rows, depth_rows, *conv_sum) = row_gather(sent, small_work)
+    conv_sum = [conv_sum[0]] + [
+        send(piece, plan.swap_z(step)) for piece, step in zip(conv_sum[1:], z_steps[1:])
+    ]
     back_early, kept_early, near, away = expand_shrink_back(incoming_early, early_preact, early)
     near, away, back_early, conv_sum = together(near, away, back_early, conv_sum)
 
@@ -1205,8 +1203,9 @@
     attend_away = send(away, plan.swap_z(half))
     far_sum = chips_scatter(far_grads)
     own, outgoing = pass_on(near, got)
-    got, near_grads = together(
+    got, own, near_grads = together(
         send(outgoing, plan.swap_z(near_bits[-1])),
+        own,
         early_grad(after(back_early, outgoing), kept_early, 0),
     )
     near_sum = chips_scatter(near_grads)

time: 638 us -> 631 us (0.989)
  waiting for transfers between devices: 189 us -> 182 us
    ppermute x84, waiting for transfers between devices: 186 us -> 179 us  [send(): return lax.ppermute(value, AXES, pairs)]
    unnamed x190 -> x188, local copies, waits for them, and re-layouts: 25.2 us -> 25 us
  transfers between devices with their start and end apart: 92 -> 92, of which waited for: 41 -> 40; matrix products, arithmetic and copies ran while one was open for 20% -> 20% of each run, Pallas kernels for 24% -> 24%
where the time goes in v5:
time: 631 us; the launch traced here: 622 us
  Pallas kernels  193 us (31%)
  waiting for transfers between devices  182 us (29%)
  other arithmetic  91.8 us (15%)
  starting transfers between devices  78.6 us (12%)
  local copies, waits for them, and re-layouts  50.6 us (8%)
  between operations  16.1 us (3%)
  matrix products  10.4 us (2%)
    ppermute x84, waiting for transfers between devices, send(): return lax.ppermute(value, AXES, pairs)  179 us
    ppermute x84, starting transfers between devices, send(): return lax.ppermute(value, AXES, pairs)  77.5 us
    pallas_call x5, Pallas kernels, pair_grad(): pl.pallas_call(partial(pair_grad_kernel, each, len(left), len(other_left)...  36.1 us
    pallas_call x3, Pallas kernels, in_place(): pl.pallas_call(kernel, out_shape=outs, in_specs=[pl.BlockSpec(memory_spac...  31.7 us
    pallas_call x8, Pallas kernels, rotated_adam(): pl.pallas_call(partial(adam_kernel, turn, rate), grid=(count,), out_shape...  26 us
    unnamed x188, local copies, waits for them, and re-layouts  25 us
    pallas_call x2, Pallas kernels, expand_shrink_back(): pl.pallas_call(partial(expand_shrink_back_kernel, len(weights), each, len...  23.9 us
    pallas_call x2, Pallas kernels, expand_shrink(): pl.pallas_call(partial(expand_shrink_kernel, len(weights), each, len(full...  21.5 us
  transfers between devices with their start and end apart: 92, of which 40 were waited for; matrix products, arithmetic and copies ran while one was open for 20% of the time, Pallas kernels for 24%

profile of v5, /device:TPU:0, one launch (start us, length us, event | category | flops | bytes accessed | tf_op | source)
XLA Modules:
  0.0 621.7 jit_solution(7973440568870017620)
XLA Ops:
  8.1 4.1 collective-permute-start.2
  34.3 3.8 convert_element_type.219.right
  67.8 3.2 collective-permute-done.15
  72.3 5.6 collective-permute-done.13.refs_1_
  80.1 6.8 %collective-permute-done.20 = bf16[128,1024]{1,0:T(8,128)(2,1)S(1)} collective-permute-done((bf16[128,1024]{1,0:T(8,128)(2,1)S(1)}, bf16[128,1024]{1,0:T(8,128)(2,1)S(1)}, u32[]{:S(2)}, u32[]{:S(2)}) %collective-permute-start.20) | collective-permute-done | bytes 262176 | tf_op jit(solution)/shard_map/ppermute | solution.py:202
  88.5 6.3 %collective-permute-done.18 = bf16[128,1024]{1,0:T(8,128)(2,1)S(1)} collective-permute-done((bf16[128,1024]{1,0:T(8,128)(2,1)S(1)}, bf16[128,1024]{1,0:T(8,128)(2,1)S(1)}, u32[]{:S(2)}, u32[]{:S(2)}) %collective-permute-start.18) | collective-permute-done | bytes 262176 | tf_op jit(solution)/shard_map/ppermute | solution.py:202
  101.4 4.4 norm.1.refs_0_.refs_1_
  109.8 11.0 %expand_shrink.2 = (f32[1024,1024]{1,0:T(8,128)}, f32[512,1024]{1,0:T(8,128)}, bf16[512,1024]{1,0:T(8,128)(2,1)}) custom-call(bf16[1024,1024]{1,0:T(8,128)(2,1)} %norm.1.refs_0_.refs_1_, bf16[1024,1024]{1,0:T(8,128)(2,1)} %copy-done.74, bf16[1024,1024]{1,0:T(8,128)(2,1)} %copy-done.74, bf16[1024,1024]{1,0:T(8,128)(2,1)} %copy-done.75, ...), custom_call_target="tpu_custom_call" | custom-call | flops 4294967296 | bytes 9437184 | tf_op jit(solution)/shard_map/expand_shrink/pallas_call | solution.py:346
  121.2 4.4 collective-permute-start.22
  125.6 5.3 collective-permute-done.24.refs_3_
  130.9 5.7 collective-permute-done.23.refs_2_
  146.8 2.5 collective-permute-start.28
  149.3 2.7 convert_add_fusion.5.refs_2_
  152.0 13.1 %collective-permute-done.26.refs_3_ = bf16[256,1024]{1,0:T(8,128)(2,1)} collective-permute-done((bf16[256,1024]{1,0:T(8,128)(2,1)}, bf16[256,1024]{1,0:T(8,128)(2,1)}, u32[]{:S(2)}, u32[]{:S(2)}) %collective-permute-start.26) | collective-permute-done | bytes 524320 | tf_op jit(solution)/shard_map/ppermute | solution.py:202
  165.1 3.7 add_norm.4
  169.5 2.7 collective-permute-done.28
  172.2 11.1 %collective-permute-done.27.refs_1_ = bf16[256,1024]{1,0:T(8,128)(2,1)} collective-permute-done((bf16[256,1024]{1,0:T(8,128)(2,1)}, bf16[256,1024]{1,0:T(8,128)(2,1)}, u32[]{:S(2)}, u32[]{:S(2)}) %collective-permute-start.27) | collective-permute-done | bytes 524320 | tf_op jit(solution)/shard_map/ppermute | solution.py:202
  187.2 12.4 %attention.1 = (bf16[1024,768]{1,0:T(8,128)(2,1)}, bf16[1024,256]{1,0:T(8,128)(2,1)}, f32[1024,256]{1,0:T(8,128)}, f32[512,1024]{1,0:T(8,128)}, bf16[512,1024]{1,0:T(8,128)(2,1)}) custom-call(bf16[256,1024]{1,0:T(8,128)(2,1)} %get-tuple-element.297.refs_0_, bf16[256,1024]{1,0:T(8,128)(2,1)} %collective-permute-done.27.refs_1_, ...), custom_call_target="tpu_custom_call" | custom-call | flops 3221225472 | bytes 11042816 | tf_op jit(solution)/shard_map/attention/pallas_call | solution.py:253
  205.9 2.4 add_convert_fusion.4
  211.0 2.5 convert_add_fusion.4.refs_1_
  213.5 15.0 %collective-permute-done.33.refs_2_ = bf16[256,1024]{1,0:T(8,128)(2,1)} collective-permute-done((bf16[256,1024]{1,0:T(8,128)(2,1)}, bf16[256,1024]{1,0:T(8,128)(2,1)}, u32[]{:S(2)}, u32[]{:S(2)}) %collective-permute-start.33) | collective-permute-done | bytes 524320 | tf_op jit(solution)/shard_map/ppermute | solution.py:202
  228.5 3.0 add_norm.5
  235.5 4.3 collective-permute-done.35
  254.5 3.0 add_norm.6
  260.0 12.1 %collective-permute-done.40.refs_1_ = bf16[256,1024]{1,0:T(8,128)(2,1)S(1)} collective-permute-done((bf16[256,1024]{1,0:T(8,128)(2,1)}, bf16[256,1024]{1,0:T(8,128)(2,1)S(1)}, u32[]{:S(2)}, u32[]{:S(2)}) %collective-permute-start.40) | collective-permute-done | bytes 524320 | tf_op jit(solution)/shard_map/ppermute | solution.py:202
  275.0 10.5 %expand_shrink.3 = (f32[1024,1024]{1,0:T(8,128)}, f32[512,1024]{1,0:T(8,128)}, bf16[512,1024]{1,0:T(8,128)(2,1)}) custom-call(bf16[256,1024]{1,0:T(8,128)(2,1)} %get-tuple-element.320.refs_0_, bf16[256,1024]{1,0:T(8,128)(2,1)} %copy-done.59, bf16[256,1024]{1,0:T(8,128)(2,1)} %collective-permute-done.41.refs_2_, ...), custom_call_target="tpu_custom_call" | custom-call | flops 4294967296 | bytes 9437184 | tf_op jit(solution)/shard_map/expand_shrink/pallas_call | solution.py:346
  285.7 2.7 collective-permute-done.43
  292.4 11.4 %collective-permute-done.44.refs_2_ = bf16[256,1024]{1,0:T(8,128)(2,1)S(1)} collective-permute-done((bf16[256,1024]{1,0:T(8,128)(2,1)S(1)}, bf16[256,1024]{1,0:T(8,128)(2,1)S(1)}, u32[]{:S(2)}, u32[]{:S(2)}) %collective-permute-start.44) | collective-permute-done | bytes 524320 | tf_op jit(solution)/shard_map/ppermute | solution.py:202
  304.7 3.0 add_norm.7
  307.7 3.3 norm_back.5
  312.4 11.9 %collective-permute-done.45.refs_1_.refs_6_ = bf16[256,1024]{1,0:T(8,128)(2,1)S(1)} collective-permute-done((bf16[256,1024]{1,0:T(8,128)(2,1)}, bf16[256,1024]{1,0:T(8,128)(2,1)S(1)}, u32[]{:S(2)}, u32[]{:S(2)}) %collective-permute-start.45) | collective-permute-done | bytes 524320 | tf_op jit(solution)/shard_map/ppermute | solution.py:202
  327.1 12.0 %expand_shrink_back.2 = (bf16[1024,1024]{1,0:T(8,128)(2,1)}, bf16[1024,1024]{1,0:T(8,128)(2,1)}, f32[512,1024]{1,0:T(8,128)}, bf16[512,1024]{1,0:T(8,128)(2,1)}) custom-call(bf16[256,1024]{1,0:T(8,128)(2,1)} %get-tuple-element.331.refs_0_.refs_5_, bf16[256,1024]{1,0:T(8,128)(2,1)} %copy-done.60, bf16[256,1024]{1,0:T(8,128)(2,1)} %copy-done.61, ...), custom_call_target="tpu_custom_call" | custom-call | flops 4294967296 | bytes 13631488 | tf_op jit(solution)/shard_map/expand_shrink_back/pallas_call | solution.py:395
  339.3 2.7 collective-permute-done.48
  346.7 9.5 %pair_grad.5 = bf16[1024,2048]{1,0:T(8,128)(2,1)} custom-call(bf16[256,1024]{1,0:T(8,128)(2,1)} %get-tuple-element.320.refs_0_, bf16[256,1024]{1,0:T(8,128)(2,1)} %copy-done.59, bf16[256,1024]{1,0:T(8,128)(2,1)} %collective-permute-done.41.refs_2_, bf16[256,1024]{1,0:T(8,128)(2,1)} %collective-permute-done.42.refs_3_, ...), custom_call_target="tpu_custom_call" | custom-call | flops 4294967296 | bytes 10485760 | tf_op jit(solution)/shard_map/pair_grad/pallas_call | solution.py:444
  358.5 4.0 norm_back.6
  363.2 3.4 collective-permute-start.50
  368.0 4.1 collective-permute-done.51
  393.0 4.0 norm_back.7
  400.3 5.6 pair_grad.6
  405.9 4.6 collective-permute-done.56.refs_1_.refs_6_
  416.8 15.0 %attention_back.1 = (bf16[1024,768]{1,0:T(8,128)(2,1)}, f32[512,1024]{1,0:T(8,128)}, bf16[512,1024]{1,0:T(8,128)(2,1)}) custom-call(bf16[256,1024]{1,0:T(8,128)(2,1)} %get-tuple-element.350.refs_0_.refs_5_, bf16[256,1024]{1,0:T(8,128)(2,1)} %collective-permute-done.56.refs_1_.refs_6_, bf16[256,1024]{1,0:T(8,128)(2,1)} %collective-permute-done.57.refs_2_.refs_7_, ...), custom_call_target="tpu_custom_call" | custom-call | flops 4831838208 | bytes 12091392 | tf_op jit(solution)/shard_map/attention_back/pallas_call | solution.py:253
  431.8 8.8 %collective-permute-done.59 = bf16[256,1024]{1,0:T(8,128)(2,1)S(1)} collective-permute-done((bf16[256,1024]{1,0:T(8,128)(2,1)S(1)}, bf16[256,1024]{1,0:T(8,128)(2,1)S(1)}, u32[]{:S(2)}, u32[]{:S(2)}) %collective-permute-start.59) | collective-permute-done | bytes 524320 | tf_op jit(solution)/shard_map/ppermute | solution.py:202
  440.7 2.8 collective-permute-done.60
  444.4 2.4 add_convert_fusion.1
  446.9 7.3 %pair_grad.7 = bf16[1024,1024]{1,0:T(8,128)(2,1)} custom-call(bf16[256,1024]{1,0:T(8,128)(2,1)} %get-tuple-element.297.refs_0_, bf16[256,1024]{1,0:T(8,128)(2,1)} %collective-permute-done.27.refs_1_, bf16[256,1024]{1,0:T(8,128)(2,1)} %collective-permute-done.29.refs_2_, bf16[256,1024]{1,0:T(8,128)(2,1)} %collective-permute-done.30.refs_3_, ...), custom_call_target="tpu_custom_call" | custom-call | flops 2147483648 | bytes 7864320 | tf_op jit(solution)/shard_map/pair_grad/pallas_call | solution.py:444
  454.1 2.5 convert_add_fusion.1.refs_2_
  456.6 4.3 collective-permute-done.61.refs_3_
  462.6 4.3 fusion.21
  466.9 4.3 norm_back.8
  480.7 4.2 collective-permute-done.62.refs_1_.refs_4_
  490.1 11.9 %expand_shrink_back.3 = (bf16[1024,1024]{1,0:T(8,128)(2,1)}, bf16[1024,1024]{1,0:T(8,128)(2,1)}, f32[512,1024]{1,0:T(8,128)}, bf16[512,1024]{1,0:T(8,128)(2,1)}) custom-call(bf16[256,1024]{1,0:T(8,128)(2,1)} %get-tuple-element.371.refs_0_.refs_3_, bf16[256,1024]{1,0:T(8,128)(2,1)} %collective-permute-done.62.refs_1_.refs_4_, ...), custom_call_target="tpu_custom_call" | custom-call | flops 4294967296 | bytes 13631488 | tf_op jit(solution)/shard_map/expand_shrink_back/pallas_call | solution.py:395
  502.7 6.7 %pair_grad.8 = bf16[1024,1024]{1,0:T(8,128)(2,1)} custom-call(s32[4]{0:T(128)} %and_select_fusion.refs_0_, bf16[1024,1024]{1,0:T(8,128)(2,1)} %norm.1.refs_0_.refs_1_, bf16[1024,1024]{1,0:T(8,128)(2,1)} %get-tuple-element.409.refs_2_, bf16[256,1024]{1,0:T(8,128)(2,1)} %get-tuple-element.371.refs_0_.refs_3_, ...), custom_call_target="tpu_custom_call" | custom-call | flops 2147483648 | bytes 8388608 | tf_op jit(solution)/shard_map/pair_grad/pallas_call | solution.py:444
  515.9 4.3 collective-permute-start.69
  520.1 7.0 %pair_grad.9 = bf16[1024,1024]{1,0:T(8,128)(2,1)} custom-call(s32[4]{0:T(128)} %and_select_fusion.refs_0_, bf16[1024,1024]{1,0:T(8,128)(2,1)} %norm.1.refs_0_.refs_1_, bf16[1024,1024]{1,0:T(8,128)(2,1)} %get-tuple-element.409.refs_2_, bf16[256,1024]{1,0:T(8,128)(2,1)} %get-tuple-element.371.refs_0_.refs_3_, ...), custom_call_target="tpu_custom_call" | custom-call | flops 2147483648 | bytes 8388608 | tf_op jit(solution)/shard_map/pair_grad/pallas_call | solution.py:444
  529.4 2.5 convert_add_fusion.refs_1_
  532.8 4.0 norm_back.9
  536.8 7.1 %collective-permute-done.71 = bf16[128,1024]{1,0:T(8,128)(2,1)} collective-permute-done((bf16[128,1024]{1,0:T(8,128)(2,1)}, bf16[128,1024]{1,0:T(8,128)(2,1)}, u32[]{:S(2)}, u32[]{:S(2)}) %collective-permute-start.71) | collective-permute-done | bytes 262176 | tf_op jit(solution)/shard_map/ppermute | solution.py:202
  543.8 2.6 reduce-scatter.14.cloned.1.call-done
  549.9 2.4 collective-permute-start.81
  556.4 4.4 rotated_adam.8
  560.9 4.5 rotated_adam.9
  590.1 3.0 rotated_adam.11
  605.7 4.6 rotated_adam.15
  610.3 4.3 rotated_adam.14
  (557 shorter events, 236.8 us)
Async XLA Ops:
  7.2 178.3 %all-gather.4.cloned.1.call-start = ((), (), s32[]{:S(2)}) async-start(), calls=%async_computation.5 | async-start | bytes 2621440 | tf_op jit(solution)/shard_map/all_gather | solution.py:1052
  8.1 8.2 %collective-permute-start.2 = (bf16[17,128]{1,0:T(8,128)(2,1)S(1)}, bf16[17,128]{1,0:T(8,128)(2,1)S(1)}, u32[]{:S(2)}, u32[]{:S(2)}) collective-permute-start(bf16[17,128]{1,0:T(8,128)(2,1)S(1)} %broadcast_multiply_fusion.1), channel_id=1, source_target_pairs={{0,2},{1,3},{2,0},{3,1},{4,6},{5,7},{6,4},{7,5},{8,10},{9,11},{10,... | collective-permute-start | bytes 13064 | tf_op jit(solution)/shard_map/ppermute | solution.py:202
  21.0 26.4 %collective-permute-start.9 = (bf16[256,1024]{1,0:T(8,128)(2,1)}, bf16[256,1024]{1,0:T(8,128)(2,1)}, u32[]{:S(2)}, u32[]{:S(2)}) collective-permute-start(bf16[256,1024]{1,0:T(8,128)(2,1)} %pad_maximum_fusion.7), channel_id=1, source_target_pairs={{0,2},{1,3},{2,0},{3,1},{4,6},{5,7},{6,4},{7,5},{8,10},{9,11},{10,... | collective-permute-start | bytes 1572872 | tf_op jit(solution)/shard_map/ppermute | solution.py:202
  24.7 20.7 %collective-permute-start.8 = (bf16[272,1024]{1,0:T(8,128)(2,1)}, bf16[272,1024]{1,0:T(8,128)(2,1)}, u32[]{:S(2)}, u32[]{:S(2)}) collective-permute-start(bf16[272,1024]{1,0:T(8,128)(2,1)} %maximum_maximum_fusion), channel_id=1, source_target_pairs={{0,16},{1,17},{2,18},{3,19},{4,20},{5,21},{6,22},{7,23},{8,0},{9,1... | collective-permute-start | bytes 1671176 | tf_op jit(solution)/shard_map/ppermute | solution.py:202
  26.2 19.2 %collective-permute-start.7 = (bf16[272,1024]{1,0:T(8,128)(2,1)}, bf16[272,1024]{1,0:T(8,128)(2,1)}, u32[]{:S(2)}, u32[]{:S(2)}) collective-permute-start(bf16[272,1024]{1,0:T(8,128)(2,1)} %maximum_maximum_fusion), channel_id=1, source_target_pairs={{0,8},{1,9},{2,10},{3,11},{4,12},{5,13},{6,14},{7,15},{8,24},{9,25... | collective-permute-start | bytes 1671176 | tf_op jit(solution)/shard_map/ppermute | solution.py:202
  30.3 11.4 %collective-permute-start.4 = (bf16[128,384]{1,0:T(8,128)(2,1)}, bf16[128,384]{1,0:T(8,128)(2,1)}, u32[]{:S(2)}, u32[]{:S(2)}) collective-permute-start(bf16[128,384]{1,0:T(8,128)(2,1)} %pad_maximum_fusion.21), channel_id=1, source_target_pairs={{0,4},{1,5},{2,6},{3,7},{4,0},{5,1},{6,2},{7,3},{8,12},{9,13},{10,... | collective-permute-start | bytes 294920 | tf_op jit(solution)/shard_map/ppermute | solution.py:202
  33.7 9.8 %collective-permute-start.5 = (bf16[128,1024]{1,0:T(8,128)(2,1)}, bf16[128,1024]{1,0:T(8,128)(2,1)}, u32[]{:S(2)}, u32[]{:S(2)}) collective-permute-start(bf16[128,1024]{1,0:T(8,128)(2,1)} %pad_maximum_fusion.17), channel_id=1, source_target_pairs={{0,4},{1,5},{2,6},{3,7},{4,0},{5,1},{6,2},{7,3},{8,12},{9,13},{10,... | collective-permute-start | bytes 786440 | tf_op jit(solution)/shard_map/ppermute | solution.py:202
  47.5 14.4 %collective-permute-start.10 = (bf16[256,1024]{1,0:T(8,128)(2,1)}, bf16[256,1024]{1,0:T(8,128)(2,1)}, u32[]{:S(2)}, u32[]{:S(2)}) collective-permute-start(bf16[256,1024]{1,0:T(8,128)(2,1)} %reorder_blocks.10), channel_id=1, source_target_pairs={{2,4},{3,5},{4,2},{5,3},{10,12},{11,13},{12,10},{13,11},{18,20},{1... | collective-permute-start | bytes 1572872 | tf_op jit(solution)/shard_map/ppermute | solution.py:202
  50.9 9.5 %collective-permute-start.12 = (bf16[136,1024]{1,0:T(8,128)(2,1)S(1)}, bf16[136,1024]{1,0:T(8,128)(2,1)S(1)}, u32[]{:S(2)}, u32[]{:S(2)}) collective-permute-start(bf16[136,1024]{1,0:T(8,128)(2,1)S(1)} %slice.588), channel_id=1, source_target_pairs={{0,16},{1,17},{2,18},{3,19},{4,20},{5,21},{6,22},{7,23},{8,0},{9,1... | collective-permute-start | bytes 835592 | tf_op jit(solution)/shard_map/ppermute | solution.py:202
  52.5 9.4 %collective-permute-start.11 = (bf16[136,1024]{1,0:T(8,128)(2,1)S(1)}, bf16[136,1024]{1,0:T(8,128)(2,1)S(1)}, u32[]{:S(2)}, u32[]{:S(2)}) collective-permute-start(bf16[136,1024]{1,0:T(8,128)(2,1)S(1)} %slice.587), channel_id=1, source_target_pairs={{0,8},{1,9},{2,10},{3,11},{4,12},{5,13},{6,14},{7,15},{8,24},{9,25... | collective-permute-start | bytes 835592 | tf_op jit(solution)/shard_map/ppermute | solution.py:202
  56.3 14.7 %collective-permute-start.15 = (bf16[256,1024]{1,0:T(8,128)(2,1)}, bf16[256,1024]{1,0:T(8,128)(2,1)S(1)}, u32[]{:S(2)}, u32[]{:S(2)}) collective-permute-start(bf16[256,1024]{1,0:T(8,128)(2,1)} %collective-permute-done.9), channel_id=1, source_target_pairs={{0,16},{1,17},{2,18},{3,19},{4,20},{5,21},{6,22},{7,23},{8,0},{9,1... | collective-permute-start | bytes 1572872 | tf_op jit(solution)/shard_map/ppermute | solution.py:202
  57.9 14.4 %collective-permute-start.14 = (bf16[256,1024]{1,0:T(8,128)(2,1)}, bf16[256,1024]{1,0:T(8,128)(2,1)S(1)}, u32[]{:S(2)}, u32[]{:S(2)}) collective-permute-start(bf16[256,1024]{1,0:T(8,128)(2,1)} %collective-permute-done.9), channel_id=1, source_target_pairs={{0,8},{1,9},{2,10},{3,11},{4,12},{5,13},{6,14},{7,15},{8,24},{9,25... | collective-permute-start | bytes 1572872 | tf_op jit(solution)/shard_map/ppermute | solution.py:202
  64.2 13.6 %collective-permute-start.13 = (bf16[256,1024]{1,0:T(8,128)(2,1)}, bf16[256,1024]{1,0:T(8,128)(2,1)}, u32[]{:S(2)}, u32[]{:S(2)}) collective-permute-start(bf16[256,1024]{1,0:T(8,128)(2,1)} %get-tuple-element.523.refs_0_), channel_id=1, source_target_pairs={{0,1},{1,0},{2,3},{3,2},{4,5},{5,4},{6,7},{7,6},{8,9},{9,8},{10,11... | collective-permute-start | bytes 1572872 | tf_op jit(solution)/shard_map/ppermute | solution.py:202
  77.9 8.9 %collective-permute-start.20 = (bf16[128,1024]{1,0:T(8,128)(2,1)S(1)}, bf16[128,1024]{1,0:T(8,128)(2,1)S(1)}, u32[]{:S(2)}, u32[]{:S(2)}) collective-permute-start(bf16[128,1024]{1,0:T(8,128)(2,1)S(1)} %slice.599), channel_id=1, source_target_pairs={{0,16},{1,17},{2,18},{3,19},{4,20},{5,21},{6,22},{7,23},{8,0},{9,1... | collective-permute-start | bytes 786440 | tf_op jit(solution)/shard_map/ppermute | solution.py:202
  79.4 9.1 %collective-permute-start.19 = (bf16[128,1024]{1,0:T(8,128)(2,1)S(1)}, bf16[128,1024]{1,0:T(8,128)(2,1)S(1)}, u32[]{:S(2)}, u32[]{:S(2)}) collective-permute-start(bf16[128,1024]{1,0:T(8,128)(2,1)S(1)} %slice.598), channel_id=1, source_target_pairs={{0,8},{1,9},{2,10},{3,11},{4,12},{5,13},{6,14},{7,15},{8,24},{9,25... | collective-permute-start | bytes 786440 | tf_op jit(solution)/shard_map/ppermute | solution.py:202
  80.0 14.8 %collective-permute-start.18 = (bf16[128,1024]{1,0:T(8,128)(2,1)S(1)}, bf16[128,1024]{1,0:T(8,128)(2,1)S(1)}, u32[]{:S(2)}, u32[]{:S(2)}) collective-permute-start(bf16[128,1024]{1,0:T(8,128)(2,1)S(1)} %pad_maximum_fusion.15), channel_id=1, source_target_pairs={{0,2},{1,3},{2,0},{3,1},{4,6},{5,7},{6,4},{7,5},{8,10},{9,11},{10,... | collective-permute-start | bytes 786440 | tf_op jit(solution)/shard_map/ppermute | solution.py:202
  105.8 135.3 %all-gather.6.cloned.1.call-start = ((), (), s32[]{:S(2)}) async-start(), calls=%async_computation.6 | async-start | bytes 3932160 | tf_op jit(solution)/shard_map/all_gather | solution.py:1052
  120.8 19.8 %collective-permute-start.25 = (bf16[512,1024]{1,0:T(8,128)(2,1)}, bf16[512,1024]{1,0:T(8,128)(2,1)}, u32[]{:S(2)}, u32[]{:S(2)}) collective-permute-start(bf16[512,1024]{1,0:T(8,128)(2,1)} %get-tuple-element.290), channel_id=1, source_target_pairs={{0,4},{1,5},{2,6},{3,7},{4,0},{5,1},{6,2},{7,3},{8,12},{9,13},{10,... | collective-permute-start | bytes 3145736 | tf_op jit(solution)/shard_map/ppermute | solution.py:202
  121.2 9.7 %collective-permute-start.24 = (bf16[256,384]{1,0:T(8,128)(2,1)S(1)}, bf16[256,384]{1,0:T(8,128)(2,1)S(1)}, u32[]{:S(2)}, u32[]{:S(2)}) collective-permute-start(bf16[256,384]{1,0:T(8,128)(2,1)S(1)} %copy-done.56), channel_id=1, source_target_pairs={{0,3},{1,2},{2,1},{3,0},{4,7},{5,6},{6,5},{7,4},{8,11},{9,10},{10,... | collective-permute-start | bytes 589832 | tf_op jit(solution)/shard_map/ppermute | solution.py:202
  121.2 15.4 %collective-permute-start.23 = (bf16[256,384]{1,0:T(8,128)(2,1)S(1)}, bf16[256,384]{1,0:T(8,128)(2,1)S(1)}, u32[]{:S(2)}, u32[]{:S(2)}) collective-permute-start(bf16[256,384]{1,0:T(8,128)(2,1)S(1)} %copy-done.56), channel_id=1, source_target_pairs={{0,1},{1,0},{2,3},{3,2},{4,5},{5,4},{6,7},{7,6},{8,9},{9,8},{10,11... | collective-permute-start | bytes 589832 | tf_op jit(solution)/shard_map/ppermute | solution.py:202
  121.2 15.4 %collective-permute-start.22 = (bf16[256,384]{1,0:T(8,128)(2,1)S(1)}, bf16[256,384]{1,0:T(8,128)(2,1)S(1)}, u32[]{:S(2)}, u32[]{:S(2)}) collective-permute-start(bf16[256,384]{1,0:T(8,128)(2,1)S(1)} %copy-done.56), channel_id=1, source_target_pairs={{0,2},{1,3},{2,0},{3,1},{4,6},{5,7},{6,4},{7,5},{8,10},{9,11},{10,... | collective-permute-start | bytes 589832 | tf_op jit(solution)/shard_map/ppermute | solution.py:202
  140.3 134.7 %all-gather.8.cloned.1.call-start = ((), (), s32[]{:S(2)}) async-start(), calls=%async_computation.7 | async-start | bytes 5242880 | tf_op jit(solution)/shard_map/all_gather | solution.py:1052
  142.8 22.2 %collective-permute-start.26 = (bf16[256,1024]{1,0:T(8,128)(2,1)}, bf16[256,1024]{1,0:T(8,128)(2,1)}, u32[]{:S(2)}, u32[]{:S(2)}) collective-permute-start(bf16[256,1024]{1,0:T(8,128)(2,1)} %add_convert_fusion.5), channel_id=1, source_target_pairs={{0,1},{1,0},{2,3},{3,2},{4,5},{5,4},{6,7},{7,6},{8,9},{9,8},{10,11... | collective-permute-start | bytes 1572872 | tf_op jit(solution)/shard_map/ppermute | solution.py:202
  146.8 25.4 %collective-permute-start.28 = (bf16[256,1024]{1,0:T(8,128)(2,1)}, bf16[256,1024]{1,0:T(8,128)(2,1)}, u32[]{:S(2)}, u32[]{:S(2)}) collective-permute-start(bf16[256,1024]{1,0:T(8,128)(2,1)} %pad_maximum_fusion.8), channel_id=1, source_target_pairs={{0,2},{1,3},{2,0},{3,1},{4,6},{5,7},{6,4},{7,5},{8,10},{9,11},{10,... | collective-permute-start | bytes 1572872 | tf_op jit(solution)/shard_map/ppermute | solution.py:202
  168.8 14.5 %collective-permute-start.27 = (bf16[256,1024]{1,0:T(8,128)(2,1)}, bf16[256,1024]{1,0:T(8,128)(2,1)}, u32[]{:S(2)}, u32[]{:S(2)}) collective-permute-start(bf16[256,1024]{1,0:T(8,128)(2,1)} %get-tuple-element.297.refs_0_), channel_id=1, source_target_pairs={{0,1},{1,0},{2,3},{3,2},{4,5},{5,4},{6,7},{7,6},{8,9},{9,8},{10,11... | collective-permute-start | bytes 1572872 | tf_op jit(solution)/shard_map/ppermute | solution.py:202
  169.0 14.3 %collective-permute-start.31 = (s32[1024]{0:T(1024)S(1)}, s32[1024]{0:T(1024)S(1)}, u32[]{:S(2)}, u32[]{:S(2)}) collective-permute-start(s32[1024]{0:T(1024)S(1)} %bitcast.159), channel_id=1, source_target_pairs={{0,4},{1,5},{2,6},{3,7},{4,0},{5,1},{6,2},{7,3},{8,12},{9,13},{10,... | collective-permute-start | bytes 12296 | tf_op jit(solution)/shard_map/ppermute | solution.py:202
  169.0 15.0 %collective-permute-start.29 = (bf16[256,1024]{1,0:T(8,128)(2,1)}, bf16[256,1024]{1,0:T(8,128)(2,1)}, u32[]{:S(2)}, u32[]{:S(2)}) collective-permute-start(bf16[256,1024]{1,0:T(8,128)(2,1)} %get-tuple-element.297.refs_0_), channel_id=1, source_target_pairs={{0,4},{1,5},{2,6},{3,7},{4,0},{5,1},{6,2},{7,3},{8,12},{9,13},{10,... | collective-permute-start | bytes 1572872 | tf_op jit(solution)/shard_map/ppermute | solution.py:202
  199.6 6.3 %collective-permute-start.32 = (bf16[512,1024]{1,0:T(8,128)(2,1)}, bf16[512,1024]{1,0:T(8,128)(2,1)}, u32[]{:S(2)}, u32[]{:S(2)}) collective-permute-start(bf16[512,1024]{1,0:T(8,128)(2,1)} %get-tuple-element.304), channel_id=1, source_target_pairs={{0,4},{1,5},{2,6},{3,7},{4,0},{5,1},{6,2},{7,3},{8,12},{9,13},{10,... | collective-permute-start | bytes 3145736 | tf_op jit(solution)/shard_map/ppermute | solution.py:202
  201.7 50.0 %collective-permute-start.39 = (bf16[256,1024]{1,0:T(8,128)(2,1)}, bf16[256,1024]{1,0:T(8,128)(2,1)}, u32[]{:S(2)}, u32[]{:S(2)}) collective-permute-start(bf16[256,1024]{1,0:T(8,128)(2,1)} %reorder_blocks.14), channel_id=1, source_target_pairs={{2,4},{3,5},{4,2},{5,3},{10,12},{11,13},{12,10},{13,11},{18,20},{1... | collective-permute-start | bytes 1572872 | tf_op jit(solution)/shard_map/ppermute | solution.py:202
  208.3 20.3 %collective-permute-start.33 = (bf16[256,1024]{1,0:T(8,128)(2,1)}, bf16[256,1024]{1,0:T(8,128)(2,1)}, u32[]{:S(2)}, u32[]{:S(2)}) collective-permute-start(bf16[256,1024]{1,0:T(8,128)(2,1)} %add_convert_fusion.4), channel_id=1, source_target_pairs={{0,1},{1,0},{2,3},{3,2},{4,5},{5,4},{6,7},{7,6},{8,9},{9,8},{10,11... | collective-permute-start | bytes 1572872 | tf_op jit(solution)/shard_map/ppermute | solution.py:202
  210.4 202.2 %reduce-scatter.6.cloned.1.call-start = ((), (), s32[]{:S(2)}) async-start(), calls=%async_computation.8 | async-start | bytes 5242880 | tf_op jit(solution)/shard_map/reduce_scatter | solution.py:1055
  233.7 6.1 collective-permute-start.35
  257.4 14.7 %collective-permute-start.40 = (bf16[256,1024]{1,0:T(8,128)(2,1)}, bf16[256,1024]{1,0:T(8,128)(2,1)S(1)}, u32[]{:S(2)}, u32[]{:S(2)}) collective-permute-start(bf16[256,1024]{1,0:T(8,128)(2,1)} %get-tuple-element.320.refs_0_), channel_id=1, source_target_pairs={{0,1},{1,0},{2,3},{3,2},{4,5},{5,4},{6,7},{7,6},{8,9},{9,8},{10,11... | collective-permute-start | bytes 1572872 | tf_op jit(solution)/shard_map/ppermute | solution.py:202
  258.9 14.2 %collective-permute-start.41 = (bf16[256,1024]{1,0:T(8,128)(2,1)}, bf16[256,1024]{1,0:T(8,128)(2,1)}, u32[]{:S(2)}, u32[]{:S(2)}) collective-permute-start(bf16[256,1024]{1,0:T(8,128)(2,1)} %get-tuple-element.320.refs_0_), channel_id=1, source_target_pairs={{0,4},{1,5},{2,6},{3,7},{4,0},{5,1},{6,2},{7,3},{8,12},{9,13},{10,... | collective-permute-start | bytes 1572872 | tf_op jit(solution)/shard_map/ppermute | solution.py:202
  289.8 14.1 %collective-permute-start.44 = (bf16[256,1024]{1,0:T(8,128)(2,1)S(1)}, bf16[256,1024]{1,0:T(8,128)(2,1)S(1)}, u32[]{:S(2)}, u32[]{:S(2)}) collective-permute-start(bf16[256,1024]{1,0:T(8,128)(2,1)S(1)} %add_convert_fusion.3), channel_id=1, source_target_pairs={{0,1},{1,0},{2,3},{3,2},{4,5},{5,4},{6,7},{7,6},{8,9},{9,8},{10,11... | collective-permute-start | bytes 1572872 | tf_op jit(solution)/shard_map/ppermute | solution.py:202
  311.0 13.4 %collective-permute-start.45 = (bf16[256,1024]{1,0:T(8,128)(2,1)}, bf16[256,1024]{1,0:T(8,128)(2,1)S(1)}, u32[]{:S(2)}, u32[]{:S(2)}) collective-permute-start(bf16[256,1024]{1,0:T(8,128)(2,1)} %get-tuple-element.331.refs_0_.refs_5_), channel_id=1, source_target_pairs={{0,1},{1,0},{2,3},{3,2},{4,5},{5,4},{6,7},{7,6},{8,9},{9,8},{10,11... | collective-permute-start | bytes 1572872 | tf_op jit(solution)/shard_map/ppermute | solution.py:202
  312.4 11.9 %collective-permute-start.46 = (bf16[256,1024]{1,0:T(8,128)(2,1)}, bf16[256,1024]{1,0:T(8,128)(2,1)S(1)}, u32[]{:S(2)}, u32[]{:S(2)}) collective-permute-start(bf16[256,1024]{1,0:T(8,128)(2,1)} %get-tuple-element.331.refs_0_.refs_5_), channel_id=1, source_target_pairs={{0,4},{1,5},{2,6},{3,7},{4,0},{5,1},{6,2},{7,3},{8,12},{9,13},{10,... | collective-permute-start | bytes 1572872 | tf_op jit(solution)/shard_map/ppermute | solution.py:202
  344.2 14.3 %collective-permute-start.49 = (bf16[256,1024]{1,0:T(8,128)(2,1)}, bf16[256,1024]{1,0:T(8,128)(2,1)}, u32[]{:S(2)}, u32[]{:S(2)}) collective-permute-start(bf16[256,1024]{1,0:T(8,128)(2,1)} %add_convert_fusion.2), channel_id=1, source_target_pairs={{0,1},{1,0},{2,3},{3,2},{4,5},{5,4},{6,7},{7,6},{8,9},{9,8},{10,11... | collective-permute-start | bytes 1572872 | tf_op jit(solution)/shard_map/ppermute | solution.py:202
  358.5 108.4 %reduce-scatter.8.cloned.1.call-start = ((), (), s32[]{:S(2)}) async-start(), calls=%async_computation.9 | async-start | bytes 3932160 | tf_op jit(solution)/shard_map/reduce_scatter | solution.py:1055
  374.3 16.0 %collective-permute-start.55 = (bf16[256,1024]{1,0:T(8,128)(2,1)}, bf16[256,1024]{1,0:T(8,128)(2,1)}, u32[]{:S(2)}, u32[]{:S(2)}) collective-permute-start(bf16[256,1024]{1,0:T(8,128)(2,1)} %reorder_blocks.15), channel_id=1, source_target_pairs={{2,4},{3,5},{4,2},{5,3},{10,12},{11,13},{12,10},{13,11},{18,20},{1... | collective-permute-start | bytes 1572872 | tf_op jit(solution)/shard_map/ppermute | solution.py:202
  397.0 13.5 %collective-permute-start.56 = (bf16[256,1024]{1,0:T(8,128)(2,1)}, bf16[256,1024]{1,0:T(8,128)(2,1)}, u32[]{:S(2)}, u32[]{:S(2)}) collective-permute-start(bf16[256,1024]{1,0:T(8,128)(2,1)} %get-tuple-element.350.refs_0_.refs_5_), channel_id=1, source_target_pairs={{0,1},{1,0},{2,3},{3,2},{4,5},{5,4},{6,7},{7,6},{8,9},{9,8},{10,11... | collective-permute-start | bytes 1572872 | tf_op jit(solution)/shard_map/ppermute | solution.py:202
  410.5 99.0 %reduce-scatter.10.cloned.1.call-start = ((), (), s32[]{:S(2)}) async-start(), calls=%async_computation.10 | async-start | bytes 2621440 | tf_op jit(solution)/shard_map/reduce_scatter | solution.py:1055
  414.6 26.0 %collective-permute-start.59 = (bf16[256,1024]{1,0:T(8,128)(2,1)S(1)}, bf16[256,1024]{1,0:T(8,128)(2,1)S(1)}, u32[]{:S(2)}, u32[]{:S(2)}) collective-permute-start(bf16[256,1024]{1,0:T(8,128)(2,1)S(1)} %pad_maximum_fusion.10), channel_id=1, source_target_pairs={{0,2},{1,3},{2,0},{3,1},{4,6},{5,7},{6,4},{7,5},{8,10},{9,11},{10,... | collective-permute-start | bytes 1572872 | tf_op jit(solution)/shard_map/ppermute | solution.py:202
  446.8 14.1 %collective-permute-start.61 = (bf16[256,1024]{1,0:T(8,128)(2,1)}, bf16[256,1024]{1,0:T(8,128)(2,1)}, u32[]{:S(2)}, u32[]{:S(2)}) collective-permute-start(bf16[256,1024]{1,0:T(8,128)(2,1)} %add_convert_fusion.1), channel_id=1, source_target_pairs={{0,1},{1,0},{2,3},{3,2},{4,5},{5,4},{6,7},{7,6},{8,9},{9,8},{10,11... | collective-permute-start | bytes 1572872 | tf_op jit(solution)/shard_map/ppermute | solution.py:202
  461.0 85.5 %reduce-scatter.14.cloned.1.call-start = ((), (), s32[]{:S(2)}) async-start(), calls=%async_computation.12 | async-start | bytes 2621440 | tf_op jit(solution)/shard_map/reduce_scatter | solution.py:1055
  471.3 13.6 %collective-permute-start.62 = (bf16[256,1024]{1,0:T(8,128)(2,1)}, bf16[256,1024]{1,0:T(8,128)(2,1)}, u32[]{:S(2)}, u32[]{:S(2)}) collective-permute-start(bf16[256,1024]{1,0:T(8,128)(2,1)} %get-tuple-element.371.refs_0_.refs_3_), channel_id=1, source_target_pairs={{0,1},{1,0},{2,3},{3,2},{4,5},{5,4},{6,7},{7,6},{8,9},{9,8},{10,11... | collective-permute-start | bytes 1572872 | tf_op jit(solution)/shard_map/ppermute | solution.py:202
  472.9 16.3 %collective-permute-start.63 = (bf16[256,1024]{1,0:T(8,128)(2,1)}, bf16[256,1024]{1,0:T(8,128)(2,1)}, u32[]{:S(2)}, u32[]{:S(2)}) collective-permute-start(bf16[256,1024]{1,0:T(8,128)(2,1)} %get-tuple-element.371.refs_0_.refs_3_), channel_id=1, source_target_pairs={{0,4},{1,5},{2,6},{3,7},{4,0},{5,1},{6,2},{7,3},{8,12},{9,13},{10,... | collective-permute-start | bytes 1572872 | tf_op jit(solution)/shard_map/ppermute | solution.py:202
  484.9 17.1 %collective-permute-start.65 = (bf16[256,384]{1,0:T(8,128)(2,1)}, bf16[256,384]{1,0:T(8,128)(2,1)}, u32[]{:S(2)}, u32[]{:S(2)}) collective-permute-start(bf16[256,384]{1,0:T(8,128)(2,1)} %get-tuple-element.396), channel_id=1, source_target_pairs={{0,2},{1,3},{2,0},{3,1},{4,6},{5,7},{6,4},{7,5},{8,10},{9,11},{10,... | collective-permute-start | bytes 589832 | tf_op jit(solution)/shard_map/ppermute | solution.py:202
  485.7 16.3 %collective-permute-start.66 = (bf16[256,384]{1,0:T(8,128)(2,1)}, bf16[256,384]{1,0:T(8,128)(2,1)}, u32[]{:S(2)}, u32[]{:S(2)}) collective-permute-start(bf16[256,384]{1,0:T(8,128)(2,1)} %get-tuple-element.397), channel_id=1, source_target_pairs={{0,1},{1,0},{2,3},{3,2},{4,5},{5,4},{6,7},{7,6},{8,9},{9,8},{10,11... | collective-permute-start | bytes 589832 | tf_op jit(solution)/shard_map/ppermute | solution.py:202
  487.2 14.8 %collective-permute-start.67 = (bf16[256,384]{1,0:T(8,128)(2,1)}, bf16[256,384]{1,0:T(8,128)(2,1)}, u32[]{:S(2)}, u32[]{:S(2)}) collective-permute-start(bf16[256,384]{1,0:T(8,128)(2,1)} %get-tuple-element.398), channel_id=1, source_target_pairs={{0,3},{1,2},{2,1},{3,0},{4,7},{5,6},{6,5},{7,4},{8,11},{9,10},{10,... | collective-permute-start | bytes 589832 | tf_op jit(solution)/shard_map/ppermute | solution.py:202
  502.0 7.4 %collective-permute-start.68 = (bf16[512,1024]{1,0:T(8,128)(2,1)}, bf16[512,1024]{1,0:T(8,128)(2,1)}, u32[]{:S(2)}, u32[]{:S(2)}) collective-permute-start(bf16[512,1024]{1,0:T(8,128)(2,1)} %get-tuple-element.400), channel_id=1, source_target_pairs={{0,4},{1,5},{2,6},{3,7},{4,0},{5,1},{6,2},{7,3},{8,12},{9,13},{10,... | collective-permute-start | bytes 3145736 | tf_op jit(solution)/shard_map/ppermute | solution.py:202
  509.5 92.9 %reduce-scatter.12.cloned.1.call-start = ((), (), s32[]{:S(2)}) async-start(), calls=%async_computation.11 | async-start | bytes 2621440 | tf_op jit(solution)/shard_map/reduce_scatter | solution.py:1055
  513.1 14.1 %collective-permute-start.70 = (bf16[128,1024]{1,0:T(8,128)(2,1)}, bf16[128,1024]{1,0:T(8,128)(2,1)S(1)}, u32[]{:S(2)}, u32[]{:S(2)}) collective-permute-start(bf16[128,1024]{1,0:T(8,128)(2,1)} %broadcast_select_fusion.21), channel_id=1, source_target_pairs={{0,4},{1,5},{2,6},{3,7},{4,0},{5,1},{6,2},{7,3},{8,12},{9,13},{10,... | collective-permute-start | bytes 786440 | tf_op jit(solution)/shard_map/ppermute | solution.py:202
  515.9 16.9 %collective-permute-start.69 = (bf16[256,1024]{1,0:T(8,128)(2,1)}, bf16[256,1024]{1,0:T(8,128)(2,1)}, u32[]{:S(2)}, u32[]{:S(2)}) collective-permute-start(bf16[256,1024]{1,0:T(8,128)(2,1)} %add_convert_fusion), channel_id=1, source_target_pairs={{0,1},{1,0},{2,3},{3,2},{4,5},{5,4},{6,7},{7,6},{8,9},{9,8},{10,11... | collective-permute-start | bytes 1572872 | tf_op jit(solution)/shard_map/ppermute | solution.py:202
  528.9 14.9 %collective-permute-start.71 = (bf16[128,1024]{1,0:T(8,128)(2,1)}, bf16[128,1024]{1,0:T(8,128)(2,1)}, u32[]{:S(2)}, u32[]{:S(2)}) collective-permute-start(bf16[128,1024]{1,0:T(8,128)(2,1)} %broadcast_select_fusion.7), channel_id=1, source_target_pairs={{0,2},{1,3},{2,0},{3,1},{4,6},{5,7},{6,4},{7,5},{8,10},{9,11},{10,... | collective-permute-start | bytes 786440 | tf_op jit(solution)/shard_map/ppermute | solution.py:202
  547.8 6.4 %collective-permute-start.82 = (bf16[128,384]{1,0:T(8,128)(2,1)S(1)}, bf16[128,384]{1,0:T(8,128)(2,1)S(1)}, u32[]{:S(2)}, u32[]{:S(2)}) collective-permute-start(bf16[128,384]{1,0:T(8,128)(2,1)S(1)} %broadcast_select_fusion.40), channel_id=1, source_target_pairs={{0,4},{1,5},{2,6},{3,7},{4,0},{5,1},{6,2},{7,3},{8,12},{9,13},{10,... | collective-permute-start | bytes 294920 | tf_op jit(solution)/shard_map/ppermute | solution.py:202
  549.4 6.8 %collective-permute-start.72 = (bf16[128,1024]{1,0:T(8,128)(2,1)S(1)}, bf16[128,1024]{1,0:T(8,128)(2,1)S(1)}, u32[]{:S(2)}, u32[]{:S(2)}) collective-permute-start(bf16[128,1024]{1,0:T(8,128)(2,1)S(1)} %broadcast_select_fusion.16), channel_id=1, source_target_pairs={{0,4},{1,5},{2,6},{3,7},{4,0},{5,1},{6,2},{7,3},{8,12},{9,13},{10,... | collective-permute-start | bytes 786440 | tf_op jit(solution)/shard_map/ppermute | solution.py:202
  549.9 51.6 %collective-permute-start.81 = (bf16[256,1024]{1,0:T(8,128)(2,1)}, bf16[256,1024]{1,0:T(8,128)(2,1)}, u32[]{:S(2)}, u32[]{:S(2)}) collective-permute-start(bf16[256,1024]{1,0:T(8,128)(2,1)} %reduce-scatter.14.cloned.1.call-done), channel_id=1, source_target_pairs={{0,2},{1,3},{2,0},{3,1},{4,6},{5,7},{6,4},{7,5},{8,10},{9,11},{10,... | collective-permute-start | bytes 1572872 | tf_op jit(solution)/shard_map/ppermute | solution.py:202
  572.8 11.0 %collective-permute-start.74 = (f32[17,256]{1,0:T(8,128)}, f32[17,256]{1,0:T(8,128)S(1)}, u32[]{:S(2)}, u32[]{:S(2)}) collective-permute-start(f32[17,256]{1,0:T(8,128)} %get-tuple-element.594), channel_id=1, source_target_pairs={{0,8},{1,9},{2,10},{3,11},{4,12},{5,13},{6,14},{7,15},{8,24},{9,25... | collective-permute-start | bytes 52232 | tf_op jit(solution)/shard_map/ppermute | solution.py:202
  574.3 9.6 %collective-permute-start.75 = (f32[17,256]{1,0:T(8,128)}, f32[17,256]{1,0:T(8,128)S(1)}, u32[]{:S(2)}, u32[]{:S(2)}) collective-permute-start(f32[17,256]{1,0:T(8,128)} %get-tuple-element.595), channel_id=1, source_target_pairs={{0,16},{1,17},{2,18},{3,19},{4,20},{5,21},{6,22},{7,23},{8,0},{9,1... | collective-permute-start | bytes 52232 | tf_op jit(solution)/shard_map/ppermute | solution.py:202
  583.1 18.4 %collective-permute-start.80 = (bf16[256,1024]{1,0:T(8,128)(2,1)}, bf16[256,1024]{1,0:T(8,128)(2,1)S(1)}, u32[]{:S(2)}, u32[]{:S(2)}) collective-permute-start(bf16[256,1024]{1,0:T(8,128)(2,1)} %reorder_blocks.19), channel_id=1, source_target_pairs={{2,4},{3,5},{4,2},{5,3},{10,12},{11,13},{12,10},{13,11},{18,20},{1... | collective-permute-start | bytes 1572872 | tf_op jit(solution)/shard_map/ppermute | solution.py:202
  583.9 9.3 %collective-permute-start.76 = (f32[17,128]{1,0:T(8,128)S(1)}, f32[17,128]{1,0:T(8,128)S(1)}, u32[]{:S(2)}, u32[]{:S(2)}) collective-permute-start(f32[17,128]{1,0:T(8,128)S(1)} %slice_select_fusion.2), channel_id=1, source_target_pairs={{0,4},{1,5},{2,6},{3,7},{4,0},{5,1},{6,2},{7,3},{8,12},{9,13},{10,... | collective-permute-start | bytes 26120 | tf_op jit(solution)/shard_map/ppermute | solution.py:202
  593.2 7.6 %collective-permute-start.79 = (f32[17,128]{1,0:T(8,128)S(1)}, f32[17,128]{1,0:T(8,128)S(1)}, u32[]{:S(2)}, u32[]{:S(2)}) collective-permute-start(f32[17,128]{1,0:T(8,128)S(1)} %select_add_fusion), channel_id=1, source_target_pairs={{0,3},{1,2},{2,1},{3,0},{4,7},{5,6},{6,5},{7,4},{8,11},{9,10},{10,... | collective-permute-start | bytes 26120 | tf_op jit(solution)/shard_map/ppermute | solution.py:202
  594.3 6.5 %collective-permute-start.78 = (f32[17,128]{1,0:T(8,128)S(1)}, f32[17,128]{1,0:T(8,128)S(1)}, u32[]{:S(2)}, u32[]{:S(2)}) collective-permute-start(f32[17,128]{1,0:T(8,128)S(1)} %select_add_fusion), channel_id=1, source_target_pairs={{0,2},{1,3},{2,0},{3,1},{4,6},{5,7},{6,4},{7,5},{8,10},{9,11},{10,... | collective-permute-start | bytes 26120 | tf_op jit(solution)/shard_map/ppermute | solution.py:202
  (117 other events, 587.3 us)
Sparse Core Ops, SparseCore 0:
  105.9 32.6 all-gather.3
  141.1 43.9 all-gather.5
  210.5 54.2 all-gather.7
  358.6 51.5 reduce-scatter.5
  413.3 43.9 reduce-scatter.7
  461.1 34.4 reduce-scatter.9
  509.6 36.7 reduce-scatter.13
  549.7 35.4 reduce-scatter.11
